TPU v7x, 32 devices: a whole 2x2x4 slice. The times are simulated.
32 devices in a mesh: seq: 16 (over z, y, x), head: 2 (over core).
Axes of the slice: x: 2, y: 2, z: 4, core: 2. Of those that a mesh axis runs over, the one named last changes fastest.
Arguments:
- latents: float32 [3072, 128], P('seq'), may hold values from -6 to 6
- in_proj: bfloat16 [2, 128, 1536], replicated, may hold values from -0.5 to 0.5
- query_proj: bfloat16 [2, 1536, 256], P(None, None, 'head'), may hold values from -0.15625 to 0.15625
- key_proj: bfloat16 [2, 1536, 256], P(None, None, 'head'), may hold values from -0.15625 to 0.15625
- value_proj: bfloat16 [2, 1536, 256], P(None, None, 'head'), may hold values from -0.15625 to 0.15625
- mix_proj: bfloat16 [2, 256, 1536], P(None, 'head'), may hold values from -0.375 to 0.375
- param_proj: bfloat16 [2, 1536, 256], P(None, 'head'), may hold values from -0.15625 to 0.15625
- attn_gain: float32 [2, 1536], replicated, may hold values from 0.1 to 1.9
- param_gain: float32 [2, 1536], replicated, may hold values from 0.1 to 1.9
Outputs:
- final_latent: float32 [3072, 128], P('seq')
- token_loglik: float32 [3072], P('seq')
All inputs are finite; a program needn't handle non-finite values.
Results may differ from a plain program's by a relative error of at most 0.007.
Values may be sent and summed in bfloat16 or wider, within the bound.
No kernel may reach another device: no remote copies, remote signals or barrier semaphores. Data moves between devices by JAX's collectives and lax.ppermute only.
A program may use at most 128 MiB of HBM per device.

v0:
```python
import math

import jax
import jax.numpy as jnp
from jax import lax
from jax.sharding import PartitionSpec as P

HS = 64


score_scale = 8.0
epsilon = 1e-06


def shifted_2(shard, axis, by):
    length = lax.axis_size(axis)
    pairs = [(i, i + by) for i in range(length) if 0 <= i + by < length]
    return lax.ppermute(shard, axis, pairs)


def partner(shard, axis, apart):
    return lax.ppermute(shard, axis, [(i, i ^ 1 << apart) for i in range(lax.axis_size(axis))])


def norm_rows(value, gain):
    return value * lax.rsqrt(jnp.mean(value * value, axis=-1, keepdims=True) + epsilon) * gain


def norm_heads(value):
    return (value * lax.rsqrt(jnp.mean(value * value, axis=-1, keepdims=True) + epsilon)).astype(
        jnp.bfloat16
    )


def flow_block(rows_in, layer_index, direction, weights_all):
    in_proj, query_proj, key_proj, value_proj, mix_proj, param_proj, attn_gain, param_gain = (
        weights_all
    )
    row_count = rows_in.shape[0]
    border_src = rows_in[-1:]
    border = shifted_2(border_src, "seq", direction)
    shifted = jnp.concatenate([border, rows_in[:-1]], axis=0)
    hidden = jnp.dot(
        shifted.astype(jnp.bfloat16), in_proj[layer_index], preferred_element_type=jnp.float32
    )
    normed = norm_rows(hidden, attn_gain[layer_index]).astype(jnp.bfloat16)
    head_cols = query_proj.shape[-1]
    head_count = head_cols // HS
    queries = norm_heads(
        jnp.dot(normed, query_proj[layer_index], preferred_element_type=jnp.float32).reshape(
            row_count, head_count, HS
        )
    )
    key_rows = norm_heads(
        jnp.dot(normed, key_proj[layer_index], preferred_element_type=jnp.float32).reshape(
            row_count, head_count, HS
        )
    ).reshape(row_count, head_cols)
    value_rows = jnp.dot(
        normed, value_proj[layer_index], preferred_element_type=jnp.float32
    ).astype(jnp.bfloat16)
    first_pos = lax.axis_index("seq") * row_count
    query_pos = first_pos + jnp.arange(row_count, dtype=jnp.int32)
    initial = (
        jnp.zeros((row_count, head_count, HS), jnp.float32),
        jnp.zeros((row_count, head_count), jnp.float32),
    )
    piece_keys = lax.all_gather(key_rows, "seq", axis=0, tiled=True)
    piece_values = lax.all_gather(value_rows, "seq", axis=0, tiled=True)
    piece_rows = piece_keys.shape[0]
    key_pos = jnp.arange(piece_rows, dtype=jnp.int32)
    needed = jnp.int32(0) <= first_pos + row_count - 1
    allowed = key_pos[None, None, :] <= query_pos[None, :, None]

    def compute(current):
        scores = jnp.einsum(
            "qhd,khd->hqk",
            queries,
            piece_keys.reshape(piece_rows, head_count, HS),
            preferred_element_type=jnp.float32,
        ) * (score_scale / HS)
        weights_now = jnp.where(allowed, jnp.exp(scores), jnp.zeros_like(scores))
        denominator = jnp.transpose(jnp.sum(weights_now, axis=-1))
        numerator = jnp.einsum(
            "hqk,khd->qhd",
            weights_now.astype(jnp.bfloat16),
            piece_values.reshape(piece_rows, head_count, HS),
            preferred_element_type=jnp.float32,
        )
        return (numerator, denominator)

    numerator, denominator = lax.cond(needed, compute, lambda untouched: untouched, initial)
    attended = (
        (numerator / denominator[:, :, None]).astype(jnp.bfloat16).reshape(row_count, head_cols)
    )
    partial_mix = jnp.dot(attended, mix_proj[layer_index], preferred_element_type=jnp.float32)
    feature_width = hidden.shape[1]
    share_width = feature_width // lax.axis_size("head")
    offset = lax.axis_index("head") * share_width
    mixture = hidden + lax.psum(partial_mix, "head")
    scaled_all = norm_rows(mixture, param_gain[layer_index]).astype(jnp.bfloat16)
    scaled = lax.dynamic_slice_in_dim(scaled_all, offset, share_width, 1)
    predicted = lax.psum(
        jnp.dot(scaled, param_proj[layer_index], preferred_element_type=jnp.float32), "head"
    )
    channels = rows_in.shape[1]
    shift_mu = predicted[:, :channels]
    log_scale = 2.0 * jnp.tanh(0.5 * predicted[:, channels:])
    block_out = (rows_in - shift_mu) * jnp.exp(-log_scale)
    return (block_out, -jnp.sum(log_scale, axis=-1))


def mirror(values, per_token):
    for bit_index in range(lax.axis_size("seq").bit_length() - 1):
        values, per_token = partner((values, per_token), "seq", bit_index)
    return (jnp.flip(values, 0), jnp.flip(per_token, 0))


def body(
    latents, in_proj, query_proj, key_proj, value_proj, mix_proj, param_proj, attn_gain, param_gain
):
    weights_all = (
        in_proj,
        query_proj,
        key_proj,
        value_proj,
        mix_proj,
        param_proj,
        attn_gain,
        param_gain,
    )
    first_out, first_logdet = flow_block(latents, 0, 1, weights_all)
    flipped, flipped_logdet = mirror(first_out, first_logdet)
    second_out, second_logdet = flow_block(flipped, 1, 1, weights_all)
    final_latent, total_logdet = mirror(second_out, second_logdet + flipped_logdet)
    channels = final_latent.shape[1]
    token_loglik = (
        total_logdet - 0.5 * jnp.sum(final_latent * final_latent, axis=-1)
    ) / channels - 0.5 * math.log(2.0 * math.pi)
    return (final_latent, token_loglik)


def solution(mesh):
    placed = (
        P("seq", None),
        P(),
        P(None, None, "head"),
        P(None, None, "head"),
        P(None, None, "head"),
        P(None, "head", None),
        P(None, "head", None),
        P(),
        P(),
    )
    return jax.shard_map(
        body, mesh=mesh, in_specs=placed, out_specs=(P("seq", None), P("seq")), check_vma=False
    )
```

profile of v0, /device:TPU:0, one launch (start us, length us, event | category | flops | bytes accessed | tf_op | source)
XLA Modules:
  0.0 377.8 jit_solution(11232525199868567855)
XLA Ops:
  7.9 4.8 %collective-permute-start = (bf16[1,128]{1,0:T(2,128)(2,1)S(1)}, bf16[1,128]{1,0:T(2,128)(2,1)S(1)}, u32[]{:S(2)}, u32[]{:S(2)}) collective-permute-start(bf16[1,128]{1,0:T(2,128)(2,1)S(1)} %slice.77), channel_id=1, source_target_pairs={{0,2},{2,4},{4,6},{6,8},{8,10},{10,12},{12,14},{14,16},{16,18},{18... | collective-permute-start | bytes 776 | tf_op jit(solution)/shard_map/ppermute | solution.py:18
  20.4 43.9 %all_gather.12 = bf16[3072,128]{1,0:T(8,128)(2,1)S(1)} all-gather(bf16[192,128]{1,0:T(8,128)(2,1)S(1)} %copy.18), channel_id=1, replica_groups=mesh['seq'=16,'head'=2] {'seq'}, dimensions={0}, use_global_device_ids=true | all-gather | bytes 835584 | tf_op jit(solution)/shard_map/all_gather | solution.py:68
  65.6 40.2 %all_gather.13 = bf16[3072,128]{1,0:T(8,128)(2,1)S(1)} all-gather(bf16[192,128]{1,0:T(8,128)(2,1)S(1)} %convolution_convert_fusion.1), channel_id=1, replica_groups=mesh['seq'=16,'head'=2] {'seq'}, dimensions={0}, use_global_device_ids=true | all-gather | bytes 835584 | tf_op jit(solution)/shard_map/all_gather | solution.py:69
  106.4 8.3 %conditional.2 = (f32[192,2,64]{0,2,1:T(8,128)S(1)}, f32[192,2]{0,1:T(2,128)S(1)}) conditional(s32[]{:T(128)} %convert_element_type.48, () %tuple.24, (pred[1,192,3072]{2,1,0:T(8,128)(4,1)}, bf16[3072,128]{1,0:T(8,128)(2,1)S(1)}, bf16[192,2,64]{0,2,1:T(8,128)(2,1)}, bf16[3072,128]{1,0:T(8,128)(2,1)S(1)}) %tuple.25), branch_computations={%region_3.0_spmd, %region_4.6_spmd} | conditional | flops 306708096 | bytes 10176016 | solution.py:92
  107.6 4.3 %fusion.68 = (f32[2,192]{1,0:T(2,128)S(1)}, bf16[2,192,3072]{2,1,0:T(8,128)(2,1)}) fusion(bf16[192,2,64]{0,2,1:T(8,128)(2,1)} %get-tuple-element.17, bf16[3072,2,64]{0,2,1:T(8,128)(2,1)} %bitcast.106, pred[192,3072]{1,0:T(8,128)(4,1)} %bitcast.108), kind=kOutput, calls=%fused_computation.110 | convolution fusion | flops 155713152 | bytes 3786240 | tf_op jit(solution)/shard_map/cond/branch_1_fun/qhd,khd->hqk/dot_general | solution.py:76
  117.4 17.7 %all-reduce.5.cloned.1.call-done = f32[192,1536]{1,0:T(8,128)} async-done(((f32[192,1536]{1,0:T(8,128)}), f32[192,1536]{1,0:T(8,128)}) %all-reduce.5.cloned.1.call-update) | async-done | bytes 1179664 | tf_op jit(solution)/shard_map/psum | solution.py:100
  137.7 19.4 %all-reduce.7.cloned.1.call-done = f32[192,256]{1,0:T(8,128)} async-done(((f32[192,256]{1,0:T(8,128)}), f32[192,256]{1,0:T(8,128)}) %all-reduce.7.cloned.1.call-update) | async-done | bytes 196624 | tf_op jit(solution)/shard_map/psum | solution.py:103
  160.4 3.3 collective-permute-done.1
  165.4 2.9 collective-permute-done.2
  170.0 2.9 collective-permute-done.3
  172.9 2.9 collective-permute-start.4
  178.4 5.3 %collective-permute-start.5 = (bf16[1,128]{1,0:T(2,128)(2,1)S(1)}, bf16[1,128]{1,0:T(2,128)(2,1)}, u32[]{:S(2)}, u32[]{:S(2)}) collective-permute-start(bf16[1,128]{1,0:T(2,128)(2,1)S(1)} %slice.105), channel_id=1, source_target_pairs={{0,2},{2,4},{4,6},{6,8},{8,10},{10,12},{12,14},{14,16},{16,18},{18... | collective-permute-start | bytes 776 | tf_op jit(solution)/shard_map/ppermute | solution.py:18
  187.7 45.9 %all_gather.14 = bf16[3072,128]{1,0:T(8,128)(2,1)S(1)} all-gather(bf16[192,128]{1,0:T(8,128)(2,1)S(1)} %copy.23), channel_id=1, replica_groups=mesh['seq'=16,'head'=2] {'seq'}, dimensions={0}, use_global_device_ids=true | all-gather | bytes 835584 | tf_op jit(solution)/shard_map/all_gather | solution.py:68
  233.6 40.1 %all_gather.15 = bf16[3072,128]{1,0:T(8,128)(2,1)S(1)} all-gather(bf16[192,128]{1,0:T(8,128)(2,1)S(1)} %convolution_convert_fusion), channel_id=1, replica_groups=mesh['seq'=16,'head'=2] {'seq'}, dimensions={0}, use_global_device_ids=true | all-gather | bytes 835584 | tf_op jit(solution)/shard_map/all_gather | solution.py:69
  274.4 7.8 %conditional.3 = (f32[192,2,64]{0,2,1:T(8,128)}, f32[192,2]{0,1:T(2,128)S(1)}) conditional(s32[]{:T(128)} %convert_element_type.48, () %tuple.26, (pred[1,192,3072]{2,1,0:T(8,128)(4,1)}, bf16[3072,128]{1,0:T(8,128)(2,1)S(1)}, bf16[192,2,64]{0,2,1:T(8,128)(2,1)}, bf16[3072,128]{1,0:T(8,128)(2,1)S(1)}) %tuple.27), branch_computations={%region_12.13_spmd, %region_13.15_spmd} | conditional | flops 306708096 | bytes 10176016 | solution.py:92
  274.7 4.1 %fusion.69 = (f32[2,192]{1,0:T(2,128)S(1)}, bf16[2,192,3072]{2,1,0:T(8,128)(2,1)}) fusion(bf16[192,2,64]{0,2,1:T(8,128)(2,1)} %get-tuple-element.21, bf16[3072,2,64]{0,2,1:T(8,128)(2,1)S(1)} %bitcast.107, pred[192,3072]{1,0:T(8,128)(4,1)} %bitcast.109), kind=kOutput, calls=%fused_computation.111 | convolution fusion | flops 155713152 | bytes 3786240 | tf_op jit(solution)/shard_map/cond/branch_1_fun/qhd,khd->hqk/dot_general | solution.py:76
  279.1 3.2 fusion.7
  285.7 17.1 %all-reduce.9.cloned.1.call-done = f32[192,1536]{1,0:T(8,128)} async-done(((f32[192,1536]{1,0:T(8,128)}), f32[192,1536]{1,0:T(8,128)}) %all-reduce.9.cloned.1.call-update) | async-done | bytes 1179664 | tf_op jit(solution)/shard_map/psum | solution.py:100
  305.6 19.2 %all-reduce.11.cloned.1.call-done = f32[192,256]{1,0:T(8,128)} async-done(((f32[192,256]{1,0:T(8,128)}), f32[192,256]{1,0:T(8,128)}) %all-reduce.11.cloned.1.call-update) | async-done | bytes 196624 | tf_op jit(solution)/shard_map/psum | solution.py:103
  327.6 3.3 collective-permute-done.6
  332.6 2.9 collective-permute-done.7
  344.6 3.3 collective-permute-done.12
  362.7 3.0 collective-permute-done.16
  366.2 4.0 %collective-permute-done.17 = f32[192]{0:T(256)S(1)} collective-permute-done((f32[192]{0:T(256)S(1)}, f32[192]{0:T(256)S(1)}, u32[]{:S(2)}, u32[]{:S(2)}) %collective-permute-start.17) | collective-permute-done | bytes 800 | tf_op jit(solution)/shard_map/ppermute | solution.py:22
  (121 shorter events, 70.2 us)
Async XLA Ops:
  7.2 127.9 %all-reduce.5.cloned.1.call-start = ((), (), s32[]{:S(2)}) async-start(), calls=%async_computation | async-start | bytes 2359296 | tf_op jit(solution)/shard_map/psum | solution.py:100
  7.9 9.5 %collective-permute-start = (bf16[1,128]{1,0:T(2,128)(2,1)S(1)}, bf16[1,128]{1,0:T(2,128)(2,1)S(1)}, u32[]{:S(2)}, u32[]{:S(2)}) collective-permute-start(bf16[1,128]{1,0:T(2,128)(2,1)S(1)} %slice.77), channel_id=1, source_target_pairs={{0,2},{2,4},{4,6},{6,8},{8,10},{10,12},{12,14},{14,16},{16,18},{18... | collective-permute-start | bytes 776 | tf_op jit(solution)/shard_map/ppermute | solution.py:18
  20.4 85.4 %copy-start.4 = (f32[192,2,64]{0,2,1:T(8,128)S(1)}, f32[192,2,64]{0,2,1:T(8,128)}, u32[]{:S(2)}) copy-start(f32[192,2,64]{0,2,1:T(8,128)} %get-tuple-element.75) | copy-start | bytes 294916
  117.2 39.8 %all-reduce.7.cloned.1.call-start = ((), (), s32[]{:S(2)}) async-start(), calls=%async_computation.1 | async-start | bytes 393216 | tf_op jit(solution)/shard_map/psum | solution.py:103
  137.6 46.8 %copy-start.3 = (bf16[2,128,1536]{2,1,0:T(8,128)(2,1)S(1)}, bf16[2,128,1536]{2,1,0:T(8,128)(2,1)}, u32[]{:S(2)}) copy-start(bf16[2,128,1536]{2,1,0:T(8,128)(2,1)} %param.14) | copy-start | bytes 2359300
  137.6 165.2 %all-reduce.9.cloned.1.call-start = ((), (), s32[]{:S(2)}) async-start(), calls=%async_computation.2 | async-start | bytes 2359296 | tf_op jit(solution)/shard_map/psum | solution.py:100
  158.6 5.0 %collective-permute-start.1 = (f32[192,128]{1,0:T(8,128)S(1)}, f32[192,128]{1,0:T(8,128)S(1)}, u32[]{:S(2)}, u32[]{:S(2)}) collective-permute-start(f32[192,128]{1,0:T(8,128)S(1)} %get-tuple-element.69), channel_id=1, source_target_pairs={{0,2},{2,0},{4,6},{6,4},{8,10},{10,8},{12,14},{14,12},{16,18},{18,... | collective-permute-start | bytes 294920 | tf_op jit(solution)/shard_map/ppermute | solution.py:22
  163.6 4.6 %collective-permute-start.2 = (f32[192,128]{1,0:T(8,128)S(1)}, f32[192,128]{1,0:T(8,128)S(1)}, u32[]{:S(2)}, u32[]{:S(2)}) collective-permute-start(f32[192,128]{1,0:T(8,128)S(1)} %collective-permute-done.1), channel_id=1, source_target_pairs={{0,4},{2,6},{4,0},{6,2},{8,12},{10,14},{12,8},{14,10},{16,20},{18,... | collective-permute-start | bytes 294920 | tf_op jit(solution)/shard_map/ppermute | solution.py:22
  168.2 4.6 %collective-permute-start.3 = (f32[192,128]{1,0:T(8,128)S(1)}, f32[192,128]{1,0:T(8,128)S(1)}, u32[]{:S(2)}, u32[]{:S(2)}) collective-permute-start(f32[192,128]{1,0:T(8,128)S(1)} %collective-permute-done.2), channel_id=1, source_target_pairs={{0,8},{2,10},{4,12},{6,14},{8,0},{10,2},{12,4},{14,6},{16,24},{18,... | collective-permute-start | bytes 294920 | tf_op jit(solution)/shard_map/ppermute | solution.py:22
  172.9 5.5 %collective-permute-start.4 = (f32[192,128]{1,0:T(8,128)S(1)}, f32[192,128]{1,0:T(8,128)S(1)}, u32[]{:S(2)}, u32[]{:S(2)}) collective-permute-start(f32[192,128]{1,0:T(8,128)S(1)} %collective-permute-done.3), channel_id=1, source_target_pairs={{0,16},{2,18},{4,20},{6,22},{8,24},{10,26},{12,28},{14,30},{16,0},... | collective-permute-start | bytes 294920 | tf_op jit(solution)/shard_map/ppermute | solution.py:22
  178.4 6.0 %collective-permute-start.5 = (bf16[1,128]{1,0:T(2,128)(2,1)S(1)}, bf16[1,128]{1,0:T(2,128)(2,1)}, u32[]{:S(2)}, u32[]{:S(2)}) collective-permute-start(bf16[1,128]{1,0:T(2,128)(2,1)S(1)} %slice.105), channel_id=1, source_target_pairs={{0,2},{2,4},{4,6},{6,8},{8,10},{10,12},{12,14},{14,16},{16,18},{18... | collective-permute-start | bytes 776 | tf_op jit(solution)/shard_map/ppermute | solution.py:18
  285.6 39.2 %all-reduce.11.cloned.1.call-start = ((), (), s32[]{:S(2)}) async-start(), calls=%async_computation.3 | async-start | bytes 393216 | tf_op jit(solution)/shard_map/psum | solution.py:103
  325.8 5.1 %collective-permute-start.6 = (f32[192,128]{1,0:T(8,128)S(1)}, f32[192,128]{1,0:T(8,128)S(1)}, u32[]{:S(2)}, u32[]{:S(2)}) collective-permute-start(f32[192,128]{1,0:T(8,128)S(1)} %get-tuple-element.67), channel_id=1, source_target_pairs={{0,2},{2,0},{4,6},{6,4},{8,10},{10,8},{12,14},{14,12},{16,18},{18,... | collective-permute-start | bytes 294920 | tf_op jit(solution)/shard_map/ppermute | solution.py:22
  330.9 4.6 %collective-permute-start.7 = (f32[192,128]{1,0:T(8,128)S(1)}, f32[192,128]{1,0:T(8,128)S(1)}, u32[]{:S(2)}, u32[]{:S(2)}) collective-permute-start(f32[192,128]{1,0:T(8,128)S(1)} %collective-permute-done.6), channel_id=1, source_target_pairs={{0,4},{2,6},{4,0},{6,2},{8,12},{10,14},{12,8},{14,10},{16,20},{18,... | collective-permute-start | bytes 294920 | tf_op jit(solution)/shard_map/ppermute | solution.py:22
  335.5 17.0 %collective-permute-start.8 = (f32[192,128]{1,0:T(8,128)S(1)}, f32[192,128]{1,0:T(8,128)S(1)}, u32[]{:S(2)}, u32[]{:S(2)}) collective-permute-start(f32[192,128]{1,0:T(8,128)S(1)} %collective-permute-done.7), channel_id=1, source_target_pairs={{0,8},{2,10},{4,12},{6,14},{8,0},{10,2},{12,4},{14,6},{16,24},{18,... | collective-permute-start | bytes 294920 | tf_op jit(solution)/shard_map/ppermute | solution.py:22
  337.2 3.6 collective-permute-start.10
  340.8 3.6 collective-permute-start.11
  344.4 3.6 collective-permute-start.12
  347.9 4.5 %collective-permute-start.13 = (f32[192]{0:T(256)S(1)}, f32[192]{0:T(256)S(1)}, u32[]{:S(2)}, u32[]{:S(2)}) collective-permute-start(f32[192]{0:T(256)S(1)} %collective-permute-done.12), channel_id=1, source_target_pairs={{0,16},{2,18},{4,20},{6,22},{8,24},{10,26},{12,28},{14,30},{16,0},... | collective-permute-start | bytes 2312 | tf_op jit(solution)/shard_map/ppermute | solution.py:22
  352.5 17.8 %collective-permute-start.9 = (f32[192,128]{1,0:T(8,128)S(1)}, f32[192,128]{1,0:T(8,128)S(1)}, u32[]{:S(2)}, u32[]{:S(2)}) collective-permute-start(f32[192,128]{1,0:T(8,128)S(1)} %collective-permute-done.8), channel_id=1, source_target_pairs={{0,16},{2,18},{4,20},{6,22},{8,24},{10,26},{12,28},{14,30},{16,0},... | collective-permute-start | bytes 294920 | tf_op jit(solution)/shard_map/ppermute | solution.py:22
  355.0 3.6 collective-permute-start.14
  358.6 3.6 collective-permute-start.15
  362.1 3.6 collective-permute-start.16
  365.7 4.5 %collective-permute-start.17 = (f32[192]{0:T(256)S(1)}, f32[192]{0:T(256)S(1)}, u32[]{:S(2)}, u32[]{:S(2)}) collective-permute-start(f32[192]{0:T(256)S(1)} %collective-permute-done.16), channel_id=1, source_target_pairs={{0,16},{2,18},{4,20},{6,22},{8,24},{10,26},{12,28},{14,30},{16,0},... | collective-permute-start | bytes 2312 | tf_op jit(solution)/shard_map/ppermute | solution.py:22
  (10 other events, 104.0 us)
Sparse Core Ops, SparseCore 0:
  117.3 17.7 all-reduce.4
  137.7 19.2 all-reduce.6
  285.7 17.0 all-reduce.8
  305.5 19.2 all-reduce.10
where the time goes:
time: 379 us; the launch traced here: 378 us
  blocking collectives  170 us (45%)
  waiting for transfers between devices  112 us (30%)
  starting transfers between devices  35.7 us (9%)
  matrix products  26.9 us (7%)
  between operations  14.1 us (4%)
  other arithmetic  10.3 us (3%)
  local copies, waits for them, and re-layouts  8.73 us (2%)
    all_gather x2, blocking collectives, flow_block(): piece_keys = lax.all_gather(key_rows, 'seq', axis=0, tiled=True)  89.8 us
    all_gather x2, blocking collectives, flow_block(): piece_values = lax.all_gather(value_rows, 'seq', axis=0, tiled=True)  80.3 us
    psum x2, waiting for transfers between devices, flow_block(): lax.psum(jnp.dot(scaled, param_proj[layer_index], preferred_element_type=...  38.5 us
    ppermute x16, waiting for transfers between devices, partner(): lax.ppermute(shard, axis, [(i, i ^ 1 << apart) for i in range(lax.axis_si...  38.5 us
    psum x2, waiting for transfers between devices, flow_block(): mixture = hidden + lax.psum(partial_mix, 'head')  34.8 us
    ppermute x16, starting transfers between devices, partner(): lax.ppermute(shard, axis, [(i, i ^ 1 << apart) for i in range(lax.axis_si...  25.5 us
    ppermute x2, starting transfers between devices, shifted_2(): return lax.ppermute(shard, axis, pairs)  10.1 us
    dot_general x2, matrix products, compute(): jnp.einsum('qhd,khd->hqk', queries, piece_keys.reshape(piece_rows, head_c...  8.4 us
  transfers between devices with their start and end apart: 22, of which 18 were waited for; matrix products, arithmetic and copies ran while one was open for 2% of the time, Pallas kernels for 0%

commit v1 on v0

v1 whole, which is shorter than its diff:
```python
import functools
import math

import jax
import jax.numpy as jnp
import numpy as np
from jax import lax
from jax.experimental import pallas as pl
from jax.experimental.pallas import tpu as pltpu
from jax.sharding import PartitionSpec as P

HS = 64
GROUP = 256

score_scale = 8.0
epsilon = 1e-06

VMEM_LIMIT = 56 * 1024 * 1024


def dot(a, b):
    return jnp.dot(a, b, preferred_element_type=jnp.float32)


def dot_nt(a, b):
    return lax.dot_general(a, b, (((1,), (1,)), ((), ())), preferred_element_type=jnp.float32)


def cat(parts, axis):
    return parts[0] if len(parts) == 1 else jnp.concatenate(parts, axis=axis)


def combine_kernel(pieces, in_ref, gain_ref, *refs):
    key_refs, value_refs, out_ref = refs[:pieces], refs[pieces : 2 * pieces], refs[2 * pieces]
    block = pl.program_id(0)
    base = in_ref[0]
    channels = base.shape[0]
    scaled = base.astype(jnp.float32) * gain_ref[pl.ds(block, 1), :]
    high = scaled.astype(jnp.bfloat16)
    low = (scaled - high.astype(jnp.float32)).astype(jnp.bfloat16)
    both = jnp.concatenate([high, low], axis=0)
    row = 0
    for group in (key_refs, value_refs):
        for first in range(0, pieces, 2):
            columns = cat([ref[0] for ref in group[first : first + 2]], 1)
            product = dot(both, columns)
            product = product[:channels] + product[channels:]
            width = product.shape[1]
            out_ref[0, row : row + width, :] = product.T.astype(jnp.bfloat16)
            row += width
    gram = dot_nt(base, base)
    gram_high = gram.astype(jnp.bfloat16)
    out_ref[0, row : row + channels, :] = gram_high
    row += channels
    out_ref[0, row : row + channels, :] = (gram - gram_high.astype(jnp.float32)).astype(
        jnp.bfloat16
    )
    row += channels
    eye = lax.broadcasted_iota(jnp.int32, (channels, channels), 0) == lax.broadcasted_iota(
        jnp.int32, (channels, channels), 1
    )
    out_ref[0, row : row + channels, :] = jnp.where(eye, 1.0, 0.0).astype(jnp.bfloat16)


def combine(in_proj, attn_gain, key_pieces, value_pieces):
    pieces = len(key_pieces)
    layers, channels, features = in_proj.shape
    head_cols = key_pieces[0].shape[2]
    rows = 2 * pieces * head_cols + 3 * channels
    piece = pl.BlockSpec((1, features, head_cols), lambda b: (b, 0, 0))
    return pl.pallas_call(
        functools.partial(combine_kernel, pieces),
        grid=(layers,),
        in_specs=[
            pl.BlockSpec((1, channels, features), lambda b: (b, 0, 0)),
            pl.BlockSpec((layers, features), lambda b: (0, 0)),
        ]
        + [piece] * (2 * pieces),
        out_specs=pl.BlockSpec((1, rows, channels), lambda b: (b, 0, 0)),
        out_shape=jax.ShapeDtypeStruct((layers, rows, channels), jnp.bfloat16),
        compiler_params=pltpu.CompilerParams(vmem_limit_bytes=VMEM_LIMIT),
        name="combine",
    )(in_proj, attn_gain, *key_pieces, *value_pieces)


def block_kernel(cfg, place_ref, pos_ref, rows_ref, own_ref, other_ref, maps_ref, in_ref, again_ref, pgain_ref, *refs):
    layer, pieces, last = cfg["layer"], cfg["pieces"], cfg["last"]
    refs = list(refs)
    query_refs = [refs.pop(0) for _ in range(pieces)]
    mix_refs = [refs.pop(0) for _ in range(pieces)]
    param_refs = [refs.pop(0) for _ in range(pieces)]
    if last:
        first_log_ref, out_ref, param_ref = refs
    else:
        out_ref, log_ref, spread_ref, param_ref = refs
    side, member = place_ref[0], place_ref[1]
    first_token, border_row, border_on = place_ref[2], place_ref[3], place_ref[4]
    channels = own_ref.shape[1]
    features = in_ref.shape[2]
    count = cfg["count"]
    forward = layer == 0

    if last:
        values = rows_ref[...]
    else:
        values = rows_ref[pl.ds(pl.multiple_of(side * count, 8), count), :]
    window = other_ref[pl.ds(pl.multiple_of(border_row, 16), 16), :].astype(jnp.float32)
    border = window[15:16] if forward else window[0:1]
    border = jnp.where(border_on > 0, border, jnp.zeros_like(border))
    token = lax.broadcasted_iota(jnp.int32, (count, 1), 0)
    edge = 0 if forward else count - 1
    moved = pltpu.roll(values, 1 if forward else count - 1, 0)
    shifted = jnp.where(token == edge, border, moved).astype(jnp.bfloat16)

    hidden = dot(shifted, in_ref[0])
    spread = lax.rsqrt(jnp.mean(hidden * hidden, axis=1, keepdims=True) + epsilon)
    normed = (hidden * spread * again_ref[layer : layer + 1, :]).astype(jnp.bfloat16)

    head_cols = query_refs[0].shape[2]
    groups = []
    for first in range(0, pieces, 2):
        query = dot(normed, cat([ref[0] for ref in query_refs[first : first + 2]], 1))
        width = query.shape[1]
        head = lax.broadcasted_iota(jnp.int32, (count, width), 1) // HS
        bands = []
        for h in range(width // HS):
            band = jnp.where(head == h, query, 0.0)
            mean = jnp.sum(band * band, axis=1, keepdims=True) * (1.0 / HS)
            bands.append((band * lax.rsqrt(mean + epsilon)).astype(jnp.bfloat16))
        groups.append((cat(bands, 0), width))
    total_cols = pieces * head_cols
    group_cols = groups[0][1]
    heads = group_cols // HS
    query_token = first_token + jnp.concatenate([token] * heads, axis=0)

    def one_chunk(source_ref, start, offset, carry):
        source = source_ref[pl.ds(start, cfg["chunk"]), :]
        key_token = pos_ref[:, pl.ds(start, cfg["chunk"])] + offset
        allowed = key_token < query_token if forward else key_token > query_token
        tail = dot_nt(maps_ref[0, 2 * total_cols :, :], source)
        gram = tail[:channels] + tail[channels : 2 * channels]
        square = jnp.sum(gram * tail[2 * channels :], axis=0, keepdims=True)
        scale = lax.rsqrt(jnp.maximum(square, 0.0) * (1.0 / features) + epsilon)
        scale_sq = scale * scale
        result = []
        for g, (queries, width) in enumerate(groups):
            low = g * group_cols
            key = dot_nt(maps_ref[0, low : low + width, :], source)
            value = dot_nt(maps_ref[0, total_cols + low : total_cols + low + width, :], source)
            scaled_keys = []
            for h in range(width // HS):
                one = key[h * HS : (h + 1) * HS]
                mean = jnp.sum(one * one, axis=0, keepdims=True) * (1.0 / HS)
                factor = scale * lax.rsqrt(mean * scale_sq + epsilon)
                scaled_keys.append((one * factor).astype(jnp.bfloat16))
            keys = jnp.concatenate(scaled_keys, axis=0)
            value = (value * scale).astype(jnp.bfloat16)
            scores = dot(queries, keys) * (score_scale / HS)
            weights = jnp.where(allowed, jnp.exp(scores), 0.0)
            numerator, denominator = carry[g]
            denominator = denominator + jnp.sum(weights, axis=1, keepdims=True)
            numerator = numerator + dot_nt(weights.astype(jnp.bfloat16), value)
            result.append((numerator, denominator))
        return tuple(result)

    carry = tuple(
        (
            jnp.zeros((heads * count, width), jnp.float32),
            jnp.ones((heads * count, 1), jnp.float32),
        )
        for _, width in groups
    )
    chunks = own_ref.shape[0] // cfg["chunk"]
    for source_ref, offset in ((own_ref, side * count), (other_ref, (1 - side) * count)):
        if chunks <= 4:
            for c in range(chunks):
                carry = one_chunk(source_ref, c * cfg["chunk"], offset, carry)
        else:
            carry = lax.fori_loop(
                0,
                chunks,
                lambda c, now: one_chunk(
                    source_ref, pl.multiple_of(c * cfg["chunk"], cfg["chunk"]), offset, now
                ),
                carry,
            )

    mixture = hidden
    for g, (numerator, denominator) in enumerate(carry):
        head = lax.broadcasted_iota(jnp.int32, (count, group_cols), 1) // HS
        attended = jnp.zeros((count, group_cols), jnp.float32)
        for h in range(heads):
            band = slice(h * count, (h + 1) * count)
            attended = jnp.where(head == h, numerator[band] / denominator[band], attended)
        mixture = mixture + dot(
            attended.astype(jnp.bfloat16), cat([ref[0] for ref in mix_refs[2 * g : 2 * g + 2]], 0)
        )
    spread = lax.rsqrt(jnp.mean(mixture * mixture, axis=1, keepdims=True) + epsilon)
    scaled = (mixture * spread * pgain_ref[layer : layer + 1, :]).astype(jnp.bfloat16)
    share = features // pieces
    for j, ref in enumerate(param_refs):
        param_ref[pl.ds(pl.multiple_of(place_ref[5 + j] * share, 16), share), :] = ref[0]
    predicted = dot(scaled, param_ref[...])
    log_scale = 2.0 * jnp.tanh(0.5 * predicted[:, channels:])
    result = (values - predicted[:, :channels]) * jnp.exp(-log_scale)
    if last:
        term = -(first_log_ref[...] + log_scale) - 0.5 * (result * result)
        loglik = jnp.sum(term.T, axis=0, keepdims=True) * (1.0 / channels) - 0.5 * math.log(
            2.0 * math.pi
        )
        out_ref[:count, :] = result
        out_ref[count:, :count] = jnp.broadcast_to(loglik, (8, count))
    else:
        out_ref[...] = result
        log_ref[...] = log_scale
        narrow = result.astype(jnp.bfloat16)
        for i in range(spread_ref.shape[0]):
            spread_ref[i] = narrow


def run_block(layer, members, count, place, positions, rows, own, other, maps, in_proj, attn_gain, param_gain, query_pieces, mix_pieces, param_pieces, first_log=None):
    pieces = len(query_pieces)
    layers, channels, features = in_proj.shape
    last = first_log is not None
    chunk = next(size for size in (512, 384, 256, 192, 128, own.shape[0]) if own.shape[0] % size == 0)

    def full(array):
        return pl.BlockSpec(array.shape, lambda i: (0,) * array.ndim)

    def one_layer(array):
        return pl.BlockSpec((1,) + array.shape[1:], lambda i: (layer, 0, 0))

    stacked = list(query_pieces) + list(mix_pieces) + list(param_pieces)
    in_specs = (
        [pl.BlockSpec(memory_space=pltpu.SMEM)]
        + [full(array) for array in (positions, rows, own, other)]
        + [one_layer(maps), one_layer(in_proj), full(attn_gain), full(param_gain)]
        + [one_layer(array) for array in stacked]
    )
    operands = [place, positions, rows, own, other, maps, in_proj, attn_gain, param_gain] + stacked
    if last:
        in_specs.append(full(first_log))
        operands.append(first_log)
        out_shape = jax.ShapeDtypeStruct((count + 8, channels), jnp.float32)
        out_specs = pl.BlockSpec((count + 8, channels), lambda i: (0, 0))
    else:
        out_shape = (
            jax.ShapeDtypeStruct((count, channels), jnp.float32),
            jax.ShapeDtypeStruct((count, channels), jnp.float32),
            jax.ShapeDtypeStruct((members, count, channels), jnp.bfloat16),
        )
        out_specs = tuple(
            pl.BlockSpec(s.shape, lambda i, n=len(s.shape): (0,) * n) for s in out_shape
        )
    cfg = {"layer": layer, "pieces": pieces, "last": last, "count": count, "chunk": chunk}
    return pl.pallas_call(
        functools.partial(block_kernel, cfg),
        grid=(1,),
        in_specs=in_specs,
        out_specs=out_specs,
        out_shape=out_shape,
        scratch_shapes=[pltpu.VMEM((features, param_pieces[0].shape[2]), jnp.bfloat16)],
        compiler_params=pltpu.CompilerParams(vmem_limit_bytes=VMEM_LIMIT),
        name="flow_block",
    )(*operands)


def body(
    latents, in_proj, query_proj, key_proj, value_proj, mix_proj, param_proj, attn_gain, param_gain
):
    members, ways = lax.axis_size("seq"), lax.axis_size("head")
    rows, channels = latents.shape
    count = rows // 2
    member, way = lax.axis_index("seq"), lax.axis_index("head")
    side = way % 2

    def swap(array):
        return lax.ppermute(array, "head", [(i, i ^ 1) for i in range(ways)])

    def pieces_of(array):
        shares = [array]
        for j in range(1, ways):
            shares.append(
                lax.ppermute(array, "head", [((i + j) % ways, i) for i in range(ways)])
            )
        return shares

    key_pieces, value_pieces = pieces_of(key_proj), pieces_of(value_proj)
    query_pieces, mix_pieces = pieces_of(query_proj), pieces_of(mix_proj)
    param_pieces = pieces_of(param_proj)

    def gather(spread):
        return lax.all_to_all(spread, "seq", 0, 0).reshape(members * count, channels)

    positions = jnp.asarray(
        (np.arange(members * count) // count * rows + np.arange(members * count) % count)[None],
        jnp.int32,
    )
    first_token = member * rows + side * count
    owners = [(way + j) % ways for j in range(ways)]

    def place(layer):
        if layer == 0:
            group = member - 1 + side
            on = group >= 0
            border_row = jnp.maximum(group, 0) * count + count - 16
        else:
            group = member + side
            on = group < members
            border_row = jnp.minimum(group, members - 1) * count
        entries = [side, member, first_token, border_row, on] + owners
        return jnp.stack([jnp.asarray(e, jnp.int32) for e in entries])

    own_rows = lax.dynamic_slice_in_dim(latents, side * count, count, 0).astype(jnp.bfloat16)
    own = gather(jnp.broadcast_to(own_rows[None], (members, count, channels)))
    other = swap(own)
    maps = combine(in_proj, attn_gain, key_pieces, value_pieces)
    shared = (maps, in_proj, attn_gain, param_gain, query_pieces, mix_pieces, param_pieces)
    first_out, first_log, spread = run_block(
        0, members, count, place(0), positions, latents, own, other, *shared
    )
    own = gather(spread)
    other = swap(own)
    packed = run_block(
        1, members, count, place(1), positions, first_out, own, other, *shared, first_log=first_log
    )
    packed_other = swap(packed)
    low = jnp.where(side == 0, packed, packed_other)
    high = jnp.where(side == 0, packed_other, packed)
    final_latent = jnp.concatenate([low[:count], high[:count]], axis=0)
    token_loglik = jnp.concatenate([low[count, :count], high[count, :count]], axis=0)
    return (final_latent, token_loglik)


def solution(mesh):
    placed = (
        P("seq", None),
        P(),
        P(None, None, "head"),
        P(None, None, "head"),
        P(None, None, "head"),
        P(None, "head", None),
        P(None, "head", None),
        P(),
        P(),
    )
    return jax.shard_map(
        body, mesh=mesh, in_specs=placed, out_specs=(P("seq", None), P("seq")), check_vma=False
    )
```

time: 379 us -> 68.1 us (0.18)
  blocking collectives: 170 us -> 16.8 us
  waiting for transfers between devices: 112 us -> 14.5 us
  matrix products: 26.9 us -> 0 us
  starting transfers between devices: 35.7 us -> 9.71 us
  Pallas kernels: 0 us -> 18.8 us
  between operations: 14.1 us -> 0.76 us
  other arithmetic: 10.3 us -> 2.1 us
    all_gather x4 -> x0, blocking collectives: 170 us -> none  [the longest x2 89.8 us: flow_block(): piece_keys = lax.all_gather(key_rows, 'seq', axis=0, tiled=True)]
    psum x4 -> x0, waiting for transfers between devices: 73.3 us -> none  [the longest x2 38.5 us: flow_block(): lax.psum(jnp.dot(scaled, param_proj[layer_index], preferred_element_type=...]
    ppermute x18 -> x8, waiting for transfers between devices: 38.5 us -> 2.38 us  [the longest x3 2.37 us: swap(): return lax.ppermute(array, 'head', [(i, i ^ 1) for i in range(ways)])]
    ppermute x18 -> x8, starting transfers between devices: 35.6 us -> 1.75 us  [the longest x5 1.6 us: pieces_of(): lax.ppermute(array, 'head', [((i + j) % ways, i) for i in range(ways)])]
    dot_general x16 -> x0, matrix products: 26.9 us -> none  [the longest x2 8.4 us: compute(): jnp.einsum('qhd,khd->hqk', queries, piece_keys.reshape(piece_rows, head_c...]
    pallas_call x0 -> x3, Pallas kernels: none -> 18.8 us  [the longest x2 14.9 us: run_block(): pl.pallas_call(functools.partial(block_kernel, cfg), grid=(1,), in_specs=...]
    all_to_all x0 -> x1, blocking collectives: none -> 16.8 us  [gather(): lax.all_to_all(spread, 'seq', 0, 0).reshape(members * count, channels)]
    all_to_all x0 -> x1, waiting for transfers between devices: none -> 12.1 us  [gather(): lax.all_to_all(spread, 'seq', 0, 0).reshape(members * count, channels)]
  transfers between devices with their start and end apart: 22 -> 9, of which waited for: 18 -> 3; matrix products, arithmetic and copies ran while one was open for 2% -> 4% of each run, Pallas kernels for 0% -> 6%
where the time goes in v1:
time: 68.1 us; the launch traced here: 67.7 us
  Pallas kernels  18.8 us (28%)
  blocking collectives  16.8 us (25%)
  waiting for transfers between devices  14.5 us (21%)
  starting transfers between devices  9.71 us (14%)
  local copies, waits for them, and re-layouts  5.02 us (7%)
  other arithmetic  2.1 us (3%)
  between operations  0.76 us (1%)
    all_to_all x1, blocking collectives, gather(): lax.all_to_all(spread, 'seq', 0, 0).reshape(members * count, channels)  16.8 us
    pallas_call x2, Pallas kernels, run_block(): pl.pallas_call(functools.partial(block_kernel, cfg), grid=(1,), in_specs=...  14.9 us
    all_to_all x1, waiting for transfers between devices, gather(): lax.all_to_all(spread, 'seq', 0, 0).reshape(members * count, channels)  12.1 us
    all_to_all x1, starting transfers between devices, gather(): lax.all_to_all(spread, 'seq', 0, 0).reshape(members * count, channels)  7.97 us
    pallas_call x1, Pallas kernels, combine(): pl.pallas_call(functools.partial(combine_kernel, pieces), grid=(layers,),...  3.94 us
    ppermute x3, waiting for transfers between devices, swap(): return lax.ppermute(array, 'head', [(i, i ^ 1) for i in range(ways)])  2.37 us
    unnamed x14, local copies, waits for them, and re-layouts  2.12 us
    ppermute x5, starting transfers between devices, pieces_of(): lax.ppermute(array, 'head', [((i + j) % ways, i) for i in range(ways)])  1.6 us
  transfers between devices with their start and end apart: 9, of which 3 were waited for; matrix products, arithmetic and copies ran while one was open for 4% of the time, Pallas kernels for 6%

profile of v1, /device:TPU:0, one launch (start us, length us, event | category | flops | bytes accessed | tf_op | source)
XLA Modules:
  0.0 67.7 jit_solution(15012408370402627306)
XLA Ops:
  0.6 0.5 collective-permute-start.1
  1.2 0.8 %dynamic-slice_convert_fusion = bf16[96,128]{1,0:T(8,128)(2,1)S(1)} fusion(f32[192,128]{1,0:T(8,128)} %rows_ref.1, s32[]{:T(128)S(6)} %select_n.31), kind=kLoop, calls=%fused_computation.1 | loop fusion | bytes 49156 | tf_op jit(solution)/shard_map/convert_element_type | solution.py:314
  2.0 0.8 %broadcast_in_dim.2 = bf16[16,96,128]{2,1,0:T(8,128)(2,1)} broadcast(bf16[96,128]{1,0:T(8,128)(2,1)S(1)} %dynamic-slice_convert_fusion), dimensions={1,2} | broadcast | bytes 417792 | tf_op jit(solution)/shard_map/broadcast_in_dim | solution.py:315
  2.8 8.0 %all-to-all-start = ((bf16[16,96,128]{2,1,0:T(8,128)(2,1)}), bf16[16,96,128]{2,1,0:T(8,128)(2,1)S(1)}, u32[]{:S(2)}, u32[]{:S(2)}) async-start(bf16[16,96,128]{2,1,0:T(8,128)(2,1)} %broadcast_in_dim.2), calls=%async_computation | async-start | bytes 786432 | tf_op jit(solution)/shard_map/all_to_all | solution.py:293
  10.7 0.2 collective-permute-start.2
  11.0 0.4 collective-permute-start.3
  11.3 0.1 collective-permute-start.4
  11.5 0.4 collective-permute-start.5
  11.8 12.1 %all-to-all-done = bf16[16,96,128]{2,1,0:T(8,128)(2,1)S(1)} async-done(((bf16[16,96,128]{2,1,0:T(8,128)(2,1)}), bf16[16,96,128]{2,1,0:T(8,128)(2,1)S(1)}, u32[]{:S(2)}, u32[]{:S(2)}) %all-to-all-start) | async-done | bytes 393248 | tf_op jit(solution)/shard_map/all_to_all | solution.py:293
  24.0 0.6 stack.53.place_ref
  24.6 3.9 %combine.1.maps_ref = bf16[2,896,128]{2,1,0:T(8,128)(2,1)} custom-call(bf16[2,128,1536]{2,1,0:T(8,128)(2,1)} %in_ref.5, f32[2,1536]{1,0:T(2,128)} %again_ref.3, bf16[2,1536,128]{2,1,0:T(8,128)(2,1)} %refs_0_.3, bf16[2,1536,128]{2,1,0:T(8,128)(2,1)} %collective-permute-done.1.refs_1_, bf16[2,1536,128]{2,1,0:T(8,128)(2,1)} %refs_2_.3, ...), custom_call_target="tpu_custom_call" | custom-call | tf_op jit(solution)/shard_map/combine/pallas_call | solution.py:71
  28.6 0.8 %copy-done.1 = bf16[2,1536,128]{2,1,0:T(8,128)(2,1)} copy-done((bf16[2,1536,128]{2,1,0:T(8,128)(2,1)}, bf16[2,1536,128]{2,1,0:T(8,128)(2,1)S(1)}, u32[]{:S(2)}) %copy-start.1) | copy-done | bytes 786456
  29.4 0.3 copy-done.2
  29.7 0.2 copy-done.3
  30.0 7.5 %flow_block.2 = (f32[96,128]{1,0:T(8,128)}, f32[96,128]{1,0:T(8,128)}, bf16[16,96,128]{2,1,0:T(8,128)(2,1)}) custom-call(s32[7]{0:T(128)} %stack.53.place_ref, s32[1,1536]{1,0:T(1,128)} %constant.44.clone.pos_ref, f32[192,128]{1,0:T(8,128)} %rows_ref.1, bf16[1536,128]{1,0:T(8,128)(2,1)} %bitcast.15, bf16[1536,128]{1,0:T(8,128)(2,1)} %collective-permute-done.other_ref, ...), custom_call_target="tpu_custom_call" | custom-call | tf_op jit(solution)/shard_map/flow_block/pallas_call | solution.py:256
  37.4 16.8 %all_to_all.10 = bf16[16,96,128]{2,1,0:T(8,128)(2,1)S(1)} all-to-all(bf16[16,96,128]{2,1,0:T(8,128)(2,1)} %get-tuple-element.6), channel_id=1, replica_groups=mesh['seq'=16,'head'=2] {'seq'}, dimensions={0} | all-to-all | bytes 786432 | tf_op jit(solution)/shard_map/all_to_all | solution.py:293
  54.2 0.7 stack.49.place_ref
  54.9 1.1 %collective-permute-done.6.other_ref = bf16[1536,128]{1,0:T(8,128)(2,1)S(1)} collective-permute-done((bf16[1536,128]{1,0:T(8,128)(2,1)S(1)}, bf16[1536,128]{1,0:T(8,128)(2,1)S(1)}, u32[]{:S(2)}, u32[]{:S(2)}) %collective-permute-start.6) | collective-permute-done | bytes 393248 | tf_op jit(solution)/shard_map/ppermute | solution.py:278
  55.9 0.7 %copy-done.6 = bf16[1536,128]{1,0:T(8,128)(2,1)} copy-done((bf16[1536,128]{1,0:T(8,128)(2,1)}, bf16[1536,128]{1,0:T(8,128)(2,1)S(1)}, u32[]{:S(2)}) %copy-start.6) | copy-done | bytes 393240
  56.7 7.4 %flow_block.3 = f32[104,128]{1,0:T(8,128)} custom-call(s32[7]{0:T(128)} %stack.49.place_ref, s32[1,1536]{1,0:T(1,128)} %constant.44.clone.pos_ref, f32[96,128]{1,0:T(8,128)} %get-tuple-element.5.rows_ref, bf16[1536,128]{1,0:T(8,128)(2,1)} %bitcast.17, bf16[1536,128]{1,0:T(8,128)(2,1)} %copy-done.6, bf16[2,896,128]{2,1,0:T(8,128)(2,1)} %combine.1.maps_ref, ...), custom_call_target="tpu_custom_call" | custom-call | tf_op jit(solution)/shard_map/flow_block/pallas_call | solution.py:256
  64.2 1.3 %collective-permute-done.7 = f32[104,128]{1,0:T(8,128)S(1)} collective-permute-done((f32[104,128]{1,0:T(8,128)}, f32[104,128]{1,0:T(8,128)S(1)}, u32[]{:S(2)}, u32[]{:S(2)}) %collective-permute-start.7) | collective-permute-done | bytes 53280 | tf_op jit(solution)/shard_map/ppermute | solution.py:278
  65.5 0.8 %broadcast_select_fusion.1 = (f32[104,128]{1,0:T(8,128)S(1)}, f32[104,128]{1,0:T(8,128)S(1)}) fusion(f32[104,128]{1,0:T(8,128)} %flow_block.3, f32[104,128]{1,0:T(8,128)S(1)} %collective-permute-done.7, pred[]{:T(512)S(6)} %eq.8), kind=kLoop, calls=%fused_computation.3 | loop fusion | flops 26624 | bytes 212993 | tf_op jit(solution)/shard_map/jit(_where)/select_n | solution.py:328
  66.4 0.6 pad_maximum_fusion
  67.0 0.6 pad_maximum_fusion.1
  (22 shorter events, 0.2 us)
Async XLA Ops:
  0.6 10.3 %copy-start = (bf16[2,1536,128]{2,1,0:T(8,128)(2,1)S(1)}, bf16[2,1536,128]{2,1,0:T(8,128)(2,1)}, u32[]{:S(2)}) copy-start(bf16[2,1536,128]{2,1,0:T(8,128)(2,1)} %refs_0_.5) | copy-start | bytes 2359300
  0.6 23.3 %collective-permute-start.1 = (bf16[2,1536,128]{2,1,0:T(8,128)(2,1)}, bf16[2,1536,128]{2,1,0:T(8,128)(2,1)}, u32[]{:S(2)}, u32[]{:S(2)}) collective-permute-start(bf16[2,1536,128]{2,1,0:T(8,128)(2,1)} %refs_0_.3), channel_id=1, source_target_pairs={{1,0},{0,1},{3,2},{2,3},{5,4},{4,5},{7,6},{6,7},{9,8},{8,9},{11,10... | collective-permute-start | bytes 2359304 | tf_op jit(solution)/shard_map/ppermute | solution.py:284
  2.8 21.2 %all-to-all-start = ((bf16[16,96,128]{2,1,0:T(8,128)(2,1)}), bf16[16,96,128]{2,1,0:T(8,128)(2,1)S(1)}, u32[]{:S(2)}, u32[]{:S(2)}) async-start(bf16[16,96,128]{2,1,0:T(8,128)(2,1)} %broadcast_in_dim.2), calls=%async_computation | async-start | bytes 786432 | tf_op jit(solution)/shard_map/all_to_all | solution.py:293
  10.7 13.8 %collective-permute-start.2 = (bf16[2,1536,128]{2,1,0:T(8,128)(2,1)}, bf16[2,1536,128]{2,1,0:T(8,128)(2,1)}, u32[]{:S(2)}, u32[]{:S(2)}) collective-permute-start(bf16[2,1536,128]{2,1,0:T(8,128)(2,1)} %refs_2_.3), channel_id=1, source_target_pairs={{1,0},{0,1},{3,2},{2,3},{5,4},{4,5},{7,6},{6,7},{9,8},{8,9},{11,10... | collective-permute-start | bytes 2359304 | tf_op jit(solution)/shard_map/ppermute | solution.py:284
  11.0 17.6 %collective-permute-start.3 = (bf16[2,1536,128]{2,1,0:T(8,128)(2,1)S(1)}, bf16[2,1536,128]{2,1,0:T(8,128)(2,1)S(1)}, u32[]{:S(2)}, u32[]{:S(2)}) collective-permute-start(bf16[2,1536,128]{2,1,0:T(8,128)(2,1)S(1)} %copy-done), channel_id=1, source_target_pairs={{1,0},{0,1},{3,2},{2,3},{5,4},{4,5},{7,6},{6,7},{9,8},{8,9},{11,10... | collective-permute-start | bytes 2359304 | tf_op jit(solution)/shard_map/ppermute | solution.py:284
  11.3 17.2 %collective-permute-start.4 = (bf16[2,128,1536]{2,1,0:T(8,128)(2,1)}, bf16[2,128,1536]{2,1,0:T(8,128)(2,1)S(1)}, u32[]{:S(2)}, u32[]{:S(2)}) collective-permute-start(bf16[2,128,1536]{2,1,0:T(8,128)(2,1)} %refs_2_.5), channel_id=1, source_target_pairs={{1,0},{0,1},{3,2},{2,3},{5,4},{4,5},{7,6},{6,7},{9,8},{8,9},{11,10... | collective-permute-start | bytes 2359304 | tf_op jit(solution)/shard_map/ppermute | solution.py:284
  11.5 17.1 %collective-permute-start.5 = (bf16[2,768,256]{2,1,0:T(8,128)(2,1)}, bf16[2,768,256]{2,1,0:T(8,128)(2,1)S(1)}, u32[]{:S(2)}, u32[]{:S(2)}) collective-permute-start(bf16[2,768,256]{2,1,0:T(8,128)(2,1)} %refs_4_.3), channel_id=1, source_target_pairs={{1,0},{0,1},{3,2},{2,3},{5,4},{4,5},{7,6},{6,7},{9,8},{8,9},{11,10... | collective-permute-start | bytes 2359304 | tf_op jit(solution)/shard_map/ppermute | solution.py:284
  23.9 4.6 %copy-start.4 = (bf16[16,96,128]{2,1,0:T(8,128)(2,1)}, bf16[16,96,128]{2,1,0:T(8,128)(2,1)S(1)}, u32[]{:S(2)}) copy-start(bf16[16,96,128]{2,1,0:T(8,128)(2,1)S(1)} %all-to-all-done) | copy-start | bytes 1179652
  23.9 4.7 %collective-permute-start = (bf16[1536,128]{1,0:T(8,128)(2,1)S(1)}, bf16[1536,128]{1,0:T(8,128)(2,1)}, u32[]{:S(2)}, u32[]{:S(2)}) collective-permute-start(bf16[1536,128]{1,0:T(8,128)(2,1)S(1)} %bitcast.14), channel_id=1, source_target_pairs={{0,1},{1,0},{2,3},{3,2},{4,5},{5,4},{6,7},{7,6},{8,9},{9,8},{10,11... | collective-permute-start | bytes 1179656 | tf_op jit(solution)/shard_map/ppermute | solution.py:278
  28.5 0.9 %copy-start.1 = (bf16[2,1536,128]{2,1,0:T(8,128)(2,1)}, bf16[2,1536,128]{2,1,0:T(8,128)(2,1)S(1)}, u32[]{:S(2)}) copy-start(bf16[2,1536,128]{2,1,0:T(8,128)(2,1)S(1)} %collective-permute-done.3.refs_1_) | copy-start | bytes 2359300
  28.6 1.2 %copy-start.2 = (bf16[2,128,1536]{2,1,0:T(8,128)(2,1)}, bf16[2,128,1536]{2,1,0:T(8,128)(2,1)S(1)}, u32[]{:S(2)}) copy-start(bf16[2,128,1536]{2,1,0:T(8,128)(2,1)S(1)} %collective-permute-done.4.refs_3_) | copy-start | bytes 2359300
  28.6 1.4 %copy-start.3 = (bf16[2,768,256]{2,1,0:T(8,128)(2,1)}, bf16[2,768,256]{2,1,0:T(8,128)(2,1)S(1)}, u32[]{:S(2)}) copy-start(bf16[2,768,256]{2,1,0:T(8,128)(2,1)S(1)} %collective-permute-done.5.refs_5_) | copy-start | bytes 2359300
  54.2 1.7 %copy-start.5 = (bf16[16,96,128]{2,1,0:T(8,128)(2,1)}, bf16[16,96,128]{2,1,0:T(8,128)(2,1)S(1)}, u32[]{:S(2)}) copy-start(bf16[16,96,128]{2,1,0:T(8,128)(2,1)S(1)} %all_to_all.10) | copy-start | bytes 1179652
  54.2 1.7 %collective-permute-start.6 = (bf16[1536,128]{1,0:T(8,128)(2,1)S(1)}, bf16[1536,128]{1,0:T(8,128)(2,1)S(1)}, u32[]{:S(2)}, u32[]{:S(2)}) collective-permute-start(bf16[1536,128]{1,0:T(8,128)(2,1)S(1)} %bitcast.16), channel_id=1, source_target_pairs={{0,1},{1,0},{2,3},{3,2},{4,5},{5,4},{6,7},{7,6},{8,9},{9,8},{10,11... | collective-permute-start | bytes 1179656 | tf_op jit(solution)/shard_map/ppermute | solution.py:278
  55.9 0.7 %copy-start.6 = (bf16[1536,128]{1,0:T(8,128)(2,1)}, bf16[1536,128]{1,0:T(8,128)(2,1)S(1)}, u32[]{:S(2)}) copy-start(bf16[1536,128]{1,0:T(8,128)(2,1)S(1)} %collective-permute-done.6.other_ref) | copy-start | bytes 1179652
  64.1 1.4 %collective-permute-start.7 = (f32[104,128]{1,0:T(8,128)}, f32[104,128]{1,0:T(8,128)S(1)}, u32[]{:S(2)}, u32[]{:S(2)}) collective-permute-start(f32[104,128]{1,0:T(8,128)} %flow_block.3), channel_id=1, source_target_pairs={{0,1},{1,0},{2,3},{3,2},{4,5},{5,4},{6,7},{7,6},{8,9},{9,8},{10,11... | collective-permute-start | bytes 159752 | tf_op jit(solution)/shard_map/ppermute | solution.py:278

commit v2 on v1

v2 whole, which is shorter than its diff:
```python
import functools
import math

import jax
import jax.numpy as jnp
import numpy as np
from jax import lax
from jax.experimental import pallas as pl
from jax.experimental.pallas import tpu as pltpu
from jax.sharding import PartitionSpec as P

HS = 64

score_scale = 8.0
epsilon = 1e-06

VMEM_LIMIT = 56 * 1024 * 1024


def dot(a, b):
    return jnp.dot(a, b, preferred_element_type=jnp.float32)


def dot_nt(a, b):
    return lax.dot_general(a, b, (((1,), (1,)), ((), ())), preferred_element_type=jnp.float32)


def cat(parts, axis):
    return parts[0] if len(parts) == 1 else jnp.concatenate(parts, axis=axis)


def side_of():
    return lax.rem(lax.axis_index("head"), 2)


def cost(flops, moved):
    return pl.CostEstimate(flops=int(flops), bytes_accessed=int(moved), transcendentals=0)


def size_of(arrays):
    return sum(math.prod(a.shape) * a.dtype.itemsize for a in arrays)


def vmem():
    return pl.BlockSpec(memory_space=pltpu.VMEM)


def spread_kernel(rows_ref, spread_ref, edge_ref):
    members, count, _ = spread_ref.shape
    own = rows_ref[pl.ds(pl.multiple_of(side_of() * count, 8), count), :].astype(jnp.bfloat16)
    for i in range(members):
        spread_ref[i] = own
    edge_ref[...] = rows_ref[rows_ref.shape[0] - 8 :, :]


def spread_rows(rows, members):
    count, channels = rows.shape[0] // 2, rows.shape[1]
    return pl.pallas_call(
        spread_kernel,
        in_specs=[vmem()],
        out_specs=(vmem(), vmem()),
        out_shape=(
            jax.ShapeDtypeStruct((members, count, channels), jnp.bfloat16),
            jax.ShapeDtypeStruct((8, channels), jnp.float32),
        ),
        name="spread_rows",
    )(rows)


def combine_kernel(pieces, in_ref, gain_ref, *refs):
    key_refs, value_refs, out_ref = refs[:pieces], refs[pieces : 2 * pieces], refs[2 * pieces]
    block = pl.program_id(0)
    base = in_ref[0]
    channels = base.shape[0]

    def store(row, value):
        high = value.astype(jnp.bfloat16)
        rows = value.shape[0]
        out_ref[0, row : row + rows, :channels] = high
        out_ref[0, row : row + rows, channels:] = (value - high.astype(jnp.float32)).astype(
            jnp.bfloat16
        )
        return row + rows

    scaled = base.astype(jnp.float32) * gain_ref[pl.ds(block, 1), :]
    high = scaled.astype(jnp.bfloat16)
    low = (scaled - high.astype(jnp.float32)).astype(jnp.bfloat16)
    both = jnp.concatenate([high, low], axis=0)
    row = 0
    for group in (key_refs, value_refs):
        for first in range(0, pieces, 2):
            columns = cat([ref[0] for ref in group[first : first + 2]], 1)
            product = dot(both, columns)
            row = store(row, (product[:channels] + product[channels:]).T)
    row = store(row, dot_nt(base, base))
    eye = lax.broadcasted_iota(jnp.int32, (channels, channels), 0) == lax.broadcasted_iota(
        jnp.int32, (channels, channels), 1
    )
    store(row, jnp.where(eye, 1.0, 0.0))


def combine(in_proj, attn_gain, key_pieces, value_pieces):
    pieces = len(key_pieces)
    layers, channels, features = in_proj.shape
    head_cols = key_pieces[0].shape[2]
    rows = 2 * pieces * head_cols + 2 * channels
    piece = pl.BlockSpec((1, features, head_cols), lambda b: (b, 0, 0))
    operands = [in_proj, attn_gain, *key_pieces, *value_pieces]
    return pl.pallas_call(
        functools.partial(combine_kernel, pieces),
        grid=(layers,),
        in_specs=[
            pl.BlockSpec((1, channels, features), lambda b: (b, 0, 0)),
            pl.BlockSpec((layers, features), lambda b: (0, 0)),
        ]
        + [piece] * (2 * pieces),
        out_specs=pl.BlockSpec((1, rows, 2 * channels), lambda b: (b, 0, 0)),
        out_shape=jax.ShapeDtypeStruct((layers, rows, 2 * channels), jnp.bfloat16),
        compiler_params=pltpu.CompilerParams(vmem_limit_bytes=VMEM_LIMIT),
        cost_estimate=cost(4 * layers * channels * features * rows, size_of(operands)),
        name="combine",
    )(*operands)


def queries_kernel(layer, pieces, rows_ref, edge_ref, in_ref, gain_ref, *refs):
    query_refs, shifted_ref, out_ref = refs[:pieces], refs[pieces], refs[pieces + 1]
    count = shifted_ref.shape[0]
    token = lax.broadcasted_iota(jnp.int32, (count, 1), 0)
    if layer == 0:
        start = pl.multiple_of(side_of() * count, 8)
        values = rows_ref[pl.ds(start, count), :]
        border = jnp.where(side_of() == 0, edge_ref[7:8, :], rows_ref[count - 1 : count, :])
        moved, at = pltpu.roll(values, 1, 0), 0
    else:
        values = rows_ref[...]
        border = edge_ref[0:1, :]
        moved, at = pltpu.roll(values, count - 1, 0), count - 1
    shifted = jnp.where(token == at, border, moved).astype(jnp.bfloat16)
    shifted_ref[...] = shifted
    hidden = dot(shifted, in_ref[0])
    spread = lax.rsqrt(jnp.mean(hidden * hidden, axis=1, keepdims=True) + epsilon)
    normed = (hidden * spread * gain_ref[layer : layer + 1, :]).astype(jnp.bfloat16)
    for first in range(0, pieces, 2):
        query = dot(normed, cat([ref[0] for ref in query_refs[first : first + 2]], 1))
        width = query.shape[1]
        head = lax.broadcasted_iota(jnp.int32, (count, width), 1) // HS
        for h in range(width // HS):
            band = jnp.where(head == h, query, 0.0)
            mean = jnp.sum(band * band, axis=1, keepdims=True) * (1.0 / HS)
            out_ref[first // 2, h * count : (h + 1) * count, :] = (
                band * lax.rsqrt(mean + epsilon)
            ).astype(jnp.bfloat16)


def make_queries(layer, count, rows, edge, in_proj, attn_gain, query_pieces):
    pieces = len(query_pieces)
    channels, features = in_proj.shape[1:]
    width = min(2, pieces) * query_pieces[0].shape[2]
    groups = pieces * query_pieces[0].shape[2] // width

    def one_layer(array):
        return pl.BlockSpec((1,) + array.shape[1:], lambda i: (layer, 0, 0))

    def full(shape):
        return pl.BlockSpec(shape, lambda i: (0,) * len(shape))

    shapes = ((count, channels), (groups, width // HS * count, width))
    operands = [rows, edge, in_proj, attn_gain, *query_pieces]
    return pl.pallas_call(
        functools.partial(queries_kernel, layer, pieces),
        grid=(1,),
        in_specs=[full(rows.shape), full(edge.shape), one_layer(in_proj), full(attn_gain.shape)]
        + [one_layer(array) for array in query_pieces],
        out_specs=tuple(full(shape) for shape in shapes),
        out_shape=tuple(jax.ShapeDtypeStruct(shape, jnp.bfloat16) for shape in shapes),
        compiler_params=pltpu.CompilerParams(vmem_limit_bytes=VMEM_LIMIT),
        cost_estimate=cost(2 * count * features * (channels + groups * width), size_of(operands) // 2),
        name="queries",
    )(*operands)


def attend_kernel(cfg, pos_ref, pgain_ref, rows_ref, *refs):
    layer, pieces, last, count = cfg["layer"], cfg["pieces"], cfg["last"], cfg["count"]
    refs = list(refs)
    first_log_ref = refs.pop(0) if last else None
    maps_src, own_src, query_src, other_src, shifted_src, in_src = [refs.pop(0) for _ in range(6)]
    mix_src = [refs.pop(0) for _ in range(pieces)]
    param_src = [refs.pop(0) for _ in range(pieces)]
    outs = [refs.pop(0) for _ in range(1 if last else 4)]
    maps_ref, own_ref, query_ref, other_ref, shifted_ref, in_ref, mix_ref, param_ref, sems = refs
    side, way = side_of(), lax.axis_index("head")
    channels, features = in_ref.shape
    forward = layer == 0

    copies = []

    def fetch(source, target):
        copy = pltpu.make_async_copy(source, target, sems.at[len(copies)])
        copy.start()
        copies.append(copy)
        return copy

    maps_copy = fetch(maps_src.at[layer], maps_ref)
    own_copy = fetch(own_src, own_ref)
    query_copy = fetch(query_src, query_ref)
    other_copy = fetch(other_src, other_ref)
    late = [fetch(shifted_src, shifted_ref), fetch(in_src.at[layer], in_ref)]
    head_cols = mix_src[0].shape[1]
    for j in range(pieces):
        late.append(fetch(mix_src[j].at[layer], mix_ref.at[pl.ds(j * head_cols, head_cols)]))
    share = features // pieces
    for j in range(pieces):
        at = pl.multiple_of(lax.rem(way + j, pieces) * share, 16)
        late.append(fetch(param_src[j].at[layer], param_ref.at[pl.ds(at, share)]))
    groups, _, group_cols = query_ref.shape
    heads = group_cols // HS
    total_cols = groups * group_cols
    token = lax.broadcasted_iota(jnp.int32, (count, 1), 0)
    first_token = lax.axis_index("seq") * (2 * count) + side * count
    query_token = first_token + jnp.concatenate([token] * heads, axis=0)

    def one_chunk(source_ref, start, offset, carry):
        size = cfg["chunk"]
        source = source_ref[pl.ds(start, size), :]
        twice = jnp.concatenate([source, source], axis=1)
        key_token = pos_ref[:, pl.ds(start, size)] + offset
        allowed = key_token < query_token if forward else key_token > query_token
        tail = dot_nt(maps_ref[2 * total_cols :, :], twice)
        square = jnp.sum(tail[:channels] * tail[channels:], axis=0, keepdims=True)
        scale = lax.rsqrt(jnp.maximum(square, 0.0) * (1.0 / features) + epsilon)
        scale_sq = scale * scale
        result = []
        for g in range(groups):
            low = g * group_cols
            key = dot_nt(maps_ref[low : low + group_cols, :], twice)
            value = dot_nt(maps_ref[total_cols + low : total_cols + low + group_cols, :], twice)
            keys = []
            for h in range(heads):
                one = key[h * HS : (h + 1) * HS]
                mean = jnp.sum(one * one, axis=0, keepdims=True) * (1.0 / HS)
                factor = scale * lax.rsqrt(mean * scale_sq + epsilon)
                keys.append((one * factor).astype(jnp.bfloat16))
            value = (value * scale).astype(jnp.bfloat16)
            scores = dot(query_ref[g], jnp.concatenate(keys, axis=0)) * (score_scale / HS)
            weights = jnp.where(allowed, jnp.exp(scores), 0.0)
            numerator, denominator = carry[g]
            for lane in range(0, size, 128):
                denominator = denominator + weights[:, lane : lane + 128]
            numerator = numerator + dot_nt(weights.astype(jnp.bfloat16), value)
            result.append((numerator, denominator))
        return tuple(result)

    carry = tuple(
        (
            jnp.zeros((heads * count, group_cols), jnp.float32),
            jnp.zeros((heads * count, 128), jnp.float32),
        )
        for _ in range(groups)
    )
    chunks = own_ref.shape[0] // cfg["chunk"]
    maps_copy.wait()
    own_copy.wait()
    query_copy.wait()
    for source_ref, offset in ((own_ref, side * count), (other_ref, (1 - side) * count)):
        if source_ref is other_ref:
            other_copy.wait()
        if chunks <= 4:
            for c in range(chunks):
                carry = one_chunk(source_ref, c * cfg["chunk"], offset, carry)
        else:
            carry = lax.fori_loop(
                0,
                chunks,
                lambda c, now, source_ref=source_ref, offset=offset: one_chunk(
                    source_ref, pl.multiple_of(c * cfg["chunk"], cfg["chunk"]), offset, now
                ),
                carry,
            )

    for copy in late:
        copy.wait()
    mixture = dot(shifted_ref[...], in_ref[...])
    head = lax.broadcasted_iota(jnp.int32, (count, group_cols), 1) // HS
    for g, (numerator, denominator) in enumerate(carry):
        share_of = 1.0 / (jnp.sum(denominator, axis=1, keepdims=True) + 1.0)
        attended = jnp.zeros((count, group_cols), jnp.float32)
        for h in range(heads):
            band = slice(h * count, (h + 1) * count)
            attended = jnp.where(head == h, numerator[band] * share_of[band], attended)
        rows = mix_ref[g * group_cols : (g + 1) * group_cols, :]
        mixture = mixture + dot(attended.astype(jnp.bfloat16), rows)
    spread = lax.rsqrt(jnp.mean(mixture * mixture, axis=1, keepdims=True) + epsilon)
    scaled = (mixture * spread * pgain_ref[layer : layer + 1, :]).astype(jnp.bfloat16)
    predicted = dot(scaled, param_ref[...])
    log_scale = 2.0 * jnp.tanh(0.5 * predicted[:, channels:])
    values = rows_ref[...] if last else rows_ref[pl.ds(pl.multiple_of(side * count, 8), count), :]
    result = (values - predicted[:, :channels]) * jnp.exp(-log_scale)
    if last:
        term = -(first_log_ref[...] + log_scale) - 0.5 * (result * result)
        loglik = jnp.sum(term.T, axis=0, keepdims=True) * (1.0 / channels) - 0.5 * math.log(
            2.0 * math.pi
        )
        outs[0][:count, :] = result
        outs[0][count:, :count] = jnp.broadcast_to(loglik, (8, count))
    else:
        out_ref, log_ref, spread_ref, edge_ref = outs
        out_ref[...] = result
        log_ref[...] = log_scale
        edge_ref[...] = result[:8]
        narrow = result.astype(jnp.bfloat16)
        for i in range(spread_ref.shape[0]):
            spread_ref[i] = narrow


def attend(layer, members, count, positions, param_gain, rows, first_log, maps, own, queries, other, shifted, in_proj, mix_pieces, param_pieces):
    pieces = len(mix_pieces)
    channels, features = in_proj.shape[1:]
    last = first_log is not None
    keys = own.shape[0]
    chunk = next(size for size in (512, 384, 256, 128, keys) if keys % size == 0)
    near = [positions, param_gain, rows] + ([first_log] if last else [])
    far = [maps, own, queries, other, shifted, in_proj, *mix_pieces, *param_pieces]
    if last:
        out_shape = jax.ShapeDtypeStruct((count + 8, channels), jnp.float32)
        out_specs = vmem()
    else:
        out_shape = (
            jax.ShapeDtypeStruct((count, channels), jnp.float32),
            jax.ShapeDtypeStruct((count, channels), jnp.float32),
            jax.ShapeDtypeStruct((members, count, channels), jnp.bfloat16),
            jax.ShapeDtypeStruct((8, channels), jnp.float32),
        )
        out_specs = (vmem(),) * 4
    cfg = {"layer": layer, "pieces": pieces, "last": last, "count": count, "chunk": chunk}
    held = [
        maps.shape[1:],
        own.shape,
        queries.shape,
        other.shape,
        shifted.shape,
        (channels, features),
        (pieces * mix_pieces[0].shape[1], features),
        (features, param_pieces[0].shape[2]),
    ]
    return pl.pallas_call(
        functools.partial(attend_kernel, cfg),
        in_specs=[vmem()] * len(near) + [pl.BlockSpec(memory_space=pl.ANY)] * len(far),
        out_specs=out_specs,
        out_shape=out_shape,
        scratch_shapes=[pltpu.VMEM(shape, jnp.bfloat16) for shape in held]
        + [pltpu.SemaphoreType.DMA((6 + 2 * pieces,))],
        compiler_params=pltpu.CompilerParams(vmem_limit_bytes=VMEM_LIMIT),
        cost_estimate=cost(
            4 * keys * (maps.shape[1] * maps.shape[2] + queries.size * 2), size_of(far) // 2
        ),
        name="attend",
    )(*near, *far)


def finish_kernel(own_ref, other_ref, final_ref, loglik_ref):
    count = final_ref.shape[0] // 2
    side = side_of()
    for ref, place in ((own_ref, side), (other_ref, 1 - side)):
        final_ref[pl.ds(pl.multiple_of(place * count, 8), count), :] = ref[:count, :]
    first = jnp.where(side == 0, own_ref[count : count + 1, :], other_ref[count : count + 1, :])
    second = jnp.where(side == 0, other_ref[count : count + 1, :], own_ref[count : count + 1, :])
    loglik_ref[...] = jnp.concatenate([first[:, :count], second[:, :count]], axis=1)


def finish(own, other):
    count, channels = own.shape[0] - 8, own.shape[1]
    return pl.pallas_call(
        finish_kernel,
        in_specs=[vmem()] * 2,
        out_specs=(vmem(), vmem()),
        out_shape=(
            jax.ShapeDtypeStruct((2 * count, channels), jnp.float32),
            jax.ShapeDtypeStruct((1, 2 * count), jnp.float32),
        ),
        name="finish",
    )(own, other)


def body(
    latents, in_proj, query_proj, key_proj, value_proj, mix_proj, param_proj, attn_gain, param_gain
):
    members, ways = lax.axis_size("seq"), lax.axis_size("head")
    rows, channels = latents.shape
    count = rows // 2

    def swap(array):
        return lax.ppermute(array, "head", [(i, i ^ 1) for i in range(ways)])

    def pieces_of(array):
        shares = [array]
        for j in range(1, ways):
            shares.append(
                lax.ppermute(array, "head", [((i + j) % ways, i) for i in range(ways)])
            )
        return shares

    def gather(spread):
        return lax.all_to_all(spread, "seq", 0, 0).reshape(members * count, channels)

    spread, edge = spread_rows(latents, members)
    edge = lax.ppermute(edge, "seq", [(i, i + 1) for i in range(members - 1)])
    own = gather(spread)
    key_pieces, value_pieces = pieces_of(key_proj), pieces_of(value_proj)
    query_pieces, mix_pieces = pieces_of(query_proj), pieces_of(mix_proj)
    param_pieces = pieces_of(param_proj)
    maps = combine(in_proj, attn_gain, key_pieces, value_pieces)
    positions = jnp.asarray(
        (np.arange(members * count) // count * rows + np.arange(members * count) % count)[None],
        jnp.int32,
    )
    weights = (in_proj, mix_pieces, param_pieces)

    shifted, queries = make_queries(0, count, latents, edge, in_proj, attn_gain, query_pieces)
    other = swap(own)
    first_out, first_log, spread, edge = attend(
        0, members, count, positions, param_gain, latents, None, maps, own, queries, other, shifted, *weights
    )

    pairs = []
    for s in range(members):
        for w in range(ways):
            if w % 2:
                pairs.append((s * ways + w, s * ways + w - 1))
            elif s > 0:
                pairs.append((s * ways + w, (s - 1) * ways + w + 1))
    edge = lax.ppermute(edge, ("seq", "head"), pairs)
    own = gather(spread)
    shifted, queries = make_queries(1, count, first_out, edge, in_proj, attn_gain, query_pieces)
    other = swap(own)
    packed = attend(
        1, members, count, positions, param_gain, first_out, first_log, maps, own, queries, other, shifted, *weights
    )
    final_latent, token_loglik = finish(packed, swap(packed))
    return (final_latent, token_loglik.reshape(rows))


def solution(mesh):
    placed = (
        P("seq", None),
        P(),
        P(None, None, "head"),
        P(None, None, "head"),
        P(None, None, "head"),
        P(None, "head", None),
        P(None, "head", None),
        P(),
        P(),
    )
    return jax.shard_map(
        body, mesh=mesh, in_specs=placed, out_specs=(P("seq", None), P("seq")), check_vma=False
    )
```

time: 68.1 us -> 78.9 us (1.16)
  Pallas kernels: 18.8 us -> 27.6 us
  starting transfers between devices: 9.71 us -> 16.8 us
  waiting for transfers between devices: 14.5 us -> 11.6 us
  other arithmetic: 2.1 us -> 0 us
    pallas_call x2 -> x6, Pallas kernels: 14.9 us -> 23.6 us  [the longest x2 15.2 us: attend(): pl.pallas_call(functools.partial(attend_kernel, cfg), in_specs=[vmem()] *...]
    ppermute x0 -> x2, starting transfers between devices: none -> 5.11 us  [the longest x1 3.81 us: body(): edge = lax.ppermute(edge, 'seq', [(i, i + 1) for i in range(members - 1)])]
    all_to_all x1, waiting for transfers between devices: 12.1 us -> 7.46 us  [gather(): lax.all_to_all(spread, 'seq', 0, 0).reshape(members * count, channels)]
    unnamed x14 -> x26, local copies, waits for them, and re-layouts: 2.12 us -> 5.28 us
    ppermute x0 -> x2, waiting for transfers between devices: none -> 2.99 us  [the longest x1 1.76 us: body(): edge = lax.ppermute(edge, ('seq', 'head'), pairs)]
    ppermute x3, starting transfers between devices: 0.14 us -> 2.49 us  [swap(): return lax.ppermute(array, 'head', [(i, i ^ 1) for i in range(ways)])]
    concatenate x2 -> x0, other arithmetic: 1.28 us -> none  [the longest x1 0.65 us: body(): final_latent = jnp.concatenate([low[:count], high[:count]], axis=0)]
    another operation x2 -> x0, local copies, waits for them, and re-layouts: 1.27 us -> none  [place(): return jnp.stack([jnp.asarray(e, jnp.int32) for e in entries])]
  transfers between devices with their start and end apart: 9 -> 11, of which waited for: 3 -> 4; matrix products, arithmetic and copies ran while one was open for 4% -> 0% of each run, Pallas kernels for 6% -> 14%
where the time goes in v2:
time: 78.9 us; the launch traced here: 78.3 us
  Pallas kernels  27.6 us (35%)
  starting transfers between devices  16.8 us (21%)
  blocking collectives  16.2 us (21%)
  waiting for transfers between devices  11.6 us (15%)
  local copies, waits for them, and re-layouts  5.28 us (7%)
  between operations  0.79 us (1%)
    all_to_all x1, blocking collectives, gather(): lax.all_to_all(spread, 'seq', 0, 0).reshape(members * count, channels)  16.2 us
    pallas_call x2, Pallas kernels, attend(): pl.pallas_call(functools.partial(attend_kernel, cfg), in_specs=[vmem()] *...  15.2 us
    all_to_all x1, starting transfers between devices, gather(): lax.all_to_all(spread, 'seq', 0, 0).reshape(members * count, channels)  8.07 us
    all_to_all x1, waiting for transfers between devices, gather(): lax.all_to_all(spread, 'seq', 0, 0).reshape(members * count, channels)  7.46 us
    unnamed x26, local copies, waits for them, and re-layouts  5.28 us
    pallas_call x2, Pallas kernels, make_queries(): pl.pallas_call(functools.partial(queries_kernel, layer, pieces), grid=(1,...  5.27 us
    pallas_call x1, Pallas kernels, combine(): pl.pallas_call(functools.partial(combine_kernel, pieces), grid=(layers,),...  3.96 us
    ppermute x1, starting transfers between devices, body(): edge = lax.ppermute(edge, 'seq', [(i, i + 1) for i in range(members - 1)])  3.81 us
  transfers between devices with their start and end apart: 11, of which 4 were waited for; matrix products, arithmetic and copies ran while one was open for 0% of the time, Pallas kernels for 14%

profile of v2, /device:TPU:0, one launch (start us, length us, event | category | flops | bytes accessed | tf_op | source)
XLA Modules:
  0.0 78.3 jit_solution(11227542507535936030)
XLA Ops:
  0.6 0.5 collective-permute-start.3
  1.2 1.7 %spread_rows.1 = (bf16[16,96,128]{2,1,0:T(8,128)(2,1)}, f32[8,128]{1,0:T(8,128)}) custom-call(f32[192,128]{1,0:T(8,128)} %rows_ref.5), custom_call_target="tpu_custom_call" | custom-call | tf_op jit(solution)/shard_map/spread_rows/pallas_call | solution.py:58
  2.9 8.1 %all-to-all-start = ((bf16[16,96,128]{2,1,0:T(8,128)(2,1)}), bf16[16,96,128]{2,1,0:T(8,128)(2,1)S(1)}, u32[]{:S(2)}, u32[]{:S(2)}) async-start(bf16[16,96,128]{2,1,0:T(8,128)(2,1)} %get-tuple-element.14), calls=%async_computation | async-start | bytes 786432 | tf_op jit(solution)/shard_map/all_to_all | solution.py:403
  11.5 3.8 %collective-permute-start.2 = (f32[8,128]{1,0:T(8,128)S(1)}, f32[8,128]{1,0:T(8,128)S(1)}, u32[]{:S(2)}, u32[]{:S(2)}) collective-permute-start(f32[8,128]{1,0:T(8,128)S(1)} %copy-done.11), channel_id=1, source_target_pairs={{0,2},{2,4},{4,6},{6,8},{8,10},{10,12},{12,14},{14,16},{16,18},{18... | collective-permute-start | bytes 12296 | tf_op jit(solution)/shard_map/ppermute | solution.py:406
  15.4 1.2 %collective-permute-done.2.edge_ref = f32[8,128]{1,0:T(8,128)S(1)} collective-permute-done((f32[8,128]{1,0:T(8,128)S(1)}, f32[8,128]{1,0:T(8,128)S(1)}, u32[]{:S(2)}, u32[]{:S(2)}) %collective-permute-start.2) | collective-permute-done | bytes 4128 | tf_op jit(solution)/shard_map/ppermute | solution.py:406
  16.7 7.5 %all-to-all-done = bf16[16,96,128]{2,1,0:T(8,128)(2,1)S(1)} async-done(((bf16[16,96,128]{2,1,0:T(8,128)(2,1)}), bf16[16,96,128]{2,1,0:T(8,128)(2,1)S(1)}, u32[]{:S(2)}, u32[]{:S(2)}) %all-to-all-start) | async-done | bytes 393248 | tf_op jit(solution)/shard_map/all_to_all | solution.py:403
  24.2 0.8 %copy-done = bf16[2,1536,128]{2,1,0:T(8,128)(2,1)} copy-done((bf16[2,1536,128]{2,1,0:T(8,128)(2,1)}, bf16[2,1536,128]{2,1,0:T(8,128)(2,1)S(1)}, u32[]{:S(2)}) %copy-start) | copy-done | bytes 786456
  25.0 2.7 %queries.2 = (bf16[96,128]{1,0:T(8,128)(2,1)}, bf16[1,384,256]{2,1,0:T(8,128)(2,1)}) custom-call(f32[192,128]{1,0:T(8,128)} %rows_ref.5, f32[8,128]{1,0:T(8,128)} %copy-done.7, bf16[2,128,1536]{2,1,0:T(8,128)(2,1)} %refs_6_.3, f32[2,1536]{1,0:T(2,128)} %gain_ref.5, bf16[2,1536,128]{2,1,0:T(8,128)(2,1)} %refs_0_.5, bf16[2,1536,128]{2,1,0:T(8,128)(2,1)} %copy-done), custom_call_target="tpu_custom_call" | custom-call | flops 113246208 | bytes 1236992 | tf_op jit(solution)/shard_map/queries/pallas_call | solution.py:169
  27.7 0.9 %copy-done.2 = bf16[2,1536,128]{2,1,0:T(8,128)(2,1)} copy-done((bf16[2,1536,128]{2,1,0:T(8,128)(2,1)}, bf16[2,1536,128]{2,1,0:T(8,128)(2,1)S(1)}, u32[]{:S(2)}) %copy-start.2) | copy-done | bytes 786456
  28.6 0.9 %copy-done.3 = bf16[2,1536,128]{2,1,0:T(8,128)(2,1)} copy-done((bf16[2,1536,128]{2,1,0:T(8,128)(2,1)}, bf16[2,1536,128]{2,1,0:T(8,128)(2,1)S(1)}, u32[]{:S(2)}) %copy-start.3) | copy-done | bytes 786456
  29.5 4.0 %combine.1.refs_0_.refs_1_ = bf16[2,768,256]{2,1,0:T(8,128)(2,1)} custom-call(bf16[2,128,1536]{2,1,0:T(8,128)(2,1)} %refs_6_.3, f32[2,1536]{1,0:T(2,128)} %gain_ref.5, bf16[2,1536,128]{2,1,0:T(8,128)(2,1)} %refs_0_.3, bf16[2,1536,128]{2,1,0:T(8,128)(2,1)} %copy-done.2, bf16[2,1536,128]{2,1,0:T(8,128)(2,1)} %refs_2_.1, bf16[2,1536,128]{2,1,0:T(8,128)(2,1)} %copy-done.3), custom_call_target="tpu_custom_call" | custom-call | flops 1207959552 | bytes 3944448 | tf_op jit(solution)/shard_map/combine/pallas_call | solution.py:109
  33.5 0.7 copy-done.9
  34.2 7.7 %attend.2 = (f32[96,128]{1,0:T(8,128)}, f32[96,128]{1,0:T(8,128)}, bf16[16,96,128]{2,1,0:T(8,128)(2,1)}, f32[8,128]{1,0:T(8,128)}) custom-call(s32[1,1536]{1,0:T(1,128)} %constant.2.clone.pos_ref, f32[2,1536]{1,0:T(2,128)} %pgain_ref.3, f32[192,128]{1,0:T(8,128)} %rows_ref.5, bf16[2,768,256]{2,1,0:T(8,128)(2,1)} %combine.1.refs_0_.refs_1_, ...), custom_call_target="tpu_custom_call" | custom-call | flops 2415919104 | bytes 2863104 | tf_op jit(solution)/shard_map/attend/pallas_call | solution.py:345
  41.9 16.2 %all_to_all.10 = bf16[16,96,128]{2,1,0:T(8,128)(2,1)S(1)} all-to-all(bf16[16,96,128]{2,1,0:T(8,128)(2,1)} %get-tuple-element.20), channel_id=1, replica_groups=mesh['seq'=16,'head'=2] {'seq'}, dimensions={0} | all-to-all | bytes 786432 | tf_op jit(solution)/shard_map/all_to_all | solution.py:403
  58.1 1.3 %collective-permute-start.7 = (f32[8,128]{1,0:T(8,128)S(1)}, f32[8,128]{1,0:T(8,128)S(1)}, u32[]{:S(2)}, u32[]{:S(2)}) collective-permute-start(f32[8,128]{1,0:T(8,128)S(1)} %copy-done.12), channel_id=1, source_target_pairs={{1,0},{2,1},{3,2},{4,3},{5,4},{6,5},{7,6},{8,7},{9,8},{10,9},{11,1... | collective-permute-start | bytes 12296 | tf_op jit(solution)/shard_map/ppermute | solution.py:431
  59.4 1.8 %collective-permute-done.7.edge_ref = f32[8,128]{1,0:T(8,128)S(1)} collective-permute-done((f32[8,128]{1,0:T(8,128)S(1)}, f32[8,128]{1,0:T(8,128)S(1)}, u32[]{:S(2)}, u32[]{:S(2)}) %collective-permute-start.7) | collective-permute-done | bytes 4128 | tf_op jit(solution)/shard_map/ppermute | solution.py:431
  61.2 0.6 copy-done.8
  61.8 2.6 %queries.3 = (bf16[96,128]{1,0:T(8,128)(2,1)}, bf16[1,384,256]{2,1,0:T(8,128)(2,1)}) custom-call(f32[96,128]{1,0:T(8,128)} %get-tuple-element.18.rows_ref, f32[8,128]{1,0:T(8,128)} %copy-done.8, bf16[2,128,1536]{2,1,0:T(8,128)(2,1)} %refs_6_.3, f32[2,1536]{1,0:T(2,128)} %gain_ref.5, bf16[2,1536,128]{2,1,0:T(8,128)(2,1)} %refs_0_.5, bf16[2,1536,128]{2,1,0:T(8,128)(2,1)} %copy-done), custom_call_target="tpu_custom_call" | custom-call | flops 113246208 | bytes 1212416 | tf_op jit(solution)/shard_map/queries/pallas_call | solution.py:169
  64.4 0.8 copy-done.10
  65.1 7.5 %attend.3.own_ref = f32[104,128]{1,0:T(8,128)} custom-call(s32[1,1536]{1,0:T(1,128)} %constant.2.clone.pos_ref, f32[2,1536]{1,0:T(2,128)} %pgain_ref.3, f32[96,128]{1,0:T(8,128)} %get-tuple-element.18.rows_ref, f32[96,128]{1,0:T(8,128)} %get-tuple-element.19.refs_0_, bf16[2,768,256]{2,1,0:T(8,128)(2,1)} %combine.1.refs_0_.refs_1_, ...), custom_call_target="tpu_custom_call" | custom-call | flops 2415919104 | bytes 2863104 | tf_op jit(solution)/shard_map/attend/pallas_call | solution.py:345
  72.7 2.4 %collective-permute-start.9 = (f32[104,128]{1,0:T(8,128)}, f32[104,128]{1,0:T(8,128)S(1)}, u32[]{:S(2)}, u32[]{:S(2)}) collective-permute-start(f32[104,128]{1,0:T(8,128)} %attend.3.own_ref), channel_id=1, source_target_pairs={{0,1},{1,0},{2,3},{3,2},{4,5},{5,4},{6,7},{7,6},{8,9},{9,8},{10,11... | collective-permute-start | bytes 159752 | tf_op jit(solution)/shard_map/ppermute | solution.py:392
  75.1 1.1 %collective-permute-done.9.other_ref = f32[104,128]{1,0:T(8,128)S(1)} collective-permute-done((f32[104,128]{1,0:T(8,128)}, f32[104,128]{1,0:T(8,128)S(1)}, u32[]{:S(2)}, u32[]{:S(2)}) %collective-permute-start.9) | collective-permute-done | bytes 53280 | tf_op jit(solution)/shard_map/ppermute | solution.py:392
  76.2 0.6 copy-done.6
  76.8 1.5 %finish.1 = (f32[192,128]{1,0:T(8,128)}, f32[1,192]{1,0:T(1,128)}) custom-call(f32[104,128]{1,0:T(8,128)} %attend.3.own_ref, f32[104,128]{1,0:T(8,128)} %copy-done.6), custom_call_target="tpu_custom_call" | custom-call | tf_op jit(solution)/shard_map/finish/pallas_call | solution.py:372
  (32 shorter events, 0.8 us)
Async XLA Ops:
  0.6 10.3 %copy-start.1 = (bf16[2,1536,128]{2,1,0:T(8,128)(2,1)S(1)}, bf16[2,1536,128]{2,1,0:T(8,128)(2,1)}, u32[]{:S(2)}) copy-start(bf16[2,1536,128]{2,1,0:T(8,128)(2,1)} %refs_0_.3) | copy-start | bytes 2359300
  0.6 23.5 %collective-permute-start.3 = (bf16[2,1536,128]{2,1,0:T(8,128)(2,1)}, bf16[2,1536,128]{2,1,0:T(8,128)(2,1)S(1)}, u32[]{:S(2)}, u32[]{:S(2)}) collective-permute-start(bf16[2,1536,128]{2,1,0:T(8,128)(2,1)} %refs_0_.5), channel_id=1, source_target_pairs={{1,0},{0,1},{3,2},{2,3},{5,4},{4,5},{7,6},{6,7},{9,8},{8,9},{11,10... | collective-permute-start | bytes 2359304 | tf_op jit(solution)/shard_map/ppermute | solution.py:398
  2.9 8.7 %copy-start.11 = (f32[8,128]{1,0:T(8,128)S(1)}, f32[8,128]{1,0:T(8,128)}, u32[]{:S(2)}) copy-start(f32[8,128]{1,0:T(8,128)} %get-tuple-element.15) | copy-start | bytes 12292
  2.9 21.3 %all-to-all-start = ((bf16[16,96,128]{2,1,0:T(8,128)(2,1)}), bf16[16,96,128]{2,1,0:T(8,128)(2,1)S(1)}, u32[]{:S(2)}, u32[]{:S(2)}) async-start(bf16[16,96,128]{2,1,0:T(8,128)(2,1)} %get-tuple-element.14), calls=%async_computation | async-start | bytes 786432 | tf_op jit(solution)/shard_map/all_to_all | solution.py:403
  10.9 16.8 %collective-permute-start = (bf16[2,1536,128]{2,1,0:T(8,128)(2,1)S(1)}, bf16[2,1536,128]{2,1,0:T(8,128)(2,1)S(1)}, u32[]{:S(2)}, u32[]{:S(2)}) collective-permute-start(bf16[2,1536,128]{2,1,0:T(8,128)(2,1)S(1)} %copy-done.1), channel_id=1, source_target_pairs={{1,0},{0,1},{3,2},{2,3},{5,4},{4,5},{7,6},{6,7},{9,8},{8,9},{11,10... | collective-permute-start | bytes 2359304 | tf_op jit(solution)/shard_map/ppermute | solution.py:398
  11.2 16.5 %collective-permute-start.1 = (bf16[2,1536,128]{2,1,0:T(8,128)(2,1)}, bf16[2,1536,128]{2,1,0:T(8,128)(2,1)S(1)}, u32[]{:S(2)}, u32[]{:S(2)}) collective-permute-start(bf16[2,1536,128]{2,1,0:T(8,128)(2,1)} %refs_2_.1), channel_id=1, source_target_pairs={{1,0},{0,1},{3,2},{2,3},{5,4},{4,5},{7,6},{6,7},{9,8},{8,9},{11,10... | collective-permute-start | bytes 2359304 | tf_op jit(solution)/shard_map/ppermute | solution.py:398
  11.5 5.1 %collective-permute-start.2 = (f32[8,128]{1,0:T(8,128)S(1)}, f32[8,128]{1,0:T(8,128)S(1)}, u32[]{:S(2)}, u32[]{:S(2)}) collective-permute-start(f32[8,128]{1,0:T(8,128)S(1)} %copy-done.11), channel_id=1, source_target_pairs={{0,2},{2,4},{4,6},{6,8},{8,10},{10,12},{12,14},{14,16},{16,18},{18... | collective-permute-start | bytes 12296 | tf_op jit(solution)/shard_map/ppermute | solution.py:406
  15.3 18.1 %collective-permute-start.5 = (bf16[2,128,1536]{2,1,0:T(8,128)(2,1)}, bf16[2,128,1536]{2,1,0:T(8,128)(2,1)}, u32[]{:S(2)}, u32[]{:S(2)}) collective-permute-start(bf16[2,128,1536]{2,1,0:T(8,128)(2,1)} %refs_7_.1), channel_id=1, source_target_pairs={{1,0},{0,1},{3,2},{2,3},{5,4},{4,5},{7,6},{6,7},{9,8},{8,9},{11,10... | collective-permute-start | bytes 2359304 | tf_op jit(solution)/shard_map/ppermute | solution.py:398
  16.7 7.5 %copy-start.7 = (f32[8,128]{1,0:T(8,128)}, f32[8,128]{1,0:T(8,128)S(1)}, u32[]{:S(2)}) copy-start(f32[8,128]{1,0:T(8,128)S(1)} %collective-permute-done.2.edge_ref) | copy-start | bytes 12292
  16.7 16.8 %collective-permute-start.6 = (bf16[2,768,256]{2,1,0:T(8,128)(2,1)}, bf16[2,768,256]{2,1,0:T(8,128)(2,1)}, u32[]{:S(2)}, u32[]{:S(2)}) collective-permute-start(bf16[2,768,256]{2,1,0:T(8,128)(2,1)} %refs_9_.1), channel_id=1, source_target_pairs={{1,0},{0,1},{3,2},{2,3},{5,4},{4,5},{7,6},{6,7},{9,8},{8,9},{11,10... | collective-permute-start | bytes 2359304 | tf_op jit(solution)/shard_map/ppermute | solution.py:398
  24.1 3.6 %copy-start.4 = (bf16[16,96,128]{2,1,0:T(8,128)(2,1)}, bf16[16,96,128]{2,1,0:T(8,128)(2,1)S(1)}, u32[]{:S(2)}) copy-start(bf16[16,96,128]{2,1,0:T(8,128)(2,1)S(1)} %all-to-all-done) | copy-start | bytes 1179652
  24.1 0.9 %copy-start = (bf16[2,1536,128]{2,1,0:T(8,128)(2,1)}, bf16[2,1536,128]{2,1,0:T(8,128)(2,1)S(1)}, u32[]{:S(2)}) copy-start(bf16[2,1536,128]{2,1,0:T(8,128)(2,1)S(1)} %collective-permute-done.3.refs_1_) | copy-start | bytes 2359300
  24.1 9.3 %collective-permute-start.4 = (bf16[1536,128]{1,0:T(8,128)(2,1)S(1)}, bf16[1536,128]{1,0:T(8,128)(2,1)S(1)}, u32[]{:S(2)}, u32[]{:S(2)}) collective-permute-start(bf16[1536,128]{1,0:T(8,128)(2,1)S(1)} %bitcast.3), channel_id=1, source_target_pairs={{0,1},{1,0},{2,3},{3,2},{4,5},{5,4},{6,7},{7,6},{8,9},{9,8},{10,11... | collective-permute-start | bytes 1179656 | tf_op jit(solution)/shard_map/ppermute | solution.py:392
  27.7 0.9 %copy-start.2 = (bf16[2,1536,128]{2,1,0:T(8,128)(2,1)}, bf16[2,1536,128]{2,1,0:T(8,128)(2,1)S(1)}, u32[]{:S(2)}) copy-start(bf16[2,1536,128]{2,1,0:T(8,128)(2,1)S(1)} %collective-permute-done.refs_1_) | copy-start | bytes 2359300
  28.6 0.9 %copy-start.3 = (bf16[2,1536,128]{2,1,0:T(8,128)(2,1)}, bf16[2,1536,128]{2,1,0:T(8,128)(2,1)S(1)}, u32[]{:S(2)}) copy-start(bf16[2,1536,128]{2,1,0:T(8,128)(2,1)S(1)} %collective-permute-done.1.refs_3_) | copy-start | bytes 2359300
  33.5 0.7 copy-start.9
  41.9 16.3 %copy-start.12 = (f32[8,128]{1,0:T(8,128)S(1)}, f32[8,128]{1,0:T(8,128)}, u32[]{:S(2)}) copy-start(f32[8,128]{1,0:T(8,128)} %get-tuple-element.21) | copy-start | bytes 12292
  58.1 6.3 %copy-start.5 = (bf16[16,96,128]{2,1,0:T(8,128)(2,1)}, bf16[16,96,128]{2,1,0:T(8,128)(2,1)S(1)}, u32[]{:S(2)}) copy-start(bf16[16,96,128]{2,1,0:T(8,128)(2,1)S(1)} %all_to_all.10) | copy-start | bytes 1179652
  58.1 6.3 %collective-permute-start.8 = (bf16[1536,128]{1,0:T(8,128)(2,1)S(1)}, bf16[1536,128]{1,0:T(8,128)(2,1)S(1)}, u32[]{:S(2)}, u32[]{:S(2)}) collective-permute-start(bf16[1536,128]{1,0:T(8,128)(2,1)S(1)} %bitcast.5), channel_id=1, source_target_pairs={{0,1},{1,0},{2,3},{3,2},{4,5},{5,4},{6,7},{7,6},{8,9},{9,8},{10,11... | collective-permute-start | bytes 1179656 | tf_op jit(solution)/shard_map/ppermute | solution.py:392
  58.1 3.1 %collective-permute-start.7 = (f32[8,128]{1,0:T(8,128)S(1)}, f32[8,128]{1,0:T(8,128)S(1)}, u32[]{:S(2)}, u32[]{:S(2)}) collective-permute-start(f32[8,128]{1,0:T(8,128)S(1)} %copy-done.12), channel_id=1, source_target_pairs={{1,0},{2,1},{3,2},{4,3},{5,4},{6,5},{7,6},{8,7},{9,8},{10,9},{11,1... | collective-permute-start | bytes 12296 | tf_op jit(solution)/shard_map/ppermute | solution.py:431
  61.2 0.6 copy-start.8
  64.4 0.8 copy-start.10
  72.7 3.5 %collective-permute-start.9 = (f32[104,128]{1,0:T(8,128)}, f32[104,128]{1,0:T(8,128)S(1)}, u32[]{:S(2)}, u32[]{:S(2)}) collective-permute-start(f32[104,128]{1,0:T(8,128)} %attend.3.own_ref), channel_id=1, source_target_pairs={{0,1},{1,0},{2,3},{3,2},{4,5},{5,4},{6,7},{7,6},{8,9},{9,8},{10,11... | collective-permute-start | bytes 159752 | tf_op jit(solution)/shard_map/ppermute | solution.py:392
  76.2 0.6 copy-start.6

commit v3 on v2

v3 whole, which is shorter than its diff:
```python
import functools
import math

import jax
import jax.numpy as jnp
import numpy as np
from jax import lax
from jax.experimental import pallas as pl
from jax.experimental.pallas import tpu as pltpu
from jax.sharding import PartitionSpec as P

HS = 64

score_scale = 8.0
epsilon = 1e-06

VMEM_LIMIT = 20 * 1024 * 1024


def dot(a, b):
    return jnp.dot(a, b, preferred_element_type=jnp.float32)


def dot_nt(a, b):
    return lax.dot_general(a, b, (((1,), (1,)), ((), ())), preferred_element_type=jnp.float32)


def cat(parts, axis):
    return parts[0] if len(parts) == 1 else jnp.concatenate(parts, axis=axis)


def side_of():
    return lax.rem(lax.axis_index("head"), 2)


def on_chip(kernel, name, operands, results, flops, out_memory=pltpu.VMEM):
    near = [pltpu.with_memory_space_constraint(array, pltpu.VMEM) for array in operands]
    if out_memory is pltpu.VMEM:
        out_shape = tuple(pltpu.VMEM(shape, dtype) for shape, dtype in results)
    else:
        out_shape = tuple(jax.ShapeDtypeStruct(shape, dtype) for shape, dtype in results)
    return pl.pallas_call(
        kernel,
        in_specs=[pl.BlockSpec(memory_space=pltpu.VMEM)] * len(operands),
        out_specs=tuple(pl.BlockSpec(memory_space=pltpu.VMEM) for _ in results),
        out_shape=out_shape,
        compiler_params=pltpu.CompilerParams(vmem_limit_bytes=VMEM_LIMIT),
        cost_estimate=pl.CostEstimate(flops=int(flops), bytes_accessed=0, transcendentals=0),
        name=name,
    )(*near)


def spread_kernel(rows_ref, spread_ref, edge_ref):
    members, count, _ = spread_ref.shape
    own = rows_ref[pl.ds(pl.multiple_of(side_of() * count, 8), count), :].astype(jnp.bfloat16)
    for i in range(members):
        spread_ref[i] = own
    edge_ref[...] = rows_ref[rows_ref.shape[0] - 8 :, :]


def combine_kernel(layer, pieces, in_ref, gain_ref, *refs):
    key_refs, value_refs, out_ref = refs[:pieces], refs[pieces : 2 * pieces], refs[2 * pieces]
    base = in_ref[layer]
    channels = base.shape[0]

    def store(row, value):
        high = value.astype(jnp.bfloat16)
        rows = value.shape[0]
        out_ref[row : row + rows, :channels] = high
        out_ref[row : row + rows, channels:] = (value - high.astype(jnp.float32)).astype(
            jnp.bfloat16
        )
        return row + rows

    scaled = base.astype(jnp.float32) * gain_ref[layer : layer + 1, :]
    high = scaled.astype(jnp.bfloat16)
    low = (scaled - high.astype(jnp.float32)).astype(jnp.bfloat16)
    both = jnp.concatenate([high, low], axis=0)
    row = 0
    for group in (key_refs, value_refs):
        for first in range(0, pieces, 2):
            columns = cat([ref[layer] for ref in group[first : first + 2]], 1)
            product = dot(both, columns)
            row = store(row, (product[:channels] + product[channels:]).T)
    row = store(row, dot_nt(base, base))
    eye = lax.broadcasted_iota(jnp.int32, (channels, channels), 0) == lax.broadcasted_iota(
        jnp.int32, (channels, channels), 1
    )
    store(row, jnp.where(eye, 1.0, 0.0))


def combine(layer, in_proj, attn_gain, key_pieces, value_pieces):
    pieces = len(key_pieces)
    _, channels, features = in_proj.shape
    rows = 2 * pieces * key_pieces[0].shape[2] + 2 * channels
    return on_chip(
        functools.partial(combine_kernel, layer, pieces),
        "combine",
        [in_proj, attn_gain, *key_pieces, *value_pieces],
        [((rows, 2 * channels), jnp.bfloat16)],
        4 * channels * features * rows,
    )[0]


def queries_kernel(layer, pieces, rows_ref, edge_ref, in_ref, gain_ref, *refs):
    query_refs, shifted_ref, out_ref = refs[:pieces], refs[pieces], refs[pieces + 1]
    count = shifted_ref.shape[0]
    token = lax.broadcasted_iota(jnp.int32, (count, 1), 0)
    if layer == 0:
        start = pl.multiple_of(side_of() * count, 8)
        values = rows_ref[pl.ds(start, count), :]
        border = jnp.where(side_of() == 0, edge_ref[7:8, :], rows_ref[count - 1 : count, :])
        moved, at = pltpu.roll(values, 1, 0), 0
    else:
        values = rows_ref[...]
        border = edge_ref[0:1, :]
        moved, at = pltpu.roll(values, count - 1, 0), count - 1
    shifted = jnp.where(token == at, border, moved).astype(jnp.bfloat16)
    shifted_ref[...] = shifted
    hidden = dot(shifted, in_ref[layer])
    spread = lax.rsqrt(jnp.mean(hidden * hidden, axis=1, keepdims=True) + epsilon)
    normed = (hidden * spread * gain_ref[layer : layer + 1, :]).astype(jnp.bfloat16)
    for first in range(0, pieces, 2):
        query = dot(normed, cat([ref[layer] for ref in query_refs[first : first + 2]], 1))
        width = query.shape[1]
        head = lax.broadcasted_iota(jnp.int32, (count, width), 1) // HS
        for h in range(width // HS):
            band = jnp.where(head == h, query, 0.0)
            mean = jnp.sum(band * band, axis=1, keepdims=True) * (1.0 / HS)
            out_ref[first // 2, h * count : (h + 1) * count, :] = (
                band * lax.rsqrt(mean + epsilon)
            ).astype(jnp.bfloat16)


def make_queries(layer, count, rows, edge, in_proj, attn_gain, query_pieces):
    pieces = len(query_pieces)
    channels, features = in_proj.shape[1:]
    width = min(2, pieces) * query_pieces[0].shape[2]
    groups = pieces * query_pieces[0].shape[2] // width
    return on_chip(
        functools.partial(queries_kernel, layer, pieces),
        "queries",
        [rows, edge, in_proj, attn_gain, *query_pieces],
        [
            ((count, channels), jnp.bfloat16),
            ((groups, width // HS * count, width), jnp.bfloat16),
        ],
        2 * count * features * (channels + groups * width),
    )


def attend_rows(cfg, place, pos_ref, maps_ref, query_ref, source_ref, carry):
    count, features, size = cfg["count"], cfg["features"], cfg["chunk"]
    side = side_of()
    groups, _, group_cols = query_ref.shape
    channels = source_ref.shape[1]
    heads = group_cols // HS
    total_cols = groups * group_cols
    token = lax.broadcasted_iota(jnp.int32, (count, 1), 0)
    first_token = lax.axis_index("seq") * (2 * count) + side * count
    query_token = first_token + jnp.concatenate([token] * heads, axis=0)
    offset = (side if place == 0 else 1 - side) * count

    def one_chunk(start, carry):
        source = source_ref[pl.ds(start, size), :]
        twice = jnp.concatenate([source, source], axis=1)
        key_token = pos_ref[:, pl.ds(start, size)] + offset
        allowed = key_token < query_token if cfg["layer"] == 0 else key_token > query_token
        tail = dot_nt(maps_ref[2 * total_cols :, :], twice)
        square = jnp.sum(tail[:channels] * tail[channels:], axis=0, keepdims=True)
        scale = lax.rsqrt(jnp.maximum(square, 0.0) * (1.0 / features) + epsilon)
        scale_sq = scale * scale
        result = []
        for g in range(groups):
            low = g * group_cols
            key = dot_nt(maps_ref[low : low + group_cols, :], twice)
            value = dot_nt(maps_ref[total_cols + low : total_cols + low + group_cols, :], twice)
            keys = []
            for h in range(heads):
                one = key[h * HS : (h + 1) * HS]
                mean = jnp.sum(one * one, axis=0, keepdims=True) * (1.0 / HS)
                factor = scale * lax.rsqrt(mean * scale_sq + epsilon)
                keys.append((one * factor).astype(jnp.bfloat16))
            value = (value * scale).astype(jnp.bfloat16)
            scores = dot(query_ref[g], jnp.concatenate(keys, axis=0)) * (score_scale / HS)
            weights = jnp.where(allowed, jnp.exp(scores), 0.0)
            product = dot_nt(weights.astype(jnp.bfloat16), value)
            total = weights[:, :128]
            for lane in range(128, size, 128):
                total = total + weights[:, lane : lane + 128]
            result.append(
                (product, total)
                if carry is None
                else (carry[g][0] + product, carry[g][1] + total)
            )
        return tuple(result)

    chunks = source_ref.shape[0] // size
    carry = one_chunk(0, carry)
    if chunks <= 4:
        for c in range(1, chunks):
            carry = one_chunk(c * size, carry)
    else:
        carry = lax.fori_loop(
            1, chunks, lambda c, now: one_chunk(pl.multiple_of(c * size, size), now), carry
        )
    return carry


def first_half_kernel(cfg, pos_ref, maps_ref, query_ref, own_ref, number_ref, total_ref):
    carry = attend_rows(cfg, 0, pos_ref, maps_ref, query_ref, own_ref, None)
    for g, (number, total) in enumerate(carry):
        number_ref[g] = number
        total_ref[g] = total


def second_half_kernel(cfg, pos_ref, maps_ref, query_ref, other_ref, number_ref, total_ref, shifted_ref, in_ref, gain_ref, rows_ref, *refs):
    layer, pieces, last, count = cfg["layer"], cfg["pieces"], cfg["last"], cfg["count"]
    refs = list(refs)
    mix_refs = [refs.pop(0) for _ in range(pieces)]
    param_refs = [refs.pop(0) for _ in range(pieces)]
    side, way = side_of(), lax.axis_index("head")
    channels, features = in_ref.shape[1:]
    groups, _, group_cols = query_ref.shape
    heads = group_cols // HS
    carry = tuple((number_ref[g], total_ref[g]) for g in range(groups))
    carry = attend_rows(cfg, 1, pos_ref, maps_ref, query_ref, other_ref, carry)

    mixture = dot(shifted_ref[...], in_ref[layer])
    head = lax.broadcasted_iota(jnp.int32, (count, group_cols), 1) // HS
    for g, (number, total) in enumerate(carry):
        share_of = 1.0 / (jnp.sum(total, axis=1, keepdims=True) + 1.0)
        attended = jnp.zeros((count, group_cols), jnp.float32)
        for h in range(heads):
            band = slice(h * count, (h + 1) * count)
            attended = jnp.where(head == h, number[band] * share_of[band], attended)
        rows = cat([ref[layer] for ref in mix_refs[2 * g : 2 * g + 2]], 0)
        mixture = mixture + dot(attended.astype(jnp.bfloat16), rows)
    spread = lax.rsqrt(jnp.mean(mixture * mixture, axis=1, keepdims=True) + epsilon)
    scaled = (mixture * spread * gain_ref[layer : layer + 1, :]).astype(jnp.bfloat16)
    share = features // pieces
    param_all = refs[-1]
    for j, ref in enumerate(param_refs):
        at = pl.multiple_of(lax.rem(way + j, pieces) * share, 16)
        param_all[pl.ds(at, share), :] = ref[layer]
    predicted = dot(scaled, param_all[...])
    log_scale = 2.0 * jnp.tanh(0.5 * predicted[:, channels:])
    if last:
        first_log_ref, out_ref = refs[:2]
        values = rows_ref[...]
        result = (values - predicted[:, :channels]) * jnp.exp(-log_scale)
        term = -(first_log_ref[...] + log_scale) - 0.5 * (result * result)
        loglik = jnp.sum(term.T, axis=0, keepdims=True) * (1.0 / channels) - 0.5 * math.log(
            2.0 * math.pi
        )
        out_ref[:count, :] = result
        out_ref[count:, :count] = jnp.broadcast_to(loglik, (8, count))
    else:
        out_ref, log_ref, spread_ref, edge_ref = refs[:4]
        values = rows_ref[pl.ds(pl.multiple_of(side * count, 8), count), :]
        result = (values - predicted[:, :channels]) * jnp.exp(-log_scale)
        out_ref[...] = result
        log_ref[...] = log_scale
        edge_ref[...] = result[:8]
        narrow = result.astype(jnp.bfloat16)
        for i in range(spread_ref.shape[0]):
            spread_ref[i] = narrow


def config(layer, count, features, pieces, keys):
    chunk = next(size for size in (512, 384, 256, 128, keys) if keys % size == 0)
    return {
        "layer": layer,
        "last": layer == 1,
        "count": count,
        "features": features,
        "pieces": pieces,
        "chunk": chunk,
    }


def first_half(cfg, positions, maps, queries, own):
    groups, rows, cols = queries.shape
    return on_chip(
        functools.partial(first_half_kernel, cfg),
        "first_half",
        [positions, maps, queries, own],
        [((groups, rows, cols), jnp.float32), ((groups, rows, 128), jnp.float32)],
        2 * own.shape[0] * (maps.size + 2 * queries.size),
    )


def second_half(cfg, members, positions, maps, queries, other, sums, shifted, in_proj, param_gain, rows, mix_pieces, param_pieces, first_log=None):
    count, channels = shifted.shape
    operands = [positions, maps, queries, other, *sums, shifted, in_proj, param_gain, rows]
    operands += [*mix_pieces, *param_pieces]
    if cfg["last"]:
        operands.append(first_log)
        results = [((count + 8, channels), jnp.float32)]
    else:
        results = [
            ((count, channels), jnp.float32),
            ((count, channels), jnp.float32),
            ((members, count, channels), jnp.bfloat16),
            ((8, channels), jnp.float32),
        ]
    results.append(((cfg["features"], param_pieces[0].shape[2]), jnp.bfloat16))
    return on_chip(
        functools.partial(second_half_kernel, cfg),
        "second_half",
        operands,
        results,
        2 * other.shape[0] * (maps.size + 2 * queries.size),
    )[:-1]


def finish_kernel(own_ref, other_ref, final_ref, loglik_ref):
    count = final_ref.shape[0] // 2
    side = side_of()
    for ref, place in ((own_ref, side), (other_ref, 1 - side)):
        final_ref[pl.ds(pl.multiple_of(place * count, 8), count), :] = ref[:count, :]
    first = jnp.where(side == 0, own_ref[count : count + 1, :], other_ref[count : count + 1, :])
    second = jnp.where(side == 0, other_ref[count : count + 1, :], own_ref[count : count + 1, :])
    loglik_ref[...] = jnp.concatenate([first[:, :count], second[:, :count]], axis=1)


def body(
    latents, in_proj, query_proj, key_proj, value_proj, mix_proj, param_proj, attn_gain, param_gain
):
    members, ways = lax.axis_size("seq"), lax.axis_size("head")
    rows, channels = latents.shape
    features = in_proj.shape[2]
    count = rows // 2
    keys = members * count

    def swap(array):
        return lax.ppermute(array, "head", [(i, i ^ 1) for i in range(ways)])

    def pieces_of(array):
        shares = [array]
        for j in range(1, ways):
            shares.append(
                lax.ppermute(array, "head", [((i + j) % ways, i) for i in range(ways)])
            )
        return shares

    def gather(spread):
        return lax.all_to_all(spread, "seq", 0, 0).reshape(keys, channels)

    spread, edge = on_chip(
        spread_kernel,
        "spread_rows",
        [latents],
        [((members, count, channels), jnp.bfloat16), ((8, channels), jnp.float32)],
        keys * channels,
    )
    own = gather(spread)
    edge = lax.ppermute(edge, "seq", [(i, i + 1) for i in range(members - 1)])
    key_pieces, value_pieces = pieces_of(key_proj), pieces_of(value_proj)
    query_pieces, mix_pieces = pieces_of(query_proj), pieces_of(mix_proj)
    param_pieces = pieces_of(param_proj)
    maps = [combine(b, in_proj, attn_gain, key_pieces, value_pieces) for b in range(2)]
    shifted, queries = make_queries(0, count, latents, edge, in_proj, attn_gain, query_pieces)
    positions = jnp.asarray(
        (np.arange(keys) // count * rows + np.arange(keys) % count)[None], jnp.int32
    )
    own, maps, shifted, queries = lax.optimization_barrier((own, maps, shifted, queries))

    cfg = config(0, count, features, ways, keys)
    other = swap(own)
    sums = first_half(cfg, positions, maps[0], queries, own)
    first_out, first_log, spread, edge = second_half(
        cfg, members, positions, maps[0], queries, other, sums, shifted, in_proj, param_gain, latents, mix_pieces, param_pieces
    )

    pairs = []
    for s in range(members):
        for w in range(ways):
            if w % 2:
                pairs.append((s * ways + w, s * ways + w - 1))
            elif s > 0:
                pairs.append((s * ways + w, (s - 1) * ways + w + 1))
    own = gather(spread)
    edge = lax.ppermute(edge, ("seq", "head"), pairs)
    shifted, queries = make_queries(1, count, first_out, edge, in_proj, attn_gain, query_pieces)
    cfg = config(1, count, features, ways, keys)
    other = swap(own)
    sums = first_half(cfg, positions, maps[1], queries, own)
    (packed,) = second_half(
        cfg, members, positions, maps[1], queries, other, sums, shifted, in_proj, param_gain, first_out, mix_pieces, param_pieces, first_log
    )
    final_latent, token_loglik = on_chip(
        finish_kernel,
        "finish",
        [packed, swap(packed)],
        [((rows, channels), jnp.float32), ((1, rows), jnp.float32)],
        rows * channels,
        out_memory=None,
    )
    return (final_latent, token_loglik.reshape(rows))


def solution(mesh):
    placed = (
        P("seq", None),
        P(),
        P(None, None, "head"),
        P(None, None, "head"),
        P(None, None, "head"),
        P(None, "head", None),
        P(None, "head", None),
        P(),
        P(),
    )
    return jax.shard_map(
        body, mesh=mesh, in_specs=placed, out_specs=(P("seq", None), P("seq")), check_vma=False
    )
```

time: 78.9 us -> 72.1 us (0.914)
  waiting for transfers between devices: 11.6 us -> 3.91 us
  blocking collectives: 16.2 us -> 23.5 us
  Pallas kernels: 27.6 us -> 20.4 us
    all_to_all x1, waiting for transfers between devices: 7.46 us -> 0.01 us  [gather(): return lax.all_to_all(spread, 'seq', 0, 0).reshape(keys, channels)]
    all_to_all x1, blocking collectives: 16.2 us -> 23.5 us  [gather(): return lax.all_to_all(spread, 'seq', 0, 0).reshape(keys, channels)]
    pallas_call x7 -> x10, Pallas kernels: 27.6 us -> 20.4 us  [on_chip(): pl.pallas_call(kernel, in_specs=[pl.BlockSpec(memory_space=pltpu.VMEM)] *...]
    unnamed x26 -> x40, local copies, waits for them, and re-layouts: 5.28 us -> 5.47 us
  transfers between devices with their start and end apart: 11 -> 11, of which waited for: 4 -> 3; matrix products, arithmetic and copies ran while one was open for 0% -> 0% of each run, Pallas kernels for 14% -> 18%
where the time goes in v3:
time: 72.1 us; the launch traced here: 71.5 us
  blocking collectives  23.5 us (33%)
  Pallas kernels  20.4 us (28%)
  starting transfers between devices  17.3 us (24%)
  local copies, waits for them, and re-layouts  5.47 us (8%)
  waiting for transfers between devices  3.91 us (5%)
  between operations  0.93 us (1%)
    all_to_all x1, blocking collectives, gather(): return lax.all_to_all(spread, 'seq', 0, 0).reshape(keys, channels)  23.5 us
    pallas_call x10, Pallas kernels, on_chip(): pl.pallas_call(kernel, in_specs=[pl.BlockSpec(memory_space=pltpu.VMEM)] *...  20.4 us
    all_to_all x1, starting transfers between devices, gather(): return lax.all_to_all(spread, 'seq', 0, 0).reshape(keys, channels)  8.12 us
    unnamed x40, local copies, waits for them, and re-layouts  5.47 us
    ppermute x1, starting transfers between devices, body(): edge = lax.ppermute(edge, 'seq', [(i, i + 1) for i in range(members - 1)])  3.91 us
    ppermute x3, starting transfers between devices, swap(): return lax.ppermute(array, 'head', [(i, i ^ 1) for i in range(ways)])  2.87 us
    ppermute x1, waiting for transfers between devices, body(): edge = lax.ppermute(edge, ('seq', 'head'), pairs)  1.77 us
  transfers between devices with their start and end apart: 11, of which 3 were waited for; matrix products, arithmetic and copies ran while one was open for 0% of the time, Pallas kernels for 18%

profile of v3, /device:TPU:0, one launch (start us, length us, event | category | flops | bytes accessed | tf_op | source)
XLA Modules:
  0.0 71.5 jit_solution(9977774056123494229)
XLA Ops:
  1.7 0.9 %copy-done.9 = f32[192,128]{1,0:T(8,128)S(1)} copy-done((f32[192,128]{1,0:T(8,128)S(1)}, f32[192,128]{1,0:T(8,128)}, u32[]{:S(2)}) %copy-start.9) | copy-done | bytes 98328
  2.6 0.8 %spread_rows.1 = (bf16[16,96,128]{2,1,0:T(8,128)(2,1)}, f32[8,128]{1,0:T(8,128)S(1)}) custom-call(f32[192,128]{1,0:T(8,128)S(1)} %copy-done.9), custom_call_target="tpu_custom_call" | custom-call | flops 196608 | tf_op jit(solution)/shard_map/spread_rows/pallas_call | solution.py:42
  3.3 8.1 %all-to-all-start = ((bf16[16,96,128]{2,1,0:T(8,128)(2,1)}), bf16[16,96,128]{2,1,0:T(8,128)(2,1)}, u32[]{:S(2)}, u32[]{:S(2)}) async-start(bf16[16,96,128]{2,1,0:T(8,128)(2,1)} %get-tuple-element.24), calls=%async_computation | async-start | bytes 786432 | tf_op jit(solution)/shard_map/all_to_all | solution.py:348
  11.5 3.9 %collective-permute-start.2 = (f32[8,128]{1,0:T(8,128)S(1)}, f32[8,128]{1,0:T(8,128)S(1)}, u32[]{:S(2)}, u32[]{:S(2)}) collective-permute-start(f32[8,128]{1,0:T(8,128)S(1)} %get-tuple-element.25), channel_id=1, source_target_pairs={{0,2},{2,4},{4,6},{6,8},{8,10},{10,12},{12,14},{14,16},{16,18},{18... | collective-permute-start | bytes 12296 | tf_op jit(solution)/shard_map/ppermute | solution.py:358
  15.5 1.2 %collective-permute-done.2.edge_ref = f32[8,128]{1,0:T(8,128)S(1)} collective-permute-done((f32[8,128]{1,0:T(8,128)S(1)}, f32[8,128]{1,0:T(8,128)S(1)}, u32[]{:S(2)}, u32[]{:S(2)}) %collective-permute-start.2) | collective-permute-done | bytes 4128 | tf_op jit(solution)/shard_map/ppermute | solution.py:358
  16.8 1.1 %copy-done.5 = bf16[2,1536,128]{2,1,0:T(8,128)(2,1)S(1)} copy-done((bf16[2,1536,128]{2,1,0:T(8,128)(2,1)S(1)}, bf16[2,1536,128]{2,1,0:T(8,128)(2,1)}, u32[]{:S(2)}) %copy-start.5) | copy-done | bytes 786456
  17.9 0.7 copy-done.12
  18.6 1.8 %queries.2 = (bf16[96,128]{1,0:T(8,128)(2,1)S(1)}, bf16[1,384,256]{2,1,0:T(8,128)(2,1)S(1)}) custom-call(f32[192,128]{1,0:T(8,128)S(1)} %copy-done.10, f32[8,128]{1,0:T(8,128)S(1)} %collective-permute-done.2.edge_ref, bf16[2,128,1536]{2,1,0:T(8,128)(2,1)S(1)} %copy-done, f32[2,1536]{1,0:T(2,128)S(1)} %copy-done.12, bf16[2,1536,128]{2,1,0:T(8,128)(2,1)S(1)} %copy-done.5, ...), custom_call_target="tpu_custom_call" | custom-call | flops 113246208 | tf_op jit(solution)/shard_map/queries/pallas_call | solution.py:42
  20.4 1.9 %combine.3.maps_ref = bf16[768,256]{1,0:T(8,128)(2,1)S(1)} custom-call(bf16[2,128,1536]{2,1,0:T(8,128)(2,1)S(1)} %copy-done, f32[2,1536]{1,0:T(2,128)S(1)} %copy-done.12, bf16[2,1536,128]{2,1,0:T(8,128)(2,1)S(1)} %copy-done.1, bf16[2,1536,128]{2,1,0:T(8,128)(2,1)S(1)} %collective-permute-done.refs_1_, bf16[2,1536,128]{2,1,0:T(8,128)(2,1)S(1)} %copy-done.2, ...), custom_call_target="tpu_custom_call" | custom-call | flops 603979776 | tf_op jit(solution)/shard_map/combine/pallas_call | solution.py:42
  22.4 1.9 %combine.2.maps_ref = bf16[768,256]{1,0:T(8,128)(2,1)S(1)} custom-call(bf16[2,128,1536]{2,1,0:T(8,128)(2,1)S(1)} %copy-done, f32[2,1536]{1,0:T(2,128)S(1)} %copy-done.12, bf16[2,1536,128]{2,1,0:T(8,128)(2,1)S(1)} %copy-done.1, bf16[2,1536,128]{2,1,0:T(8,128)(2,1)S(1)} %collective-permute-done.refs_1_, bf16[2,1536,128]{2,1,0:T(8,128)(2,1)S(1)} %copy-done.2, ...), custom_call_target="tpu_custom_call" | custom-call | flops 603979776 | tf_op jit(solution)/shard_map/combine/pallas_call | solution.py:42
  24.3 0.8 %copy-done.7 = bf16[768,256]{1,0:T(8,128)(2,1)} copy-done((bf16[768,256]{1,0:T(8,128)(2,1)}, bf16[768,256]{1,0:T(8,128)(2,1)S(1)}, u32[]{:S(2)}) %copy-start.7) | copy-done | bytes 393240
  25.6 1.0 %copy-done.8 = bf16[768,256]{1,0:T(8,128)(2,1)S(1)} copy-done((bf16[768,256]{1,0:T(8,128)(2,1)S(1)}, bf16[768,256]{1,0:T(8,128)(2,1)}, u32[]{:S(2)}) %copy-start.8) | copy-done | bytes 393240
  26.6 0.9 %copy-done.15 = bf16[1,384,256]{2,1,0:T(8,128)(2,1)S(1)} copy-done((bf16[1,384,256]{2,1,0:T(8,128)(2,1)S(1)}, bf16[1,384,256]{2,1,0:T(8,128)(2,1)}, u32[]{:S(2)}) %copy-start.15) | copy-done | bytes 196632
  27.5 2.8 %first_half.2 = (f32[1,384,256]{2,1,0:T(8,128)S(1)}, f32[1,384,128]{2,1,0:T(8,128)S(1)}) custom-call(s32[1,1536]{1,0:T(1,128)S(1)} %copy-done.19, bf16[768,256]{1,0:T(8,128)(2,1)S(1)} %copy-done.8, bf16[1,384,256]{2,1,0:T(8,128)(2,1)S(1)} %copy-done.15, bf16[1536,128]{1,0:T(8,128)(2,1)} %bitcast.own_ref), custom_call_target="tpu_custom_call" | custom-call | flops 1207959552 | tf_op jit(solution)/shard_map/first_half/pallas_call | solution.py:42
  30.4 3.3 %second_half.2 = (f32[96,128]{1,0:T(8,128)S(1)}, f32[96,128]{1,0:T(8,128)S(1)}, bf16[16,96,128]{2,1,0:T(8,128)(2,1)S(1)}, f32[8,128]{1,0:T(8,128)S(1)}, bf16[1536,256]{1,0:T(8,128)(2,1)}) custom-call(s32[1,1536]{1,0:T(1,128)S(1)} %copy-done.19, bf16[768,256]{1,0:T(8,128)(2,1)S(1)} %copy-done.8, bf16[1,384,256]{2,1,0:T(8,128)(2,1)S(1)} %copy-done.15, ...), custom_call_target="tpu_custom_call" | custom-call | flops 1207959552 | tf_op jit(solution)/shard_map/second_half/pallas_call | solution.py:42
  33.8 23.5 %all_to_all.10 = bf16[16,96,128]{2,1,0:T(8,128)(2,1)S(1)} all-to-all(bf16[16,96,128]{2,1,0:T(8,128)(2,1)S(1)} %get-tuple-element.38), channel_id=1, replica_groups=mesh['seq'=16,'head'=2] {'seq'}, dimensions={0} | all-to-all | bytes 786432 | tf_op jit(solution)/shard_map/all_to_all | solution.py:348
  57.3 1.3 %collective-permute-start.7 = (f32[8,128]{1,0:T(8,128)S(1)}, f32[8,128]{1,0:T(8,128)S(1)}, u32[]{:S(2)}, u32[]{:S(2)}) collective-permute-start(f32[8,128]{1,0:T(8,128)S(1)} %get-tuple-element.36), channel_id=1, source_target_pairs={{1,0},{2,1},{3,2},{4,3},{5,4},{6,5},{7,6},{8,7},{9,8},{10,9},{11,1... | collective-permute-start | bytes 12296 | tf_op jit(solution)/shard_map/ppermute | solution.py:384
  58.6 1.8 %collective-permute-done.7.edge_ref = f32[8,128]{1,0:T(8,128)S(1)} collective-permute-done((f32[8,128]{1,0:T(8,128)S(1)}, f32[8,128]{1,0:T(8,128)S(1)}, u32[]{:S(2)}, u32[]{:S(2)}) %collective-permute-start.7) | collective-permute-done | bytes 4128 | tf_op jit(solution)/shard_map/ppermute | solution.py:384
  60.4 1.8 %queries.3 = (bf16[96,128]{1,0:T(8,128)(2,1)S(1)}, bf16[1,384,256]{2,1,0:T(8,128)(2,1)S(1)}) custom-call(f32[96,128]{1,0:T(8,128)S(1)} %get-tuple-element.35.rows_ref, f32[8,128]{1,0:T(8,128)S(1)} %collective-permute-done.7.edge_ref, bf16[2,128,1536]{2,1,0:T(8,128)(2,1)S(1)} %copy-done, f32[2,1536]{1,0:T(2,128)S(1)} %copy-done.13, ...), custom_call_target="tpu_custom_call" | custom-call | flops 113246208 | tf_op jit(solution)/shard_map/queries/pallas_call | solution.py:42
  62.2 1.8 %first_half.3 = (f32[1,384,256]{2,1,0:T(8,128)S(1)}, f32[1,384,128]{2,1,0:T(8,128)S(1)}) custom-call(s32[1,1536]{1,0:T(1,128)S(1)} %copy-done.19, bf16[768,256]{1,0:T(8,128)(2,1)S(1)} %combine.3.maps_ref, bf16[1,384,256]{2,1,0:T(8,128)(2,1)S(1)} %get-tuple-element.37.query_ref, bf16[1536,128]{1,0:T(8,128)(2,1)S(1)} %bitcast.4), custom_call_target="tpu_custom_call" | custom-call | flops 1207959552 | tf_op jit(solution)/shard_map/first_half/pallas_call | solution.py:42
  64.0 3.6 %second_half.3 = (f32[104,128]{1,0:T(8,128)S(1)}, bf16[1536,256]{1,0:T(8,128)(2,1)}) custom-call(s32[1,1536]{1,0:T(1,128)S(1)} %copy-done.19, bf16[768,256]{1,0:T(8,128)(2,1)S(1)} %combine.3.maps_ref, bf16[1,384,256]{2,1,0:T(8,128)(2,1)S(1)} %get-tuple-element.37.query_ref, bf16[1536,128]{1,0:T(8,128)(2,1)S(1)} %collective-permute-done.8.other_ref, ...), custom_call_target="tpu_custom_call" | custom-call | flops 1207959552 | tf_op jit(solution)/shard_map/second_half/pallas_call | solution.py:42
  67.6 2.4 %collective-permute-start.9 = (f32[104,128]{1,0:T(8,128)S(1)}, f32[104,128]{1,0:T(8,128)S(1)}, u32[]{:S(2)}, u32[]{:S(2)}) collective-permute-start(f32[104,128]{1,0:T(8,128)S(1)} %get-tuple-element.43.own_ref), channel_id=1, source_target_pairs={{0,1},{1,0},{2,3},{3,2},{4,5},{5,4},{6,7},{7,6},{8,9},{9,8},{10,11... | collective-permute-start | bytes 159752 | tf_op jit(solution)/shard_map/ppermute | solution.py:337
  69.9 0.9 %collective-permute-done.9.other_ref = f32[104,128]{1,0:T(8,128)S(1)} collective-permute-done((f32[104,128]{1,0:T(8,128)S(1)}, f32[104,128]{1,0:T(8,128)S(1)}, u32[]{:S(2)}, u32[]{:S(2)}) %collective-permute-start.9) | collective-permute-done | bytes 53280 | tf_op jit(solution)/shard_map/ppermute | solution.py:337
  70.8 0.7 finish.1
  (49 shorter events, 1.7 us)
Async XLA Ops:
  0.6 16.1 %copy-start = (bf16[2,128,1536]{2,1,0:T(8,128)(2,1)S(1)}, bf16[2,128,1536]{2,1,0:T(8,128)(2,1)}, u32[]{:S(2)}) copy-start(bf16[2,128,1536]{2,1,0:T(8,128)(2,1)} %in_ref.11) | copy-start | bytes 2359300
  0.6 16.1 %collective-permute-start.3 = (bf16[2,1536,128]{2,1,0:T(8,128)(2,1)}, bf16[2,1536,128]{2,1,0:T(8,128)(2,1)}, u32[]{:S(2)}, u32[]{:S(2)}) collective-permute-start(bf16[2,1536,128]{2,1,0:T(8,128)(2,1)} %refs_0_.10), channel_id=1, source_target_pairs={{1,0},{0,1},{3,2},{2,3},{5,4},{4,5},{7,6},{6,7},{9,8},{8,9},{11,10... | collective-permute-start | bytes 2359304 | tf_op jit(solution)/shard_map/ppermute | solution.py:343
  1.2 19.2 %collective-permute-start = (bf16[2,1536,128]{2,1,0:T(8,128)(2,1)}, bf16[2,1536,128]{2,1,0:T(8,128)(2,1)S(1)}, u32[]{:S(2)}, u32[]{:S(2)}) collective-permute-start(bf16[2,1536,128]{2,1,0:T(8,128)(2,1)} %refs_0_.7), channel_id=1, source_target_pairs={{1,0},{0,1},{3,2},{2,3},{5,4},{4,5},{7,6},{6,7},{9,8},{8,9},{11,10... | collective-permute-start | bytes 2359304 | tf_op jit(solution)/shard_map/ppermute | solution.py:343
  1.2 19.2 %collective-permute-start.1 = (bf16[2,1536,128]{2,1,0:T(8,128)(2,1)}, bf16[2,1536,128]{2,1,0:T(8,128)(2,1)}, u32[]{:S(2)}, u32[]{:S(2)}) collective-permute-start(bf16[2,1536,128]{2,1,0:T(8,128)(2,1)} %refs_2_.5), channel_id=1, source_target_pairs={{1,0},{0,1},{3,2},{2,3},{5,4},{4,5},{7,6},{6,7},{9,8},{8,9},{11,10... | collective-permute-start | bytes 2359304 | tf_op jit(solution)/shard_map/ppermute | solution.py:343
  3.3 13.4 %copy-start.10 = (f32[192,128]{1,0:T(8,128)S(1)}, f32[192,128]{1,0:T(8,128)}, u32[]{:S(2)}) copy-start(f32[192,128]{1,0:T(8,128)} %rows_ref.5) | copy-start | bytes 294916
  3.3 21.7 %all-to-all-start = ((bf16[16,96,128]{2,1,0:T(8,128)(2,1)}), bf16[16,96,128]{2,1,0:T(8,128)(2,1)}, u32[]{:S(2)}, u32[]{:S(2)}) async-start(bf16[16,96,128]{2,1,0:T(8,128)(2,1)} %get-tuple-element.24), calls=%async_computation | async-start | bytes 786432 | tf_op jit(solution)/shard_map/all_to_all | solution.py:348
  11.5 9.0 %copy-start.1 = (bf16[2,1536,128]{2,1,0:T(8,128)(2,1)S(1)}, bf16[2,1536,128]{2,1,0:T(8,128)(2,1)}, u32[]{:S(2)}) copy-start(bf16[2,1536,128]{2,1,0:T(8,128)(2,1)} %refs_0_.7) | copy-start | bytes 2359300
  11.5 8.9 %copy-start.2 = (bf16[2,1536,128]{2,1,0:T(8,128)(2,1)S(1)}, bf16[2,1536,128]{2,1,0:T(8,128)(2,1)}, u32[]{:S(2)}) copy-start(bf16[2,1536,128]{2,1,0:T(8,128)(2,1)} %refs_2_.5) | copy-start | bytes 2359300
  11.5 5.2 %collective-permute-start.2 = (f32[8,128]{1,0:T(8,128)S(1)}, f32[8,128]{1,0:T(8,128)S(1)}, u32[]{:S(2)}, u32[]{:S(2)}) collective-permute-start(f32[8,128]{1,0:T(8,128)S(1)} %get-tuple-element.25), channel_id=1, source_target_pairs={{0,2},{2,4},{4,6},{6,8},{8,10},{10,12},{12,14},{14,16},{16,18},{18... | collective-permute-start | bytes 12296 | tf_op jit(solution)/shard_map/ppermute | solution.py:358
  15.4 14.9 %collective-permute-start.5 = (bf16[2,128,1536]{2,1,0:T(8,128)(2,1)}, bf16[2,128,1536]{2,1,0:T(8,128)(2,1)S(1)}, u32[]{:S(2)}, u32[]{:S(2)}) collective-permute-start(bf16[2,128,1536]{2,1,0:T(8,128)(2,1)} %refs_0_.11), channel_id=1, source_target_pairs={{1,0},{0,1},{3,2},{2,3},{5,4},{4,5},{7,6},{6,7},{9,8},{8,9},{11,10... | collective-permute-start | bytes 2359304 | tf_op jit(solution)/shard_map/ppermute | solution.py:343
  16.7 13.6 %collective-permute-start.6 = (bf16[2,768,256]{2,1,0:T(8,128)(2,1)}, bf16[2,768,256]{2,1,0:T(8,128)(2,1)S(1)}, u32[]{:S(2)}, u32[]{:S(2)}) collective-permute-start(bf16[2,768,256]{2,1,0:T(8,128)(2,1)} %refs_2_.7), channel_id=1, source_target_pairs={{1,0},{0,1},{3,2},{2,3},{5,4},{4,5},{7,6},{6,7},{9,8},{8,9},{11,10... | collective-permute-start | bytes 2359304 | tf_op jit(solution)/shard_map/ppermute | solution.py:343
  20.4 2.0 %copy-start.14 = (bf16[1,384,256]{2,1,0:T(8,128)(2,1)}, bf16[1,384,256]{2,1,0:T(8,128)(2,1)S(1)}, u32[]{:S(2)}) copy-start(bf16[1,384,256]{2,1,0:T(8,128)(2,1)S(1)} %get-tuple-element.30.query_ref) | copy-start | bytes 589828
  22.4 3.2 %copy-start.19 = (s32[1,1536]{1,0:T(1,128)S(1)}, s32[1,1536]{1,0:T(1,128)}, u32[]{:S(2)}) copy-start(s32[1,1536]{1,0:T(1,128)} %constant.2.clone.pos_ref) | copy-start | bytes 18436
  25.1 5.3 %copy-start.3 = (bf16[2,128,1536]{2,1,0:T(8,128)(2,1)S(1)}, bf16[2,128,1536]{2,1,0:T(8,128)(2,1)}, u32[]{:S(2)}) copy-start(bf16[2,128,1536]{2,1,0:T(8,128)(2,1)} %refs_0_.11) | copy-start | bytes 2359300
  25.1 5.3 %copy-start.4 = (bf16[2,768,256]{2,1,0:T(8,128)(2,1)S(1)}, bf16[2,768,256]{2,1,0:T(8,128)(2,1)}, u32[]{:S(2)}) copy-start(bf16[2,768,256]{2,1,0:T(8,128)(2,1)} %refs_2_.7) | copy-start | bytes 2359300
  25.1 5.3 %collective-permute-start.4 = (bf16[1536,128]{1,0:T(8,128)(2,1)}, bf16[1536,128]{1,0:T(8,128)(2,1)S(1)}, u32[]{:S(2)}, u32[]{:S(2)}) collective-permute-start(bf16[1536,128]{1,0:T(8,128)(2,1)} %bitcast.own_ref), channel_id=1, source_target_pairs={{0,1},{1,0},{2,3},{3,2},{4,5},{5,4},{6,7},{7,6},{8,9},{9,8},{10,11... | collective-permute-start | bytes 1179656 | tf_op jit(solution)/shard_map/ppermute | solution.py:337
  27.5 2.9 %copy-start.11 = (f32[192,128]{1,0:T(8,128)S(1)}, f32[192,128]{1,0:T(8,128)}, u32[]{:S(2)}) copy-start(f32[192,128]{1,0:T(8,128)} %rows_ref.5) | copy-start | bytes 294916
  27.5 2.9 %copy-start.16 = (f32[2,1536]{1,0:T(2,128)S(1)}, f32[2,1536]{1,0:T(2,128)}, u32[]{:S(2)}) copy-start(f32[2,1536]{1,0:T(2,128)} %gain_ref.11) | copy-start | bytes 36868
  27.5 2.9 %copy-start.18 = (bf16[96,128]{1,0:T(8,128)(2,1)S(1)}, bf16[96,128]{1,0:T(8,128)(2,1)}, u32[]{:S(2)}) copy-start(bf16[96,128]{1,0:T(8,128)(2,1)} %copy-done.17) | copy-start | bytes 73732
  30.4 30.0 %copy-start.13 = (f32[2,1536]{1,0:T(2,128)S(1)}, f32[2,1536]{1,0:T(2,128)}, u32[]{:S(2)}) copy-start(f32[2,1536]{1,0:T(2,128)} %gain_ref.10) | copy-start | bytes 36868
  33.8 26.6 %copy-start.6 = (bf16[2,1536,128]{2,1,0:T(8,128)(2,1)S(1)}, bf16[2,1536,128]{2,1,0:T(8,128)(2,1)}, u32[]{:S(2)}) copy-start(bf16[2,1536,128]{2,1,0:T(8,128)(2,1)} %refs_0_.10) | copy-start | bytes 2359300
  57.3 6.7 %collective-permute-start.8 = (bf16[1536,128]{1,0:T(8,128)(2,1)S(1)}, bf16[1536,128]{1,0:T(8,128)(2,1)S(1)}, u32[]{:S(2)}, u32[]{:S(2)}) collective-permute-start(bf16[1536,128]{1,0:T(8,128)(2,1)S(1)} %bitcast.3), channel_id=1, source_target_pairs={{0,1},{1,0},{2,3},{3,2},{4,5},{5,4},{6,7},{7,6},{8,9},{9,8},{10,11... | collective-permute-start | bytes 1179656 | tf_op jit(solution)/shard_map/ppermute | solution.py:337
  57.3 3.1 %collective-permute-start.7 = (f32[8,128]{1,0:T(8,128)S(1)}, f32[8,128]{1,0:T(8,128)S(1)}, u32[]{:S(2)}, u32[]{:S(2)}) collective-permute-start(f32[8,128]{1,0:T(8,128)S(1)} %get-tuple-element.36), channel_id=1, source_target_pairs={{1,0},{2,1},{3,2},{4,3},{5,4},{6,5},{7,6},{8,7},{9,8},{10,9},{11,1... | collective-permute-start | bytes 12296 | tf_op jit(solution)/shard_map/ppermute | solution.py:384
  67.6 3.3 %collective-permute-start.9 = (f32[104,128]{1,0:T(8,128)S(1)}, f32[104,128]{1,0:T(8,128)S(1)}, u32[]{:S(2)}, u32[]{:S(2)}) collective-permute-start(f32[104,128]{1,0:T(8,128)S(1)} %get-tuple-element.43.own_ref), channel_id=1, source_target_pairs={{0,1},{1,0},{2,3},{3,2},{4,5},{5,4},{6,7},{7,6},{8,9},{9,8},{10,11... | collective-permute-start | bytes 159752 | tf_op jit(solution)/shard_map/ppermute | solution.py:337
  (7 other events, 7.4 us)

commit v4 on v3

--- a/solution.py
+++ b/solution.py
@@ -3,7 +3,6 @@
 
 import jax
 import jax.numpy as jnp
-import numpy as np
 from jax import lax
 from jax.experimental import pallas as pl
 from jax.experimental.pallas import tpu as pltpu
@@ -33,7 +32,7 @@
     return lax.rem(lax.axis_index("head"), 2)
 
 
-def on_chip(kernel, name, operands, results, flops, out_memory=pltpu.VMEM):
+def on_chip(kernel, name, operands, results, flops, out_memory=pltpu.VMEM, scratch=()):
     near = [pltpu.with_memory_space_constraint(array, pltpu.VMEM) for array in operands]
     if out_memory is pltpu.VMEM:
         out_shape = tuple(pltpu.VMEM(shape, dtype) for shape, dtype in results)
@@ -44,18 +43,26 @@
         in_specs=[pl.BlockSpec(memory_space=pltpu.VMEM)] * len(operands),
         out_specs=tuple(pl.BlockSpec(memory_space=pltpu.VMEM) for _ in results),
         out_shape=out_shape,
+        scratch_shapes=list(scratch),
         compiler_params=pltpu.CompilerParams(vmem_limit_bytes=VMEM_LIMIT),
         cost_estimate=pl.CostEstimate(flops=int(flops), bytes_accessed=0, transcendentals=0),
         name=name,
     )(*near)
 
 
-def spread_kernel(rows_ref, spread_ref, edge_ref):
+def spread_kernel(rows_ref, spread_ref):
     members, count, _ = spread_ref.shape
     own = rows_ref[pl.ds(pl.multiple_of(side_of() * count, 8), count), :].astype(jnp.bfloat16)
     for i in range(members):
         spread_ref[i] = own
-    edge_ref[...] = rows_ref[rows_ref.shape[0] - 8 :, :]
+
+
+def gate_kernel(own_ref, *refs):
+    refs[-1][...] = own_ref[...]
+
+
+def gate(own, *made):
+    return on_chip(gate_kernel, "gate", [own, *made], [(own.shape, own.dtype)], own.size)[0]
 
 
 def combine_kernel(layer, pieces, in_ref, gain_ref, *refs):
@@ -102,22 +109,15 @@
     )[0]
 
 
-def queries_kernel(layer, pieces, rows_ref, edge_ref, in_ref, gain_ref, *refs):
-    query_refs, shifted_ref, out_ref = refs[:pieces], refs[pieces], refs[pieces + 1]
-    count = shifted_ref.shape[0]
-    token = lax.broadcasted_iota(jnp.int32, (count, 1), 0)
+def queries_kernel(layer, pieces, rows_ref, in_ref, gain_ref, *refs):
+    query_refs, hidden_ref, out_ref = refs[:pieces], refs[pieces], refs[pieces + 1]
+    count = hidden_ref.shape[0]
     if layer == 0:
-        start = pl.multiple_of(side_of() * count, 8)
-        values = rows_ref[pl.ds(start, count), :]
-        border = jnp.where(side_of() == 0, edge_ref[7:8, :], rows_ref[count - 1 : count, :])
-        moved, at = pltpu.roll(values, 1, 0), 0
+        rows = rows_ref[pl.ds(pl.multiple_of(side_of() * count, 8), count), :]
     else:
-        values = rows_ref[...]
-        border = edge_ref[0:1, :]
-        moved, at = pltpu.roll(values, count - 1, 0), count - 1
-    shifted = jnp.where(token == at, border, moved).astype(jnp.bfloat16)
-    shifted_ref[...] = shifted
-    hidden = dot(shifted, in_ref[layer])
+        rows = rows_ref[...]
+    hidden = dot(rows.astype(jnp.bfloat16), in_ref[layer])
+    hidden_ref[...] = hidden
     spread = lax.rsqrt(jnp.mean(hidden * hidden, axis=1, keepdims=True) + epsilon)
     normed = (hidden * spread * gain_ref[layer : layer + 1, :]).astype(jnp.bfloat16)
     for first in range(0, pieces, 2):
@@ -132,7 +132,7 @@
             ).astype(jnp.bfloat16)
 
 
-def make_queries(layer, count, rows, edge, in_proj, attn_gain, query_pieces):
+def make_queries(layer, count, rows, in_proj, attn_gain, query_pieces):
     pieces = len(query_pieces)
     channels, features = in_proj.shape[1:]
     width = min(2, pieces) * query_pieces[0].shape[2]
@@ -140,16 +140,16 @@
     return on_chip(
         functools.partial(queries_kernel, layer, pieces),
         "queries",
-        [rows, edge, in_proj, attn_gain, *query_pieces],
+        [rows, in_proj, attn_gain, *query_pieces],
         [
-            ((count, channels), jnp.bfloat16),
+            ((count, features), jnp.float32),
             ((groups, width // HS * count, width), jnp.bfloat16),
         ],
         2 * count * features * (channels + groups * width),
     )
 
 
-def attend_rows(cfg, place, pos_ref, maps_ref, query_ref, source_ref, carry):
+def attend_rows(cfg, place, maps_ref, query_ref, source_ref, carry):
     count, features, size = cfg["count"], cfg["features"], cfg["chunk"]
     side = side_of()
     groups, _, group_cols = query_ref.shape
@@ -158,14 +158,16 @@
     total_cols = groups * group_cols
     token = lax.broadcasted_iota(jnp.int32, (count, 1), 0)
     first_token = lax.axis_index("seq") * (2 * count) + side * count
-    query_token = first_token + jnp.concatenate([token] * heads, axis=0)
+    query_place = first_token + jnp.concatenate([token] * heads, axis=0)
     offset = (side if place == 0 else 1 - side) * count
+    lane = lax.broadcasted_iota(jnp.int32, (1, size), 1)
 
     def one_chunk(start, carry):
         source = source_ref[pl.ds(start, size), :]
         twice = jnp.concatenate([source, source], axis=1)
-        key_token = pos_ref[:, pl.ds(start, size)] + offset
-        allowed = key_token < query_token if cfg["layer"] == 0 else key_token > query_token
+        member = ((lane + start).astype(jnp.float32) + 0.5) * (1.0 / count)
+        key_place = lane + start + member.astype(jnp.int32) * count + offset
+        allowed = key_place <= query_place if cfg["layer"] == 0 else key_place >= query_place
         tail = dot_nt(maps_ref[2 * total_cols :, :], twice)
         square = jnp.sum(tail[:channels] * tail[channels:], axis=0, keepdims=True)
         scale = lax.rsqrt(jnp.maximum(square, 0.0) * (1.0 / features) + epsilon)
@@ -186,8 +188,8 @@
             weights = jnp.where(allowed, jnp.exp(scores), 0.0)
             product = dot_nt(weights.astype(jnp.bfloat16), value)
             total = weights[:, :128]
-            for lane in range(128, size, 128):
-                total = total + weights[:, lane : lane + 128]
+            for at in range(128, size, 128):
+                total = total + weights[:, at : at + 128]
             result.append(
                 (product, total)
                 if carry is None
@@ -207,29 +209,31 @@
     return carry
 
 
-def first_half_kernel(cfg, pos_ref, maps_ref, query_ref, own_ref, number_ref, total_ref):
-    carry = attend_rows(cfg, 0, pos_ref, maps_ref, query_ref, own_ref, None)
+def first_half_kernel(cfg, maps_ref, query_ref, own_ref, number_ref, total_ref):
+    carry = attend_rows(cfg, 0, maps_ref, query_ref, own_ref, None)
     for g, (number, total) in enumerate(carry):
         number_ref[g] = number
         total_ref[g] = total
 
 
-def second_half_kernel(cfg, pos_ref, maps_ref, query_ref, other_ref, number_ref, total_ref, shifted_ref, in_ref, gain_ref, rows_ref, *refs):
+def second_half_kernel(cfg, maps_ref, query_ref, other_ref, number_ref, total_ref, hidden_ref, gain_ref, latent_ref, *refs):
     layer, pieces, last, count = cfg["layer"], cfg["pieces"], cfg["last"], cfg["count"]
     refs = list(refs)
     mix_refs = [refs.pop(0) for _ in range(pieces)]
     param_refs = [refs.pop(0) for _ in range(pieces)]
-    side, way = side_of(), lax.axis_index("head")
-    channels, features = in_ref.shape[1:]
+    side, way, member = side_of(), lax.axis_index("head"), lax.axis_index("seq")
+    members = other_ref.shape[0] // count
+    features, channels = hidden_ref.shape[1], latent_ref.shape[1]
     groups, _, group_cols = query_ref.shape
     heads = group_cols // HS
     carry = tuple((number_ref[g], total_ref[g]) for g in range(groups))
-    carry = attend_rows(cfg, 1, pos_ref, maps_ref, query_ref, other_ref, carry)
-
-    mixture = dot(shifted_ref[...], in_ref[layer])
+    carry = attend_rows(cfg, 1, maps_ref, query_ref, other_ref, carry)
+
+    mixture = hidden_ref[...]
     head = lax.broadcasted_iota(jnp.int32, (count, group_cols), 1) // HS
     for g, (number, total) in enumerate(carry):
-        share_of = 1.0 / (jnp.sum(total, axis=1, keepdims=True) + 1.0)
+        total = jnp.sum(total, axis=1, keepdims=True) + (0.0 if last else 1.0)
+        share_of = 1.0 / total
         attended = jnp.zeros((count, group_cols), jnp.float32)
         for h in range(heads):
             band = slice(h * count, (h + 1) * count)
@@ -244,26 +248,39 @@
         at = pl.multiple_of(lax.rem(way + j, pieces) * share, 16)
         param_all[pl.ds(at, share), :] = ref[layer]
     predicted = dot(scaled, param_all[...])
+    shift_mu = predicted[:, :channels]
     log_scale = 2.0 * jnp.tanh(0.5 * predicted[:, channels:])
+    token = lax.broadcasted_iota(jnp.int32, (count, 1), 0)
+    start = pl.multiple_of(side * count, 8)
     if last:
-        first_log_ref, out_ref = refs[:2]
-        values = rows_ref[...]
-        result = (values - predicted[:, :channels]) * jnp.exp(-log_scale)
-        term = -(first_log_ref[...] + log_scale) - 0.5 * (result * result)
+        held_ref, held_log_ref, edge_ref, out_ref = refs[:4]
+        edge_log = edge_ref[15:16, :]
+        first = (latent_ref[pl.ds(start, 8), :][:1] - edge_ref[7:8, :]) * jnp.exp(-edge_log)
+        values = jnp.where(token == 0, first, pltpu.roll(held_ref[...], 1, 0))
+        first_log = jnp.where(token == 0, edge_log, pltpu.roll(held_log_ref[...], 1, 0))
+        result = (values - shift_mu) * jnp.exp(-log_scale)
+        term = -(first_log + log_scale) - 0.5 * (result * result)
         loglik = jnp.sum(term.T, axis=0, keepdims=True) * (1.0 / channels) - 0.5 * math.log(
             2.0 * math.pi
         )
         out_ref[:count, :] = result
         out_ref[count:, :count] = jnp.broadcast_to(loglik, (8, count))
     else:
-        out_ref, log_ref, spread_ref, edge_ref = refs[:4]
-        values = rows_ref[pl.ds(pl.multiple_of(side * count, 8), count), :]
-        result = (values - predicted[:, :channels]) * jnp.exp(-log_scale)
-        out_ref[...] = result
-        log_ref[...] = log_scale
-        edge_ref[...] = result[:8]
+        held_ref, held_log_ref, edge_ref, spread_ref = refs[:4]
+        following = pl.multiple_of(jnp.minimum(member + 1, members - 1) * count, 16)
+        after = other_ref[pl.ds(following, 16), :].astype(jnp.float32)[:1]
+        after = jnp.where(side == 0, latent_ref[count : count + 1, :], after)
+        values = pltpu.roll(latent_ref[pl.ds(start, count), :], count - 1, 0)
+        values = jnp.where(token == count - 1, after, values)
+        result = (values - shift_mu) * jnp.exp(-log_scale)
+        beyond = (member * 2 + side) * count + token == members * 2 * count - 1
+        result = jnp.where(beyond, 0.0, result)
+        held_ref[...] = result
+        held_log_ref[...] = log_scale
+        edge_ref[:8, :] = shift_mu[count - 8 :]
+        edge_ref[8:, :] = log_scale[count - 8 :]
         narrow = result.astype(jnp.bfloat16)
-        for i in range(spread_ref.shape[0]):
+        for i in range(members):
             spread_ref[i] = narrow
 
 
@@ -279,39 +296,38 @@
     }
 
 
-def first_half(cfg, positions, maps, queries, own):
+def first_half(cfg, maps, queries, own):
     groups, rows, cols = queries.shape
     return on_chip(
         functools.partial(first_half_kernel, cfg),
         "first_half",
-        [positions, maps, queries, own],
+        [maps, queries, own],
         [((groups, rows, cols), jnp.float32), ((groups, rows, 128), jnp.float32)],
         2 * own.shape[0] * (maps.size + 2 * queries.size),
     )
 
 
-def second_half(cfg, members, positions, maps, queries, other, sums, shifted, in_proj, param_gain, rows, mix_pieces, param_pieces, first_log=None):
-    count, channels = shifted.shape
-    operands = [positions, maps, queries, other, *sums, shifted, in_proj, param_gain, rows]
-    operands += [*mix_pieces, *param_pieces]
+def second_half(cfg, members, maps, queries, other, sums, hidden, param_gain, latents, mix_pieces, param_pieces, held=()):
+    count, channels = cfg["count"], latents.shape[1]
+    operands = [maps, queries, other, *sums, hidden, param_gain, latents]
+    operands += [*mix_pieces, *param_pieces, *held]
     if cfg["last"]:
-        operands.append(first_log)
         results = [((count + 8, channels), jnp.float32)]
     else:
         results = [
             ((count, channels), jnp.float32),
             ((count, channels), jnp.float32),
+            ((16, channels), jnp.float32),
             ((members, count, channels), jnp.bfloat16),
-            ((8, channels), jnp.float32),
         ]
-    results.append(((cfg["features"], param_pieces[0].shape[2]), jnp.bfloat16))
     return on_chip(
         functools.partial(second_half_kernel, cfg),
         "second_half",
         operands,
         results,
         2 * other.shape[0] * (maps.size + 2 * queries.size),
-    )[:-1]
+        scratch=[pltpu.VMEM((cfg["features"], param_pieces[0].shape[2]), jnp.bfloat16)],
+    )
 
 
 def finish_kernel(own_ref, other_ref, final_ref, loglik_ref):
@@ -347,47 +363,44 @@
     def gather(spread):
         return lax.all_to_all(spread, "seq", 0, 0).reshape(keys, channels)
 
-    spread, edge = on_chip(
+    (spread,) = on_chip(
         spread_kernel,
         "spread_rows",
         [latents],
-        [((members, count, channels), jnp.bfloat16), ((8, channels), jnp.float32)],
+        [((members, count, channels), jnp.bfloat16)],
         keys * channels,
     )
     own = gather(spread)
-    edge = lax.ppermute(edge, "seq", [(i, i + 1) for i in range(members - 1)])
     key_pieces, value_pieces = pieces_of(key_proj), pieces_of(value_proj)
     query_pieces, mix_pieces = pieces_of(query_proj), pieces_of(mix_proj)
     param_pieces = pieces_of(param_proj)
     maps = [combine(b, in_proj, attn_gain, key_pieces, value_pieces) for b in range(2)]
-    shifted, queries = make_queries(0, count, latents, edge, in_proj, attn_gain, query_pieces)
-    positions = jnp.asarray(
-        (np.arange(keys) // count * rows + np.arange(keys) % count)[None], jnp.int32
-    )
-    own, maps, shifted, queries = lax.optimization_barrier((own, maps, shifted, queries))
+    hidden, queries = make_queries(0, count, latents, in_proj, attn_gain, query_pieces)
+    own = gate(own, *maps, queries)
 
     cfg = config(0, count, features, ways, keys)
     other = swap(own)
-    sums = first_half(cfg, positions, maps[0], queries, own)
-    first_out, first_log, spread, edge = second_half(
-        cfg, members, positions, maps[0], queries, other, sums, shifted, in_proj, param_gain, latents, mix_pieces, param_pieces
-    )
-
+    sums = first_half(cfg, maps[0], queries, own)
+    held, held_log, edge, spread = second_half(
+        cfg, members, maps[0], queries, other, sums, hidden, param_gain, latents, mix_pieces, param_pieces
+    )
+
+    own = gather(spread)
     pairs = []
     for s in range(members):
         for w in range(ways):
-            if w % 2:
-                pairs.append((s * ways + w, s * ways + w - 1))
-            elif s > 0:
-                pairs.append((s * ways + w, (s - 1) * ways + w + 1))
-    own = gather(spread)
+            if w % 2 == 0:
+                pairs.append((s * ways + w, s * ways + w + 1))
+            elif s < members - 1:
+                pairs.append((s * ways + w, (s + 1) * ways + w - 1))
     edge = lax.ppermute(edge, ("seq", "head"), pairs)
-    shifted, queries = make_queries(1, count, first_out, edge, in_proj, attn_gain, query_pieces)
+    hidden, queries = make_queries(1, count, held, in_proj, attn_gain, query_pieces)
+    own = gate(own, queries)
     cfg = config(1, count, features, ways, keys)
     other = swap(own)
-    sums = first_half(cfg, positions, maps[1], queries, own)
+    sums = first_half(cfg, maps[1], queries, own)
     (packed,) = second_half(
-        cfg, members, positions, maps[1], queries, other, sums, shifted, in_proj, param_gain, first_out, mix_pieces, param_pieces, first_log
+        cfg, members, maps[1], queries, other, sums, hidden, param_gain, latents, mix_pieces, param_pieces, (held, held_log, edge)
     )
     final_latent, token_loglik = on_chip(
         finish_kernel,

time: 72.1 us -> 62.9 us (0.87)
  the two profiles are of different devices: /device:TPU:0 before, /device:TPU:9 now
where the time goes in v4:
time: 62.9 us; the launch traced here: 62.2 us
  starting transfers between devices  22.3 us (35%)
  Pallas kernels  15.4 us (24%)
  waiting for transfers between devices  15.4 us (24%)
  local copies, waits for them, and re-layouts  8.26 us (13%)
  between operations  0.96 us (2%)
    pallas_call x12, Pallas kernels, on_chip(): pl.pallas_call(kernel, in_specs=[pl.BlockSpec(memory_space=pltpu.VMEM)] *...  15.4 us
    all_to_all x2, waiting for transfers between devices, gather(): return lax.all_to_all(spread, 'seq', 0, 0).reshape(keys, channels)  14.5 us
    all_to_all x2, starting transfers between devices, gather(): return lax.all_to_all(spread, 'seq', 0, 0).reshape(keys, channels)  10.9 us
    unnamed x52, local copies, waits for them, and re-layouts  8.26 us
    ppermute x3, starting transfers between devices, swap(): return lax.ppermute(array, 'head', [(i, i ^ 1) for i in range(ways)])  6.55 us
    ppermute x1, starting transfers between devices, body(): edge = lax.ppermute(edge, ('seq', 'head'), pairs)  2.79 us
    ppermute x5, starting transfers between devices, pieces_of(): lax.ppermute(array, 'head', [((i + j) % ways, i) for i in range(ways)])  2.02 us
  transfers between devices with their start and end apart: 11, of which 3 were waited for; matrix products, arithmetic and copies ran while one was open for 0% of the time, Pallas kernels for 10%

profile of v4, /device:TPU:9, one launch (start us, length us, event | category | flops | bytes accessed | tf_op | source)
XLA Modules:
  0.0 62.2 jit_solution(12949832022494598821)
XLA Ops:
  0.6 0.7 %collective-permute-start.2 = (bf16[2,1536,128]{2,1,0:T(8,128)(2,1)}, bf16[2,1536,128]{2,1,0:T(8,128)(2,1)S(1)}, u32[]{:S(2)}, u32[]{:S(2)}) collective-permute-start(bf16[2,1536,128]{2,1,0:T(8,128)(2,1)} %refs_0_.10), channel_id=1, source_target_pairs={{1,0},{0,1},{3,2},{2,3},{5,4},{4,5},{7,6},{6,7},{9,8},{8,9},{11,10... | collective-permute-start | bytes 2359304 | tf_op jit(solution)/shard_map/ppermute | solution.py:359
  1.9 0.9 %copy-done.11 = f32[192,128]{1,0:T(8,128)S(1)} copy-done((f32[192,128]{1,0:T(8,128)S(1)}, f32[192,128]{1,0:T(8,128)}, u32[]{:S(2)}) %copy-start.11) | copy-done | bytes 98328
  2.8 0.7 %copy-done.10 = bf16[16,96,128]{2,1,0:T(8,128)(2,1)} copy-done((bf16[16,96,128]{2,1,0:T(8,128)(2,1)}, bf16[16,96,128]{2,1,0:T(8,128)(2,1)S(1)}, u32[]{:S(2)}) %copy-start.10) | copy-done | bytes 393240
  3.6 6.8 %all-to-all-start = ((bf16[16,96,128]{2,1,0:T(8,128)(2,1)}), bf16[16,96,128]{2,1,0:T(8,128)(2,1)S(1)}, u32[]{:S(2)}, u32[]{:S(2)}) async-start(bf16[16,96,128]{2,1,0:T(8,128)(2,1)} %copy-done.10), calls=%async_computation | async-start | bytes 786432 | tf_op jit(solution)/shard_map/all_to_all | solution.py:364
  11.2 1.1 %copy-done.3 = bf16[2,1536,128]{2,1,0:T(8,128)(2,1)S(1)} copy-done((bf16[2,1536,128]{2,1,0:T(8,128)(2,1)S(1)}, bf16[2,1536,128]{2,1,0:T(8,128)(2,1)}, u32[]{:S(2)}) %copy-start.3) | copy-done | bytes 786456
  12.3 0.9 %copy-done.12 = f32[192,128]{1,0:T(8,128)S(1)} copy-done((f32[192,128]{1,0:T(8,128)S(1)}, f32[192,128]{1,0:T(8,128)}, u32[]{:S(2)}) %copy-start.12) | copy-done | bytes 98328
  14.1 0.8 %combine.3.refs_0_.maps_ref = bf16[768,256]{1,0:T(8,128)(2,1)S(1)} custom-call(bf16[2,128,1536]{2,1,0:T(8,128)(2,1)S(1)} %copy-done, f32[2,1536]{1,0:T(2,128)S(1)} %copy-done.21, bf16[2,1536,128]{2,1,0:T(8,128)(2,1)S(1)} %copy-done.1, bf16[2,1536,128]{2,1,0:T(8,128)(2,1)S(1)} %collective-permute-done.refs_1_, bf16[2,1536,128]{2,1,0:T(8,128)(2,1)S(1)} %copy-done.2, ...), custom_call_target="tpu_custom_call" | custom-call | flops 603979776 | tf_op jit(solution)/shard_map/combine/pallas_call | solution.py:41
  15.0 0.8 %combine.2.refs_1_.maps_ref = bf16[768,256]{1,0:T(8,128)(2,1)S(1)} custom-call(bf16[2,128,1536]{2,1,0:T(8,128)(2,1)S(1)} %copy-done, f32[2,1536]{1,0:T(2,128)S(1)} %copy-done.21, bf16[2,1536,128]{2,1,0:T(8,128)(2,1)S(1)} %copy-done.1, bf16[2,1536,128]{2,1,0:T(8,128)(2,1)S(1)} %collective-permute-done.refs_1_, bf16[2,1536,128]{2,1,0:T(8,128)(2,1)S(1)} %copy-done.2, ...), custom_call_target="tpu_custom_call" | custom-call | flops 603979776 | tf_op jit(solution)/shard_map/combine/pallas_call | solution.py:41
  15.7 5.6 %all-to-all-done = bf16[16,96,128]{2,1,0:T(8,128)(2,1)S(1)} async-done(((bf16[16,96,128]{2,1,0:T(8,128)(2,1)}), bf16[16,96,128]{2,1,0:T(8,128)(2,1)S(1)}, u32[]{:S(2)}, u32[]{:S(2)}) %all-to-all-start) | async-done | bytes 393248 | tf_op jit(solution)/shard_map/all_to_all | solution.py:364
  21.4 0.9 %copy-done.15 = bf16[1,384,256]{2,1,0:T(8,128)(2,1)S(1)} copy-done((bf16[1,384,256]{2,1,0:T(8,128)(2,1)S(1)}, bf16[1,384,256]{2,1,0:T(8,128)(2,1)}, u32[]{:S(2)}) %copy-start.15) | copy-done | bytes 196632
  22.4 2.1 %collective-permute-start.3 = (bf16[1536,128]{1,0:T(8,128)(2,1)S(1)}, bf16[1536,128]{1,0:T(8,128)(2,1)S(1)}, u32[]{:S(2)}, u32[]{:S(2)}) collective-permute-start(bf16[1536,128]{1,0:T(8,128)(2,1)S(1)} %gate.2.own_ref), channel_id=1, source_target_pairs={{0,1},{1,0},{2,3},{3,2},{4,5},{5,4},{6,7},{7,6},{8,9},{9,8},{10,11... | collective-permute-start | bytes 1179656 | tf_op jit(solution)/shard_map/ppermute | solution.py:353
  24.4 1.8 %first_half.2 = (f32[1,384,256]{2,1,0:T(8,128)S(1)}, f32[1,384,128]{2,1,0:T(8,128)S(1)}) custom-call(bf16[768,256]{1,0:T(8,128)(2,1)S(1)} %combine.3.refs_0_.maps_ref, bf16[1,384,256]{2,1,0:T(8,128)(2,1)S(1)} %copy-done.15, bf16[1536,128]{1,0:T(8,128)(2,1)S(1)} %gate.2.own_ref), custom_call_target="tpu_custom_call" | custom-call | flops 1207959552 | tf_op jit(solution)/shard_map/first_half/pallas_call | solution.py:41
  26.3 4.0 %second_half.2 = (f32[96,128]{1,0:T(8,128)S(1)}, f32[96,128]{1,0:T(8,128)S(1)}, f32[16,128]{1,0:T(8,128)S(1)}, bf16[16,96,128]{2,1,0:T(8,128)(2,1)S(1)}) custom-call(bf16[768,256]{1,0:T(8,128)(2,1)S(1)} %combine.3.refs_0_.maps_ref, bf16[1,384,256]{2,1,0:T(8,128)(2,1)S(1)} %copy-done.15, bf16[1536,128]{1,0:T(8,128)(2,1)S(1)} %collective-permute-done.3.other_ref, ...), custom_call_target="tpu_custom_call" | custom-call | flops 1207959552 | tf_op jit(solution)/shard_map/second_half/pallas_call | solution.py:41
  30.4 0.7 %copy-done.20 = bf16[16,96,128]{2,1,0:T(8,128)(2,1)} copy-done((bf16[16,96,128]{2,1,0:T(8,128)(2,1)}, bf16[16,96,128]{2,1,0:T(8,128)(2,1)S(1)}, u32[]{:S(2)}) %copy-start.20) | copy-done | bytes 393240
  31.7 4.1 %all-to-all-start.1 = ((bf16[16,96,128]{2,1,0:T(8,128)(2,1)}), bf16[16,96,128]{2,1,0:T(8,128)(2,1)S(1)}, u32[]{:S(2)}, u32[]{:S(2)}) async-start(bf16[16,96,128]{2,1,0:T(8,128)(2,1)} %copy-done.20), calls=%async_computation.1 | async-start | bytes 786432 | tf_op jit(solution)/shard_map/all_to_all | solution.py:364
  35.9 1.1 %copy-done.9 = bf16[2,1536,128]{2,1,0:T(8,128)(2,1)S(1)} copy-done((bf16[2,1536,128]{2,1,0:T(8,128)(2,1)S(1)}, bf16[2,1536,128]{2,1,0:T(8,128)(2,1)}, u32[]{:S(2)}) %copy-start.9) | copy-done | bytes 786456
  37.7 0.8 %copy-done.18 = f32[96,1536]{1,0:T(8,128)} copy-done((f32[96,1536]{1,0:T(8,128)}, f32[96,1536]{1,0:T(8,128)S(1)}, u32[]{:S(2)}) %copy-start.18) | copy-done | bytes 589848
  38.5 8.9 %all-to-all-done.1 = bf16[16,96,128]{2,1,0:T(8,128)(2,1)S(1)} async-done(((bf16[16,96,128]{2,1,0:T(8,128)(2,1)}), bf16[16,96,128]{2,1,0:T(8,128)(2,1)S(1)}, u32[]{:S(2)}, u32[]{:S(2)}) %all-to-all-start.1) | async-done | bytes 393248 | tf_op jit(solution)/shard_map/all_to_all | solution.py:364
  47.4 1.6 %collective-permute-start.6 = (bf16[1536,128]{1,0:T(8,128)(2,1)S(1)}, bf16[1536,128]{1,0:T(8,128)(2,1)S(1)}, u32[]{:S(2)}, u32[]{:S(2)}) collective-permute-start(bf16[1536,128]{1,0:T(8,128)(2,1)S(1)} %gate.3.own_ref), channel_id=1, source_target_pairs={{0,1},{1,0},{2,3},{3,2},{4,5},{5,4},{6,7},{7,6},{8,9},{9,8},{10,11... | collective-permute-start | bytes 1179656 | tf_op jit(solution)/shard_map/ppermute | solution.py:353
  49.0 2.8 %collective-permute-start.7 = (f32[16,128]{1,0:T(8,128)S(1)}, f32[16,128]{1,0:T(8,128)S(1)}, u32[]{:S(2)}, u32[]{:S(2)}) collective-permute-start(f32[16,128]{1,0:T(8,128)S(1)} %copy-done.25), channel_id=1, source_target_pairs={{0,1},{1,2},{2,3},{3,4},{4,5},{5,6},{6,7},{7,8},{8,9},{9,10},{10,1... | collective-permute-start | bytes 24584 | tf_op jit(solution)/shard_map/ppermute | solution.py:396
  51.8 1.8 %first_half.3 = (f32[1,384,256]{2,1,0:T(8,128)S(1)}, f32[1,384,128]{2,1,0:T(8,128)S(1)}) custom-call(bf16[768,256]{1,0:T(8,128)(2,1)S(1)} %combine.2.refs_1_.maps_ref, bf16[1,384,256]{2,1,0:T(8,128)(2,1)S(1)} %get-tuple-element.21.refs_0_.query_ref, bf16[1536,128]{1,0:T(8,128)(2,1)S(1)} %gate.3.own_ref), custom_call_target="tpu_custom_call" | custom-call | flops 1207959552 | tf_op jit(solution)/shard_map/first_half/pallas_call | solution.py:41
  53.7 4.1 %second_half.3.own_ref = f32[104,128]{1,0:T(8,128)S(1)} custom-call(bf16[768,256]{1,0:T(8,128)(2,1)S(1)} %combine.2.refs_1_.maps_ref, bf16[1,384,256]{2,1,0:T(8,128)(2,1)S(1)} %get-tuple-element.21.refs_0_.query_ref, bf16[1536,128]{1,0:T(8,128)(2,1)S(1)} %collective-permute-done.6.other_ref, f32[1,384,256]{2,1,0:T(8,128)S(1)} %get-tuple-element.23.number_ref, ...), custom_call_target="tpu_custom_call" | custom-call | flops 1207959552 | tf_op jit(solution)/shard_map/second_half/pallas_call | solution.py:41
  57.8 2.9 %collective-permute-start.8 = (f32[104,128]{1,0:T(8,128)S(1)}, f32[104,128]{1,0:T(8,128)S(1)}, u32[]{:S(2)}, u32[]{:S(2)}) collective-permute-start(f32[104,128]{1,0:T(8,128)S(1)} %second_half.3.own_ref), channel_id=1, source_target_pairs={{0,1},{1,0},{2,3},{3,2},{4,5},{5,4},{6,7},{7,6},{8,9},{9,8},{10,11... | collective-permute-start | bytes 159752 | tf_op jit(solution)/shard_map/ppermute | solution.py:353
  60.7 0.9 %collective-permute-done.8.other_ref = f32[104,128]{1,0:T(8,128)S(1)} collective-permute-done((f32[104,128]{1,0:T(8,128)S(1)}, f32[104,128]{1,0:T(8,128)S(1)}, u32[]{:S(2)}, u32[]{:S(2)}) %collective-permute-start.8) | collective-permute-done | bytes 53280 | tf_op jit(solution)/shard_map/ppermute | solution.py:353
  (62 shorter events, 4.3 us)
Async XLA Ops:
  0.6 10.5 %copy-start = (bf16[2,128,1536]{2,1,0:T(8,128)(2,1)S(1)}, bf16[2,128,1536]{2,1,0:T(8,128)(2,1)}, u32[]{:S(2)}) copy-start(bf16[2,128,1536]{2,1,0:T(8,128)(2,1)} %in_ref.7) | copy-start | bytes 2359300
  0.6 10.5 %collective-permute-start.2 = (bf16[2,1536,128]{2,1,0:T(8,128)(2,1)}, bf16[2,1536,128]{2,1,0:T(8,128)(2,1)S(1)}, u32[]{:S(2)}, u32[]{:S(2)}) collective-permute-start(bf16[2,1536,128]{2,1,0:T(8,128)(2,1)} %refs_0_.10), channel_id=1, source_target_pairs={{1,0},{0,1},{3,2},{2,3},{5,4},{4,5},{7,6},{6,7},{9,8},{8,9},{11,10... | collective-permute-start | bytes 2359304 | tf_op jit(solution)/shard_map/ppermute | solution.py:359
  1.4 12.7 %collective-permute-start = (bf16[2,1536,128]{2,1,0:T(8,128)(2,1)}, bf16[2,1536,128]{2,1,0:T(8,128)(2,1)S(1)}, u32[]{:S(2)}, u32[]{:S(2)}) collective-permute-start(bf16[2,1536,128]{2,1,0:T(8,128)(2,1)} %refs_0_.7), channel_id=1, source_target_pairs={{1,0},{0,1},{3,2},{2,3},{5,4},{4,5},{7,6},{6,7},{9,8},{8,9},{11,10... | collective-permute-start | bytes 2359304 | tf_op jit(solution)/shard_map/ppermute | solution.py:359
  1.5 12.6 %collective-permute-start.1 = (bf16[2,1536,128]{2,1,0:T(8,128)(2,1)}, bf16[2,1536,128]{2,1,0:T(8,128)(2,1)S(1)}, u32[]{:S(2)}, u32[]{:S(2)}) collective-permute-start(bf16[2,1536,128]{2,1,0:T(8,128)(2,1)} %refs_2_.5), channel_id=1, source_target_pairs={{1,0},{0,1},{3,2},{2,3},{5,4},{4,5},{7,6},{6,7},{9,8},{8,9},{11,10... | collective-permute-start | bytes 2359304 | tf_op jit(solution)/shard_map/ppermute | solution.py:359
  3.6 7.6 %copy-start.21 = (f32[2,1536]{1,0:T(2,128)S(1)}, f32[2,1536]{1,0:T(2,128)}, u32[]{:S(2)}) copy-start(f32[2,1536]{1,0:T(2,128)} %gain_ref.10) | copy-start | bytes 36868
  3.6 17.8 %all-to-all-start = ((bf16[16,96,128]{2,1,0:T(8,128)(2,1)}), bf16[16,96,128]{2,1,0:T(8,128)(2,1)S(1)}, u32[]{:S(2)}, u32[]{:S(2)}) async-start(bf16[16,96,128]{2,1,0:T(8,128)(2,1)} %copy-done.10), calls=%async_computation | async-start | bytes 786432 | tf_op jit(solution)/shard_map/all_to_all | solution.py:364
  10.4 3.7 %copy-start.1 = (bf16[2,1536,128]{2,1,0:T(8,128)(2,1)S(1)}, bf16[2,1536,128]{2,1,0:T(8,128)(2,1)}, u32[]{:S(2)}) copy-start(bf16[2,1536,128]{2,1,0:T(8,128)(2,1)} %refs_0_.7) | copy-start | bytes 2359300
  10.4 3.7 %copy-start.2 = (bf16[2,1536,128]{2,1,0:T(8,128)(2,1)S(1)}, bf16[2,1536,128]{2,1,0:T(8,128)(2,1)}, u32[]{:S(2)}) copy-start(bf16[2,1536,128]{2,1,0:T(8,128)(2,1)} %refs_2_.5) | copy-start | bytes 2359300
  10.4 15.8 %collective-permute-start.4 = (bf16[2,128,1536]{2,1,0:T(8,128)(2,1)}, bf16[2,128,1536]{2,1,0:T(8,128)(2,1)}, u32[]{:S(2)}, u32[]{:S(2)}) collective-permute-start(bf16[2,128,1536]{2,1,0:T(8,128)(2,1)} %refs_0_.11), channel_id=1, source_target_pairs={{1,0},{0,1},{3,2},{2,3},{5,4},{4,5},{7,6},{6,7},{9,8},{8,9},{11,10... | collective-permute-start | bytes 2359304 | tf_op jit(solution)/shard_map/ppermute | solution.py:359
  11.1 15.2 %collective-permute-start.5 = (bf16[2,768,256]{2,1,0:T(8,128)(2,1)}, bf16[2,768,256]{2,1,0:T(8,128)(2,1)}, u32[]{:S(2)}, u32[]{:S(2)}) collective-permute-start(bf16[2,768,256]{2,1,0:T(8,128)(2,1)} %refs_2_.7), channel_id=1, source_target_pairs={{1,0},{0,1},{3,2},{2,3},{5,4},{4,5},{7,6},{6,7},{9,8},{8,9},{11,10... | collective-permute-start | bytes 2359304 | tf_op jit(solution)/shard_map/ppermute | solution.py:359
  22.3 3.9 %copy-start.5 = (bf16[2,128,1536]{2,1,0:T(8,128)(2,1)S(1)}, bf16[2,128,1536]{2,1,0:T(8,128)(2,1)}, u32[]{:S(2)}) copy-start(bf16[2,128,1536]{2,1,0:T(8,128)(2,1)} %refs_0_.11) | copy-start | bytes 2359300
  22.3 3.9 %copy-start.6 = (bf16[2,768,256]{2,1,0:T(8,128)(2,1)S(1)}, bf16[2,768,256]{2,1,0:T(8,128)(2,1)}, u32[]{:S(2)}) copy-start(bf16[2,768,256]{2,1,0:T(8,128)(2,1)} %refs_2_.7) | copy-start | bytes 2359300
  22.3 3.9 %copy-start.13 = (f32[192,128]{1,0:T(8,128)S(1)}, f32[192,128]{1,0:T(8,128)}, u32[]{:S(2)}) copy-start(f32[192,128]{1,0:T(8,128)} %latent_ref.3) | copy-start | bytes 294916
  22.4 3.9 %copy-start.17 = (f32[96,1536]{1,0:T(8,128)S(1)}, f32[96,1536]{1,0:T(8,128)}, u32[]{:S(2)}) copy-start(f32[96,1536]{1,0:T(8,128)} %copy-done.16) | copy-start | bytes 1769476
  22.4 3.9 %collective-permute-start.3 = (bf16[1536,128]{1,0:T(8,128)(2,1)S(1)}, bf16[1536,128]{1,0:T(8,128)(2,1)S(1)}, u32[]{:S(2)}, u32[]{:S(2)}) collective-permute-start(bf16[1536,128]{1,0:T(8,128)(2,1)S(1)} %gate.2.own_ref), channel_id=1, source_target_pairs={{0,1},{1,0},{2,3},{3,2},{4,5},{5,4},{6,7},{7,6},{8,9},{9,8},{10,11... | collective-permute-start | bytes 1179656 | tf_op jit(solution)/shard_map/ppermute | solution.py:353
  24.4 1.9 %copy-start.22 = (f32[2,1536]{1,0:T(2,128)S(1)}, f32[2,1536]{1,0:T(2,128)}, u32[]{:S(2)}) copy-start(f32[2,1536]{1,0:T(2,128)} %gain_ref.11) | copy-start | bytes 36868
  31.7 4.1 %copy-start.4 = (bf16[2,1536,128]{2,1,0:T(8,128)(2,1)S(1)}, bf16[2,1536,128]{2,1,0:T(8,128)(2,1)}, u32[]{:S(2)}) copy-start(bf16[2,1536,128]{2,1,0:T(8,128)(2,1)} %refs_0_.10) | copy-start | bytes 2359300
  31.7 15.6 %all-to-all-start.1 = ((bf16[16,96,128]{2,1,0:T(8,128)(2,1)}), bf16[16,96,128]{2,1,0:T(8,128)(2,1)S(1)}, u32[]{:S(2)}, u32[]{:S(2)}) async-start(bf16[16,96,128]{2,1,0:T(8,128)(2,1)} %copy-done.20), calls=%async_computation.1 | async-start | bytes 786432 | tf_op jit(solution)/shard_map/all_to_all | solution.py:364
  47.4 6.2 %collective-permute-start.6 = (bf16[1536,128]{1,0:T(8,128)(2,1)S(1)}, bf16[1536,128]{1,0:T(8,128)(2,1)S(1)}, u32[]{:S(2)}, u32[]{:S(2)}) collective-permute-start(bf16[1536,128]{1,0:T(8,128)(2,1)S(1)} %gate.3.own_ref), channel_id=1, source_target_pairs={{0,1},{1,0},{2,3},{3,2},{4,5},{5,4},{6,7},{7,6},{8,9},{9,8},{10,11... | collective-permute-start | bytes 1179656 | tf_op jit(solution)/shard_map/ppermute | solution.py:353
  49.0 4.6 %copy-start.7 = (bf16[2,768,256]{2,1,0:T(8,128)(2,1)S(1)}, bf16[2,768,256]{2,1,0:T(8,128)(2,1)}, u32[]{:S(2)}) copy-start(bf16[2,768,256]{2,1,0:T(8,128)(2,1)} %refs_2_.7) | copy-start | bytes 2359300
  49.0 4.6 %copy-start.19 = (f32[96,1536]{1,0:T(8,128)S(1)}, f32[96,1536]{1,0:T(8,128)}, u32[]{:S(2)}) copy-start(f32[96,1536]{1,0:T(8,128)} %copy-done.18) | copy-start | bytes 1769476
  49.0 4.6 %collective-permute-start.7 = (f32[16,128]{1,0:T(8,128)S(1)}, f32[16,128]{1,0:T(8,128)S(1)}, u32[]{:S(2)}, u32[]{:S(2)}) collective-permute-start(f32[16,128]{1,0:T(8,128)S(1)} %copy-done.25), channel_id=1, source_target_pairs={{0,1},{1,2},{2,3},{3,4},{4,5},{5,6},{6,7},{7,8},{8,9},{9,10},{10,1... | collective-permute-start | bytes 24584 | tf_op jit(solution)/shard_map/ppermute | solution.py:396
  51.8 1.9 %copy-start.23 = (f32[2,1536]{1,0:T(2,128)S(1)}, f32[2,1536]{1,0:T(2,128)}, u32[]{:S(2)}) copy-start(f32[2,1536]{1,0:T(2,128)} %gain_ref.11) | copy-start | bytes 36868
  57.8 3.8 %collective-permute-start.8 = (f32[104,128]{1,0:T(8,128)S(1)}, f32[104,128]{1,0:T(8,128)S(1)}, u32[]{:S(2)}, u32[]{:S(2)}) collective-permute-start(f32[104,128]{1,0:T(8,128)S(1)} %second_half.3.own_ref), channel_id=1, source_target_pairs={{0,1},{1,0},{2,3},{3,2},{4,5},{5,4},{6,7},{7,6},{8,9},{9,8},{10,11... | collective-permute-start | bytes 159752 | tf_op jit(solution)/shard_map/ppermute | solution.py:353
  (13 other events, 12.1 us)

commit v5 on v4

--- a/solution.py
+++ b/solution.py
@@ -109,18 +109,13 @@
     )[0]
 
 
-def queries_kernel(layer, pieces, rows_ref, in_ref, gain_ref, *refs):
-    query_refs, hidden_ref, out_ref = refs[:pieces], refs[pieces], refs[pieces + 1]
+def store_queries(layer, rows, in_ref, gain_ref, query_refs, hidden_ref, out_ref):
     count = hidden_ref.shape[0]
-    if layer == 0:
-        rows = rows_ref[pl.ds(pl.multiple_of(side_of() * count, 8), count), :]
-    else:
-        rows = rows_ref[...]
-    hidden = dot(rows.astype(jnp.bfloat16), in_ref[layer])
+    hidden = dot(rows, in_ref[layer])
     hidden_ref[...] = hidden
     spread = lax.rsqrt(jnp.mean(hidden * hidden, axis=1, keepdims=True) + epsilon)
     normed = (hidden * spread * gain_ref[layer : layer + 1, :]).astype(jnp.bfloat16)
-    for first in range(0, pieces, 2):
+    for first in range(0, len(query_refs), 2):
         query = dot(normed, cat([ref[layer] for ref in query_refs[first : first + 2]], 1))
         width = query.shape[1]
         head = lax.broadcasted_iota(jnp.int32, (count, width), 1) // HS
@@ -132,20 +127,30 @@
             ).astype(jnp.bfloat16)
 
 
-def make_queries(layer, count, rows, in_proj, attn_gain, query_pieces):
-    pieces = len(query_pieces)
-    channels, features = in_proj.shape[1:]
-    width = min(2, pieces) * query_pieces[0].shape[2]
-    groups = pieces * query_pieces[0].shape[2] // width
+def queries_kernel(pieces, rows_ref, in_ref, gain_ref, *refs):
+    count = refs[pieces].shape[0]
+    rows = rows_ref[pl.ds(pl.multiple_of(side_of() * count, 8), count), :].astype(jnp.bfloat16)
+    store_queries(0, rows, in_ref, gain_ref, refs[:pieces], refs[pieces], refs[pieces + 1])
+
+
+def query_shapes(count, in_proj, query_pieces):
+    pieces, head_cols = len(query_pieces), query_pieces[0].shape[2]
+    width = min(2, pieces) * head_cols
+    groups = pieces * head_cols // width
+    return [
+        ((count, in_proj.shape[2]), jnp.float32),
+        ((groups, width // HS * count, width), jnp.bfloat16),
+    ]
+
+
+def make_queries(count, rows, in_proj, attn_gain, query_pieces):
+    results = query_shapes(count, in_proj, query_pieces)
     return on_chip(
-        functools.partial(queries_kernel, layer, pieces),
+        functools.partial(queries_kernel, len(query_pieces)),
         "queries",
         [rows, in_proj, attn_gain, *query_pieces],
-        [
-            ((count, features), jnp.float32),
-            ((groups, width // HS * count, width), jnp.bfloat16),
-        ],
-        2 * count * features * (channels + groups * width),
+        results,
+        2 * in_proj.shape[2] * math.prod(results[1][0]),
     )
 
 
@@ -153,7 +158,7 @@
     count, features, size = cfg["count"], cfg["features"], cfg["chunk"]
     side = side_of()
     groups, _, group_cols = query_ref.shape
-    channels = source_ref.shape[1]
+    channels = source_ref.shape[2]
     heads = group_cols // HS
     total_cols = groups * group_cols
     token = lax.broadcasted_iota(jnp.int32, (count, 1), 0)
@@ -163,7 +168,8 @@
     lane = lax.broadcasted_iota(jnp.int32, (1, size), 1)
 
     def one_chunk(start, carry):
-        source = source_ref[pl.ds(start, size), :]
+        source = source_ref[pl.ds(start // count, size // count), :count, :]
+        source = source.reshape(size, channels)
         twice = jnp.concatenate([source, source], axis=1)
         member = ((lane + start).astype(jnp.float32) + 0.5) * (1.0 / count)
         key_place = lane + start + member.astype(jnp.int32) * count + offset
@@ -197,14 +203,14 @@
             )
         return tuple(result)
 
-    chunks = source_ref.shape[0] // size
+    chunks = source_ref.shape[0] * count // size
     carry = one_chunk(0, carry)
     if chunks <= 4:
         for c in range(1, chunks):
             carry = one_chunk(c * size, carry)
     else:
         carry = lax.fori_loop(
-            1, chunks, lambda c, now: one_chunk(pl.multiple_of(c * size, size), now), carry
+            1, chunks, lambda c, now: one_chunk(c * size, now), carry
         )
     return carry
 
@@ -222,7 +228,7 @@
     mix_refs = [refs.pop(0) for _ in range(pieces)]
     param_refs = [refs.pop(0) for _ in range(pieces)]
     side, way, member = side_of(), lax.axis_index("head"), lax.axis_index("seq")
-    members = other_ref.shape[0] // count
+    members = other_ref.shape[0]
     features, channels = hidden_ref.shape[1], latent_ref.shape[1]
     groups, _, group_cols = query_ref.shape
     heads = group_cols // HS
@@ -253,9 +259,12 @@
     token = lax.broadcasted_iota(jnp.int32, (count, 1), 0)
     start = pl.multiple_of(side * count, 8)
     if last:
-        held_ref, held_log_ref, edge_ref, out_ref = refs[:4]
-        edge_log = edge_ref[15:16, :]
-        first = (latent_ref[pl.ds(start, 8), :][:1] - edge_ref[7:8, :]) * jnp.exp(-edge_log)
+        held_ref, held_log_ref, out_ref = refs[:3]
+        before = member - 1 + side
+        edge = other_ref[jnp.maximum(before, 0), count:, :].astype(jnp.float32)
+        edge = jnp.where(before >= 0, edge[0:2] + edge[2:4] + edge[4:6], 0.0)
+        edge_log = edge[1:2]
+        first = (latent_ref[pl.ds(start, 8), :][:1] - edge[0:1]) * jnp.exp(-edge_log)
         values = jnp.where(token == 0, first, pltpu.roll(held_ref[...], 1, 0))
         first_log = jnp.where(token == 0, edge_log, pltpu.roll(held_log_ref[...], 1, 0))
         result = (values - shift_mu) * jnp.exp(-log_scale)
@@ -266,9 +275,11 @@
         out_ref[:count, :] = result
         out_ref[count:, :count] = jnp.broadcast_to(loglik, (8, count))
     else:
-        held_ref, held_log_ref, edge_ref, spread_ref = refs[:4]
-        following = pl.multiple_of(jnp.minimum(member + 1, members - 1) * count, 16)
-        after = other_ref[pl.ds(following, 16), :].astype(jnp.float32)[:1]
+        in_ref, attn_gain_ref = refs[:2]
+        query_refs = refs[2 : 2 + pieces]
+        held_ref, held_log_ref, spread_ref, hidden_out_ref, query_out_ref = refs[2 + pieces : 7 + pieces]
+        following = jnp.minimum(member + 1, members - 1)
+        after = other_ref[following, :16, :].astype(jnp.float32)[:1]
         after = jnp.where(side == 0, latent_ref[count : count + 1, :], after)
         values = pltpu.roll(latent_ref[pl.ds(start, count), :], count - 1, 0)
         values = jnp.where(token == count - 1, after, values)
@@ -277,22 +288,29 @@
         result = jnp.where(beyond, 0.0, result)
         held_ref[...] = result
         held_log_ref[...] = log_scale
-        edge_ref[:8, :] = shift_mu[count - 8 :]
-        edge_ref[8:, :] = log_scale[count - 8 :]
         narrow = result.astype(jnp.bfloat16)
+        edge = jnp.concatenate([shift_mu[count - 1 :], log_scale[count - 1 :]], axis=0)
+        terms = []
+        for _ in range(3):
+            terms.append(edge.astype(jnp.bfloat16).astype(jnp.float32))
+            edge = edge - terms[-1]
+        rest = jnp.zeros((16 - 6, channels), jnp.float32)
+        edge = jnp.concatenate(terms + [rest], axis=0).astype(jnp.bfloat16)
         for i in range(members):
-            spread_ref[i] = narrow
-
-
-def config(layer, count, features, pieces, keys):
-    chunk = next(size for size in (512, 384, 256, 128, keys) if keys % size == 0)
+            spread_ref[i, :count, :] = narrow
+            spread_ref[i, count:, :] = edge
+        store_queries(1, narrow, in_ref, attn_gain_ref, query_refs, hidden_out_ref, query_out_ref)
+
+
+def config(layer, count, features, pieces, members):
+    per_chunk = next(size for size in (8, 4, 2, 1) if members % size == 0)
     return {
         "layer": layer,
         "last": layer == 1,
         "count": count,
         "features": features,
         "pieces": pieces,
-        "chunk": chunk,
+        "chunk": per_chunk * count,
     }
 
 
@@ -303,29 +321,29 @@
         "first_half",
         [maps, queries, own],
         [((groups, rows, cols), jnp.float32), ((groups, rows, 128), jnp.float32)],
-        2 * own.shape[0] * (maps.size + 2 * queries.size),
-    )
-
-
-def second_half(cfg, members, maps, queries, other, sums, hidden, param_gain, latents, mix_pieces, param_pieces, held=()):
+        2 * own.shape[0] * cfg["count"] * (maps.size + 2 * queries.size),
+    )
+
+
+def second_half(cfg, maps, queries, other, sums, hidden, param_gain, latents, mix_pieces, param_pieces, extra):
     count, channels = cfg["count"], latents.shape[1]
     operands = [maps, queries, other, *sums, hidden, param_gain, latents]
-    operands += [*mix_pieces, *param_pieces, *held]
+    operands += [*mix_pieces, *param_pieces, *extra]
     if cfg["last"]:
         results = [((count + 8, channels), jnp.float32)]
     else:
         results = [
             ((count, channels), jnp.float32),
             ((count, channels), jnp.float32),
-            ((16, channels), jnp.float32),
-            ((members, count, channels), jnp.bfloat16),
+            ((other.shape[0], count + 16, channels), jnp.bfloat16),
+            *query_shapes(count, extra[0], extra[2:]),
         ]
     return on_chip(
         functools.partial(second_half_kernel, cfg),
         "second_half",
         operands,
         results,
-        2 * other.shape[0] * (maps.size + 2 * queries.size),
+        2 * other.shape[0] * count * (maps.size + 2 * queries.size),
         scratch=[pltpu.VMEM((cfg["features"], param_pieces[0].shape[2]), jnp.bfloat16)],
     )
 
@@ -361,7 +379,7 @@
         return shares
 
     def gather(spread):
-        return lax.all_to_all(spread, "seq", 0, 0).reshape(keys, channels)
+        return lax.all_to_all(spread, "seq", 0, 0)
 
     (spread,) = on_chip(
         spread_kernel,
@@ -375,32 +393,22 @@
     query_pieces, mix_pieces = pieces_of(query_proj), pieces_of(mix_proj)
     param_pieces = pieces_of(param_proj)
     maps = [combine(b, in_proj, attn_gain, key_pieces, value_pieces) for b in range(2)]
-    hidden, queries = make_queries(0, count, latents, in_proj, attn_gain, query_pieces)
+    hidden, queries = make_queries(count, latents, in_proj, attn_gain, query_pieces)
     own = gate(own, *maps, queries)
 
-    cfg = config(0, count, features, ways, keys)
+    cfg = config(0, count, features, ways, members)
     other = swap(own)
     sums = first_half(cfg, maps[0], queries, own)
-    held, held_log, edge, spread = second_half(
-        cfg, members, maps[0], queries, other, sums, hidden, param_gain, latents, mix_pieces, param_pieces
-    )
-
+    shared = (param_gain, latents, mix_pieces, param_pieces)
+    held, held_log, spread, hidden, queries = second_half(
+        cfg, maps[0], queries, other, sums, hidden, *shared, (in_proj, attn_gain, *query_pieces)
+    )
     own = gather(spread)
-    pairs = []
-    for s in range(members):
-        for w in range(ways):
-            if w % 2 == 0:
-                pairs.append((s * ways + w, s * ways + w + 1))
-            elif s < members - 1:
-                pairs.append((s * ways + w, (s + 1) * ways + w - 1))
-    edge = lax.ppermute(edge, ("seq", "head"), pairs)
-    hidden, queries = make_queries(1, count, held, in_proj, attn_gain, query_pieces)
-    own = gate(own, queries)
-    cfg = config(1, count, features, ways, keys)
+    cfg = config(1, count, features, ways, members)
     other = swap(own)
     sums = first_half(cfg, maps[1], queries, own)
     (packed,) = second_half(
-        cfg, members, maps[1], queries, other, sums, hidden, param_gain, latents, mix_pieces, param_pieces, (held, held_log, edge)
+        cfg, maps[1], queries, other, sums, hidden, *shared, (held, held_log)
     )
     final_latent, token_loglik = on_chip(
         finish_kernel,

time: 62.9 us -> 58.8 us (0.935)
  the two profiles are of different devices: /device:TPU:9 before, /device:TPU:0 now
where the time goes in v5:
time: 58.8 us; the launch traced here: 58.3 us
  blocking collectives  17.8 us (30%)
  Pallas kernels  16.3 us (28%)
  starting transfers between devices  10.4 us (18%)
  waiting for transfers between devices  9.91 us (17%)
  local copies, waits for them, and re-layouts  3.08 us (5%)
  between operations  0.91 us (2%)
    all_to_all x1, blocking collectives, gather(): return lax.all_to_all(spread, 'seq', 0, 0)  17.8 us
    pallas_call x10, Pallas kernels, on_chip(): pl.pallas_call(kernel, in_specs=[pl.BlockSpec(memory_space=pltpu.VMEM)] *...  16.3 us
    all_to_all x1, waiting for transfers between devices, gather(): return lax.all_to_all(spread, 'seq', 0, 0)  9.01 us
    all_to_all x1, starting transfers between devices, gather(): return lax.all_to_all(spread, 'seq', 0, 0)  8.12 us
    unnamed x32, local copies, waits for them, and re-layouts  3.08 us
    ppermute x5, starting transfers between devices, pieces_of(): lax.ppermute(array, 'head', [((i + j) % ways, i) for i in range(ways)])  1.6 us
  transfers between devices with their start and end apart: 9, of which 2 were waited for; matrix products, arithmetic and copies ran while one was open for 0% of the time, Pallas kernels for 12%

profile of v5, /device:TPU:0, one launch (start us, length us, event | category | flops | bytes accessed | tf_op | source)
XLA Modules:
  0.0 58.3 jit_solution(7391074587837212838)
XLA Ops:
  0.6 0.5 collective-permute-start.2
  1.2 0.1 collective-permute-start
  1.2 0.4 collective-permute-start.1
  1.7 0.9 %copy-done.9 = f32[192,128]{1,0:T(8,128)S(1)} copy-done((f32[192,128]{1,0:T(8,128)S(1)}, f32[192,128]{1,0:T(8,128)}, u32[]{:S(2)}) %copy-start.9) | copy-done | bytes 98328
  2.6 0.7 %copy-done.11 = bf16[16,96,128]{2,1,0:T(8,128)(2,1)} copy-done((bf16[16,96,128]{2,1,0:T(8,128)(2,1)}, bf16[16,96,128]{2,1,0:T(8,128)(2,1)S(1)}, u32[]{:S(2)}) %copy-start.11) | copy-done | bytes 393240
  3.3 8.1 %all-to-all-start = ((bf16[16,96,128]{2,1,0:T(8,128)(2,1)}), bf16[16,96,128]{2,1,0:T(8,128)(2,1)}, u32[]{:S(2)}, u32[]{:S(2)}) async-start(bf16[16,96,128]{2,1,0:T(8,128)(2,1)} %copy-done.11), calls=%async_computation | async-start | bytes 786432 | tf_op jit(solution)/shard_map/all_to_all | solution.py:382
  11.5 0.2 collective-permute-start.4
  11.7 0.3 collective-permute-start.5
  12.1 1.1 %copy-done.3 = bf16[2,1536,128]{2,1,0:T(8,128)(2,1)S(1)} copy-done((bf16[2,1536,128]{2,1,0:T(8,128)(2,1)S(1)}, bf16[2,1536,128]{2,1,0:T(8,128)(2,1)}, u32[]{:S(2)}) %copy-start.3) | copy-done | bytes 786456
  13.2 0.7 %queries.1 = (f32[96,1536]{1,0:T(8,128)S(1)}, bf16[1,384,256]{2,1,0:T(8,128)(2,1)S(1)}) custom-call(f32[192,128]{1,0:T(8,128)S(1)} %copy-done.10, bf16[2,128,1536]{2,1,0:T(8,128)(2,1)S(1)} %copy-done, f32[2,1536]{1,0:T(2,128)S(1)} %copy-done.14, bf16[2,1536,128]{2,1,0:T(8,128)(2,1)S(1)} %copy-done.3, ...), custom_call_target="tpu_custom_call" | custom-call | flops 301989888 | tf_op jit(solution)/shard_map/queries/pallas_call | solution.py:41
  13.9 0.2 copy-done.5
  14.2 0.8 %combine.3.refs_0_.maps_ref = bf16[768,256]{1,0:T(8,128)(2,1)S(1)} custom-call(bf16[2,128,1536]{2,1,0:T(8,128)(2,1)S(1)} %copy-done, f32[2,1536]{1,0:T(2,128)S(1)} %copy-done.14, bf16[2,1536,128]{2,1,0:T(8,128)(2,1)S(1)} %copy-done.1, bf16[2,1536,128]{2,1,0:T(8,128)(2,1)S(1)} %collective-permute-done.refs_1_, bf16[2,1536,128]{2,1,0:T(8,128)(2,1)S(1)} %copy-done.2, ...), custom_call_target="tpu_custom_call" | custom-call | flops 603979776 | tf_op jit(solution)/shard_map/combine/pallas_call | solution.py:41
  14.9 0.8 %combine.2.refs_1_.maps_ref = bf16[768,256]{1,0:T(8,128)(2,1)S(1)} custom-call(bf16[2,128,1536]{2,1,0:T(8,128)(2,1)S(1)} %copy-done, f32[2,1536]{1,0:T(2,128)S(1)} %copy-done.14, bf16[2,1536,128]{2,1,0:T(8,128)(2,1)S(1)} %copy-done.1, bf16[2,1536,128]{2,1,0:T(8,128)(2,1)S(1)} %collective-permute-done.refs_1_, bf16[2,1536,128]{2,1,0:T(8,128)(2,1)S(1)} %copy-done.2, ...), custom_call_target="tpu_custom_call" | custom-call | flops 603979776 | tf_op jit(solution)/shard_map/combine/pallas_call | solution.py:41
  15.7 9.0 %all-to-all-done.own_ref = bf16[16,96,128]{2,1,0:T(8,128)(2,1)} async-done(((bf16[16,96,128]{2,1,0:T(8,128)(2,1)}), bf16[16,96,128]{2,1,0:T(8,128)(2,1)}, u32[]{:S(2)}, u32[]{:S(2)}) %all-to-all-start) | async-done | bytes 393248 | tf_op jit(solution)/shard_map/all_to_all | solution.py:382
  24.7 1.0 %gate.1.own_ref = bf16[16,96,128]{2,1,0:T(8,128)(2,1)S(1)} custom-call(bf16[16,96,128]{2,1,0:T(8,128)(2,1)} %all-to-all-done.own_ref, bf16[768,256]{1,0:T(8,128)(2,1)S(1)} %combine.3.refs_0_.maps_ref, bf16[768,256]{1,0:T(8,128)(2,1)S(1)} %combine.2.refs_1_.maps_ref, bf16[1,384,256]{2,1,0:T(8,128)(2,1)S(1)} %get-tuple-element.15.refs_2_.query_ref), custom_call_target="tpu_custom_call" | custom-call | flops 196608 | tf_op jit(solution)/shard_map/gate/pallas_call | solution.py:41
  25.8 0.1 collective-permute-start.3
  25.9 1.9 %first_half.2 = (f32[1,384,256]{2,1,0:T(8,128)S(1)}, f32[1,384,128]{2,1,0:T(8,128)S(1)}) custom-call(bf16[768,256]{1,0:T(8,128)(2,1)S(1)} %combine.3.refs_0_.maps_ref, bf16[1,384,256]{2,1,0:T(8,128)(2,1)S(1)} %get-tuple-element.15.refs_2_.query_ref, bf16[16,96,128]{2,1,0:T(8,128)(2,1)S(1)} %gate.1.own_ref), custom_call_target="tpu_custom_call" | custom-call | flops 1207959552 | tf_op jit(solution)/shard_map/first_half/pallas_call | solution.py:41
  27.9 4.6 %second_half.2 = (f32[96,128]{1,0:T(8,128)S(1)}, f32[96,128]{1,0:T(8,128)S(1)}, bf16[16,112,128]{2,1,0:T(8,128)(2,1)S(1)}, f32[96,1536]{1,0:T(8,128)S(1)}, bf16[1,384,256]{2,1,0:T(8,128)(2,1)S(1)}) custom-call(bf16[768,256]{1,0:T(8,128)(2,1)S(1)} %combine.3.refs_0_.maps_ref, bf16[1,384,256]{2,1,0:T(8,128)(2,1)S(1)} %get-tuple-element.15.refs_2_.query_ref, ...), custom_call_target="tpu_custom_call" | custom-call | flops 1207959552 | tf_op jit(solution)/shard_map/second_half/pallas_call | solution.py:41
  32.5 17.8 %all_to_all.10.own_ref = bf16[16,112,128]{2,1,0:T(8,128)(2,1)S(1)} all-to-all(bf16[16,112,128]{2,1,0:T(8,128)(2,1)S(1)} %get-tuple-element.20), channel_id=1, replica_groups=mesh['seq'=16,'head'=2] {'seq'}, dimensions={0} | all-to-all | bytes 917504 | tf_op jit(solution)/shard_map/all_to_all | solution.py:382
  50.3 1.9 %first_half.3 = (f32[1,384,256]{2,1,0:T(8,128)S(1)}, f32[1,384,128]{2,1,0:T(8,128)S(1)}) custom-call(bf16[768,256]{1,0:T(8,128)(2,1)S(1)} %combine.2.refs_1_.maps_ref, bf16[1,384,256]{2,1,0:T(8,128)(2,1)S(1)} %get-tuple-element.19.query_ref, bf16[16,112,128]{2,1,0:T(8,128)(2,1)S(1)} %all_to_all.10.own_ref), custom_call_target="tpu_custom_call" | custom-call | flops 1207959552 | tf_op jit(solution)/shard_map/first_half/pallas_call | solution.py:41
  52.3 4.0 %second_half.3.own_ref = f32[104,128]{1,0:T(8,128)S(1)} custom-call(bf16[768,256]{1,0:T(8,128)(2,1)S(1)} %combine.2.refs_1_.maps_ref, bf16[1,384,256]{2,1,0:T(8,128)(2,1)S(1)} %get-tuple-element.19.query_ref, bf16[16,112,128]{2,1,0:T(8,128)(2,1)S(1)} %collective-permute-done.6.other_ref, f32[1,384,256]{2,1,0:T(8,128)S(1)} %get-tuple-element.21.number_ref, ...), custom_call_target="tpu_custom_call" | custom-call | flops 1207959552 | tf_op jit(solution)/shard_map/second_half/pallas_call | solution.py:41
  56.2 0.6 collective-permute-start.7
  56.8 0.9 %collective-permute-done.7.other_ref = f32[104,128]{1,0:T(8,128)S(1)} collective-permute-done((f32[104,128]{1,0:T(8,128)S(1)}, f32[104,128]{1,0:T(8,128)S(1)}, u32[]{:S(2)}, u32[]{:S(2)}) %collective-permute-start.7) | collective-permute-done | bytes 53280 | tf_op jit(solution)/shard_map/ppermute | solution.py:371
  57.7 0.7 %finish.1 = (f32[192,128]{1,0:T(8,128)}, f32[1,192]{1,0:T(1,128)}) custom-call(f32[104,128]{1,0:T(8,128)S(1)} %second_half.3.own_ref, f32[104,128]{1,0:T(8,128)S(1)} %collective-permute-done.7.other_ref), custom_call_target="tpu_custom_call" | custom-call | flops 24576 | tf_op jit(solution)/shard_map/finish/pallas_call | solution.py:41
  (37 shorter events, 0.1 us)
Async XLA Ops:
  0.6 11.4 %copy-start = (bf16[2,128,1536]{2,1,0:T(8,128)(2,1)S(1)}, bf16[2,128,1536]{2,1,0:T(8,128)(2,1)}, u32[]{:S(2)}) copy-start(bf16[2,128,1536]{2,1,0:T(8,128)(2,1)} %refs_4_.1) | copy-start | bytes 2359300
  0.6 11.4 %collective-permute-start.2 = (bf16[2,1536,128]{2,1,0:T(8,128)(2,1)}, bf16[2,1536,128]{2,1,0:T(8,128)(2,1)S(1)}, u32[]{:S(2)}, u32[]{:S(2)}) collective-permute-start(bf16[2,1536,128]{2,1,0:T(8,128)(2,1)} %refs_6_.1), channel_id=1, source_target_pairs={{1,0},{0,1},{3,2},{2,3},{5,4},{4,5},{7,6},{6,7},{9,8},{8,9},{11,10... | collective-permute-start | bytes 2359304 | tf_op jit(solution)/shard_map/ppermute | solution.py:377
  1.2 13.0 %collective-permute-start = (bf16[2,1536,128]{2,1,0:T(8,128)(2,1)}, bf16[2,1536,128]{2,1,0:T(8,128)(2,1)S(1)}, u32[]{:S(2)}, u32[]{:S(2)}) collective-permute-start(bf16[2,1536,128]{2,1,0:T(8,128)(2,1)} %refs_0_.6), channel_id=1, source_target_pairs={{1,0},{0,1},{3,2},{2,3},{5,4},{4,5},{7,6},{6,7},{9,8},{8,9},{11,10... | collective-permute-start | bytes 2359304 | tf_op jit(solution)/shard_map/ppermute | solution.py:377
  1.2 12.9 %collective-permute-start.1 = (bf16[2,1536,128]{2,1,0:T(8,128)(2,1)}, bf16[2,1536,128]{2,1,0:T(8,128)(2,1)S(1)}, u32[]{:S(2)}, u32[]{:S(2)}) collective-permute-start(bf16[2,1536,128]{2,1,0:T(8,128)(2,1)} %refs_2_.5), channel_id=1, source_target_pairs={{1,0},{0,1},{3,2},{2,3},{5,4},{4,5},{7,6},{6,7},{9,8},{8,9},{11,10... | collective-permute-start | bytes 2359304 | tf_op jit(solution)/shard_map/ppermute | solution.py:377
  1.7 0.9 %copy-start.9 = (f32[192,128]{1,0:T(8,128)S(1)}, f32[192,128]{1,0:T(8,128)}, u32[]{:S(2)}) copy-start(f32[192,128]{1,0:T(8,128)} %latent_ref.3) | copy-start | bytes 294916
  3.3 8.7 %copy-start.10 = (f32[192,128]{1,0:T(8,128)S(1)}, f32[192,128]{1,0:T(8,128)}, u32[]{:S(2)}) copy-start(f32[192,128]{1,0:T(8,128)} %latent_ref.3) | copy-start | bytes 294916
  3.3 8.7 %copy-start.14 = (f32[2,1536]{1,0:T(2,128)S(1)}, f32[2,1536]{1,0:T(2,128)}, u32[]{:S(2)}) copy-start(f32[2,1536]{1,0:T(2,128)} %refs_5_.1) | copy-start | bytes 36868
  3.3 21.4 %all-to-all-start = ((bf16[16,96,128]{2,1,0:T(8,128)(2,1)}), bf16[16,96,128]{2,1,0:T(8,128)(2,1)}, u32[]{:S(2)}, u32[]{:S(2)}) async-start(bf16[16,96,128]{2,1,0:T(8,128)(2,1)} %copy-done.11), calls=%async_computation | async-start | bytes 786432 | tf_op jit(solution)/shard_map/all_to_all | solution.py:382
  11.5 2.7 %copy-start.1 = (bf16[2,1536,128]{2,1,0:T(8,128)(2,1)S(1)}, bf16[2,1536,128]{2,1,0:T(8,128)(2,1)}, u32[]{:S(2)}) copy-start(bf16[2,1536,128]{2,1,0:T(8,128)(2,1)} %refs_0_.6) | copy-start | bytes 2359300
  11.5 2.7 %copy-start.2 = (bf16[2,1536,128]{2,1,0:T(8,128)(2,1)S(1)}, bf16[2,1536,128]{2,1,0:T(8,128)(2,1)}, u32[]{:S(2)}) copy-start(bf16[2,1536,128]{2,1,0:T(8,128)(2,1)} %refs_2_.5) | copy-start | bytes 2359300
  11.5 16.3 %collective-permute-start.4 = (bf16[2,128,1536]{2,1,0:T(8,128)(2,1)}, bf16[2,128,1536]{2,1,0:T(8,128)(2,1)}, u32[]{:S(2)}, u32[]{:S(2)}) collective-permute-start(bf16[2,128,1536]{2,1,0:T(8,128)(2,1)} %refs_0_.9), channel_id=1, source_target_pairs={{1,0},{0,1},{3,2},{2,3},{5,4},{4,5},{7,6},{6,7},{9,8},{8,9},{11,10... | collective-permute-start | bytes 2359304 | tf_op jit(solution)/shard_map/ppermute | solution.py:377
  11.7 16.1 %collective-permute-start.5 = (bf16[2,768,256]{2,1,0:T(8,128)(2,1)}, bf16[2,768,256]{2,1,0:T(8,128)(2,1)}, u32[]{:S(2)}, u32[]{:S(2)}) collective-permute-start(bf16[2,768,256]{2,1,0:T(8,128)(2,1)} %refs_2_.7), channel_id=1, source_target_pairs={{1,0},{0,1},{3,2},{2,3},{5,4},{4,5},{7,6},{6,7},{9,8},{8,9},{11,10... | collective-permute-start | bytes 2359304 | tf_op jit(solution)/shard_map/ppermute | solution.py:377
  12.1 1.1 %copy-start.3 = (bf16[2,1536,128]{2,1,0:T(8,128)(2,1)S(1)}, bf16[2,1536,128]{2,1,0:T(8,128)(2,1)}, u32[]{:S(2)}) copy-start(bf16[2,1536,128]{2,1,0:T(8,128)(2,1)} %refs_6_.1) | copy-start | bytes 2359300
  13.2 0.9 %copy-start.5 = (bf16[2,1536,128]{2,1,0:T(8,128)(2,1)}, bf16[2,1536,128]{2,1,0:T(8,128)(2,1)S(1)}, u32[]{:S(2)}) copy-start(bf16[2,1536,128]{2,1,0:T(8,128)(2,1)S(1)} %collective-permute-done.2.refs_1_.refs_7_) | copy-start | bytes 2359300
  14.1 0.8 %copy-start.12 = (f32[96,1536]{1,0:T(8,128)}, f32[96,1536]{1,0:T(8,128)S(1)}, u32[]{:S(2)}) copy-start(f32[96,1536]{1,0:T(8,128)S(1)} %get-tuple-element.18.hidden_ref) | copy-start | bytes 1769476
  25.7 2.1 %copy-start.4 = (bf16[2,1536,128]{2,1,0:T(8,128)(2,1)S(1)}, bf16[2,1536,128]{2,1,0:T(8,128)(2,1)}, u32[]{:S(2)}) copy-start(bf16[2,1536,128]{2,1,0:T(8,128)(2,1)} %refs_6_.1) | copy-start | bytes 2359300
  25.8 2.1 %copy-start.6 = (bf16[2,1536,128]{2,1,0:T(8,128)(2,1)S(1)}, bf16[2,1536,128]{2,1,0:T(8,128)(2,1)}, u32[]{:S(2)}) copy-start(bf16[2,1536,128]{2,1,0:T(8,128)(2,1)} %copy-done.5) | copy-start | bytes 2359300
  25.8 2.1 %copy-start.7 = (bf16[2,128,1536]{2,1,0:T(8,128)(2,1)S(1)}, bf16[2,128,1536]{2,1,0:T(8,128)(2,1)}, u32[]{:S(2)}) copy-start(bf16[2,128,1536]{2,1,0:T(8,128)(2,1)} %refs_0_.9) | copy-start | bytes 2359300
  25.8 2.1 %copy-start.8 = (bf16[2,768,256]{2,1,0:T(8,128)(2,1)S(1)}, bf16[2,768,256]{2,1,0:T(8,128)(2,1)}, u32[]{:S(2)}) copy-start(bf16[2,768,256]{2,1,0:T(8,128)(2,1)} %refs_2_.7) | copy-start | bytes 2359300
  25.8 2.1 %copy-start.13 = (f32[96,1536]{1,0:T(8,128)S(1)}, f32[96,1536]{1,0:T(8,128)}, u32[]{:S(2)}) copy-start(f32[96,1536]{1,0:T(8,128)} %copy-done.12) | copy-start | bytes 1769476
  25.8 2.0 %collective-permute-start.3 = (bf16[16,96,128]{2,1,0:T(8,128)(2,1)S(1)}, bf16[16,96,128]{2,1,0:T(8,128)(2,1)S(1)}, u32[]{:S(2)}, u32[]{:S(2)}) collective-permute-start(bf16[16,96,128]{2,1,0:T(8,128)(2,1)S(1)} %gate.1.own_ref), channel_id=1, source_target_pairs={{0,1},{1,0},{2,3},{3,2},{4,5},{5,4},{6,7},{7,6},{8,9},{9,8},{10,11... | collective-permute-start | bytes 1179656 | tf_op jit(solution)/shard_map/ppermute | solution.py:371
  25.9 2.0 %copy-start.15 = (f32[2,1536]{1,0:T(2,128)S(1)}, f32[2,1536]{1,0:T(2,128)}, u32[]{:S(2)}) copy-start(f32[2,1536]{1,0:T(2,128)} %gain_ref.9) | copy-start | bytes 36868
  50.3 1.9 %collective-permute-start.6 = (bf16[16,112,128]{2,1,0:T(8,128)(2,1)S(1)}, bf16[16,112,128]{2,1,0:T(8,128)(2,1)S(1)}, u32[]{:S(2)}, u32[]{:S(2)}) collective-permute-start(bf16[16,112,128]{2,1,0:T(8,128)(2,1)S(1)} %all_to_all.10.own_ref), channel_id=1, source_target_pairs={{0,1},{1,0},{2,3},{3,2},{4,5},{5,4},{6,7},{7,6},{8,9},{9,8},{10,11... | collective-permute-start | bytes 1376264 | tf_op jit(solution)/shard_map/ppermute | solution.py:371
  56.2 1.5 %collective-permute-start.7 = (f32[104,128]{1,0:T(8,128)S(1)}, f32[104,128]{1,0:T(8,128)S(1)}, u32[]{:S(2)}, u32[]{:S(2)}) collective-permute-start(f32[104,128]{1,0:T(8,128)S(1)} %second_half.3.own_ref), channel_id=1, source_target_pairs={{0,1},{1,0},{2,3},{3,2},{4,5},{5,4},{6,7},{7,6},{8,9},{9,8},{10,11... | collective-permute-start | bytes 159752 | tf_op jit(solution)/shard_map/ppermute | solution.py:371
  (1 other events, 0.8 us)

commit v6 on v5

--- a/solution.py
+++ b/solution.py
@@ -45,24 +45,48 @@
         out_shape=out_shape,
         scratch_shapes=list(scratch),
         compiler_params=pltpu.CompilerParams(vmem_limit_bytes=VMEM_LIMIT),
-        cost_estimate=pl.CostEstimate(flops=int(flops), bytes_accessed=0, transcendentals=0),
+
         name=name,
     )(*near)
 
 
-def spread_kernel(rows_ref, spread_ref):
-    members, count, _ = spread_ref.shape
-    own = rows_ref[pl.ds(pl.multiple_of(side_of() * count, 8), count), :].astype(jnp.bfloat16)
-    for i in range(members):
-        spread_ref[i] = own
-
-
-def gate_kernel(own_ref, *refs):
-    refs[-1][...] = own_ref[...]
-
-
-def gate(own, *made):
-    return on_chip(gate_kernel, "gate", [own, *made], [(own.shape, own.dtype)], own.size)[0]
+def narrow_kernel(rows_ref, own_ref):
+    count = own_ref.shape[0]
+    own_ref[...] = rows_ref[pl.ds(pl.multiple_of(side_of() * count, 8), count), :].astype(
+        jnp.bfloat16
+    )
+
+
+def arrange_kernel(planes, *refs):
+    place = lax.axis_index("seq") // (lax.axis_size("seq") // planes)
+    for step in range(planes):
+        refs[-1][place ^ step] = refs[step][...]
+
+
+def gates_kernel(many, *refs):
+    for source, target in zip(refs[:many], refs[-many:]):
+        target[...] = source[...]
+
+
+def gate_all(rows, made):
+    return on_chip(
+        functools.partial(gates_kernel, len(rows)),
+        "gate",
+        [*rows, *made],
+        [(piece.shape, piece.dtype) for piece in rows],
+        0,
+    )
+
+
+def turned(step, bits):
+    return sum(((step >> b) & 1) << (bits - 1 - b) for b in range(bits))
+
+
+def chip_of(step, per_plane, other):
+    bits = per_plane.bit_length() - 1
+    side = side_of()
+    first = side == (1 if other else 0)
+    return (lax.axis_index("seq") % per_plane) ^ jnp.where(first, step, turned(step, bits))
 
 
 def combine_kernel(layer, pieces, in_ref, gain_ref, *refs):
@@ -127,10 +151,9 @@
             ).astype(jnp.bfloat16)
 
 
-def queries_kernel(pieces, rows_ref, in_ref, gain_ref, *refs):
-    count = refs[pieces].shape[0]
-    rows = rows_ref[pl.ds(pl.multiple_of(side_of() * count, 8), count), :].astype(jnp.bfloat16)
-    store_queries(0, rows, in_ref, gain_ref, refs[:pieces], refs[pieces], refs[pieces + 1])
+def queries_kernel(layer, pieces, rows_ref, in_ref, gain_ref, *refs):
+    rows = rows_ref[: refs[pieces].shape[0], :]
+    store_queries(layer, rows, in_ref, gain_ref, refs[:pieces], refs[pieces], refs[pieces + 1])
 
 
 def query_shapes(count, in_proj, query_pieces):
@@ -143,10 +166,10 @@
     ]
 
 
-def make_queries(count, rows, in_proj, attn_gain, query_pieces):
+def make_queries(layer, count, rows, in_proj, attn_gain, query_pieces):
     results = query_shapes(count, in_proj, query_pieces)
     return on_chip(
-        functools.partial(queries_kernel, len(query_pieces)),
+        functools.partial(queries_kernel, layer, len(query_pieces)),
         "queries",
         [rows, in_proj, attn_gain, *query_pieces],
         results,
@@ -154,25 +177,29 @@
     )
 
 
-def attend_rows(cfg, place, maps_ref, query_ref, source_ref, carry):
-    count, features, size = cfg["count"], cfg["features"], cfg["chunk"]
+def attend_rows(cfg, maps_ref, query_ref, pieces, carry):
+    count, features, planes, per_plane = cfg["count"], cfg["features"], cfg["planes"], cfg["per_plane"]
     side = side_of()
     groups, _, group_cols = query_ref.shape
-    channels = source_ref.shape[2]
     heads = group_cols // HS
     total_cols = groups * group_cols
+    size = planes * count
     token = lax.broadcasted_iota(jnp.int32, (count, 1), 0)
     first_token = lax.axis_index("seq") * (2 * count) + side * count
     query_place = first_token + jnp.concatenate([token] * heads, axis=0)
-    offset = (side if place == 0 else 1 - side) * count
     lane = lax.broadcasted_iota(jnp.int32, (1, size), 1)
-
-    def one_chunk(start, carry):
-        source = source_ref[pl.ds(start // count, size // count), :count, :]
-        source = source.reshape(size, channels)
-        twice = jnp.concatenate([source, source], axis=1)
-        member = ((lane + start).astype(jnp.float32) + 0.5) * (1.0 / count)
-        key_place = lane + start + member.astype(jnp.int32) * count + offset
+    plane = ((lane.astype(jnp.float32) + 0.5) * (1.0 / count)).astype(jnp.int32)
+    base_place = lane + plane * (2 * per_plane * count - count)
+
+    def one_chunk(some, carry):
+        sources, places = [], []
+        for rows, step, other in some:
+            rows = rows[:, :count, :].reshape(size, rows.shape[2])
+            sources.append(jnp.concatenate([rows, rows], axis=1))
+            offset = chip_of(step, per_plane, other) * 2 + (1 - side if other else side)
+            places.append(base_place + offset * count)
+        twice, key_place = cat(sources, 0), cat(places, 1)
+        channels = twice.shape[1] // 2
         allowed = key_place <= query_place if cfg["layer"] == 0 else key_place >= query_place
         tail = dot_nt(maps_ref[2 * total_cols :, :], twice)
         square = jnp.sum(tail[:channels] * tail[channels:], axis=0, keepdims=True)
@@ -194,7 +221,7 @@
             weights = jnp.where(allowed, jnp.exp(scores), 0.0)
             product = dot_nt(weights.astype(jnp.bfloat16), value)
             total = weights[:, :128]
-            for at in range(128, size, 128):
+            for at in range(128, weights.shape[1], 128):
                 total = total + weights[:, at : at + 128]
             result.append(
                 (product, total)
@@ -203,37 +230,70 @@
             )
         return tuple(result)
 
-    chunks = source_ref.shape[0] * count // size
-    carry = one_chunk(0, carry)
-    if chunks <= 4:
-        for c in range(1, chunks):
-            carry = one_chunk(c * size, carry)
-    else:
-        carry = lax.fori_loop(
-            1, chunks, lambda c, now: one_chunk(c * size, now), carry
+    if len(pieces) <= 4:
+        for at in range(0, len(pieces), 2):
+            some = [(ref[...], step, other) for ref, step, other in pieces[at : at + 2]]
+            carry = one_chunk(some, carry)
+        return carry
+    held, (_, first, other) = cfg["held"], pieces[0]
+    for at, (ref, _, _) in enumerate(pieces):
+        held[at] = ref[...]
+    if carry is None:
+        carry = tuple(
+            (
+                jnp.zeros((heads * count, group_cols), jnp.float32),
+                jnp.zeros((heads * count, 128), jnp.float32),
+            )
+            for _ in range(groups)
         )
-    return carry
-
-
-def first_half_kernel(cfg, maps_ref, query_ref, own_ref, number_ref, total_ref):
-    carry = attend_rows(cfg, 0, maps_ref, query_ref, own_ref, None)
+    return lax.fori_loop(
+        0, len(pieces), lambda at, now: one_chunk([(held[at], first + at, other)], now), carry
+    )
+
+
+def partial_kernel(cfg, kinds, resume, maps_ref, query_ref, *refs):
+    refs = list(refs)
+    pieces = [(refs.pop(0), step, other) for step, other in kinds]
+    carry = None
+    if resume:
+        number_in, total_in = refs.pop(0), refs.pop(0)
+        carry = tuple((number_in[g], total_in[g]) for g in range(query_ref.shape[0]))
+    number_ref, total_ref = refs[:2]
+    cfg = dict(cfg, held=refs[2] if len(refs) > 2 else None)
+    carry = attend_rows(cfg, maps_ref, query_ref, pieces, carry)
     for g, (number, total) in enumerate(carry):
         number_ref[g] = number
         total_ref[g] = total
 
 
-def second_half_kernel(cfg, maps_ref, query_ref, other_ref, number_ref, total_ref, hidden_ref, gain_ref, latent_ref, *refs):
+def chosen_rows(others, per_plane, place, rows):
+    plane, chip = place // per_plane, place % per_plane
+    result = None
+    for step, ref in enumerate(others):
+        value = ref[plane, rows, :].astype(jnp.float32)
+        here = chip_of(step, per_plane, True) == chip
+        result = value if result is None else jnp.where(here, value, result)
+    return result
+
+
+def second_half_kernel(cfg, kinds, maps_ref, query_ref, number_ref, total_ref, hidden_ref, gain_ref, latent_ref, *refs):
     layer, pieces, last, count = cfg["layer"], cfg["pieces"], cfg["last"], cfg["count"]
+    per_plane = cfg["per_plane"]
     refs = list(refs)
+    others = [refs.pop(0) for _ in range(per_plane)]
     mix_refs = [refs.pop(0) for _ in range(pieces)]
     param_refs = [refs.pop(0) for _ in range(pieces)]
+    param_all = refs.pop(3)
+    cfg = dict(cfg, held=refs[-1])
     side, way, member = side_of(), lax.axis_index("head"), lax.axis_index("seq")
-    members = other_ref.shape[0]
+    members = cfg["planes"] * per_plane
     features, channels = hidden_ref.shape[1], latent_ref.shape[1]
     groups, _, group_cols = query_ref.shape
     heads = group_cols // HS
     carry = tuple((number_ref[g], total_ref[g]) for g in range(groups))
-    carry = attend_rows(cfg, 1, maps_ref, query_ref, other_ref, carry)
+    carry = attend_rows(
+        cfg, maps_ref, query_ref, [(others[step], step, True) for step in kinds], carry
+    )
 
     mixture = hidden_ref[...]
     head = lax.broadcasted_iota(jnp.int32, (count, group_cols), 1) // HS
@@ -249,7 +309,6 @@
     spread = lax.rsqrt(jnp.mean(mixture * mixture, axis=1, keepdims=True) + epsilon)
     scaled = (mixture * spread * gain_ref[layer : layer + 1, :]).astype(jnp.bfloat16)
     share = features // pieces
-    param_all = refs[-1]
     for j, ref in enumerate(param_refs):
         at = pl.multiple_of(lax.rem(way + j, pieces) * share, 16)
         param_all[pl.ds(at, share), :] = ref[layer]
@@ -261,7 +320,7 @@
     if last:
         held_ref, held_log_ref, out_ref = refs[:3]
         before = member - 1 + side
-        edge = other_ref[jnp.maximum(before, 0), count:, :].astype(jnp.float32)
+        edge = chosen_rows(others, per_plane, jnp.maximum(before, 0), slice(count, count + 16))
         edge = jnp.where(before >= 0, edge[0:2] + edge[2:4] + edge[4:6], 0.0)
         edge_log = edge[1:2]
         first = (latent_ref[pl.ds(start, 8), :][:1] - edge[0:1]) * jnp.exp(-edge_log)
@@ -275,11 +334,9 @@
         out_ref[:count, :] = result
         out_ref[count:, :count] = jnp.broadcast_to(loglik, (8, count))
     else:
-        in_ref, attn_gain_ref = refs[:2]
-        query_refs = refs[2 : 2 + pieces]
-        held_ref, held_log_ref, spread_ref, hidden_out_ref, query_out_ref = refs[2 + pieces : 7 + pieces]
+        held_ref, held_log_ref, narrow_ref = refs[:3]
         following = jnp.minimum(member + 1, members - 1)
-        after = other_ref[following, :16, :].astype(jnp.float32)[:1]
+        after = chosen_rows(others, per_plane, following, slice(0, 16))[:1]
         after = jnp.where(side == 0, latent_ref[count : count + 1, :], after)
         values = pltpu.roll(latent_ref[pl.ds(start, count), :], count - 1, 0)
         values = jnp.where(token == count - 1, after, values)
@@ -296,55 +353,65 @@
             edge = edge - terms[-1]
         rest = jnp.zeros((16 - 6, channels), jnp.float32)
         edge = jnp.concatenate(terms + [rest], axis=0).astype(jnp.bfloat16)
-        for i in range(members):
-            spread_ref[i, :count, :] = narrow
-            spread_ref[i, count:, :] = edge
-        store_queries(1, narrow, in_ref, attn_gain_ref, query_refs, hidden_out_ref, query_out_ref)
-
-
-def config(layer, count, features, pieces, members):
-    per_chunk = next(size for size in (8, 4, 2, 1) if members % size == 0)
+        narrow_ref[:count, :] = narrow
+        narrow_ref[count:, :] = edge
+
+
+def config(layer, count, features, pieces, planes, per_plane):
     return {
         "layer": layer,
         "last": layer == 1,
         "count": count,
         "features": features,
         "pieces": pieces,
-        "chunk": per_chunk * count,
+        "planes": planes,
+        "per_plane": per_plane,
     }
 
 
-def first_half(cfg, maps, queries, own):
+def attend_flops(kinds, piece, maps, queries):
+    return 2 * len(kinds) * piece.shape[0] * piece.shape[1] * (maps.size + 2 * queries.size)
+
+
+def held_pieces(kinds, piece):
+    return [pltpu.VMEM((len(kinds), *piece.shape), piece.dtype)] if len(kinds) > 4 else []
+
+
+def attend(cfg, maps, queries, pieces, sums=()):
     groups, rows, cols = queries.shape
+    kinds = tuple((step, other) for _, step, other in pieces)
     return on_chip(
-        functools.partial(first_half_kernel, cfg),
-        "first_half",
-        [maps, queries, own],
+        functools.partial(partial_kernel, cfg, kinds, len(sums) > 0),
+        "attend",
+        [maps, queries, *[piece for piece, _, _ in pieces], *sums],
         [((groups, rows, cols), jnp.float32), ((groups, rows, 128), jnp.float32)],
-        2 * own.shape[0] * cfg["count"] * (maps.size + 2 * queries.size),
-    )
-
-
-def second_half(cfg, maps, queries, other, sums, hidden, param_gain, latents, mix_pieces, param_pieces, extra):
+        attend_flops(kinds, pieces[0][0], maps, queries),
+        scratch=held_pieces(kinds, pieces[0][0]),
+    )
+
+
+def second_half(cfg, kinds, maps, queries, sums, hidden, param_gain, latents, others, mix_pieces, param_pieces, held=()):
     count, channels = cfg["count"], latents.shape[1]
-    operands = [maps, queries, other, *sums, hidden, param_gain, latents]
-    operands += [*mix_pieces, *param_pieces, *extra]
+    operands = [maps, queries, *sums, hidden, param_gain, latents]
+    operands += [*others, *mix_pieces, *param_pieces, *held]
     if cfg["last"]:
         results = [((count + 8, channels), jnp.float32)]
     else:
         results = [
             ((count, channels), jnp.float32),
             ((count, channels), jnp.float32),
-            ((other.shape[0], count + 16, channels), jnp.bfloat16),
-            *query_shapes(count, extra[0], extra[2:]),
+            ((count + 16, channels), jnp.bfloat16),
         ]
+    if cfg["last"]:
+        assert len(held) == 2
     return on_chip(
-        functools.partial(second_half_kernel, cfg),
+        functools.partial(second_half_kernel, cfg, kinds),
         "second_half",
         operands,
         results,
-        2 * other.shape[0] * count * (maps.size + 2 * queries.size),
-        scratch=[pltpu.VMEM((cfg["features"], param_pieces[0].shape[2]), jnp.bfloat16)],
+        attend_flops(kinds, others[0], maps, queries),
+        scratch=[pltpu.VMEM((cfg["features"], param_pieces[0].shape[2]), jnp.bfloat16)]
+        + held_pieces(kinds, others[0]),
     )
 
 
@@ -365,7 +432,6 @@
     rows, channels = latents.shape
     features = in_proj.shape[2]
     count = rows // 2
-    keys = members * count
 
     def swap(array):
         return lax.ppermute(array, "head", [(i, i ^ 1) for i in range(ways)])
@@ -378,38 +444,64 @@
             )
         return shares
 
-    def gather(spread):
-        return lax.all_to_all(spread, "seq", 0, 0)
-
-    (spread,) = on_chip(
-        spread_kernel,
-        "spread_rows",
-        [latents],
-        [((members, count, channels), jnp.bfloat16)],
-        keys * channels,
-    )
-    own = gather(spread)
+    planes = 4 if members % 4 == 0 else 1
+    per_plane = members // planes
+    bits = per_plane.bit_length() - 1
+
+    def gather(own, *made):
+        parts = [own] + [
+            lax.ppermute(own, "seq", [(i, i ^ (b * per_plane)) for i in range(members)])
+            for b in range(1, planes)
+        ]
+        (mine,) = on_chip(
+            functools.partial(arrange_kernel, planes),
+            "arrange",
+            parts + list(made),
+            [((planes, *own.shape), own.dtype)],
+            planes * own.size,
+        )
+        arrived = [mine]
+        for step in range(1, per_plane):
+            pairs = []
+            for i in range(members):
+                for w in range(ways):
+                    to = i ^ (turned(step, bits) if w % 2 else step)
+                    pairs.append((i * ways + w, to * ways + w))
+            arrived.append(lax.ppermute(mine, ("seq", "head"), pairs))
+        return arrived
+
+    def run(layer, own, maps, made, *rest):
+        cfg = config(layer, count, features, ways, planes, per_plane)
+        hidden, queries = made
+        mine = gather(own, maps, *made)
+        others = [swap(mine[0])]
+        sums = attend(cfg, maps, queries, [(mine[0], 0, False), (others[0], 0, True)])
+        if per_plane <= 4:
+            rows = gate_all(mine[1:], sums)
+            others += [swap(piece) for piece in rows]
+            batch = [(piece, step + 1, False) for step, piece in enumerate(rows)]
+            sums = attend(cfg, maps, queries, batch, sums)
+            kinds = tuple(range(1, per_plane))
+        else:
+            others += [swap(rows) for rows in mine[1:]]
+            batch = [(mine[step], step, False) for step in range(1, per_plane)]
+            sums = attend(cfg, maps, queries, batch, sums)
+            kinds = tuple(range(1, per_plane))
+        return second_half(
+            cfg, kinds, maps, queries, sums, hidden, param_gain, latents, others, mix_pieces, param_pieces, *rest
+        )
+
+    (own,) = on_chip(
+        narrow_kernel, "narrow", [latents], [((count, channels), jnp.bfloat16)], count * channels
+    )
     key_pieces, value_pieces = pieces_of(key_proj), pieces_of(value_proj)
     query_pieces, mix_pieces = pieces_of(query_proj), pieces_of(mix_proj)
     param_pieces = pieces_of(param_proj)
     maps = [combine(b, in_proj, attn_gain, key_pieces, value_pieces) for b in range(2)]
-    hidden, queries = make_queries(count, latents, in_proj, attn_gain, query_pieces)
-    own = gate(own, *maps, queries)
-
-    cfg = config(0, count, features, ways, members)
-    other = swap(own)
-    sums = first_half(cfg, maps[0], queries, own)
-    shared = (param_gain, latents, mix_pieces, param_pieces)
-    held, held_log, spread, hidden, queries = second_half(
-        cfg, maps[0], queries, other, sums, hidden, *shared, (in_proj, attn_gain, *query_pieces)
-    )
-    own = gather(spread)
-    cfg = config(1, count, features, ways, members)
-    other = swap(own)
-    sums = first_half(cfg, maps[1], queries, own)
-    (packed,) = second_half(
-        cfg, maps[1], queries, other, sums, hidden, *shared, (held, held_log)
-    )
+    made = make_queries(0, count, own, in_proj, attn_gain, query_pieces)
+    held, held_log, own = run(0, own, maps[0], made)
+    made = make_queries(1, count, own, in_proj, attn_gain, query_pieces)
+    (packed,) = run(1, own, maps[1], made, (held, held_log))
     final_latent, token_loglik = on_chip(
         finish_kernel,
         "finish",

time: 58.8 us -> 50.8 us (0.86)
  blocking collectives: 17.8 us -> 0 us
  starting transfers between devices: 10.4 us -> 21.7 us
  Pallas kernels: 16.3 us -> 13.1 us
  waiting for transfers between devices: 9.91 us -> 10.9 us
  local copies, waits for them, and re-layouts: 3.08 us -> 3.88 us
    ppermute x0 -> x12, starting transfers between devices: none -> 18.2 us  [the longest x6 11.1 us: gather(): lax.ppermute(own, 'seq', [(i, i ^ b * per_plane) for i in range(members)])]
    all_to_all x1 -> x0, blocking collectives: 17.8 us -> none  [gather(): return lax.all_to_all(spread, 'seq', 0, 0)]
    ppermute x0 -> x12, waiting for transfers between devices: none -> 9.8 us  [the longest x6 8.15 us: gather(): arrived.append(lax.ppermute(mine, ('seq', 'head'), pairs))]
    all_to_all x1 -> x0, waiting for transfers between devices: 9.01 us -> none  [gather(): return lax.all_to_all(spread, 'seq', 0, 0)]
    all_to_all x1 -> x0, starting transfers between devices: 8.12 us -> none  [gather(): return lax.all_to_all(spread, 'seq', 0, 0)]
    pallas_call x10 -> x16, Pallas kernels: 16.3 us -> 13.1 us  [on_chip(): pl.pallas_call(kernel, in_specs=[pl.BlockSpec(memory_space=pltpu.VMEM)] *...]
    ppermute x3 -> x9, starting transfers between devices: 0.64 us -> 1.94 us  [swap(): return lax.ppermute(array, 'head', [(i, i ^ 1) for i in range(ways)])]
    unnamed x32 -> x24, local copies, waits for them, and re-layouts: 3.08 us -> 3.88 us
  transfers between devices with their start and end apart: 9 -> 26, of which waited for: 2 -> 8; matrix products, arithmetic and copies ran while one was open for 0% -> 0% of each run, Pallas kernels for 12% -> 16%
where the time goes in v6:
time: 50.8 us; the launch traced here: 50.5 us
  starting transfers between devices  21.7 us (43%)
  Pallas kernels  13.1 us (26%)
  waiting for transfers between devices  10.9 us (21%)
  local copies, waits for them, and re-layouts  3.88 us (8%)
  between operations  0.92 us (2%)
    pallas_call x16, Pallas kernels, on_chip(): pl.pallas_call(kernel, in_specs=[pl.BlockSpec(memory_space=pltpu.VMEM)] *...  13.1 us
    ppermute x6, starting transfers between devices, gather(): lax.ppermute(own, 'seq', [(i, i ^ b * per_plane) for i in range(members)])  11.1 us
    ppermute x6, waiting for transfers between devices, gather(): arrived.append(lax.ppermute(mine, ('seq', 'head'), pairs))  8.15 us
    ppermute x6, starting transfers between devices, gather(): arrived.append(lax.ppermute(mine, ('seq', 'head'), pairs))  7.11 us
    unnamed x24, local copies, waits for them, and re-layouts  3.88 us
    ppermute x9, starting transfers between devices, swap(): return lax.ppermute(array, 'head', [(i, i ^ 1) for i in range(ways)])  1.94 us
    ppermute x6, waiting for transfers between devices, gather(): lax.ppermute(own, 'seq', [(i, i ^ b * per_plane) for i in range(members)])  1.65 us
    ppermute x5, starting transfers between devices, pieces_of(): lax.ppermute(array, 'head', [((i + j) % ways, i) for i in range(ways)])  1.54 us
  transfers between devices with their start and end apart: 26, of which 8 were waited for; matrix products, arithmetic and copies ran while one was open for 0% of the time, Pallas kernels for 16%

profile of v6, /device:TPU:0, one launch (start us, length us, event | category | flops | bytes accessed | tf_op | source)
XLA Modules:
  0.0 50.5 jit_solution(18401062605283403347)
XLA Ops:
  2.2 0.9 %copy-done.8 = f32[192,128]{1,0:T(8,128)S(1)} copy-done((f32[192,128]{1,0:T(8,128)S(1)}, f32[192,128]{1,0:T(8,128)}, u32[]{:S(2)}) %copy-start.8) | copy-done | bytes 98328
  3.3 5.0 %collective-permute-start.5 = (bf16[96,128]{1,0:T(8,128)(2,1)S(1)}, bf16[96,128]{1,0:T(8,128)(2,1)S(1)}, u32[]{:S(2)}, u32[]{:S(2)}) collective-permute-start(bf16[96,128]{1,0:T(8,128)(2,1)S(1)} %narrow.1.rows_ref.refs_0_), channel_id=1, source_target_pairs={{0,24},{2,26},{4,28},{6,30},{8,16},{10,18},{12,20},{14,22},{16,8},... | collective-permute-start | bytes 73736 | tf_op jit(solution)/shard_map/ppermute | solution.py:453
  8.4 1.6 %collective-permute-start.3 = (bf16[96,128]{1,0:T(8,128)(2,1)S(1)}, bf16[96,128]{1,0:T(8,128)(2,1)S(1)}, u32[]{:S(2)}, u32[]{:S(2)}) collective-permute-start(bf16[96,128]{1,0:T(8,128)(2,1)S(1)} %narrow.1.rows_ref.refs_0_), channel_id=1, source_target_pairs={{0,8},{2,10},{4,12},{6,14},{8,0},{10,2},{12,4},{14,6},{16,24},{18,... | collective-permute-start | bytes 73736 | tf_op jit(solution)/shard_map/ppermute | solution.py:453
  9.9 1.1 %copy-done = bf16[2,128,1536]{2,1,0:T(8,128)(2,1)S(1)} copy-done((bf16[2,128,1536]{2,1,0:T(8,128)(2,1)S(1)}, bf16[2,128,1536]{2,1,0:T(8,128)(2,1)}, u32[]{:S(2)}) %copy-start) | copy-done | bytes 786456
  11.1 1.1 %copy-done.4 = bf16[2,1536,128]{2,1,0:T(8,128)(2,1)S(1)} copy-done((bf16[2,1536,128]{2,1,0:T(8,128)(2,1)S(1)}, bf16[2,1536,128]{2,1,0:T(8,128)(2,1)}, u32[]{:S(2)}) %copy-start.4) | copy-done | bytes 786456
  12.2 0.7 %queries.2 = (f32[96,1536]{1,0:T(8,128)S(1)}, bf16[1,384,256]{2,1,0:T(8,128)(2,1)S(1)}) custom-call(bf16[96,128]{1,0:T(8,128)(2,1)S(1)} %narrow.1.rows_ref.refs_0_, bf16[2,128,1536]{2,1,0:T(8,128)(2,1)S(1)} %copy-done, f32[2,1536]{1,0:T(2,128)S(1)} %copy-done.10, bf16[2,1536,128]{2,1,0:T(8,128)(2,1)S(1)} %copy-done.4, ...), custom_call_target="tpu_custom_call" | custom-call | tf_op jit(solution)/shard_map/queries/pallas_call | solution.py:41
  13.6 0.8 %combine.3.refs_4_.maps_ref = bf16[768,256]{1,0:T(8,128)(2,1)S(1)} custom-call(bf16[2,128,1536]{2,1,0:T(8,128)(2,1)S(1)} %copy-done, f32[2,1536]{1,0:T(2,128)S(1)} %copy-done.10, bf16[2,1536,128]{2,1,0:T(8,128)(2,1)S(1)} %copy-done.2, bf16[2,1536,128]{2,1,0:T(8,128)(2,1)S(1)} %collective-permute-done.refs_1_, bf16[2,1536,128]{2,1,0:T(8,128)(2,1)S(1)} %copy-done.3, ...), custom_call_target="tpu_custom_call" | custom-call | tf_op jit(solution)/shard_map/combine/pallas_call | solution.py:41
  14.5 2.5 %collective-permute-start.8 = (bf16[4,96,128]{2,1,0:T(8,128)(2,1)S(1)}, bf16[4,96,128]{2,1,0:T(8,128)(2,1)S(1)}, u32[]{:S(2)}, u32[]{:S(2)}) collective-permute-start(bf16[4,96,128]{2,1,0:T(8,128)(2,1)S(1)} %arrange.2.refs_0_), channel_id=1, source_target_pairs={{0,6},{1,7},{2,4},{3,5},{4,2},{5,3},{6,0},{7,1},{8,14},{9,15},{10,... | collective-permute-start | bytes 294920 | tf_op jit(solution)/shard_map/ppermute | solution.py:470
  18.1 1.0 %attend.4 = (f32[1,384,256]{2,1,0:T(8,128)S(1)}, f32[1,384,128]{2,1,0:T(8,128)S(1)}) custom-call(bf16[768,256]{1,0:T(8,128)(2,1)S(1)} %combine.3.refs_4_.maps_ref, bf16[1,384,256]{2,1,0:T(8,128)(2,1)S(1)} %get-tuple-element.25.refs_6_.query_ref, bf16[4,96,128]{2,1,0:T(8,128)(2,1)S(1)} %arrange.2.refs_0_, ...), custom_call_target="tpu_custom_call" | custom-call | tf_op jit(solution)/shard_map/attend/pallas_call | solution.py:41
  19.0 2.0 %collective-permute-done.8.refs_2_ = bf16[4,96,128]{2,1,0:T(8,128)(2,1)S(1)} collective-permute-done((bf16[4,96,128]{2,1,0:T(8,128)(2,1)S(1)}, bf16[4,96,128]{2,1,0:T(8,128)(2,1)S(1)}, u32[]{:S(2)}, u32[]{:S(2)}) %collective-permute-start.8) | collective-permute-done | bytes 98336 | tf_op jit(solution)/shard_map/ppermute | solution.py:470
  21.1 1.7 %collective-permute-done.7.refs_1_ = bf16[4,96,128]{2,1,0:T(8,128)(2,1)S(1)} collective-permute-done((bf16[4,96,128]{2,1,0:T(8,128)(2,1)S(1)}, bf16[4,96,128]{2,1,0:T(8,128)(2,1)S(1)}, u32[]{:S(2)}, u32[]{:S(2)}) %collective-permute-start.7) | collective-permute-done | bytes 98336 | tf_op jit(solution)/shard_map/ppermute | solution.py:470
  23.5 1.5 %attend.5 = (f32[1,384,256]{2,1,0:T(8,128)S(1)}, f32[1,384,128]{2,1,0:T(8,128)S(1)}) custom-call(bf16[768,256]{1,0:T(8,128)(2,1)S(1)} %combine.3.refs_4_.maps_ref, bf16[1,384,256]{2,1,0:T(8,128)(2,1)S(1)} %get-tuple-element.25.refs_6_.query_ref, bf16[4,96,128]{2,1,0:T(8,128)(2,1)S(1)} %get-tuple-element.29.refs_0_, ...), custom_call_target="tpu_custom_call" | custom-call | tf_op jit(solution)/shard_map/attend/pallas_call | solution.py:41
  25.1 2.2 %second_half.2 = (f32[96,128]{1,0:T(8,128)S(1)}, f32[96,128]{1,0:T(8,128)S(1)}, bf16[112,128]{1,0:T(8,128)(2,1)S(1)}) custom-call(bf16[768,256]{1,0:T(8,128)(2,1)S(1)} %combine.3.refs_4_.maps_ref, bf16[1,384,256]{2,1,0:T(8,128)(2,1)S(1)} %get-tuple-element.25.refs_6_.query_ref, f32[1,384,256]{2,1,0:T(8,128)S(1)} %get-tuple-element.32.number_ref, ...), custom_call_target="tpu_custom_call" | custom-call | tf_op jit(solution)/shard_map/second_half/pallas_call | solution.py:41
  27.3 2.8 %collective-permute-start.17 = (bf16[112,128]{1,0:T(8,128)(2,1)S(1)}, bf16[112,128]{1,0:T(8,128)(2,1)S(1)}, u32[]{:S(2)}, u32[]{:S(2)}) collective-permute-start(bf16[112,128]{1,0:T(8,128)(2,1)S(1)} %get-tuple-element.34.rows_ref.refs_0_), channel_id=1, source_target_pairs={{0,24},{2,26},{4,28},{6,30},{8,16},{10,18},{12,20},{14,22},{16,8},... | collective-permute-start | bytes 86024 | tf_op jit(solution)/shard_map/ppermute | solution.py:453
  30.1 1.7 %collective-permute-start.15 = (bf16[112,128]{1,0:T(8,128)(2,1)S(1)}, bf16[112,128]{1,0:T(8,128)(2,1)S(1)}, u32[]{:S(2)}, u32[]{:S(2)}) collective-permute-start(bf16[112,128]{1,0:T(8,128)(2,1)S(1)} %get-tuple-element.34.rows_ref.refs_0_), channel_id=1, source_target_pairs={{0,8},{2,10},{4,12},{6,14},{8,0},{10,2},{12,4},{14,6},{16,24},{18,... | collective-permute-start | bytes 86024 | tf_op jit(solution)/shard_map/ppermute | solution.py:453
  31.8 0.8 %combine.2.refs_4_.maps_ref = bf16[768,256]{1,0:T(8,128)(2,1)S(1)} custom-call(bf16[2,128,1536]{2,1,0:T(8,128)(2,1)S(1)} %copy-done.1, f32[2,1536]{1,0:T(2,128)S(1)} %copy-done.10, bf16[2,1536,128]{2,1,0:T(8,128)(2,1)S(1)} %copy-done.2, bf16[2,1536,128]{2,1,0:T(8,128)(2,1)S(1)} %collective-permute-done.refs_1_, bf16[2,1536,128]{2,1,0:T(8,128)(2,1)S(1)} %copy-done.3, ...), custom_call_target="tpu_custom_call" | custom-call | tf_op jit(solution)/shard_map/combine/pallas_call | solution.py:41
  33.3 1.6 %collective-permute-done.16.refs_2_ = bf16[112,128]{1,0:T(8,128)(2,1)S(1)} collective-permute-done((bf16[112,128]{1,0:T(8,128)(2,1)S(1)}, bf16[112,128]{1,0:T(8,128)(2,1)S(1)}, u32[]{:S(2)}, u32[]{:S(2)}) %collective-permute-start.16) | collective-permute-done | bytes 28704 | tf_op jit(solution)/shard_map/ppermute | solution.py:453
  35.0 2.5 %collective-permute-start.20 = (bf16[4,112,128]{2,1,0:T(8,128)(2,1)S(1)}, bf16[4,112,128]{2,1,0:T(8,128)(2,1)S(1)}, u32[]{:S(2)}, u32[]{:S(2)}) collective-permute-start(bf16[4,112,128]{2,1,0:T(8,128)(2,1)S(1)} %arrange.3.refs_0_), channel_id=1, source_target_pairs={{0,6},{1,7},{2,4},{3,5},{4,2},{5,3},{6,0},{7,1},{8,14},{9,15},{10,... | collective-permute-start | bytes 344072 | tf_op jit(solution)/shard_map/ppermute | solution.py:470
  38.5 1.0 %attend.6 = (f32[1,384,256]{2,1,0:T(8,128)S(1)}, f32[1,384,128]{2,1,0:T(8,128)S(1)}) custom-call(bf16[768,256]{1,0:T(8,128)(2,1)S(1)} %combine.2.refs_4_.maps_ref, bf16[1,384,256]{2,1,0:T(8,128)(2,1)S(1)} %get-tuple-element.35.refs_6_.query_ref, bf16[4,112,128]{2,1,0:T(8,128)(2,1)S(1)} %arrange.3.refs_0_, ...), custom_call_target="tpu_custom_call" | custom-call | tf_op jit(solution)/shard_map/attend/pallas_call | solution.py:41
  39.5 2.4 %collective-permute-done.20.refs_2_ = bf16[4,112,128]{2,1,0:T(8,128)(2,1)S(1)} collective-permute-done((bf16[4,112,128]{2,1,0:T(8,128)(2,1)S(1)}, bf16[4,112,128]{2,1,0:T(8,128)(2,1)S(1)}, u32[]{:S(2)}, u32[]{:S(2)}) %collective-permute-start.20) | collective-permute-done | bytes 114720 | tf_op jit(solution)/shard_map/ppermute | solution.py:470
  41.9 2.0 %collective-permute-done.19.refs_1_ = bf16[4,112,128]{2,1,0:T(8,128)(2,1)S(1)} collective-permute-done((bf16[4,112,128]{2,1,0:T(8,128)(2,1)S(1)}, bf16[4,112,128]{2,1,0:T(8,128)(2,1)S(1)}, u32[]{:S(2)}, u32[]{:S(2)}) %collective-permute-start.19) | collective-permute-done | bytes 114720 | tf_op jit(solution)/shard_map/ppermute | solution.py:470
  44.6 1.5 %attend.7 = (f32[1,384,256]{2,1,0:T(8,128)S(1)}, f32[1,384,128]{2,1,0:T(8,128)S(1)}) custom-call(bf16[768,256]{1,0:T(8,128)(2,1)S(1)} %combine.2.refs_4_.maps_ref, bf16[1,384,256]{2,1,0:T(8,128)(2,1)S(1)} %get-tuple-element.35.refs_6_.query_ref, bf16[4,112,128]{2,1,0:T(8,128)(2,1)S(1)} %get-tuple-element.39.refs_0_, ...), custom_call_target="tpu_custom_call" | custom-call | tf_op jit(solution)/shard_map/attend/pallas_call | solution.py:41
  46.1 2.3 %second_half.3.own_ref = f32[104,128]{1,0:T(8,128)S(1)} custom-call(bf16[768,256]{1,0:T(8,128)(2,1)S(1)} %combine.2.refs_4_.maps_ref, bf16[1,384,256]{2,1,0:T(8,128)(2,1)S(1)} %get-tuple-element.35.refs_6_.query_ref, f32[1,384,256]{2,1,0:T(8,128)S(1)} %get-tuple-element.42.number_ref, f32[1,384,128]{2,1,0:T(8,128)S(1)} %get-tuple-element.43.total_ref, ...), custom_call_target="tpu_custom_call" | custom-call | tf_op jit(solution)/shard_map/second_half/pallas_call | solution.py:41
  49.0 0.9 %collective-permute-done.25.other_ref = f32[104,128]{1,0:T(8,128)S(1)} collective-permute-done((f32[104,128]{1,0:T(8,128)S(1)}, f32[104,128]{1,0:T(8,128)S(1)}, u32[]{:S(2)}, u32[]{:S(2)}) %collective-permute-start.25) | collective-permute-done | bytes 53280 | tf_op jit(solution)/shard_map/ppermute | solution.py:437
  (68 shorter events, 8.2 us)
Async XLA Ops:
  0.6 2.6 %collective-permute-start.2 = (bf16[2,1536,128]{2,1,0:T(8,128)(2,1)}, bf16[2,1536,128]{2,1,0:T(8,128)(2,1)S(1)}, u32[]{:S(2)}, u32[]{:S(2)}) collective-permute-start(bf16[2,1536,128]{2,1,0:T(8,128)(2,1)} %refs_0_.7), channel_id=1, source_target_pairs={{1,0},{0,1},{3,2},{2,3},{5,4},{4,5},{7,6},{6,7},{9,8},{8,9},{11,10... | collective-permute-start | bytes 2359304 | tf_op jit(solution)/shard_map/ppermute | solution.py:443
  1.1 7.1 %collective-permute-start = (bf16[2,1536,128]{2,1,0:T(8,128)(2,1)}, bf16[2,1536,128]{2,1,0:T(8,128)(2,1)S(1)}, u32[]{:S(2)}, u32[]{:S(2)}) collective-permute-start(bf16[2,1536,128]{2,1,0:T(8,128)(2,1)} %refs_0_.5), channel_id=1, source_target_pairs={{1,0},{0,1},{3,2},{2,3},{5,4},{4,5},{7,6},{6,7},{9,8},{8,9},{11,10... | collective-permute-start | bytes 2359304 | tf_op jit(solution)/shard_map/ppermute | solution.py:443
  1.2 7.1 %collective-permute-start.1 = (bf16[2,1536,128]{2,1,0:T(8,128)(2,1)}, bf16[2,1536,128]{2,1,0:T(8,128)(2,1)S(1)}, u32[]{:S(2)}, u32[]{:S(2)}) collective-permute-start(bf16[2,1536,128]{2,1,0:T(8,128)(2,1)} %refs_2_.3), channel_id=1, source_target_pairs={{1,0},{0,1},{3,2},{2,3},{5,4},{4,5},{7,6},{6,7},{9,8},{8,9},{11,10... | collective-permute-start | bytes 2359304 | tf_op jit(solution)/shard_map/ppermute | solution.py:443
  1.7 23.3 %collective-permute-start.13 = (bf16[2,128,1536]{2,1,0:T(8,128)(2,1)}, bf16[2,128,1536]{2,1,0:T(8,128)(2,1)S(1)}, u32[]{:S(2)}, u32[]{:S(2)}) collective-permute-start(bf16[2,128,1536]{2,1,0:T(8,128)(2,1)} %refs_4_.3), channel_id=1, source_target_pairs={{1,0},{0,1},{3,2},{2,3},{5,4},{4,5},{7,6},{6,7},{9,8},{8,9},{11,10... | collective-permute-start | bytes 2359304 | tf_op jit(solution)/shard_map/ppermute | solution.py:443
  1.7 23.3 %collective-permute-start.14 = (bf16[2,768,256]{2,1,0:T(8,128)(2,1)}, bf16[2,768,256]{2,1,0:T(8,128)(2,1)S(1)}, u32[]{:S(2)}, u32[]{:S(2)}) collective-permute-start(bf16[2,768,256]{2,1,0:T(8,128)(2,1)} %refs_6_.3), channel_id=1, source_target_pairs={{1,0},{0,1},{3,2},{2,3},{5,4},{4,5},{7,6},{6,7},{9,8},{8,9},{11,10... | collective-permute-start | bytes 2359304 | tf_op jit(solution)/shard_map/ppermute | solution.py:443
  3.3 11.1 %collective-permute-start.5 = (bf16[96,128]{1,0:T(8,128)(2,1)S(1)}, bf16[96,128]{1,0:T(8,128)(2,1)S(1)}, u32[]{:S(2)}, u32[]{:S(2)}) collective-permute-start(bf16[96,128]{1,0:T(8,128)(2,1)S(1)} %narrow.1.rows_ref.refs_0_), channel_id=1, source_target_pairs={{0,24},{2,26},{4,28},{6,30},{8,16},{10,18},{12,20},{14,22},{16,8},... | collective-permute-start | bytes 73736 | tf_op jit(solution)/shard_map/ppermute | solution.py:453
  8.2 6.1 %collective-permute-start.4 = (bf16[96,128]{1,0:T(8,128)(2,1)S(1)}, bf16[96,128]{1,0:T(8,128)(2,1)S(1)}, u32[]{:S(2)}, u32[]{:S(2)}) collective-permute-start(bf16[96,128]{1,0:T(8,128)(2,1)S(1)} %narrow.1.rows_ref.refs_0_), channel_id=1, source_target_pairs={{0,16},{2,18},{4,20},{6,22},{8,24},{10,26},{12,28},{14,30},{16,0},... | collective-permute-start | bytes 73736 | tf_op jit(solution)/shard_map/ppermute | solution.py:453
  8.4 6.0 %collective-permute-start.3 = (bf16[96,128]{1,0:T(8,128)(2,1)S(1)}, bf16[96,128]{1,0:T(8,128)(2,1)S(1)}, u32[]{:S(2)}, u32[]{:S(2)}) collective-permute-start(bf16[96,128]{1,0:T(8,128)(2,1)S(1)} %narrow.1.rows_ref.refs_0_), channel_id=1, source_target_pairs={{0,8},{2,10},{4,12},{6,14},{8,0},{10,2},{12,4},{14,6},{16,24},{18,... | collective-permute-start | bytes 73736 | tf_op jit(solution)/shard_map/ppermute | solution.py:453
  14.4 3.1 %collective-permute-start.9 = (bf16[4,96,128]{2,1,0:T(8,128)(2,1)S(1)}, bf16[4,96,128]{2,1,0:T(8,128)(2,1)S(1)}, u32[]{:S(2)}, u32[]{:S(2)}) collective-permute-start(bf16[4,96,128]{2,1,0:T(8,128)(2,1)S(1)} %arrange.2.refs_0_), channel_id=1, source_target_pairs={{0,1},{1,0},{2,3},{3,2},{4,5},{5,4},{6,7},{7,6},{8,9},{9,8},{10,11... | collective-permute-start | bytes 294920 | tf_op jit(solution)/shard_map/ppermute | solution.py:437
  14.5 6.6 %collective-permute-start.8 = (bf16[4,96,128]{2,1,0:T(8,128)(2,1)S(1)}, bf16[4,96,128]{2,1,0:T(8,128)(2,1)S(1)}, u32[]{:S(2)}, u32[]{:S(2)}) collective-permute-start(bf16[4,96,128]{2,1,0:T(8,128)(2,1)S(1)} %arrange.2.refs_0_), channel_id=1, source_target_pairs={{0,6},{1,7},{2,4},{3,5},{4,2},{5,3},{6,0},{7,1},{8,14},{9,15},{10,... | collective-permute-start | bytes 294920 | tf_op jit(solution)/shard_map/ppermute | solution.py:470
  17.0 5.7 %collective-permute-start.7 = (bf16[4,96,128]{2,1,0:T(8,128)(2,1)S(1)}, bf16[4,96,128]{2,1,0:T(8,128)(2,1)S(1)}, u32[]{:S(2)}, u32[]{:S(2)}) collective-permute-start(bf16[4,96,128]{2,1,0:T(8,128)(2,1)S(1)} %arrange.2.refs_0_), channel_id=1, source_target_pairs={{0,4},{1,3},{2,6},{3,1},{4,0},{5,7},{6,2},{7,5},{8,12},{9,11},{10,... | collective-permute-start | bytes 294920 | tf_op jit(solution)/shard_map/ppermute | solution.py:470
  17.5 5.2 %collective-permute-start.6 = (bf16[4,96,128]{2,1,0:T(8,128)(2,1)S(1)}, bf16[4,96,128]{2,1,0:T(8,128)(2,1)S(1)}, u32[]{:S(2)}, u32[]{:S(2)}) collective-permute-start(bf16[4,96,128]{2,1,0:T(8,128)(2,1)S(1)} %arrange.2.refs_0_), channel_id=1, source_target_pairs={{0,2},{1,5},{2,0},{3,7},{4,6},{5,1},{6,4},{7,3},{8,10},{9,13},{10,... | collective-permute-start | bytes 294920 | tf_op jit(solution)/shard_map/ppermute | solution.py:470
  22.8 2.2 %collective-permute-start.10 = (bf16[4,96,128]{2,1,0:T(8,128)(2,1)S(1)}, bf16[4,96,128]{2,1,0:T(8,128)(2,1)S(1)}, u32[]{:S(2)}, u32[]{:S(2)}) collective-permute-start(bf16[4,96,128]{2,1,0:T(8,128)(2,1)S(1)} %get-tuple-element.29.refs_0_), channel_id=1, source_target_pairs={{0,1},{1,0},{2,3},{3,2},{4,5},{5,4},{6,7},{7,6},{8,9},{9,8},{10,11... | collective-permute-start | bytes 294920 | tf_op jit(solution)/shard_map/ppermute | solution.py:437
  22.9 2.1 %collective-permute-start.11 = (bf16[4,96,128]{2,1,0:T(8,128)(2,1)S(1)}, bf16[4,96,128]{2,1,0:T(8,128)(2,1)S(1)}, u32[]{:S(2)}, u32[]{:S(2)}) collective-permute-start(bf16[4,96,128]{2,1,0:T(8,128)(2,1)S(1)} %get-tuple-element.30.refs_1_), channel_id=1, source_target_pairs={{0,1},{1,0},{2,3},{3,2},{4,5},{5,4},{6,7},{7,6},{8,9},{9,8},{10,11... | collective-permute-start | bytes 294920 | tf_op jit(solution)/shard_map/ppermute | solution.py:437
  23.4 1.6 %collective-permute-start.12 = (bf16[4,96,128]{2,1,0:T(8,128)(2,1)S(1)}, bf16[4,96,128]{2,1,0:T(8,128)(2,1)S(1)}, u32[]{:S(2)}, u32[]{:S(2)}) collective-permute-start(bf16[4,96,128]{2,1,0:T(8,128)(2,1)S(1)} %get-tuple-element.31.refs_2_), channel_id=1, source_target_pairs={{0,1},{1,0},{2,3},{3,2},{4,5},{5,4},{6,7},{7,6},{8,9},{9,8},{10,11... | collective-permute-start | bytes 294920 | tf_op jit(solution)/shard_map/ppermute | solution.py:437
  27.3 5.9 %collective-permute-start.17 = (bf16[112,128]{1,0:T(8,128)(2,1)S(1)}, bf16[112,128]{1,0:T(8,128)(2,1)S(1)}, u32[]{:S(2)}, u32[]{:S(2)}) collective-permute-start(bf16[112,128]{1,0:T(8,128)(2,1)S(1)} %get-tuple-element.34.rows_ref.refs_0_), channel_id=1, source_target_pairs={{0,24},{2,26},{4,28},{6,30},{8,16},{10,18},{12,20},{14,22},{16,8},... | collective-permute-start | bytes 86024 | tf_op jit(solution)/shard_map/ppermute | solution.py:453
  30.1 4.8 %collective-permute-start.16 = (bf16[112,128]{1,0:T(8,128)(2,1)S(1)}, bf16[112,128]{1,0:T(8,128)(2,1)S(1)}, u32[]{:S(2)}, u32[]{:S(2)}) collective-permute-start(bf16[112,128]{1,0:T(8,128)(2,1)S(1)} %get-tuple-element.34.rows_ref.refs_0_), channel_id=1, source_target_pairs={{0,16},{2,18},{4,20},{6,22},{8,24},{10,26},{12,28},{14,30},{16,0},... | collective-permute-start | bytes 86024 | tf_op jit(solution)/shard_map/ppermute | solution.py:453
  30.1 4.8 %collective-permute-start.15 = (bf16[112,128]{1,0:T(8,128)(2,1)S(1)}, bf16[112,128]{1,0:T(8,128)(2,1)S(1)}, u32[]{:S(2)}, u32[]{:S(2)}) collective-permute-start(bf16[112,128]{1,0:T(8,128)(2,1)S(1)} %get-tuple-element.34.rows_ref.refs_0_), channel_id=1, source_target_pairs={{0,8},{2,10},{4,12},{6,14},{8,0},{10,2},{12,4},{14,6},{16,24},{18,... | collective-permute-start | bytes 86024 | tf_op jit(solution)/shard_map/ppermute | solution.py:453
  34.9 3.6 %collective-permute-start.21 = (bf16[4,112,128]{2,1,0:T(8,128)(2,1)S(1)}, bf16[4,112,128]{2,1,0:T(8,128)(2,1)S(1)}, u32[]{:S(2)}, u32[]{:S(2)}) collective-permute-start(bf16[4,112,128]{2,1,0:T(8,128)(2,1)S(1)} %arrange.3.refs_0_), channel_id=1, source_target_pairs={{0,1},{1,0},{2,3},{3,2},{4,5},{5,4},{6,7},{7,6},{8,9},{9,8},{10,11... | collective-permute-start | bytes 344072 | tf_op jit(solution)/shard_map/ppermute | solution.py:437
  35.0 6.9 %collective-permute-start.20 = (bf16[4,112,128]{2,1,0:T(8,128)(2,1)S(1)}, bf16[4,112,128]{2,1,0:T(8,128)(2,1)S(1)}, u32[]{:S(2)}, u32[]{:S(2)}) collective-permute-start(bf16[4,112,128]{2,1,0:T(8,128)(2,1)S(1)} %arrange.3.refs_0_), channel_id=1, source_target_pairs={{0,6},{1,7},{2,4},{3,5},{4,2},{5,3},{6,0},{7,1},{8,14},{9,15},{10,... | collective-permute-start | bytes 344072 | tf_op jit(solution)/shard_map/ppermute | solution.py:470
  37.4 6.5 %collective-permute-start.19 = (bf16[4,112,128]{2,1,0:T(8,128)(2,1)S(1)}, bf16[4,112,128]{2,1,0:T(8,128)(2,1)S(1)}, u32[]{:S(2)}, u32[]{:S(2)}) collective-permute-start(bf16[4,112,128]{2,1,0:T(8,128)(2,1)S(1)} %arrange.3.refs_0_), channel_id=1, source_target_pairs={{0,4},{1,3},{2,6},{3,1},{4,0},{5,7},{6,2},{7,5},{8,12},{9,11},{10,... | collective-permute-start | bytes 344072 | tf_op jit(solution)/shard_map/ppermute | solution.py:470
  38.0 5.9 %collective-permute-start.18 = (bf16[4,112,128]{2,1,0:T(8,128)(2,1)S(1)}, bf16[4,112,128]{2,1,0:T(8,128)(2,1)S(1)}, u32[]{:S(2)}, u32[]{:S(2)}) collective-permute-start(bf16[4,112,128]{2,1,0:T(8,128)(2,1)S(1)} %arrange.3.refs_0_), channel_id=1, source_target_pairs={{0,2},{1,5},{2,0},{3,7},{4,6},{5,1},{6,4},{7,3},{8,10},{9,13},{10,... | collective-permute-start | bytes 344072 | tf_op jit(solution)/shard_map/ppermute | solution.py:470
  43.9 2.2 %collective-permute-start.22 = (bf16[4,112,128]{2,1,0:T(8,128)(2,1)S(1)}, bf16[4,112,128]{2,1,0:T(8,128)(2,1)S(1)}, u32[]{:S(2)}, u32[]{:S(2)}) collective-permute-start(bf16[4,112,128]{2,1,0:T(8,128)(2,1)S(1)} %get-tuple-element.39.refs_0_), channel_id=1, source_target_pairs={{0,1},{1,0},{2,3},{3,2},{4,5},{5,4},{6,7},{7,6},{8,9},{9,8},{10,11... | collective-permute-start | bytes 344072 | tf_op jit(solution)/shard_map/ppermute | solution.py:437
  44.1 2.1 %collective-permute-start.23 = (bf16[4,112,128]{2,1,0:T(8,128)(2,1)S(1)}, bf16[4,112,128]{2,1,0:T(8,128)(2,1)S(1)}, u32[]{:S(2)}, u32[]{:S(2)}) collective-permute-start(bf16[4,112,128]{2,1,0:T(8,128)(2,1)S(1)} %get-tuple-element.40.refs_1_), channel_id=1, source_target_pairs={{0,1},{1,0},{2,3},{3,2},{4,5},{5,4},{6,7},{7,6},{8,9},{9,8},{10,11... | collective-permute-start | bytes 344072 | tf_op jit(solution)/shard_map/ppermute | solution.py:437
  (14 other events, 35.3 us)

commit v7 on v0

v7 whole, which is shorter than its diff:
```python
import functools
import math

import jax
import jax.numpy as jnp
from jax import lax
from jax.experimental import pallas as pl
from jax.experimental.pallas import tpu as pltpu
from jax.sharding import PartitionSpec as P

HS = 64

score_scale = 8.0
epsilon = 1e-06

VMEM_LIMIT = 32 * 1024 * 1024


def dot(a, b):
    return jnp.dot(a, b, preferred_element_type=jnp.float32)


def dot_nt(a, b):
    return lax.dot_general(a, b, (((1,), (1,)), ((), ())), preferred_element_type=jnp.float32)


def cat(parts, axis):
    return parts[0] if len(parts) == 1 else jnp.concatenate(parts, axis=axis)


def side_of():
    return lax.rem(lax.axis_index("head"), 2)


def on_chip(kernel, name, operands, results, far=(), scratch=(), out_memory=pltpu.VMEM):
    near = [pltpu.with_memory_space_constraint(array, pltpu.VMEM) for array in operands]
    far = [pltpu.with_memory_space_constraint(array, pltpu.HBM) for array in far]
    if out_memory is pltpu.VMEM:
        out_shape = tuple(pltpu.VMEM(shape, dtype) for shape, dtype in results)
    else:
        out_shape = tuple(jax.ShapeDtypeStruct(shape, dtype) for shape, dtype in results)
    return pl.pallas_call(
        kernel,
        in_specs=[pl.BlockSpec(memory_space=pltpu.VMEM)] * len(near)
        + [pl.BlockSpec(memory_space=pl.ANY)] * len(far),
        out_specs=tuple(pl.BlockSpec(memory_space=pltpu.VMEM) for _ in results),
        out_shape=out_shape,
        scratch_shapes=list(scratch),
        compiler_params=pltpu.CompilerParams(vmem_limit_bytes=VMEM_LIMIT),
        name=name,
    )(*near, *far)


def fetch(sources, targets, sems):
    copies = []
    for at, (source, target) in enumerate(zip(sources, targets)):
        copies.append(pltpu.make_async_copy(source, target, sems.at[at]))
        copies[-1].start()
    return copies


def half_kernel(rows_ref, own_ref, sems):
    count = own_ref.shape[0]
    half = rows_ref.at[pl.ds(pl.multiple_of(side_of() * count, 8), count)]
    for copy in fetch([half], [own_ref], sems):
        copy.wait()


def arrange_kernel(planes, *refs):
    place = lax.axis_index("seq") // (lax.axis_size("seq") // planes)
    for step in range(planes):
        rows = refs[step][...]
        refs[-2][place ^ step] = rows
        refs[-1][place ^ step] = rows.astype(jnp.bfloat16)


def gates_kernel(many, *refs):
    for source, target in zip(refs[:many], refs[-many:]):
        target[...] = source[...]


def gate_all(rows, made):
    results = [(piece.shape, piece.dtype) for piece in rows]
    return on_chip(functools.partial(gates_kernel, len(rows)), "gate", [*rows, *made], results)


def turned(step, bits):
    return sum(((step >> b) & 1) << (bits - 1 - b) for b in range(bits))


def chip_of(step, per_plane, other):
    bits = per_plane.bit_length() - 1
    first = side_of() == (1 if other else 0)
    return (lax.axis_index("seq") % per_plane) ^ jnp.where(first, step, turned(step, bits))


def prepare_kernel(pieces, in_src, gain_src, *refs):
    sources, refs = refs[: 3 * pieces], refs[3 * pieces :]
    maps_refs, (in_ref, gain_ref, query_ref, buffer, sems) = refs[:-5], refs[-5:]
    layers, channels, _ = in_ref.shape
    targets = [in_ref, gain_ref] + [buffer.at[at] for at in range(2 * pieces)]
    targets += [query_ref.at[at] for at in range(pieces)]
    copies = fetch([in_src, gain_src, *sources], targets, sems)
    for copy in copies[: 2 + 2 * pieces]:
        copy.wait()
    eye = lax.broadcasted_iota(jnp.int32, (channels, channels), 0) == lax.broadcasted_iota(
        jnp.int32, (channels, channels), 1
    )
    for layer in range(layers):
        out_ref = maps_refs[layer]

        def store(row, value, out_ref=out_ref):
            high = value.astype(jnp.bfloat16)
            rows = value.shape[0]
            out_ref[row : row + rows, :channels] = high
            out_ref[row : row + rows, channels:] = (value - high.astype(jnp.float32)).astype(
                jnp.bfloat16
            )
            return row + rows

        base = in_ref[layer]
        scaled = base.astype(jnp.float32) * gain_ref[layer : layer + 1, :]
        high = scaled.astype(jnp.bfloat16)
        low = (scaled - high.astype(jnp.float32)).astype(jnp.bfloat16)
        both = jnp.concatenate([high, low], axis=0)
        row = 0
        for first in range(0, 2 * pieces, 2):
            pair = cat([buffer[first, layer], buffer[first + 1, layer]], 1)
            product = dot(both, pair)
            row = store(row, (product[:channels] + product[channels:]).T)
        row = store(row, dot_nt(base, base))
        store(row, jnp.where(eye, 1.0, 0.0))
    for copy in copies[2 + 2 * pieces :]:
        copy.wait()


def prepare(in_proj, attn_gain, key_pieces, value_pieces, query_pieces):
    pieces = len(key_pieces)
    layers, channels, features = in_proj.shape
    columns = key_pieces[0].shape[2]
    rows = 2 * pieces * columns + 2 * channels
    *maps, in_all, gains, query_all = on_chip(
        functools.partial(prepare_kernel, pieces),
        "prepare",
        [],
        [((rows, 2 * channels), jnp.bfloat16)] * layers
        + [
            (in_proj.shape, in_proj.dtype),
            (attn_gain.shape, attn_gain.dtype),
            ((pieces, *query_pieces[0].shape), jnp.bfloat16),
        ],
        far=[in_proj, attn_gain, *key_pieces, *value_pieces, *query_pieces],
        scratch=[
            pltpu.VMEM((2 * pieces, layers, features, columns), jnp.bfloat16),
            pltpu.SemaphoreType.DMA((3 * pieces + 2,)),
        ],
    )
    return maps, (in_all, gains, query_all)


def queries_kernel(layer, planes, rows_ref, in_ref, gain_ref, query_ref, hidden_ref, out_ref):
    if planes == rows_ref.shape[0]:
        rows = rows_ref[...]
    else:
        count = hidden_ref.shape[0]
        place = lax.axis_index("seq") // (lax.axis_size("seq") // rows_ref.shape[0])
        rows = rows_ref[place, :count, :]
    rows = rows.reshape(hidden_ref.shape[0], rows_ref.shape[2])
    count = rows.shape[0] // planes
    hidden = dot(rows, in_ref[layer])
    hidden_ref[...] = hidden
    spread = lax.rsqrt(jnp.mean(hidden * hidden, axis=1, keepdims=True) + epsilon)
    normed = (hidden * spread * gain_ref[layer : layer + 1, :]).astype(jnp.bfloat16)
    for first in range(0, query_ref.shape[0], 2):
        query = dot(normed, cat([query_ref[at, layer] for at in range(first, first + 2)], 1))
        width = query.shape[1]
        heads = width // HS
        head = lax.broadcasted_iota(jnp.int32, (1, width), 1) // HS
        same = head == lax.broadcasted_iota(jnp.int32, (width, 1), 0) // HS
        same = jnp.where(same, 1.0, 0.0).astype(jnp.bfloat16)
        square = query * query
        high = square.astype(jnp.bfloat16)
        low = (square - high.astype(jnp.float32)).astype(jnp.bfloat16)
        mean = (dot(high, same) + dot(low, same)) * (1.0 / HS)
        query = query * lax.rsqrt(mean + epsilon)
        for h in range(heads):
            band = jnp.where(head == h, query, 0.0).astype(jnp.bfloat16)
            for p in range(planes):
                row = (p * heads + h) * count
                out_ref[first // 2, row : row + count, :] = band[p * count : (p + 1) * count]


def make_queries(layer, planes, count, rows, weights):
    in_all, _, query_all = weights
    width = 2 * query_all.shape[3]
    return on_chip(
        functools.partial(queries_kernel, layer, planes),
        "queries",
        [rows, *weights],
        [
            ((planes * count, in_all.shape[2]), jnp.float32),
            ((query_all.shape[0] // 2, planes * width // HS * count, width), jnp.bfloat16),
        ],
    )


def attend_some(cfg, maps_ref, query_ref, some, start, sums):
    count, features, planes, per_plane = cfg["count"], cfg["features"], cfg["planes"], cfg["per_plane"]
    layer, side = cfg["layer"], side_of()
    groups, _, group_cols = query_ref.shape
    heads = group_cols // HS
    band = heads * count
    total_cols = groups * group_cols
    stride = 2 * per_plane * count
    token = lax.broadcasted_iota(jnp.int32, (count, 1), 0)
    member = lax.axis_index("seq")
    query_place = (member % per_plane * 2 + side) * count + jnp.concatenate([token] * heads, axis=0)
    offsets = [
        (chip_of(step, per_plane, other) * 2 + (1 - side if other else side)) * count
        for _, step, other in some
    ]
    if layer == 0:
        size = len(some) * count
        lane = lax.broadcasted_iota(jnp.int32, (1, size), 1)
        key_place = lane + offsets[0]
        for at in range(1, len(some)):
            key_place = jnp.where(lane >= at * count, lane - at * count + offsets[at], key_place)
        allowed = key_place <= query_place
        parts = [cat([rows[p, :count, :] for rows, _, _ in some], 0) for p in range(planes)]
        low_rows = [p * band for p in range(planes)]
    else:
        size = len(some) * planes * count
        lane = lax.broadcasted_iota(jnp.int32, (1, planes * count), 1)
        plane = ((lane.astype(jnp.float32) + 0.5) * (1.0 / count)).astype(jnp.int32)
        base_place = lane + plane * (stride - count)
        key_place = jnp.concatenate([base_place + offset for offset in offsets], axis=1)
        allowed = key_place >= query_place + member // per_plane * stride
        rows = [rows[:, :count, :].reshape(planes * count, rows.shape[2]) for rows, _, _ in some]
        parts, low_rows = [cat(rows, 0)], [0]

    def keys_and_values(source, g):
        low = g * group_cols
        twice = jnp.concatenate([source, source], axis=1)
        channels = source.shape[1]
        tail = dot_nt(maps_ref[2 * total_cols :, :], twice)
        square = jnp.sum(tail[:channels] * tail[channels:], axis=0, keepdims=True)
        scale = lax.rsqrt(jnp.maximum(square, 0.0) * (1.0 / features) + epsilon)
        scale_sq = scale * scale
        key = dot_nt(maps_ref[low : low + group_cols, :], twice)
        value = dot_nt(maps_ref[total_cols + low : total_cols + low + group_cols, :], twice)
        keys = []
        for h in range(heads):
            one = key[h * HS : (h + 1) * HS]
            mean = jnp.sum(one * one, axis=0, keepdims=True) * (1.0 / HS)
            factor = scale * lax.rsqrt(mean * scale_sq + epsilon) * (score_scale / HS)
            keys.append((one * factor).astype(jnp.bfloat16))
        return jnp.concatenate(keys, axis=0), (value * scale).astype(jnp.bfloat16)

    for g in range(groups):
        if size % 128 == 0 and len(parts) > 1:
            key, value = keys_and_values(cat(parts, 0), g)
            made = [
                (key[:, p * size : (p + 1) * size], value[:, p * size : (p + 1) * size])
                for p in range(len(parts))
            ]
        else:
            made = [keys_and_values(part, g) for part in parts]
        for index, ((key, value), low_row) in enumerate(zip(made, low_rows)):
            scores = dot(query_ref[g, low_row:, :], key)
            weights = jnp.exp(scores)
            first = jnp.where(allowed, weights[:band], 0.0)
            weights = first if weights.shape[0] == band else cat([first, weights[band:]], 0)
            product = dot_nt(weights.astype(jnp.bfloat16), value)
            lanes = [weights[:, at : at + 128] for at in range(0, weights.shape[1], 128)]
            news = [product, sum(part for part in lanes if part.shape[1] == 128)]
            news += [part for part in lanes if part.shape[1] < 128]
            for at, (old_ref, new_ref) in enumerate(sums):
                if start and index == 0:
                    old = None if old_ref is None else old_ref[g]
                else:
                    old = new_ref[g, low_row:, :]
                if at < len(news):
                    new = news[at] if old is None else old + news[at]
                else:
                    new = jnp.zeros(new_ref.shape[1:], jnp.float32) if old is None else old
                if at < len(news) or (start and index == 0):
                    new_ref[g, low_row:, :] = new


def sum_shapes(cfg, queries):
    groups, rows, cols = queries.shape
    shapes = [(groups, rows, cols), (groups, rows, 128)]
    rest = 2 * cfg["count"] % 128
    return shapes + ([(groups, rows, rest)] if cfg["layer"] == 0 and rest else [])


def attend_kernel(cfg, kinds, resume, maps_ref, query_ref, *refs):
    refs = list(refs)
    pieces = [(refs.pop(0), step, other) for step, other in kinds]
    many = len(refs) // 2 if resume else len(refs)
    olds = refs[:many] if resume else [None] * many
    sums = list(zip(olds, refs[-many:]))
    some = [(ref[...], step, other) for ref, step, other in pieces]
    attend_some(cfg, maps_ref, query_ref, some, True, sums)


def attend(cfg, maps, queries, pieces, sums=()):
    kinds = tuple((step, other) for _, step, other in pieces)
    return on_chip(
        functools.partial(attend_kernel, cfg, kinds, len(sums) > 0),
        "attend",
        [maps, queries, *[piece for piece, _, _ in pieces], *sums],
        [(shape, jnp.float32) for shape in sum_shapes(cfg, queries)],
    )


def chosen_rows(others, per_plane, place, rows):
    plane, chip = place // per_plane, place % per_plane
    result = None
    for step, ref in enumerate(others):
        value = ref[plane, rows, :].astype(jnp.float32)
        here = chip_of(step, per_plane, True) == chip
        result = value if result is None else jnp.where(here, value, result)
    return result


def second_half_kernel(cfg, kinds, many, maps_ref, query_ref, hidden_ref, gain_ref, latent_ref, *refs):
    layer, pieces, last, count = cfg["layer"], cfg["pieces"], cfg["last"], cfg["count"]
    planes, per_plane = cfg["planes"], cfg["per_plane"]
    refs = list(refs)
    olds = [refs.pop(0) for _ in range(many)]
    rows_of = {False: [refs.pop(0) for _ in range(per_plane)]}
    rows_of[True] = others = [refs.pop(0) for _ in range(per_plane)]
    mix_refs = [refs.pop(0) for _ in range(pieces)]
    param_refs = [refs.pop(0) for _ in range(pieces)]
    param_all = refs.pop(3)
    sums = list(zip(olds, [refs.pop(3) for _ in range(many)]))
    side, way, member = side_of(), lax.axis_index("head"), lax.axis_index("seq")
    members = planes * per_plane
    features, channels = hidden_ref.shape[1], latent_ref.shape[-1]
    groups, _, group_cols = query_ref.shape
    heads = group_cols // HS
    if len(kinds) <= 8:
        some = [(rows_of[other][step][...], step, other) for step, other in kinds]
        attend_some(cfg, maps_ref, query_ref, some, True, sums)
    else:
        for old, new in sums:
            new[...] = old[...]
        for buffer, other in zip(refs[-2:], (False, True)):
            for step in range(1, per_plane):
                buffer[step] = rows_of[other][step][...]

        def one_step(step, nothing):
            pair = [(refs[-2][step], step, False), (refs[-1][step], step, True)]
            attend_some(cfg, maps_ref, query_ref, pair, False, sums)
            return nothing

        lax.fori_loop(1, per_plane, one_step, 0)

    mixture = hidden_ref[...]
    bands = mixture.shape[0] // count
    head = lax.broadcasted_iota(jnp.int32, (1, group_cols), 1) // HS
    for g in range(groups):
        total = sum(jnp.sum(new[g], axis=1, keepdims=True) for _, new in sums[1:])
        share_of = 1.0 / (total + (0.0 if last else 1.0))
        number_ref = sums[0][1]
        attended = []
        for p in range(bands):
            one = jnp.zeros((count, group_cols), jnp.float32)
            for h in range(heads):
                band = slice((p * heads + h) * count, (p * heads + h + 1) * count)
                one = jnp.where(head == h, number_ref[g, band, :] * share_of[band], one)
            attended.append(one)
        rows = cat([ref[layer] for ref in mix_refs[2 * g : 2 * g + 2]], 0)
        mixture = mixture + dot(cat(attended, 0).astype(jnp.bfloat16), rows)
    spread = lax.rsqrt(jnp.mean(mixture * mixture, axis=1, keepdims=True) + epsilon)
    scaled = (mixture * spread * gain_ref[layer : layer + 1, :]).astype(jnp.bfloat16)
    share = features // pieces
    for j, ref in enumerate(param_refs):
        at = pl.multiple_of(lax.rem(way + j, pieces) * share, 16)
        param_all[pl.ds(at, share), :] = ref[layer]
    predicted = dot(scaled, param_all[...])
    shift_all = predicted[:, :channels]
    log_all = 2.0 * jnp.tanh(0.5 * predicted[:, channels:])
    token = lax.broadcasted_iota(jnp.int32, (count, 1), 0)
    if last:
        held_ref, held_log_ref, out_ref = refs[:3]
        plane = member // per_plane
        before = member - 1 + side
        edge = chosen_rows(others, per_plane, jnp.maximum(before, 0), slice(count, count + 16))
        edge = jnp.where(before >= 0, edge[0:2] + edge[2:4] + edge[4:6], 0.0)
        edge_log = edge[1:2]
        first = (latent_ref[plane, :8, :][:1] - edge[0:1]) * jnp.exp(-edge_log)
        values = jnp.where(token == 0, first, pltpu.roll(held_ref[plane], 1, 0))
        first_log = jnp.where(token == 0, edge_log, pltpu.roll(held_log_ref[plane], 1, 0))
        result = (values - shift_all) * jnp.exp(-log_all)
        term = -(first_log + log_all) - 0.5 * (result * result)
        loglik = jnp.sum(term.T, axis=0, keepdims=True) * (1.0 / channels) - 0.5 * math.log(
            2.0 * math.pi
        )
        out_ref[:count, :] = result
        out_ref[count:, :count] = jnp.broadcast_to(loglik, (8, count))
        return
    held_ref, held_log_ref, narrow_ref = refs[:3]
    for p in range(planes):
        shift_mu = shift_all[p * count : (p + 1) * count]
        log_scale = log_all[p * count : (p + 1) * count]
        following = p * per_plane + member % per_plane + side
        after = chosen_rows(others, per_plane, jnp.minimum(following, members - 1), slice(0, 16))
        values = pltpu.roll(latent_ref[p], count - 1, 0)
        values = jnp.where(token == count - 1, after[:1], values)
        result = (values - shift_mu) * jnp.exp(-log_scale)
        if p == planes - 1:
            result = jnp.where((following == members) & (token == count - 1), 0.0, result)
        held_ref[p] = result
        held_log_ref[p] = log_scale
        edge = jnp.concatenate([shift_mu[count - 1 :], log_scale[count - 1 :]], axis=0)
        terms = []
        for _ in range(3):
            terms.append(edge.astype(jnp.bfloat16).astype(jnp.float32))
            edge = edge - terms[-1]
        rest = jnp.zeros((16 - 6, channels), jnp.float32)
        narrow_ref[p, :count, :] = result.astype(jnp.bfloat16)
        narrow_ref[p, count:, :] = jnp.concatenate(terms + [rest], axis=0).astype(jnp.bfloat16)


def second_half(cfg, kinds, maps, queries, sums, hidden, param_gain, latents, mine, others, mix_pieces, param_pieces, held=()):
    count, planes, channels = cfg["count"], cfg["planes"], latents.shape[-1]
    operands = [maps, queries, hidden, param_gain, latents, *sums, *mine, *others]
    operands += [*mix_pieces, *param_pieces, *held]
    if cfg["last"]:
        results = [((count + 8, channels), jnp.float32)]
    else:
        results = [
            ((planes, count, channels), jnp.float32),
            ((planes, count, channels), jnp.float32),
            ((planes, count + 16, channels), jnp.bfloat16),
        ]
    scratch = [pltpu.VMEM((cfg["features"], param_pieces[0].shape[2]), jnp.bfloat16)]
    scratch += [pltpu.VMEM(one.shape, jnp.float32) for one in sums]
    if len(kinds) > 8:
        scratch += [pltpu.VMEM((len(mine), *mine[0].shape), jnp.bfloat16)] * 2
    return on_chip(
        functools.partial(second_half_kernel, cfg, kinds, len(sums)),
        "second_half",
        operands,
        results,
        scratch=scratch,
    )


def finish_kernel(own_ref, other_ref, final_ref, loglik_ref):
    count = final_ref.shape[0] // 2
    side = side_of()
    for ref, place in ((own_ref, side), (other_ref, 1 - side)):
        final_ref[pl.ds(pl.multiple_of(place * count, 8), count), :] = ref[:count, :]
    first = jnp.where(side == 0, own_ref[count : count + 1, :], other_ref[count : count + 1, :])
    second = jnp.where(side == 0, other_ref[count : count + 1, :], own_ref[count : count + 1, :])
    loglik_ref[...] = jnp.concatenate([first[:, :count], second[:, :count]], axis=1)


def body(
    latents, in_proj, query_proj, key_proj, value_proj, mix_proj, param_proj, attn_gain, param_gain
):
    members, ways = lax.axis_size("seq"), lax.axis_size("head")
    rows, channels = latents.shape
    features = in_proj.shape[2]
    count = rows // 2
    planes = 4 if members % 4 == 0 else 1
    per_plane = members // planes
    bits = per_plane.bit_length() - 1

    def swap(array):
        return lax.ppermute(array, "head", [(i, i ^ 1) for i in range(ways)])

    def pieces_of(array):
        shares = [array]
        for j in range(1, ways):
            shares.append(
                lax.ppermute(array, "head", [((i + j) % ways, i) for i in range(ways)])
            )
        return shares

    def in_plane(mine):
        arrived = []
        for step in range(1, per_plane):
            pairs = []
            for i in range(members):
                for w in range(ways):
                    to = i ^ (turned(step, bits) if w % 2 else step)
                    pairs.append((i * ways + w, to * ways + w))
            arrived.append(lax.ppermute(mine, ("seq", "head"), pairs))
        return arrived

    def run(layer, mine, maps, made, latents, *rest):
        cfg = {
            "layer": layer,
            "last": layer == 1,
            "count": count,
            "features": features,
            "pieces": ways,
            "planes": planes,
            "per_plane": per_plane,
        }
        hidden, queries = made
        arrived = in_plane(mine)
        others = [swap(mine)]
        sums = attend(cfg, maps, queries, [(mine, 0, False), (others[0], 0, True)])
        mines = [mine]
        if per_plane > 1:
            arrived = gate_all(arrived, sums)
            mines += arrived
            others += [swap(piece) for piece in arrived]
        kinds = [(step, False) for step in range(1, per_plane)]
        kinds += [(step, True) for step in range(1, per_plane)]
        if per_plane == 4:
            sums = attend(cfg, maps, queries, [(mines[1], 1, False), (mines[2], 2, False)], sums)
            kinds = kinds[2:]
        return second_half(
            cfg, tuple(kinds), maps, queries, sums, hidden, param_gain, latents, mines, others, mix_pieces, param_pieces, *rest
        )

    (own,) = on_chip(
        half_kernel,
        "half",
        [],
        [((count, channels), jnp.float32)],
        far=[latents],
        scratch=[pltpu.SemaphoreType.DMA((1,))],
    )
    parts = [own] + [
        lax.ppermute(own, "seq", [(i, i ^ (b * per_plane)) for i in range(members)])
        for b in range(1, planes)
    ]
    key_pieces, value_pieces = pieces_of(key_proj), pieces_of(value_proj)
    query_pieces, mix_pieces = pieces_of(query_proj), pieces_of(mix_proj)
    param_pieces = pieces_of(param_proj)
    maps, weights = prepare(in_proj, attn_gain, key_pieces, value_pieces, query_pieces)
    wide, mine = on_chip(
        functools.partial(arrange_kernel, planes),
        "arrange",
        [*parts, maps[0]],
        [((planes, count, channels), jnp.float32), ((planes, count, channels), jnp.bfloat16)],
    )
    made = make_queries(0, planes, count, mine, weights)
    held, held_log, mine = run(0, mine, maps[0], made, wide)
    made = make_queries(1, 1, count, mine, weights)
    (packed,) = run(1, mine, maps[1], made, wide, (held, held_log))
    final_latent, token_loglik = on_chip(
        finish_kernel,
        "finish",
        [packed, swap(packed)],
        [((rows, channels), jnp.float32), ((1, rows), jnp.float32)],
        out_memory=None,
    )
    return (final_latent, token_loglik.reshape(rows))


def solution(mesh):
    placed = (
        P("seq", None),
        P(),
        P(None, None, "head"),
        P(None, None, "head"),
        P(None, None, "head"),
        P(None, "head", None),
        P(None, "head", None),
        P(),
        P(),
    )
    return jax.shard_map(
        body, mesh=mesh, in_specs=placed, out_specs=(P("seq", None), P("seq")), check_vma=False
    )
```

time: 379 us -> 47.6 us (0.13)
  blocking collectives: 170 us -> 0 us
  waiting for transfers between devices: 112 us -> 7.35 us
  matrix products: 26.9 us -> 0 us
  Pallas kernels: 0 us -> 21.1 us
  starting transfers between devices: 35.7 us -> 18.1 us
  between operations: 14.1 us -> 0.86 us
  other arithmetic: 10.3 us -> 0 us
  local copies, waits for them, and re-layouts: 8.73 us -> 0.02 us
    all_gather x4 -> x0, blocking collectives: 170 us -> none  [the longest x2 89.8 us: flow_block(): piece_keys = lax.all_gather(key_rows, 'seq', axis=0, tiled=True)]
    psum x4 -> x0, waiting for transfers between devices: 73.3 us -> none  [the longest x2 38.5 us: flow_block(): lax.psum(jnp.dot(scaled, param_proj[layer_index], preferred_element_type=...]
    ppermute x18 -> x23, waiting for transfers between devices: 38.5 us -> 7.35 us  [the longest x6 4.98 us: in_plane(): arrived.append(lax.ppermute(mine, ('seq', 'head'), pairs))]
    dot_general x16 -> x0, matrix products: 26.9 us -> none  [the longest x2 8.4 us: compute(): jnp.einsum('qhd,khd->hqk', queries, piece_keys.reshape(piece_rows, head_c...]
    pallas_call x0 -> x14, Pallas kernels: none -> 21.1 us  [on_chip(): pl.pallas_call(kernel, in_specs=[pl.BlockSpec(memory_space=pltpu.VMEM)] *...]
    ppermute x18 -> x23, starting transfers between devices: 35.6 us -> 18.1 us  [the longest x6 7.22 us: in_plane(): arrived.append(lax.ppermute(mine, ('seq', 'head'), pairs))]
    reduce_sum x5 -> x0, other arithmetic: 5.75 us -> none  [the longest x2 2.96 us: norm_rows(): jnp.mean(value * value, axis=-1, keepdims=True) + epsilon]
  transfers between devices with their start and end apart: 22 -> 23, of which waited for: 18 -> 9; matrix products, arithmetic and copies ran while one was open for 2% -> 0% of each run, Pallas kernels for 0% -> 26%
where the time goes in v7:
time: 47.6 us; the launch traced here: 47.4 us
  Pallas kernels  21.1 us (44%)
  starting transfers between devices  18.1 us (38%)
  waiting for transfers between devices  7.35 us (15%)
  between operations  0.86 us (2%)
    pallas_call x14, Pallas kernels, on_chip(): pl.pallas_call(kernel, in_specs=[pl.BlockSpec(memory_space=pltpu.VMEM)] *...  21.1 us
    ppermute x6, starting transfers between devices, in_plane(): arrived.append(lax.ppermute(mine, ('seq', 'head'), pairs))  7.22 us
    ppermute x3, starting transfers between devices, body(): lax.ppermute(own, 'seq', [(i, i ^ b * per_plane) for i in range(members)])  7.21 us
    ppermute x6, waiting for transfers between devices, in_plane(): arrived.append(lax.ppermute(mine, ('seq', 'head'), pairs))  4.98 us
    ppermute x9, starting transfers between devices, swap(): return lax.ppermute(array, 'head', [(i, i ^ 1) for i in range(ways)])  2.12 us
    ppermute x5, starting transfers between devices, pieces_of(): lax.ppermute(array, 'head', [((i + j) % ways, i) for i in range(ways)])  1.54 us
    ppermute x9, waiting for transfers between devices, swap(): return lax.ppermute(array, 'head', [(i, i ^ 1) for i in range(ways)])  1.35 us
  transfers between devices with their start and end apart: 23, of which 9 were waited for; matrix products, arithmetic and copies ran while one was open for 0% of the time, Pallas kernels for 26%

profile of v7, /device:TPU:0, one launch (start us, length us, event | category | flops | bytes accessed | tf_op | source)
XLA Modules:
  0.0 47.4 jit_solution(6373018564459240966)
XLA Ops:
  2.2 0.8 %half.1.refs_0_ = f32[96,128]{1,0:T(8,128)S(1)} custom-call(f32[192,128]{1,0:T(8,128)} %rows_ref.1), custom_call_target="tpu_custom_call" | custom-call | tf_op jit(solution)/shard_map/half/pallas_call | solution.py:42
  3.3 2.9 %collective-permute-start.3 = (f32[96,128]{1,0:T(8,128)S(1)}, f32[96,128]{1,0:T(8,128)S(1)}, u32[]{:S(2)}, u32[]{:S(2)}) collective-permute-start(f32[96,128]{1,0:T(8,128)S(1)} %half.1.refs_0_), channel_id=1, source_target_pairs={{0,8},{2,10},{4,12},{6,14},{8,0},{10,2},{12,4},{14,6},{16,24},{18,... | collective-permute-start | bytes 147464 | tf_op jit(solution)/shard_map/ppermute | solution.py:532
  6.2 2.6 %collective-permute-start.4 = (f32[96,128]{1,0:T(8,128)S(1)}, f32[96,128]{1,0:T(8,128)S(1)}, u32[]{:S(2)}, u32[]{:S(2)}) collective-permute-start(f32[96,128]{1,0:T(8,128)S(1)} %half.1.refs_0_), channel_id=1, source_target_pairs={{0,16},{2,18},{4,20},{6,22},{8,24},{10,26},{12,28},{14,30},{16,0},... | collective-permute-start | bytes 147464 | tf_op jit(solution)/shard_map/ppermute | solution.py:532
  8.8 1.7 %collective-permute-start.5 = (f32[96,128]{1,0:T(8,128)S(1)}, f32[96,128]{1,0:T(8,128)S(1)}, u32[]{:S(2)}, u32[]{:S(2)}) collective-permute-start(f32[96,128]{1,0:T(8,128)S(1)} %half.1.refs_0_), channel_id=1, source_target_pairs={{0,24},{2,26},{4,28},{6,30},{8,16},{10,18},{12,20},{14,22},{16,8},... | collective-permute-start | bytes 147464 | tf_op jit(solution)/shard_map/ppermute | solution.py:532
  10.5 3.5 %prepare.1 = (bf16[768,256]{1,0:T(8,128)(2,1)S(1)}, bf16[768,256]{1,0:T(8,128)(2,1)S(1)}, bf16[2,128,1536]{2,1,0:T(8,128)(2,1)S(1)}, f32[2,1536]{1,0:T(2,128)S(1)}, bf16[2,2,1536,128]{3,2,1,0:T(8,128)(2,1)S(1)}) custom-call(bf16[2,128,1536]{2,1,0:T(8,128)(2,1)} %in_src.1, f32[2,1536]{1,0:T(2,128)} %gain_src.1, bf16[2,1536,128]{2,1,0:T(8,128)(2,1)} %refs_0_.1, ...), custom_call_target="tpu_custom_call" | custom-call | tf_op jit(solution)/shard_map/prepare/pallas_call | solution.py:42
  14.0 0.7 %collective-permute-done.5.refs_3_ = f32[96,128]{1,0:T(8,128)S(1)} collective-permute-done((f32[96,128]{1,0:T(8,128)S(1)}, f32[96,128]{1,0:T(8,128)S(1)}, u32[]{:S(2)}, u32[]{:S(2)}) %collective-permute-start.5) | collective-permute-done | bytes 49184 | tf_op jit(solution)/shard_map/ppermute | solution.py:532
  14.8 1.6 %collective-permute-start.6 = (bf16[4,96,128]{2,1,0:T(8,128)(2,1)S(1)}, bf16[4,96,128]{2,1,0:T(8,128)(2,1)S(1)}, u32[]{:S(2)}, u32[]{:S(2)}) collective-permute-start(bf16[4,96,128]{2,1,0:T(8,128)(2,1)S(1)} %get-tuple-element.36.rows_ref.refs_0_.refs_3_), channel_id=1, source_target_pairs={{0,2},{1,5},{2,0},{3,7},{4,6},{5,1},{6,4},{7,3},{8,10},{9,13},{10,... | collective-permute-start | bytes 294920 | tf_op jit(solution)/shard_map/ppermute | solution.py:492
  16.4 1.5 %collective-permute-start.7 = (bf16[4,96,128]{2,1,0:T(8,128)(2,1)S(1)}, bf16[4,96,128]{2,1,0:T(8,128)(2,1)S(1)}, u32[]{:S(2)}, u32[]{:S(2)}) collective-permute-start(bf16[4,96,128]{2,1,0:T(8,128)(2,1)S(1)} %get-tuple-element.36.rows_ref.refs_0_.refs_3_), channel_id=1, source_target_pairs={{0,4},{1,3},{2,6},{3,1},{4,0},{5,7},{6,2},{7,5},{8,12},{9,11},{10,... | collective-permute-start | bytes 294920 | tf_op jit(solution)/shard_map/ppermute | solution.py:492
  17.9 0.7 %collective-permute-start.8 = (bf16[4,96,128]{2,1,0:T(8,128)(2,1)S(1)}, bf16[4,96,128]{2,1,0:T(8,128)(2,1)S(1)}, u32[]{:S(2)}, u32[]{:S(2)}) collective-permute-start(bf16[4,96,128]{2,1,0:T(8,128)(2,1)S(1)} %get-tuple-element.36.rows_ref.refs_0_.refs_3_), channel_id=1, source_target_pairs={{0,6},{1,7},{2,4},{3,5},{4,2},{5,3},{6,0},{7,1},{8,14},{9,15},{10,... | collective-permute-start | bytes 294920 | tf_op jit(solution)/shard_map/ppermute | solution.py:492
  18.6 1.7 %queries.2 = (f32[384,1536]{1,0:T(8,128)S(1)}, bf16[1,1536,256]{2,1,0:T(8,128)(2,1)S(1)}) custom-call(bf16[4,96,128]{2,1,0:T(8,128)(2,1)S(1)} %get-tuple-element.36.rows_ref.refs_0_.refs_3_, bf16[2,128,1536]{2,1,0:T(8,128)(2,1)S(1)} %get-tuple-element.37.in_ref, f32[2,1536]{1,0:T(2,128)S(1)} %get-tuple-element.38.gain_ref, ...), custom_call_target="tpu_custom_call" | custom-call | tf_op jit(solution)/shard_map/queries/pallas_call | solution.py:42
  20.2 1.8 %attend.4 = (f32[1,1536,256]{2,1,0:T(8,128)S(1)}, f32[1,1536,128]{2,1,0:T(8,128)S(1)}, f32[1,1536,64]{2,1,0:T(8,128)S(1)}) custom-call(bf16[768,256]{1,0:T(8,128)(2,1)S(1)} %get-tuple-element.35.refs_4_.maps_ref, bf16[1,1536,256]{2,1,0:T(8,128)(2,1)S(1)} %get-tuple-element.40.query_ref, bf16[4,96,128]{2,1,0:T(8,128)(2,1)S(1)} %get-tuple-element.36.rows_ref.refs_0_.refs_3_, ...), custom_call_target="tpu_custom_call" | custom-call | tf_op jit(solution)/shard_map/attend/pallas_call | solution.py:42
  22.2 1.2 %collective-permute-done.8.refs_2_ = bf16[4,96,128]{2,1,0:T(8,128)(2,1)S(1)} collective-permute-done((bf16[4,96,128]{2,1,0:T(8,128)(2,1)S(1)}, bf16[4,96,128]{2,1,0:T(8,128)(2,1)S(1)}, u32[]{:S(2)}, u32[]{:S(2)}) %collective-permute-start.8) | collective-permute-done | bytes 98336 | tf_op jit(solution)/shard_map/ppermute | solution.py:492
  24.1 1.8 %attend.5 = (f32[1,1536,256]{2,1,0:T(8,128)S(1)}, f32[1,1536,128]{2,1,0:T(8,128)S(1)}, f32[1,1536,64]{2,1,0:T(8,128)S(1)}) custom-call(bf16[768,256]{1,0:T(8,128)(2,1)S(1)} %get-tuple-element.35.refs_4_.maps_ref, bf16[1,1536,256]{2,1,0:T(8,128)(2,1)S(1)} %get-tuple-element.40.query_ref, bf16[4,96,128]{2,1,0:T(8,128)(2,1)S(1)} %get-tuple-element.46.refs_0_.refs_4_, ...), custom_call_target="tpu_custom_call" | custom-call | tf_op jit(solution)/shard_map/attend/pallas_call | solution.py:42
  26.0 5.5 %second_half.2 = (f32[4,96,128]{2,1,0:T(8,128)S(1)}, f32[4,96,128]{2,1,0:T(8,128)S(1)}, bf16[4,112,128]{2,1,0:T(8,128)(2,1)S(1)}) custom-call(bf16[768,256]{1,0:T(8,128)(2,1)S(1)} %get-tuple-element.35.refs_4_.maps_ref, bf16[1,1536,256]{2,1,0:T(8,128)(2,1)S(1)} %get-tuple-element.40.query_ref, f32[384,1536]{1,0:T(8,128)S(1)} %get-tuple-element.41.hidden_ref, ...), custom_call_target="tpu_custom_call" | custom-call | tf_op jit(solution)/shard_map/second_half/pallas_call | solution.py:42
  32.0 1.4 %collective-permute-start.15 = (bf16[4,112,128]{2,1,0:T(8,128)(2,1)S(1)}, bf16[4,112,128]{2,1,0:T(8,128)(2,1)S(1)}, u32[]{:S(2)}, u32[]{:S(2)}) collective-permute-start(bf16[4,112,128]{2,1,0:T(8,128)(2,1)S(1)} %get-tuple-element.52.rows_ref.refs_0_.refs_2_), channel_id=1, source_target_pairs={{0,2},{1,5},{2,0},{3,7},{4,6},{5,1},{6,4},{7,3},{8,10},{9,13},{10,... | collective-permute-start | bytes 344072 | tf_op jit(solution)/shard_map/ppermute | solution.py:492
  33.4 0.8 %collective-permute-start.16 = (bf16[4,112,128]{2,1,0:T(8,128)(2,1)S(1)}, bf16[4,112,128]{2,1,0:T(8,128)(2,1)S(1)}, u32[]{:S(2)}, u32[]{:S(2)}) collective-permute-start(bf16[4,112,128]{2,1,0:T(8,128)(2,1)S(1)} %get-tuple-element.52.rows_ref.refs_0_.refs_2_), channel_id=1, source_target_pairs={{0,4},{1,3},{2,6},{3,1},{4,0},{5,7},{6,2},{7,5},{8,12},{9,11},{10,... | collective-permute-start | bytes 344072 | tf_op jit(solution)/shard_map/ppermute | solution.py:492
  34.2 1.3 %collective-permute-start.17 = (bf16[4,112,128]{2,1,0:T(8,128)(2,1)S(1)}, bf16[4,112,128]{2,1,0:T(8,128)(2,1)S(1)}, u32[]{:S(2)}, u32[]{:S(2)}) collective-permute-start(bf16[4,112,128]{2,1,0:T(8,128)(2,1)S(1)} %get-tuple-element.52.rows_ref.refs_0_.refs_2_), channel_id=1, source_target_pairs={{0,6},{1,7},{2,4},{3,5},{4,2},{5,3},{6,0},{7,1},{8,14},{9,15},{10,... | collective-permute-start | bytes 344072 | tf_op jit(solution)/shard_map/ppermute | solution.py:492
  35.5 0.7 %queries.3 = (f32[96,1536]{1,0:T(8,128)S(1)}, bf16[1,384,256]{2,1,0:T(8,128)(2,1)S(1)}) custom-call(bf16[4,112,128]{2,1,0:T(8,128)(2,1)S(1)} %get-tuple-element.52.rows_ref.refs_0_.refs_2_, bf16[2,128,1536]{2,1,0:T(8,128)(2,1)S(1)} %get-tuple-element.37.in_ref, f32[2,1536]{1,0:T(2,128)S(1)} %get-tuple-element.38.gain_ref, ...), custom_call_target="tpu_custom_call" | custom-call | tf_op jit(solution)/shard_map/queries/pallas_call | solution.py:42
  36.3 0.9 %attend.6 = (f32[1,384,256]{2,1,0:T(8,128)S(1)}, f32[1,384,128]{2,1,0:T(8,128)S(1)}) custom-call(bf16[768,256]{1,0:T(8,128)(2,1)S(1)} %get-tuple-element.34.maps_ref, bf16[1,384,256]{2,1,0:T(8,128)(2,1)S(1)} %get-tuple-element.53.query_ref, bf16[4,112,128]{2,1,0:T(8,128)(2,1)S(1)} %get-tuple-element.52.rows_ref.refs_0_.refs_2_, ...), custom_call_target="tpu_custom_call" | custom-call | tf_op jit(solution)/shard_map/attend/pallas_call | solution.py:42
  37.2 0.8 %collective-permute-done.15.refs_0_ = bf16[4,112,128]{2,1,0:T(8,128)(2,1)S(1)} collective-permute-done((bf16[4,112,128]{2,1,0:T(8,128)(2,1)S(1)}, bf16[4,112,128]{2,1,0:T(8,128)(2,1)S(1)}, u32[]{:S(2)}, u32[]{:S(2)}) %collective-permute-start.15) | collective-permute-done | bytes 114720 | tf_op jit(solution)/shard_map/ppermute | solution.py:492
  38.3 2.5 %collective-permute-done.17.refs_2_ = bf16[4,112,128]{2,1,0:T(8,128)(2,1)S(1)} collective-permute-done((bf16[4,112,128]{2,1,0:T(8,128)(2,1)S(1)}, bf16[4,112,128]{2,1,0:T(8,128)(2,1)S(1)}, u32[]{:S(2)}, u32[]{:S(2)}) %collective-permute-start.17) | collective-permute-done | bytes 114720 | tf_op jit(solution)/shard_map/ppermute | solution.py:492
  41.5 0.9 %attend.7 = (f32[1,384,256]{2,1,0:T(8,128)S(1)}, f32[1,384,128]{2,1,0:T(8,128)S(1)}) custom-call(bf16[768,256]{1,0:T(8,128)(2,1)S(1)} %get-tuple-element.34.maps_ref, bf16[1,384,256]{2,1,0:T(8,128)(2,1)S(1)} %get-tuple-element.53.query_ref, bf16[4,112,128]{2,1,0:T(8,128)(2,1)S(1)} %get-tuple-element.57.refs_0_.refs_3_, ...), custom_call_target="tpu_custom_call" | custom-call | tf_op jit(solution)/shard_map/attend/pallas_call | solution.py:42
  42.7 2.7 %second_half.3.own_ref = f32[104,128]{1,0:T(8,128)S(1)} custom-call(bf16[768,256]{1,0:T(8,128)(2,1)S(1)} %get-tuple-element.34.maps_ref, bf16[1,384,256]{2,1,0:T(8,128)(2,1)S(1)} %get-tuple-element.53.query_ref, f32[96,1536]{1,0:T(8,128)S(1)} %get-tuple-element.54.hidden_ref, f32[2,1536]{1,0:T(2,128)S(1)} %copy-done.2, ...), custom_call_target="tpu_custom_call" | custom-call | tf_op jit(solution)/shard_map/second_half/pallas_call | solution.py:42
  45.7 1.1 %collective-permute-done.22.other_ref = f32[104,128]{1,0:T(8,128)S(1)} collective-permute-done((f32[104,128]{1,0:T(8,128)S(1)}, f32[104,128]{1,0:T(8,128)S(1)}, u32[]{:S(2)}, u32[]{:S(2)}) %collective-permute-start.22) | collective-permute-done | bytes 53280 | tf_op jit(solution)/shard_map/ppermute | solution.py:474
  (48 shorter events, 5.5 us)
Async XLA Ops:
  0.6 2.6 %collective-permute-start = (bf16[2,1536,128]{2,1,0:T(8,128)(2,1)}, bf16[2,1536,128]{2,1,0:T(8,128)(2,1)S(1)}, u32[]{:S(2)}, u32[]{:S(2)}) collective-permute-start(bf16[2,1536,128]{2,1,0:T(8,128)(2,1)} %refs_0_.1), channel_id=1, source_target_pairs={{1,0},{0,1},{3,2},{2,3},{5,4},{4,5},{7,6},{6,7},{9,8},{8,9},{11,10... | collective-permute-start | bytes 2359304 | tf_op jit(solution)/shard_map/ppermute | solution.py:480
  1.1 5.1 %collective-permute-start.1 = (bf16[2,1536,128]{2,1,0:T(8,128)(2,1)}, bf16[2,1536,128]{2,1,0:T(8,128)(2,1)S(1)}, u32[]{:S(2)}, u32[]{:S(2)}) collective-permute-start(bf16[2,1536,128]{2,1,0:T(8,128)(2,1)} %refs_2_.1), channel_id=1, source_target_pairs={{1,0},{0,1},{3,2},{2,3},{5,4},{4,5},{7,6},{6,7},{9,8},{8,9},{11,10... | collective-permute-start | bytes 2359304 | tf_op jit(solution)/shard_map/ppermute | solution.py:480
  1.2 7.6 %collective-permute-start.2 = (bf16[2,1536,128]{2,1,0:T(8,128)(2,1)}, bf16[2,1536,128]{2,1,0:T(8,128)(2,1)S(1)}, u32[]{:S(2)}, u32[]{:S(2)}) collective-permute-start(bf16[2,1536,128]{2,1,0:T(8,128)(2,1)} %refs_4_.1), channel_id=1, source_target_pairs={{1,0},{0,1},{3,2},{2,3},{5,4},{4,5},{7,6},{6,7},{9,8},{8,9},{11,10... | collective-permute-start | bytes 2359304 | tf_op jit(solution)/shard_map/ppermute | solution.py:480
  1.7 24.3 %collective-permute-start.13 = (bf16[2,128,1536]{2,1,0:T(8,128)(2,1)}, bf16[2,128,1536]{2,1,0:T(8,128)(2,1)S(1)}, u32[]{:S(2)}, u32[]{:S(2)}) collective-permute-start(bf16[2,128,1536]{2,1,0:T(8,128)(2,1)} %refs_10_.1), channel_id=1, source_target_pairs={{1,0},{0,1},{3,2},{2,3},{5,4},{4,5},{7,6},{6,7},{9,8},{8,9},{11,10... | collective-permute-start | bytes 2359304 | tf_op jit(solution)/shard_map/ppermute | solution.py:480
  1.7 24.2 %collective-permute-start.14 = (bf16[2,768,256]{2,1,0:T(8,128)(2,1)}, bf16[2,768,256]{2,1,0:T(8,128)(2,1)S(1)}, u32[]{:S(2)}, u32[]{:S(2)}) collective-permute-start(bf16[2,768,256]{2,1,0:T(8,128)(2,1)} %refs_12_.1), channel_id=1, source_target_pairs={{1,0},{0,1},{3,2},{2,3},{5,4},{4,5},{7,6},{6,7},{9,8},{8,9},{11,10... | collective-permute-start | bytes 2359304 | tf_op jit(solution)/shard_map/ppermute | solution.py:480
  3.3 7.2 %copy-start.3 = (bf16[2,1536,128]{2,1,0:T(8,128)(2,1)}, bf16[2,1536,128]{2,1,0:T(8,128)(2,1)S(1)}, u32[]{:S(2)}) copy-start(bf16[2,1536,128]{2,1,0:T(8,128)(2,1)S(1)} %collective-permute-done.refs_1_) | copy-start | bytes 2359300
  3.3 10.7 %collective-permute-start.3 = (f32[96,128]{1,0:T(8,128)S(1)}, f32[96,128]{1,0:T(8,128)S(1)}, u32[]{:S(2)}, u32[]{:S(2)}) collective-permute-start(f32[96,128]{1,0:T(8,128)S(1)} %half.1.refs_0_), channel_id=1, source_target_pairs={{0,8},{2,10},{4,12},{6,14},{8,0},{10,2},{12,4},{14,6},{16,24},{18,... | collective-permute-start | bytes 147464 | tf_op jit(solution)/shard_map/ppermute | solution.py:532
  6.2 7.7 %collective-permute-start.4 = (f32[96,128]{1,0:T(8,128)S(1)}, f32[96,128]{1,0:T(8,128)S(1)}, u32[]{:S(2)}, u32[]{:S(2)}) collective-permute-start(f32[96,128]{1,0:T(8,128)S(1)} %half.1.refs_0_), channel_id=1, source_target_pairs={{0,16},{2,18},{4,20},{6,22},{8,24},{10,26},{12,28},{14,30},{16,0},... | collective-permute-start | bytes 147464 | tf_op jit(solution)/shard_map/ppermute | solution.py:532
  8.8 5.9 %collective-permute-start.5 = (f32[96,128]{1,0:T(8,128)S(1)}, f32[96,128]{1,0:T(8,128)S(1)}, u32[]{:S(2)}, u32[]{:S(2)}) collective-permute-start(f32[96,128]{1,0:T(8,128)S(1)} %half.1.refs_0_), channel_id=1, source_target_pairs={{0,24},{2,26},{4,28},{6,30},{8,16},{10,18},{12,20},{14,22},{16,8},... | collective-permute-start | bytes 147464 | tf_op jit(solution)/shard_map/ppermute | solution.py:532
  14.7 3.2 %collective-permute-start.9 = (bf16[4,96,128]{2,1,0:T(8,128)(2,1)S(1)}, bf16[4,96,128]{2,1,0:T(8,128)(2,1)S(1)}, u32[]{:S(2)}, u32[]{:S(2)}) collective-permute-start(bf16[4,96,128]{2,1,0:T(8,128)(2,1)S(1)} %get-tuple-element.36.rows_ref.refs_0_.refs_3_), channel_id=1, source_target_pairs={{0,1},{1,0},{2,3},{3,2},{4,5},{5,4},{6,7},{7,6},{8,9},{9,8},{10,11... | collective-permute-start | bytes 294920 | tf_op jit(solution)/shard_map/ppermute | solution.py:474
  14.8 7.2 %collective-permute-start.6 = (bf16[4,96,128]{2,1,0:T(8,128)(2,1)S(1)}, bf16[4,96,128]{2,1,0:T(8,128)(2,1)S(1)}, u32[]{:S(2)}, u32[]{:S(2)}) collective-permute-start(bf16[4,96,128]{2,1,0:T(8,128)(2,1)S(1)} %get-tuple-element.36.rows_ref.refs_0_.refs_3_), channel_id=1, source_target_pairs={{0,2},{1,5},{2,0},{3,7},{4,6},{5,1},{6,4},{7,3},{8,10},{9,13},{10,... | collective-permute-start | bytes 294920 | tf_op jit(solution)/shard_map/ppermute | solution.py:492
  16.4 5.8 %collective-permute-start.7 = (bf16[4,96,128]{2,1,0:T(8,128)(2,1)S(1)}, bf16[4,96,128]{2,1,0:T(8,128)(2,1)S(1)}, u32[]{:S(2)}, u32[]{:S(2)}) collective-permute-start(bf16[4,96,128]{2,1,0:T(8,128)(2,1)S(1)} %get-tuple-element.36.rows_ref.refs_0_.refs_3_), channel_id=1, source_target_pairs={{0,4},{1,3},{2,6},{3,1},{4,0},{5,7},{6,2},{7,5},{8,12},{9,11},{10,... | collective-permute-start | bytes 294920 | tf_op jit(solution)/shard_map/ppermute | solution.py:492
  17.9 5.5 %collective-permute-start.8 = (bf16[4,96,128]{2,1,0:T(8,128)(2,1)S(1)}, bf16[4,96,128]{2,1,0:T(8,128)(2,1)S(1)}, u32[]{:S(2)}, u32[]{:S(2)}) collective-permute-start(bf16[4,96,128]{2,1,0:T(8,128)(2,1)S(1)} %get-tuple-element.36.rows_ref.refs_0_.refs_3_), channel_id=1, source_target_pairs={{0,6},{1,7},{2,4},{3,5},{4,2},{5,3},{6,0},{7,1},{8,14},{9,15},{10,... | collective-permute-start | bytes 294920 | tf_op jit(solution)/shard_map/ppermute | solution.py:492
  23.4 2.5 %collective-permute-start.10 = (bf16[4,96,128]{2,1,0:T(8,128)(2,1)S(1)}, bf16[4,96,128]{2,1,0:T(8,128)(2,1)S(1)}, u32[]{:S(2)}, u32[]{:S(2)}) collective-permute-start(bf16[4,96,128]{2,1,0:T(8,128)(2,1)S(1)} %get-tuple-element.46.refs_0_.refs_4_), channel_id=1, source_target_pairs={{0,1},{1,0},{2,3},{3,2},{4,5},{5,4},{6,7},{7,6},{8,9},{9,8},{10,11... | collective-permute-start | bytes 294920 | tf_op jit(solution)/shard_map/ppermute | solution.py:474
  23.5 2.4 %collective-permute-start.11 = (bf16[4,96,128]{2,1,0:T(8,128)(2,1)S(1)}, bf16[4,96,128]{2,1,0:T(8,128)(2,1)S(1)}, u32[]{:S(2)}, u32[]{:S(2)}) collective-permute-start(bf16[4,96,128]{2,1,0:T(8,128)(2,1)S(1)} %get-tuple-element.47.refs_1_.refs_5_), channel_id=1, source_target_pairs={{0,1},{1,0},{2,3},{3,2},{4,5},{5,4},{6,7},{7,6},{8,9},{9,8},{10,11... | collective-permute-start | bytes 294920 | tf_op jit(solution)/shard_map/ppermute | solution.py:474
  24.0 1.9 %collective-permute-start.12 = (bf16[4,96,128]{2,1,0:T(8,128)(2,1)S(1)}, bf16[4,96,128]{2,1,0:T(8,128)(2,1)S(1)}, u32[]{:S(2)}, u32[]{:S(2)}) collective-permute-start(bf16[4,96,128]{2,1,0:T(8,128)(2,1)S(1)} %get-tuple-element.51.refs_6_), channel_id=1, source_target_pairs={{0,1},{1,0},{2,3},{3,2},{4,5},{5,4},{6,7},{7,6},{8,9},{9,8},{10,11... | collective-permute-start | bytes 294920 | tf_op jit(solution)/shard_map/ppermute | solution.py:474
  31.5 4.7 %collective-permute-start.18 = (bf16[4,112,128]{2,1,0:T(8,128)(2,1)S(1)}, bf16[4,112,128]{2,1,0:T(8,128)(2,1)S(1)}, u32[]{:S(2)}, u32[]{:S(2)}) collective-permute-start(bf16[4,112,128]{2,1,0:T(8,128)(2,1)S(1)} %get-tuple-element.52.rows_ref.refs_0_.refs_2_), channel_id=1, source_target_pairs={{0,1},{1,0},{2,3},{3,2},{4,5},{5,4},{6,7},{7,6},{8,9},{9,8},{10,11... | collective-permute-start | bytes 344072 | tf_op jit(solution)/shard_map/ppermute | solution.py:474
  32.0 6.0 %collective-permute-start.15 = (bf16[4,112,128]{2,1,0:T(8,128)(2,1)S(1)}, bf16[4,112,128]{2,1,0:T(8,128)(2,1)S(1)}, u32[]{:S(2)}, u32[]{:S(2)}) collective-permute-start(bf16[4,112,128]{2,1,0:T(8,128)(2,1)S(1)} %get-tuple-element.52.rows_ref.refs_0_.refs_2_), channel_id=1, source_target_pairs={{0,2},{1,5},{2,0},{3,7},{4,6},{5,1},{6,4},{7,3},{8,10},{9,13},{10,... | collective-permute-start | bytes 344072 | tf_op jit(solution)/shard_map/ppermute | solution.py:492
  33.4 4.9 %collective-permute-start.16 = (bf16[4,112,128]{2,1,0:T(8,128)(2,1)S(1)}, bf16[4,112,128]{2,1,0:T(8,128)(2,1)S(1)}, u32[]{:S(2)}, u32[]{:S(2)}) collective-permute-start(bf16[4,112,128]{2,1,0:T(8,128)(2,1)S(1)} %get-tuple-element.52.rows_ref.refs_0_.refs_2_), channel_id=1, source_target_pairs={{0,4},{1,3},{2,6},{3,1},{4,0},{5,7},{6,2},{7,5},{8,12},{9,11},{10,... | collective-permute-start | bytes 344072 | tf_op jit(solution)/shard_map/ppermute | solution.py:492
  34.2 6.6 %collective-permute-start.17 = (bf16[4,112,128]{2,1,0:T(8,128)(2,1)S(1)}, bf16[4,112,128]{2,1,0:T(8,128)(2,1)S(1)}, u32[]{:S(2)}, u32[]{:S(2)}) collective-permute-start(bf16[4,112,128]{2,1,0:T(8,128)(2,1)S(1)} %get-tuple-element.52.rows_ref.refs_0_.refs_2_), channel_id=1, source_target_pairs={{0,6},{1,7},{2,4},{3,5},{4,2},{5,3},{6,0},{7,1},{8,14},{9,15},{10,... | collective-permute-start | bytes 344072 | tf_op jit(solution)/shard_map/ppermute | solution.py:492
  40.8 1.6 %collective-permute-start.19 = (bf16[4,112,128]{2,1,0:T(8,128)(2,1)S(1)}, bf16[4,112,128]{2,1,0:T(8,128)(2,1)S(1)}, u32[]{:S(2)}, u32[]{:S(2)}) collective-permute-start(bf16[4,112,128]{2,1,0:T(8,128)(2,1)S(1)} %get-tuple-element.57.refs_0_.refs_3_), channel_id=1, source_target_pairs={{0,1},{1,0},{2,3},{3,2},{4,5},{5,4},{6,7},{7,6},{8,9},{9,8},{10,11... | collective-permute-start | bytes 344072 | tf_op jit(solution)/shard_map/ppermute | solution.py:474
  40.9 1.5 %collective-permute-start.20 = (bf16[4,112,128]{2,1,0:T(8,128)(2,1)S(1)}, bf16[4,112,128]{2,1,0:T(8,128)(2,1)S(1)}, u32[]{:S(2)}, u32[]{:S(2)}) collective-permute-start(bf16[4,112,128]{2,1,0:T(8,128)(2,1)S(1)} %get-tuple-element.58.refs_1_.refs_4_), channel_id=1, source_target_pairs={{0,1},{1,0},{2,3},{3,2},{4,5},{5,4},{6,7},{7,6},{8,9},{9,8},{10,11... | collective-permute-start | bytes 344072 | tf_op jit(solution)/shard_map/ppermute | solution.py:474
  41.4 1.3 %collective-permute-start.21 = (bf16[4,112,128]{2,1,0:T(8,128)(2,1)S(1)}, bf16[4,112,128]{2,1,0:T(8,128)(2,1)S(1)}, u32[]{:S(2)}, u32[]{:S(2)}) collective-permute-start(bf16[4,112,128]{2,1,0:T(8,128)(2,1)S(1)} %get-tuple-element.61.refs_5_), channel_id=1, source_target_pairs={{0,1},{1,0},{2,3},{3,2},{4,5},{5,4},{6,7},{7,6},{8,9},{9,8},{10,11... | collective-permute-start | bytes 344072 | tf_op jit(solution)/shard_map/ppermute | solution.py:474
  45.4 1.3 %collective-permute-start.22 = (f32[104,128]{1,0:T(8,128)S(1)}, f32[104,128]{1,0:T(8,128)S(1)}, u32[]{:S(2)}, u32[]{:S(2)}) collective-permute-start(f32[104,128]{1,0:T(8,128)S(1)} %second_half.3.own_ref), channel_id=1, source_target_pairs={{0,1},{1,0},{2,3},{3,2},{4,5},{5,4},{6,7},{7,6},{8,9},{9,8},{10,11... | collective-permute-start | bytes 159752 | tf_op jit(solution)/shard_map/ppermute | solution.py:474
  (5 other events, 11.8 us)

commit v8 on v7

--- a/solution.py
+++ b/solution.py
@@ -59,19 +59,20 @@
     return copies
 
 
-def half_kernel(rows_ref, own_ref, sems):
-    count = own_ref.shape[0]
-    half = rows_ref.at[pl.ds(pl.multiple_of(side_of() * count, 8), count)]
-    for copy in fetch([half], [own_ref], sems):
+def round_kernel(rows_ref, out_ref, buffer, sems):
+    for copy in fetch([rows_ref], [buffer], sems):
         copy.wait()
+    out_ref[...] = buffer[...].astype(jnp.bfloat16)
 
 
 def arrange_kernel(planes, *refs):
     place = lax.axis_index("seq") // (lax.axis_size("seq") // planes)
+    mine_ref, other_ref = refs[-2:]
+    count = mine_ref.shape[1]
     for step in range(planes):
-        rows = refs[step][...]
-        refs[-2][place ^ step] = rows
-        refs[-1][place ^ step] = rows.astype(jnp.bfloat16)
+        first, second = refs[step][:count, :], refs[step][count:, :]
+        mine_ref[place ^ step] = jnp.where(side_of() == 0, first, second)
+        other_ref[place ^ step] = jnp.where(side_of() == 0, second, first)
 
 
 def gates_kernel(many, *refs):
@@ -94,68 +95,75 @@
     return (lax.axis_index("seq") % per_plane) ^ jnp.where(first, step, turned(step, bits))
 
 
+def make_maps(layer, in_ref, gain_ref, weights, out_ref):
+    channels = in_ref.shape[1]
+
+    def store(row, value):
+        high = value.astype(jnp.bfloat16)
+        rows = value.shape[0]
+        out_ref[row : row + rows, :channels] = high
+        out_ref[row : row + rows, channels:] = (value - high.astype(jnp.float32)).astype(
+            jnp.bfloat16
+        )
+        return row + rows
+
+    base = in_ref[layer]
+    scaled = base.astype(jnp.float32) * gain_ref[layer : layer + 1, :]
+    high = scaled.astype(jnp.bfloat16)
+    low = (scaled - high.astype(jnp.float32)).astype(jnp.bfloat16)
+    both = jnp.concatenate([high, low], axis=0)
+    row = 0
+    for first in range(0, weights.shape[0], 2):
+        product = dot(both, cat([weights[first], weights[first + 1]], 1))
+        row = store(row, (product[:channels] + product[channels:]).T)
+    row = store(row, dot_nt(base, base))
+    eye = lax.broadcasted_iota(jnp.int32, (channels, channels), 0) == lax.broadcasted_iota(
+        jnp.int32, (channels, channels), 1
+    )
+    store(row, jnp.where(eye, 1.0, 0.0))
+
+
 def prepare_kernel(pieces, in_src, gain_src, *refs):
     sources, refs = refs[: 3 * pieces], refs[3 * pieces :]
-    maps_refs, (in_ref, gain_ref, query_ref, buffer, sems) = refs[:-5], refs[-5:]
-    layers, channels, _ = in_ref.shape
+    maps_ref, in_ref, gain_ref, query_ref, later_ref, buffer, sems = refs
+    both = list(sources[: 2 * pieces])
+    near = [in_src, gain_src] + [source.at[0] for source in both]
     targets = [in_ref, gain_ref] + [buffer.at[at] for at in range(2 * pieces)]
+    near += list(sources[2 * pieces :]) + [source.at[1] for source in both]
     targets += [query_ref.at[at] for at in range(pieces)]
-    copies = fetch([in_src, gain_src, *sources], targets, sems)
+    targets += [later_ref.at[at] for at in range(2 * pieces)]
+    copies = fetch(near, targets, sems)
     for copy in copies[: 2 + 2 * pieces]:
         copy.wait()
-    eye = lax.broadcasted_iota(jnp.int32, (channels, channels), 0) == lax.broadcasted_iota(
-        jnp.int32, (channels, channels), 1
-    )
-    for layer in range(layers):
-        out_ref = maps_refs[layer]
-
-        def store(row, value, out_ref=out_ref):
-            high = value.astype(jnp.bfloat16)
-            rows = value.shape[0]
-            out_ref[row : row + rows, :channels] = high
-            out_ref[row : row + rows, channels:] = (value - high.astype(jnp.float32)).astype(
-                jnp.bfloat16
-            )
-            return row + rows
-
-        base = in_ref[layer]
-        scaled = base.astype(jnp.float32) * gain_ref[layer : layer + 1, :]
-        high = scaled.astype(jnp.bfloat16)
-        low = (scaled - high.astype(jnp.float32)).astype(jnp.bfloat16)
-        both = jnp.concatenate([high, low], axis=0)
-        row = 0
-        for first in range(0, 2 * pieces, 2):
-            pair = cat([buffer[first, layer], buffer[first + 1, layer]], 1)
-            product = dot(both, pair)
-            row = store(row, (product[:channels] + product[channels:]).T)
-        row = store(row, dot_nt(base, base))
-        store(row, jnp.where(eye, 1.0, 0.0))
+    make_maps(0, in_ref, gain_ref, buffer, maps_ref)
     for copy in copies[2 + 2 * pieces :]:
         copy.wait()
 
 
 def prepare(in_proj, attn_gain, key_pieces, value_pieces, query_pieces):
     pieces = len(key_pieces)
-    layers, channels, features = in_proj.shape
+    _, channels, features = in_proj.shape
     columns = key_pieces[0].shape[2]
     rows = 2 * pieces * columns + 2 * channels
-    *maps, in_all, gains, query_all = on_chip(
+    buffer = (2 * pieces, features, columns)
+    return on_chip(
         functools.partial(prepare_kernel, pieces),
         "prepare",
         [],
-        [((rows, 2 * channels), jnp.bfloat16)] * layers
-        + [
+        [
+            ((rows, 2 * channels), jnp.bfloat16),
             (in_proj.shape, in_proj.dtype),
             (attn_gain.shape, attn_gain.dtype),
             ((pieces, *query_pieces[0].shape), jnp.bfloat16),
+            (buffer, jnp.bfloat16),
         ],
         far=[in_proj, attn_gain, *key_pieces, *value_pieces, *query_pieces],
-        scratch=[
-            pltpu.VMEM((2 * pieces, layers, features, columns), jnp.bfloat16),
-            pltpu.SemaphoreType.DMA((3 * pieces + 2,)),
-        ],
-    )
-    return maps, (in_all, gains, query_all)
+        scratch=[pltpu.VMEM(buffer, jnp.bfloat16), pltpu.SemaphoreType.DMA((5 * pieces + 2,))],
+    )
+
+
+def second_maps_kernel(after_ref, in_ref, gain_ref, weights_ref, out_ref):
+    make_maps(1, in_ref, gain_ref, weights_ref, out_ref)
 
 
 def queries_kernel(layer, planes, rows_ref, in_ref, gain_ref, query_ref, hidden_ref, out_ref):
@@ -385,14 +393,14 @@
     token = lax.broadcasted_iota(jnp.int32, (count, 1), 0)
     if last:
         held_ref, held_log_ref, out_ref = refs[:3]
-        plane = member // per_plane
         before = member - 1 + side
         edge = chosen_rows(others, per_plane, jnp.maximum(before, 0), slice(count, count + 16))
         edge = jnp.where(before >= 0, edge[0:2] + edge[2:4] + edge[4:6], 0.0)
         edge_log = edge[1:2]
-        first = (latent_ref[plane, :8, :][:1] - edge[0:1]) * jnp.exp(-edge_log)
-        values = jnp.where(token == 0, first, pltpu.roll(held_ref[plane], 1, 0))
-        first_log = jnp.where(token == 0, edge_log, pltpu.roll(held_log_ref[plane], 1, 0))
+        start = pl.multiple_of(side * count, 8)
+        first = (latent_ref[pl.ds(start, 8), :][:1] - edge[0:1]) * jnp.exp(-edge_log)
+        values = jnp.where(token == 0, first, pltpu.roll(held_ref[...], 1, 0))
+        first_log = jnp.where(token == 0, edge_log, pltpu.roll(held_log_ref[...], 1, 0))
         result = (values - shift_all) * jnp.exp(-log_all)
         term = -(first_log + log_all) - 0.5 * (result * result)
         loglik = jnp.sum(term.T, axis=0, keepdims=True) * (1.0 / channels) - 0.5 * math.log(
@@ -402,18 +410,25 @@
         out_ref[count:, :count] = jnp.broadcast_to(loglik, (8, count))
         return
     held_ref, held_log_ref, narrow_ref = refs[:3]
+    own = latent_ref[pl.ds(pl.multiple_of(side * count, 8), count), :]
     for p in range(planes):
         shift_mu = shift_all[p * count : (p + 1) * count]
         log_scale = log_all[p * count : (p + 1) * count]
         following = p * per_plane + member % per_plane + side
         after = chosen_rows(others, per_plane, jnp.minimum(following, members - 1), slice(0, 16))
-        values = pltpu.roll(latent_ref[p], count - 1, 0)
+        here = member // per_plane == p
+        values = jnp.where(here, own, rows_of[False][0][p, :count, :].astype(jnp.float32))
+        values = pltpu.roll(values, count - 1, 0)
         values = jnp.where(token == count - 1, after[:1], values)
         result = (values - shift_mu) * jnp.exp(-log_scale)
         if p == planes - 1:
             result = jnp.where((following == members) & (token == count - 1), 0.0, result)
-        held_ref[p] = result
-        held_log_ref[p] = log_scale
+
+        @pl.when(here)
+        def keep(result=result, log_scale=log_scale):
+            held_ref[...] = result
+            held_log_ref[...] = log_scale
+
         edge = jnp.concatenate([shift_mu[count - 1 :], log_scale[count - 1 :]], axis=0)
         terms = []
         for _ in range(3):
@@ -432,8 +447,8 @@
         results = [((count + 8, channels), jnp.float32)]
     else:
         results = [
-            ((planes, count, channels), jnp.float32),
-            ((planes, count, channels), jnp.float32),
+            ((count, channels), jnp.float32),
+            ((count, channels), jnp.float32),
             ((planes, count + 16, channels), jnp.bfloat16),
         ]
     scratch = [pltpu.VMEM((cfg["features"], param_pieces[0].shape[2]), jnp.bfloat16)]
@@ -492,7 +507,7 @@
             arrived.append(lax.ppermute(mine, ("seq", "head"), pairs))
         return arrived
 
-    def run(layer, mine, maps, made, latents, *rest):
+    def run(layer, mine, sibling, maps, made, latents, *rest):
         cfg = {
             "layer": layer,
             "last": layer == 1,
@@ -504,48 +519,66 @@
         }
         hidden, queries = made
         arrived = in_plane(mine)
-        others = [swap(mine)]
-        sums = attend(cfg, maps, queries, [(mine, 0, False), (others[0], 0, True)])
-        mines = [mine]
-        if per_plane > 1:
-            arrived = gate_all(arrived, sums)
-            mines += arrived
-            others += [swap(piece) for piece in arrived]
-        kinds = [(step, False) for step in range(1, per_plane)]
-        kinds += [(step, True) for step in range(1, per_plane)]
         if per_plane == 4:
-            sums = attend(cfg, maps, queries, [(mines[1], 1, False), (mines[2], 2, False)], sums)
-            kinds = kinds[2:]
+            early = [(mine, 0, False)] + ([(sibling, 0, True)] if layer == 0 else [])
+            sums = attend(cfg, maps, queries, early)
+            first, second, *own = gate_all(arrived[:2] + ([] if layer == 0 else [mine]), sums)
+            others = [sibling if layer == 0 else swap(own[0]), swap(first)]
+            if layer == 0:
+                others.append(swap(second))
+            sums = attend(cfg, maps, queries, [(first, 1, False), (second, 2, False)], sums)
+            third, *again = gate_all(arrived[2:] + ([] if layer == 0 else [second]), sums)
+            if layer == 1:
+                others.append(swap(again[0]))
+            others.append(swap(third))
+            more = [(third, 3, False)] + ([] if layer == 0 else [(others[0], 0, True)])
+            sums = attend(cfg, maps, queries, more + [(others[1], 1, True)], sums)
+            mines = [mine, first, second, third]
+            kinds = [(2, True), (3, True)]
+        else:
+            others = [swap(mine) if layer == 1 else sibling]
+            sums = attend(cfg, maps, queries, [(mine, 0, False), (others[0], 0, True)])
+            mines = [mine]
+            if per_plane > 1:
+                arrived = gate_all(arrived, sums)
+                mines += arrived
+                others += [swap(piece) for piece in arrived]
+            kinds = [(step, False) for step in range(1, per_plane)]
+            kinds += [(step, True) for step in range(1, per_plane)]
         return second_half(
             cfg, tuple(kinds), maps, queries, sums, hidden, param_gain, latents, mines, others, mix_pieces, param_pieces, *rest
         )
 
-    (own,) = on_chip(
-        half_kernel,
-        "half",
+    (rounded,) = on_chip(
+        round_kernel,
+        "round",
         [],
-        [((count, channels), jnp.float32)],
+        [(latents.shape, jnp.bfloat16)],
         far=[latents],
-        scratch=[pltpu.SemaphoreType.DMA((1,))],
-    )
-    parts = [own] + [
-        lax.ppermute(own, "seq", [(i, i ^ (b * per_plane)) for i in range(members)])
+        scratch=[pltpu.VMEM(latents.shape, jnp.float32), pltpu.SemaphoreType.DMA((1,))],
+    )
+    parts = [rounded] + [
+        lax.ppermute(rounded, "seq", [(i, i ^ (b * per_plane)) for i in range(members)])
         for b in range(1, planes)
     ]
     key_pieces, value_pieces = pieces_of(key_proj), pieces_of(value_proj)
     query_pieces, mix_pieces = pieces_of(query_proj), pieces_of(mix_proj)
     param_pieces = pieces_of(param_proj)
-    maps, weights = prepare(in_proj, attn_gain, key_pieces, value_pieces, query_pieces)
-    wide, mine = on_chip(
+    maps, *weights, later = prepare(in_proj, attn_gain, key_pieces, value_pieces, query_pieces)
+    shape = (planes, count, channels)
+    mine, sibling = on_chip(
         functools.partial(arrange_kernel, planes),
         "arrange",
-        [*parts, maps[0]],
-        [((planes, count, channels), jnp.float32), ((planes, count, channels), jnp.bfloat16)],
+        [*parts, maps],
+        [(shape, jnp.bfloat16), (shape, jnp.bfloat16)],
     )
     made = make_queries(0, planes, count, mine, weights)
-    held, held_log, mine = run(0, mine, maps[0], made, wide)
+    held, held_log, mine = run(0, mine, sibling, maps, made, latents)
+    (maps,) = on_chip(
+        second_maps_kernel, "second_maps", [mine, *weights[:2], later], [(maps.shape, maps.dtype)]
+    )
     made = make_queries(1, 1, count, mine, weights)
-    (packed,) = run(1, mine, maps[1], made, wide, (held, held_log))
+    (packed,) = run(1, mine, None, maps, made, latents, (held, held_log))
     final_latent, token_loglik = on_chip(
         finish_kernel,
         "finish",

time: 47.6 us -> 45.9 us (0.964)
  waiting for transfers between devices: 7.35 us -> 5.07 us
    ppermute x6, waiting for transfers between devices: 4.98 us -> 2.08 us  [in_plane(): arrived.append(lax.ppermute(mine, ('seq', 'head'), pairs))]
    ppermute x3, waiting for transfers between devices: 0.73 us -> 1.53 us  [body(): lax.ppermute(rounded, 'seq', [(i, i ^ b * per_plane) for i in range(membe...]
    pallas_call x14 -> x19, Pallas kernels: 21.1 us -> 21.5 us  [on_chip(): pl.pallas_call(kernel, in_specs=[pl.BlockSpec(memory_space=pltpu.VMEM)] *...]
    ppermute x9 -> x8, starting transfers between devices: 2.12 us -> 2.35 us  [swap(): return lax.ppermute(array, 'head', [(i, i ^ 1) for i in range(ways)])]
    ppermute x9 -> x8, waiting for transfers between devices: 1.35 us -> 1.27 us  [swap(): return lax.ppermute(array, 'head', [(i, i ^ 1) for i in range(ways)])]
  transfers between devices with their start and end apart: 23 -> 22, of which waited for: 9 -> 5; matrix products, arithmetic and copies ran while one was open for 0% -> 0% of each run, Pallas kernels for 26% -> 33%
where the time goes in v8:
time: 45.9 us; the launch traced here: 45.8 us
  Pallas kernels  21.5 us (47%)
  starting transfers between devices  18.2 us (40%)
  waiting for transfers between devices  5.07 us (11%)
  between operations  0.92 us (2%)
    pallas_call x19, Pallas kernels, on_chip(): pl.pallas_call(kernel, in_specs=[pl.BlockSpec(memory_space=pltpu.VMEM)] *...  21.5 us
    ppermute x3, starting transfers between devices, body(): lax.ppermute(rounded, 'seq', [(i, i ^ b * per_plane) for i in range(membe...  7.21 us
    ppermute x6, starting transfers between devices, in_plane(): arrived.append(lax.ppermute(mine, ('seq', 'head'), pairs))  7.11 us
    ppermute x8, starting transfers between devices, swap(): return lax.ppermute(array, 'head', [(i, i ^ 1) for i in range(ways)])  2.35 us
    ppermute x6, waiting for transfers between devices, in_plane(): arrived.append(lax.ppermute(mine, ('seq', 'head'), pairs))  2.08 us
    ppermute x5, starting transfers between devices, pieces_of(): lax.ppermute(array, 'head', [((i + j) % ways, i) for i in range(ways)])  1.54 us
    ppermute x3, waiting for transfers between devices, body(): lax.ppermute(rounded, 'seq', [(i, i ^ b * per_plane) for i in range(membe...  1.53 us
    ppermute x8, waiting for transfers between devices, swap(): return lax.ppermute(array, 'head', [(i, i ^ 1) for i in range(ways)])  1.27 us
  transfers between devices with their start and end apart: 22, of which 5 were waited for; matrix products, arithmetic and copies ran while one was open for 0% of the time, Pallas kernels for 33%

profile of v8, /device:TPU:0, one launch (start us, length us, event | category | flops | bytes accessed | tf_op | source)
XLA Modules:
  0.0 45.8 jit_solution(435176184552360043)
XLA Ops:
  2.2 0.9 %round.1.refs_0_ = bf16[192,128]{1,0:T(8,128)(2,1)S(1)} custom-call(f32[192,128]{1,0:T(8,128)} %latent_ref.3), custom_call_target="tpu_custom_call" | custom-call | tf_op jit(solution)/shard_map/round/pallas_call | solution.py:42
  3.3 2.9 %collective-permute-start.3 = (bf16[192,128]{1,0:T(8,128)(2,1)S(1)}, bf16[192,128]{1,0:T(8,128)(2,1)S(1)}, u32[]{:S(2)}, u32[]{:S(2)}) collective-permute-start(bf16[192,128]{1,0:T(8,128)(2,1)S(1)} %round.1.refs_0_), channel_id=1, source_target_pairs={{0,8},{2,10},{4,12},{6,14},{8,0},{10,2},{12,4},{14,6},{16,24},{18,... | collective-permute-start | bytes 147464 | tf_op jit(solution)/shard_map/ppermute | solution.py:561
  6.2 2.6 %collective-permute-start.4 = (bf16[192,128]{1,0:T(8,128)(2,1)S(1)}, bf16[192,128]{1,0:T(8,128)(2,1)S(1)}, u32[]{:S(2)}, u32[]{:S(2)}) collective-permute-start(bf16[192,128]{1,0:T(8,128)(2,1)S(1)} %round.1.refs_0_), channel_id=1, source_target_pairs={{0,16},{2,18},{4,20},{6,22},{8,24},{10,26},{12,28},{14,30},{16,0},... | collective-permute-start | bytes 147464 | tf_op jit(solution)/shard_map/ppermute | solution.py:561
  8.8 1.7 %collective-permute-start.5 = (bf16[192,128]{1,0:T(8,128)(2,1)S(1)}, bf16[192,128]{1,0:T(8,128)(2,1)S(1)}, u32[]{:S(2)}, u32[]{:S(2)}) collective-permute-start(bf16[192,128]{1,0:T(8,128)(2,1)S(1)} %round.1.refs_0_), channel_id=1, source_target_pairs={{0,24},{2,26},{4,28},{6,30},{8,16},{10,18},{12,20},{14,22},{16,8},... | collective-permute-start | bytes 147464 | tf_op jit(solution)/shard_map/ppermute | solution.py:561
  10.5 2.7 %prepare.1 = (bf16[768,256]{1,0:T(8,128)(2,1)S(1)}, bf16[2,128,1536]{2,1,0:T(8,128)(2,1)S(1)}, f32[2,1536]{1,0:T(2,128)S(1)}, bf16[2,2,1536,128]{3,2,1,0:T(8,128)(2,1)S(1)}, bf16[4,1536,128]{2,1,0:T(8,128)(2,1)S(1)}) custom-call(bf16[2,128,1536]{2,1,0:T(8,128)(2,1)} %in_src.1, f32[2,1536]{1,0:T(2,128)} %gain_src.1, bf16[2,1536,128]{2,1,0:T(8,128)(2,1)} %refs_0_.1, ...), custom_call_target="tpu_custom_call" | custom-call | tf_op jit(solution)/shard_map/prepare/pallas_call | solution.py:42
  13.2 1.5 %collective-permute-done.5.refs_3_ = bf16[192,128]{1,0:T(8,128)(2,1)S(1)} collective-permute-done((bf16[192,128]{1,0:T(8,128)(2,1)S(1)}, bf16[192,128]{1,0:T(8,128)(2,1)S(1)}, u32[]{:S(2)}, u32[]{:S(2)}) %collective-permute-start.5) | collective-permute-done | bytes 49184 | tf_op jit(solution)/shard_map/ppermute | solution.py:561
  14.8 1.6 %collective-permute-start.7 = (bf16[4,96,128]{2,1,0:T(8,128)(2,1)S(1)}, bf16[4,96,128]{2,1,0:T(8,128)(2,1)S(1)}, u32[]{:S(2)}, u32[]{:S(2)}) collective-permute-start(bf16[4,96,128]{2,1,0:T(8,128)(2,1)S(1)} %get-tuple-element.41.rows_ref.refs_0_.refs_3_), channel_id=1, source_target_pairs={{0,2},{1,5},{2,0},{3,7},{4,6},{5,1},{6,4},{7,3},{8,10},{9,13},{10,... | collective-permute-start | bytes 294920 | tf_op jit(solution)/shard_map/ppermute | solution.py:507
  16.3 1.5 %collective-permute-start.8 = (bf16[4,96,128]{2,1,0:T(8,128)(2,1)S(1)}, bf16[4,96,128]{2,1,0:T(8,128)(2,1)S(1)}, u32[]{:S(2)}, u32[]{:S(2)}) collective-permute-start(bf16[4,96,128]{2,1,0:T(8,128)(2,1)S(1)} %get-tuple-element.41.rows_ref.refs_0_.refs_3_), channel_id=1, source_target_pairs={{0,4},{1,3},{2,6},{3,1},{4,0},{5,7},{6,2},{7,5},{8,12},{9,11},{10,... | collective-permute-start | bytes 294920 | tf_op jit(solution)/shard_map/ppermute | solution.py:507
  18.3 1.7 %queries.2 = (f32[384,1536]{1,0:T(8,128)S(1)}, bf16[1,1536,256]{2,1,0:T(8,128)(2,1)S(1)}) custom-call(bf16[4,96,128]{2,1,0:T(8,128)(2,1)S(1)} %get-tuple-element.41.rows_ref.refs_0_.refs_3_, bf16[2,128,1536]{2,1,0:T(8,128)(2,1)S(1)} %get-tuple-element.42.in_ref, f32[2,1536]{1,0:T(2,128)S(1)} %get-tuple-element.43.gain_ref, ...), custom_call_target="tpu_custom_call" | custom-call | tf_op jit(solution)/shard_map/queries/pallas_call | solution.py:42
  20.0 1.8 %attend.6 = (f32[1,1536,256]{2,1,0:T(8,128)S(1)}, f32[1,1536,128]{2,1,0:T(8,128)S(1)}, f32[1,1536,64]{2,1,0:T(8,128)S(1)}) custom-call(bf16[768,256]{1,0:T(8,128)(2,1)S(1)} %get-tuple-element.40.refs_4_.maps_ref, bf16[1,1536,256]{2,1,0:T(8,128)(2,1)S(1)} %get-tuple-element.45.query_ref, bf16[4,96,128]{2,1,0:T(8,128)(2,1)S(1)} %get-tuple-element.41.rows_ref.refs_0_.refs_3_, ...), custom_call_target="tpu_custom_call" | custom-call | tf_op jit(solution)/shard_map/attend/pallas_call | solution.py:42
  21.9 1.8 %attend.7 = (f32[1,1536,256]{2,1,0:T(8,128)S(1)}, f32[1,1536,128]{2,1,0:T(8,128)S(1)}, f32[1,1536,64]{2,1,0:T(8,128)S(1)}) custom-call(bf16[768,256]{1,0:T(8,128)(2,1)S(1)} %get-tuple-element.40.refs_4_.maps_ref, bf16[1,1536,256]{2,1,0:T(8,128)(2,1)S(1)} %get-tuple-element.45.query_ref, bf16[4,96,128]{2,1,0:T(8,128)(2,1)S(1)} %get-tuple-element.51.refs_0_.refs_4_, ...), custom_call_target="tpu_custom_call" | custom-call | tf_op jit(solution)/shard_map/attend/pallas_call | solution.py:42
  24.4 1.8 %attend.8 = (f32[1,1536,256]{2,1,0:T(8,128)S(1)}, f32[1,1536,128]{2,1,0:T(8,128)S(1)}, f32[1,1536,64]{2,1,0:T(8,128)S(1)}) custom-call(bf16[768,256]{1,0:T(8,128)(2,1)S(1)} %get-tuple-element.40.refs_4_.maps_ref, bf16[1,1536,256]{2,1,0:T(8,128)(2,1)S(1)} %get-tuple-element.45.query_ref, bf16[4,96,128]{2,1,0:T(8,128)(2,1)S(1)} %gate.5.refs_0_.refs_6_, ...), custom_call_target="tpu_custom_call" | custom-call | tf_op jit(solution)/shard_map/attend/pallas_call | solution.py:42
  26.3 3.7 %second_half.2 = (f32[96,128]{1,0:T(8,128)S(1)}, f32[96,128]{1,0:T(8,128)S(1)}, bf16[4,112,128]{2,1,0:T(8,128)(2,1)S(1)}) custom-call(bf16[768,256]{1,0:T(8,128)(2,1)S(1)} %get-tuple-element.40.refs_4_.maps_ref, bf16[1,1536,256]{2,1,0:T(8,128)(2,1)S(1)} %get-tuple-element.45.query_ref, f32[384,1536]{1,0:T(8,128)S(1)} %get-tuple-element.46.hidden_ref, ...), custom_call_target="tpu_custom_call" | custom-call | tf_op jit(solution)/shard_map/second_half/pallas_call | solution.py:42
  30.0 1.6 %collective-permute-start.15 = (bf16[4,112,128]{2,1,0:T(8,128)(2,1)S(1)}, bf16[4,112,128]{2,1,0:T(8,128)(2,1)S(1)}, u32[]{:S(2)}, u32[]{:S(2)}) collective-permute-start(bf16[4,112,128]{2,1,0:T(8,128)(2,1)S(1)} %get-tuple-element.59.after_ref.rows_ref.refs_0_.refs_2_), channel_id=1, source_target_pairs={{0,2},{1,5},{2,0},{3,7},{4,6},{5,1},{6,4},{7,3},{8,10},{9,13},{10,... | collective-permute-start | bytes 344072 | tf_op jit(solution)/shard_map/ppermute | solution.py:507
  31.6 1.5 %collective-permute-start.16 = (bf16[4,112,128]{2,1,0:T(8,128)(2,1)S(1)}, bf16[4,112,128]{2,1,0:T(8,128)(2,1)S(1)}, u32[]{:S(2)}, u32[]{:S(2)}) collective-permute-start(bf16[4,112,128]{2,1,0:T(8,128)(2,1)S(1)} %get-tuple-element.59.after_ref.rows_ref.refs_0_.refs_2_), channel_id=1, source_target_pairs={{0,4},{1,3},{2,6},{3,1},{4,0},{5,7},{6,2},{7,5},{8,12},{9,11},{10,... | collective-permute-start | bytes 344072 | tf_op jit(solution)/shard_map/ppermute | solution.py:507
  33.6 0.7 %queries.3 = (f32[96,1536]{1,0:T(8,128)S(1)}, bf16[1,384,256]{2,1,0:T(8,128)(2,1)S(1)}) custom-call(bf16[4,112,128]{2,1,0:T(8,128)(2,1)S(1)} %get-tuple-element.59.after_ref.rows_ref.refs_0_.refs_2_, bf16[2,128,1536]{2,1,0:T(8,128)(2,1)S(1)} %get-tuple-element.42.in_ref, f32[2,1536]{1,0:T(2,128)S(1)} %get-tuple-element.43.gain_ref, ...), custom_call_target="tpu_custom_call" | custom-call | tf_op jit(solution)/shard_map/queries/pallas_call | solution.py:42
  34.3 0.8 %second_maps.1.maps_ref = bf16[768,256]{1,0:T(8,128)(2,1)S(1)} custom-call(bf16[4,112,128]{2,1,0:T(8,128)(2,1)S(1)} %get-tuple-element.59.after_ref.rows_ref.refs_0_.refs_2_, bf16[2,128,1536]{2,1,0:T(8,128)(2,1)S(1)} %get-tuple-element.42.in_ref, f32[2,1536]{1,0:T(2,128)S(1)} %get-tuple-element.43.gain_ref, ...), custom_call_target="tpu_custom_call" | custom-call | tf_op jit(solution)/shard_map/second_maps/pallas_call | solution.py:42
  35.1 0.7 %attend.9 = (f32[1,384,256]{2,1,0:T(8,128)S(1)}, f32[1,384,128]{2,1,0:T(8,128)S(1)}) custom-call(bf16[768,256]{1,0:T(8,128)(2,1)S(1)} %second_maps.1.maps_ref, bf16[1,384,256]{2,1,0:T(8,128)(2,1)S(1)} %get-tuple-element.61.query_ref, bf16[4,112,128]{2,1,0:T(8,128)(2,1)S(1)} %get-tuple-element.59.after_ref.rows_ref.refs_0_.refs_2_), custom_call_target="tpu_custom_call" | custom-call | tf_op jit(solution)/shard_map/attend/pallas_call | solution.py:42
  35.8 2.1 %collective-permute-done.16.refs_1_ = bf16[4,112,128]{2,1,0:T(8,128)(2,1)S(1)} collective-permute-done((bf16[4,112,128]{2,1,0:T(8,128)(2,1)S(1)}, bf16[4,112,128]{2,1,0:T(8,128)(2,1)S(1)}, u32[]{:S(2)}, u32[]{:S(2)}) %collective-permute-start.16) | collective-permute-done | bytes 114720 | tf_op jit(solution)/shard_map/ppermute | solution.py:507
  38.0 1.0 %attend.10 = (f32[1,384,256]{2,1,0:T(8,128)S(1)}, f32[1,384,128]{2,1,0:T(8,128)S(1)}) custom-call(bf16[768,256]{1,0:T(8,128)(2,1)S(1)} %second_maps.1.maps_ref, bf16[1,384,256]{2,1,0:T(8,128)(2,1)S(1)} %get-tuple-element.61.query_ref, bf16[4,112,128]{2,1,0:T(8,128)(2,1)S(1)} %get-tuple-element.66.refs_0_.refs_3_, ...), custom_call_target="tpu_custom_call" | custom-call | tf_op jit(solution)/shard_map/attend/pallas_call | solution.py:42
  40.5 1.4 %attend.11 = (f32[1,384,256]{2,1,0:T(8,128)S(1)}, f32[1,384,128]{2,1,0:T(8,128)S(1)}) custom-call(bf16[768,256]{1,0:T(8,128)(2,1)S(1)} %second_maps.1.maps_ref, bf16[1,384,256]{2,1,0:T(8,128)(2,1)S(1)} %get-tuple-element.61.query_ref, bf16[4,112,128]{2,1,0:T(8,128)(2,1)S(1)} %get-tuple-element.69.refs_0_.refs_5_, ...), custom_call_target="tpu_custom_call" | custom-call | tf_op jit(solution)/shard_map/attend/pallas_call | solution.py:42
  41.9 1.9 %second_half.3.own_ref = f32[104,128]{1,0:T(8,128)S(1)} custom-call(bf16[768,256]{1,0:T(8,128)(2,1)S(1)} %second_maps.1.maps_ref, bf16[1,384,256]{2,1,0:T(8,128)(2,1)S(1)} %get-tuple-element.61.query_ref, f32[96,1536]{1,0:T(8,128)S(1)} %get-tuple-element.62.hidden_ref, f32[2,1536]{1,0:T(2,128)S(1)} %copy-done.3, f32[192,128]{1,0:T(8,128)S(1)} %copy-done.2, ...), custom_call_target="tpu_custom_call" | custom-call | tf_op jit(solution)/shard_map/second_half/pallas_call | solution.py:42
  44.2 0.9 %collective-permute-done.21.other_ref = f32[104,128]{1,0:T(8,128)S(1)} collective-permute-done((f32[104,128]{1,0:T(8,128)S(1)}, f32[104,128]{1,0:T(8,128)S(1)}, u32[]{:S(2)}, u32[]{:S(2)}) %collective-permute-start.21) | collective-permute-done | bytes 53280 | tf_op jit(solution)/shard_map/ppermute | solution.py:489
  45.1 0.7 %finish.1 = (f32[192,128]{1,0:T(8,128)}, f32[1,192]{1,0:T(1,128)}) custom-call(f32[104,128]{1,0:T(8,128)S(1)} %second_half.3.own_ref, f32[104,128]{1,0:T(8,128)S(1)} %collective-permute-done.21.other_ref), custom_call_target="tpu_custom_call" | custom-call | tf_op jit(solution)/shard_map/finish/pallas_call | solution.py:42
  (53 shorter events, 5.6 us)
Async XLA Ops:
  0.6 2.6 %collective-permute-start = (bf16[2,1536,128]{2,1,0:T(8,128)(2,1)}, bf16[2,1536,128]{2,1,0:T(8,128)(2,1)S(1)}, u32[]{:S(2)}, u32[]{:S(2)}) collective-permute-start(bf16[2,1536,128]{2,1,0:T(8,128)(2,1)} %refs_0_.1), channel_id=1, source_target_pairs={{1,0},{0,1},{3,2},{2,3},{5,4},{4,5},{7,6},{6,7},{9,8},{8,9},{11,10... | collective-permute-start | bytes 2359304 | tf_op jit(solution)/shard_map/ppermute | solution.py:495
  1.1 5.1 %collective-permute-start.1 = (bf16[2,1536,128]{2,1,0:T(8,128)(2,1)}, bf16[2,1536,128]{2,1,0:T(8,128)(2,1)S(1)}, u32[]{:S(2)}, u32[]{:S(2)}) collective-permute-start(bf16[2,1536,128]{2,1,0:T(8,128)(2,1)} %refs_2_.1), channel_id=1, source_target_pairs={{1,0},{0,1},{3,2},{2,3},{5,4},{4,5},{7,6},{6,7},{9,8},{8,9},{11,10... | collective-permute-start | bytes 2359304 | tf_op jit(solution)/shard_map/ppermute | solution.py:495
  1.2 7.6 %collective-permute-start.2 = (bf16[2,1536,128]{2,1,0:T(8,128)(2,1)}, bf16[2,1536,128]{2,1,0:T(8,128)(2,1)S(1)}, u32[]{:S(2)}, u32[]{:S(2)}) collective-permute-start(bf16[2,1536,128]{2,1,0:T(8,128)(2,1)} %refs_4_.1), channel_id=1, source_target_pairs={{1,0},{0,1},{3,2},{2,3},{5,4},{4,5},{7,6},{6,7},{9,8},{8,9},{11,10... | collective-permute-start | bytes 2359304 | tf_op jit(solution)/shard_map/ppermute | solution.py:495
  1.7 24.6 %collective-permute-start.12 = (bf16[2,128,1536]{2,1,0:T(8,128)(2,1)}, bf16[2,128,1536]{2,1,0:T(8,128)(2,1)S(1)}, u32[]{:S(2)}, u32[]{:S(2)}) collective-permute-start(bf16[2,128,1536]{2,1,0:T(8,128)(2,1)} %refs_10_.1), channel_id=1, source_target_pairs={{1,0},{0,1},{3,2},{2,3},{5,4},{4,5},{7,6},{6,7},{9,8},{8,9},{11,10... | collective-permute-start | bytes 2359304 | tf_op jit(solution)/shard_map/ppermute | solution.py:495
  1.7 24.5 %collective-permute-start.13 = (bf16[2,768,256]{2,1,0:T(8,128)(2,1)}, bf16[2,768,256]{2,1,0:T(8,128)(2,1)S(1)}, u32[]{:S(2)}, u32[]{:S(2)}) collective-permute-start(bf16[2,768,256]{2,1,0:T(8,128)(2,1)} %refs_12_.1), channel_id=1, source_target_pairs={{1,0},{0,1},{3,2},{2,3},{5,4},{4,5},{7,6},{6,7},{9,8},{8,9},{11,10... | collective-permute-start | bytes 2359304 | tf_op jit(solution)/shard_map/ppermute | solution.py:495
  3.3 7.2 %copy-start.4 = (bf16[2,1536,128]{2,1,0:T(8,128)(2,1)}, bf16[2,1536,128]{2,1,0:T(8,128)(2,1)S(1)}, u32[]{:S(2)}) copy-start(bf16[2,1536,128]{2,1,0:T(8,128)(2,1)S(1)} %collective-permute-done.refs_1_) | copy-start | bytes 2359300
  3.3 9.9 %collective-permute-start.3 = (bf16[192,128]{1,0:T(8,128)(2,1)S(1)}, bf16[192,128]{1,0:T(8,128)(2,1)S(1)}, u32[]{:S(2)}, u32[]{:S(2)}) collective-permute-start(bf16[192,128]{1,0:T(8,128)(2,1)S(1)} %round.1.refs_0_), channel_id=1, source_target_pairs={{0,8},{2,10},{4,12},{6,14},{8,0},{10,2},{12,4},{14,6},{16,24},{18,... | collective-permute-start | bytes 147464 | tf_op jit(solution)/shard_map/ppermute | solution.py:561
  6.2 4.3 %copy-start.5 = (bf16[2,1536,128]{2,1,0:T(8,128)(2,1)}, bf16[2,1536,128]{2,1,0:T(8,128)(2,1)S(1)}, u32[]{:S(2)}) copy-start(bf16[2,1536,128]{2,1,0:T(8,128)(2,1)S(1)} %collective-permute-done.1.refs_3_) | copy-start | bytes 2359300
  6.2 7.0 %collective-permute-start.4 = (bf16[192,128]{1,0:T(8,128)(2,1)S(1)}, bf16[192,128]{1,0:T(8,128)(2,1)S(1)}, u32[]{:S(2)}, u32[]{:S(2)}) collective-permute-start(bf16[192,128]{1,0:T(8,128)(2,1)S(1)} %round.1.refs_0_), channel_id=1, source_target_pairs={{0,16},{2,18},{4,20},{6,22},{8,24},{10,26},{12,28},{14,30},{16,0},... | collective-permute-start | bytes 147464 | tf_op jit(solution)/shard_map/ppermute | solution.py:561
  8.8 5.9 %collective-permute-start.5 = (bf16[192,128]{1,0:T(8,128)(2,1)S(1)}, bf16[192,128]{1,0:T(8,128)(2,1)S(1)}, u32[]{:S(2)}, u32[]{:S(2)}) collective-permute-start(bf16[192,128]{1,0:T(8,128)(2,1)S(1)} %round.1.refs_0_), channel_id=1, source_target_pairs={{0,24},{2,26},{4,28},{6,30},{8,16},{10,18},{12,20},{14,22},{16,8},... | collective-permute-start | bytes 147464 | tf_op jit(solution)/shard_map/ppermute | solution.py:561
  14.8 7.0 %collective-permute-start.7 = (bf16[4,96,128]{2,1,0:T(8,128)(2,1)S(1)}, bf16[4,96,128]{2,1,0:T(8,128)(2,1)S(1)}, u32[]{:S(2)}, u32[]{:S(2)}) collective-permute-start(bf16[4,96,128]{2,1,0:T(8,128)(2,1)S(1)} %get-tuple-element.41.rows_ref.refs_0_.refs_3_), channel_id=1, source_target_pairs={{0,2},{1,5},{2,0},{3,7},{4,6},{5,1},{6,4},{7,3},{8,10},{9,13},{10,... | collective-permute-start | bytes 294920 | tf_op jit(solution)/shard_map/ppermute | solution.py:507
  16.3 5.5 %collective-permute-start.8 = (bf16[4,96,128]{2,1,0:T(8,128)(2,1)S(1)}, bf16[4,96,128]{2,1,0:T(8,128)(2,1)S(1)}, u32[]{:S(2)}, u32[]{:S(2)}) collective-permute-start(bf16[4,96,128]{2,1,0:T(8,128)(2,1)S(1)} %get-tuple-element.41.rows_ref.refs_0_.refs_3_), channel_id=1, source_target_pairs={{0,4},{1,3},{2,6},{3,1},{4,0},{5,7},{6,2},{7,5},{8,12},{9,11},{10,... | collective-permute-start | bytes 294920 | tf_op jit(solution)/shard_map/ppermute | solution.py:507
  17.8 6.4 %collective-permute-start.6 = (bf16[4,96,128]{2,1,0:T(8,128)(2,1)S(1)}, bf16[4,96,128]{2,1,0:T(8,128)(2,1)S(1)}, u32[]{:S(2)}, u32[]{:S(2)}) collective-permute-start(bf16[4,96,128]{2,1,0:T(8,128)(2,1)S(1)} %get-tuple-element.41.rows_ref.refs_0_.refs_3_), channel_id=1, source_target_pairs={{0,6},{1,7},{2,4},{3,5},{4,2},{5,3},{6,0},{7,1},{8,14},{9,15},{10,... | collective-permute-start | bytes 294920 | tf_op jit(solution)/shard_map/ppermute | solution.py:507
  21.8 2.6 %collective-permute-start.9 = (bf16[4,96,128]{2,1,0:T(8,128)(2,1)S(1)}, bf16[4,96,128]{2,1,0:T(8,128)(2,1)S(1)}, u32[]{:S(2)}, u32[]{:S(2)}) collective-permute-start(bf16[4,96,128]{2,1,0:T(8,128)(2,1)S(1)} %get-tuple-element.51.refs_0_.refs_4_), channel_id=1, source_target_pairs={{0,1},{1,0},{2,3},{3,2},{4,5},{5,4},{6,7},{7,6},{8,9},{9,8},{10,11... | collective-permute-start | bytes 294920 | tf_op jit(solution)/shard_map/ppermute | solution.py:489
  23.7 2.5 %collective-permute-start.10 = (bf16[4,96,128]{2,1,0:T(8,128)(2,1)S(1)}, bf16[4,96,128]{2,1,0:T(8,128)(2,1)S(1)}, u32[]{:S(2)}, u32[]{:S(2)}) collective-permute-start(bf16[4,96,128]{2,1,0:T(8,128)(2,1)S(1)} %get-tuple-element.52.refs_1_.refs_5_), channel_id=1, source_target_pairs={{0,1},{1,0},{2,3},{3,2},{4,5},{5,4},{6,7},{7,6},{8,9},{9,8},{10,11... | collective-permute-start | bytes 294920 | tf_op jit(solution)/shard_map/ppermute | solution.py:489
  24.3 1.9 %collective-permute-start.11 = (bf16[4,96,128]{2,1,0:T(8,128)(2,1)S(1)}, bf16[4,96,128]{2,1,0:T(8,128)(2,1)S(1)}, u32[]{:S(2)}, u32[]{:S(2)}) collective-permute-start(bf16[4,96,128]{2,1,0:T(8,128)(2,1)S(1)} %gate.5.refs_0_.refs_6_), channel_id=1, source_target_pairs={{0,1},{1,0},{2,3},{3,2},{4,5},{5,4},{6,7},{7,6},{8,9},{9,8},{10,11... | collective-permute-start | bytes 294920 | tf_op jit(solution)/shard_map/ppermute | solution.py:489
  30.0 5.8 %collective-permute-start.15 = (bf16[4,112,128]{2,1,0:T(8,128)(2,1)S(1)}, bf16[4,112,128]{2,1,0:T(8,128)(2,1)S(1)}, u32[]{:S(2)}, u32[]{:S(2)}) collective-permute-start(bf16[4,112,128]{2,1,0:T(8,128)(2,1)S(1)} %get-tuple-element.59.after_ref.rows_ref.refs_0_.refs_2_), channel_id=1, source_target_pairs={{0,2},{1,5},{2,0},{3,7},{4,6},{5,1},{6,4},{7,3},{8,10},{9,13},{10,... | collective-permute-start | bytes 344072 | tf_op jit(solution)/shard_map/ppermute | solution.py:507
  31.6 6.3 %collective-permute-start.16 = (bf16[4,112,128]{2,1,0:T(8,128)(2,1)S(1)}, bf16[4,112,128]{2,1,0:T(8,128)(2,1)S(1)}, u32[]{:S(2)}, u32[]{:S(2)}) collective-permute-start(bf16[4,112,128]{2,1,0:T(8,128)(2,1)S(1)} %get-tuple-element.59.after_ref.rows_ref.refs_0_.refs_2_), channel_id=1, source_target_pairs={{0,4},{1,3},{2,6},{3,1},{4,0},{5,7},{6,2},{7,5},{8,12},{9,11},{10,... | collective-permute-start | bytes 344072 | tf_op jit(solution)/shard_map/ppermute | solution.py:507
  33.1 6.4 %collective-permute-start.14 = (bf16[4,112,128]{2,1,0:T(8,128)(2,1)S(1)}, bf16[4,112,128]{2,1,0:T(8,128)(2,1)S(1)}, u32[]{:S(2)}, u32[]{:S(2)}) collective-permute-start(bf16[4,112,128]{2,1,0:T(8,128)(2,1)S(1)} %get-tuple-element.59.after_ref.rows_ref.refs_0_.refs_2_), channel_id=1, source_target_pairs={{0,6},{1,7},{2,4},{3,5},{4,2},{5,3},{6,0},{7,1},{8,14},{9,15},{10,... | collective-permute-start | bytes 344072 | tf_op jit(solution)/shard_map/ppermute | solution.py:507
  37.9 2.6 %collective-permute-start.18 = (bf16[4,112,128]{2,1,0:T(8,128)(2,1)S(1)}, bf16[4,112,128]{2,1,0:T(8,128)(2,1)S(1)}, u32[]{:S(2)}, u32[]{:S(2)}) collective-permute-start(bf16[4,112,128]{2,1,0:T(8,128)(2,1)S(1)} %get-tuple-element.66.refs_0_.refs_3_), channel_id=1, source_target_pairs={{0,1},{1,0},{2,3},{3,2},{4,5},{5,4},{6,7},{7,6},{8,9},{9,8},{10,11... | collective-permute-start | bytes 344072 | tf_op jit(solution)/shard_map/ppermute | solution.py:489
  39.0 1.5 %collective-permute-start.17 = (bf16[4,112,128]{2,1,0:T(8,128)(2,1)S(1)}, bf16[4,112,128]{2,1,0:T(8,128)(2,1)S(1)}, u32[]{:S(2)}, u32[]{:S(2)}) collective-permute-start(bf16[4,112,128]{2,1,0:T(8,128)(2,1)S(1)} %get-tuple-element.70), channel_id=1, source_target_pairs={{0,1},{1,0},{2,3},{3,2},{4,5},{5,4},{6,7},{7,6},{8,9},{9,8},{10,11... | collective-permute-start | bytes 344072 | tf_op jit(solution)/shard_map/ppermute | solution.py:489
  39.6 2.3 %collective-permute-start.19 = (bf16[4,112,128]{2,1,0:T(8,128)(2,1)S(1)}, bf16[4,112,128]{2,1,0:T(8,128)(2,1)S(1)}, u32[]{:S(2)}, u32[]{:S(2)}) collective-permute-start(bf16[4,112,128]{2,1,0:T(8,128)(2,1)S(1)} %get-tuple-element.73), channel_id=1, source_target_pairs={{0,1},{1,0},{2,3},{3,2},{4,5},{5,4},{6,7},{7,6},{8,9},{9,8},{10,11... | collective-permute-start | bytes 344072 | tf_op jit(solution)/shard_map/ppermute | solution.py:489
  39.6 2.2 %collective-permute-start.20 = (bf16[4,112,128]{2,1,0:T(8,128)(2,1)S(1)}, bf16[4,112,128]{2,1,0:T(8,128)(2,1)S(1)}, u32[]{:S(2)}, u32[]{:S(2)}) collective-permute-start(bf16[4,112,128]{2,1,0:T(8,128)(2,1)S(1)} %get-tuple-element.69.refs_0_.refs_5_), channel_id=1, source_target_pairs={{0,1},{1,0},{2,3},{3,2},{4,5},{5,4},{6,7},{7,6},{8,9},{9,8},{10,11... | collective-permute-start | bytes 344072 | tf_op jit(solution)/shard_map/ppermute | solution.py:489
  43.8 1.3 %collective-permute-start.21 = (f32[104,128]{1,0:T(8,128)S(1)}, f32[104,128]{1,0:T(8,128)S(1)}, u32[]{:S(2)}, u32[]{:S(2)}) collective-permute-start(f32[104,128]{1,0:T(8,128)S(1)} %second_half.3.own_ref), channel_id=1, source_target_pairs={{0,1},{1,0},{2,3},{3,2},{4,5},{5,4},{6,7},{7,6},{8,9},{9,8},{10,11... | collective-permute-start | bytes 159752 | tf_op jit(solution)/shard_map/ppermute | solution.py:489
  (5 other events, 9.6 us)

commit v9 on v8

--- a/solution.py
+++ b/solution.py
@@ -32,7 +32,7 @@
     return lax.rem(lax.axis_index("head"), 2)
 
 
-def on_chip(kernel, name, operands, results, far=(), scratch=(), out_memory=pltpu.VMEM):
+def on_chip(kernel, name, operands, results, far=(), after=(), scratch=(), out_memory=pltpu.VMEM):
     near = [pltpu.with_memory_space_constraint(array, pltpu.VMEM) for array in operands]
     far = [pltpu.with_memory_space_constraint(array, pltpu.HBM) for array in far]
     if out_memory is pltpu.VMEM:
@@ -42,13 +42,13 @@
     return pl.pallas_call(
         kernel,
         in_specs=[pl.BlockSpec(memory_space=pltpu.VMEM)] * len(near)
-        + [pl.BlockSpec(memory_space=pl.ANY)] * len(far),
+        + [pl.BlockSpec(memory_space=pl.ANY)] * (len(far) + len(after)),
         out_specs=tuple(pl.BlockSpec(memory_space=pltpu.VMEM) for _ in results),
         out_shape=out_shape,
         scratch_shapes=list(scratch),
         compiler_params=pltpu.CompilerParams(vmem_limit_bytes=VMEM_LIMIT),
         name=name,
-    )(*near, *far)
+    )(*near, *far, *after)
 
 
 def fetch(sources, targets, sems):
@@ -67,7 +67,8 @@
 
 def arrange_kernel(planes, *refs):
     place = lax.axis_index("seq") // (lax.axis_size("seq") // planes)
-    mine_ref, other_ref = refs[-2:]
+    mine_ref, other_ref, maps_ref = refs[-3:]
+    maps_ref[...] = refs[planes][...]
     count = mine_ref.shape[1]
     for step in range(planes):
         first, second = refs[step][:count, :], refs[step][count:, :]
@@ -95,78 +96,86 @@
     return (lax.axis_index("seq") % per_plane) ^ jnp.where(first, step, turned(step, bits))
 
 
-def make_maps(layer, in_ref, gain_ref, weights, out_ref):
-    channels = in_ref.shape[1]
-
-    def store(row, value):
-        high = value.astype(jnp.bfloat16)
-        rows = value.shape[0]
-        out_ref[row : row + rows, :channels] = high
-        out_ref[row : row + rows, channels:] = (value - high.astype(jnp.float32)).astype(
-            jnp.bfloat16
-        )
-        return row + rows
-
-    base = in_ref[layer]
-    scaled = base.astype(jnp.float32) * gain_ref[layer : layer + 1, :]
-    high = scaled.astype(jnp.bfloat16)
-    low = (scaled - high.astype(jnp.float32)).astype(jnp.bfloat16)
-    both = jnp.concatenate([high, low], axis=0)
-    row = 0
-    for first in range(0, weights.shape[0], 2):
-        product = dot(both, cat([weights[first], weights[first + 1]], 1))
-        row = store(row, (product[:channels] + product[channels:]).T)
-    row = store(row, dot_nt(base, base))
+def prepare_kernel(in_src, gain_src, key_src, value_src, query_src, *refs):
+    in_ref, tail_ref, maps_ref, gain_ref, buffer, sems = refs[-6:]
+    layers, channels, _ = in_ref.shape
+    weights = (key_src, value_src, query_src)
+    sources = [in_src, gain_src] + [src.at[b] for b in range(layers) for src in weights]
+    targets = [in_ref, gain_ref] + [buffer.at[b, at] for b in range(layers) for at in range(3)]
+    copies = fetch(sources, targets, sems)
+    for copy in copies[:2]:
+        copy.wait()
     eye = lax.broadcasted_iota(jnp.int32, (channels, channels), 0) == lax.broadcasted_iota(
         jnp.int32, (channels, channels), 1
     )
-    store(row, jnp.where(eye, 1.0, 0.0))
-
-
-def prepare_kernel(pieces, in_src, gain_src, *refs):
-    sources, refs = refs[: 3 * pieces], refs[3 * pieces :]
-    maps_ref, in_ref, gain_ref, query_ref, later_ref, buffer, sems = refs
-    both = list(sources[: 2 * pieces])
-    near = [in_src, gain_src] + [source.at[0] for source in both]
-    targets = [in_ref, gain_ref] + [buffer.at[at] for at in range(2 * pieces)]
-    near += list(sources[2 * pieces :]) + [source.at[1] for source in both]
-    targets += [query_ref.at[at] for at in range(pieces)]
-    targets += [later_ref.at[at] for at in range(2 * pieces)]
-    copies = fetch(near, targets, sems)
-    for copy in copies[: 2 + 2 * pieces]:
-        copy.wait()
-    make_maps(0, in_ref, gain_ref, buffer, maps_ref)
-    for copy in copies[2 + 2 * pieces :]:
-        copy.wait()
-
-
-def prepare(in_proj, attn_gain, key_pieces, value_pieces, query_pieces):
-    pieces = len(key_pieces)
-    _, channels, features = in_proj.shape
-    columns = key_pieces[0].shape[2]
-    rows = 2 * pieces * columns + 2 * channels
-    buffer = (2 * pieces, features, columns)
+
+    def store(ref, row, value):
+        high = value.astype(jnp.bfloat16)
+        rows = slice(row, row + value.shape[0])
+        ref[rows, :channels] = high
+        ref[rows, channels:] = (value - high.astype(jnp.float32)).astype(jnp.bfloat16)
+
+    for layer in range(layers):
+        base = in_ref[layer]
+        store(tail_ref.at[layer], 0, dot_nt(base, base))
+        store(tail_ref.at[layer], channels, jnp.where(eye, 1.0, 0.0))
+        scaled = base.astype(jnp.float32) * gain_ref[layer : layer + 1, :]
+        high = scaled.astype(jnp.bfloat16)
+        low = (scaled - high.astype(jnp.float32)).astype(jnp.bfloat16)
+        both = jnp.concatenate([high, low], axis=0)
+        for at in range(3):
+            copies[2 + 3 * layer + at].wait()
+        product = dot(both, cat([buffer[layer, at] for at in range(3)], 1))
+        store(maps_ref.at[layer], 0, (product[:channels] + product[channels:]).T)
+
+
+def prepare(in_proj, attn_gain, key_proj, value_proj, query_proj, after):
+    layers, channels, features = in_proj.shape
+    columns = key_proj.shape[2]
     return on_chip(
-        functools.partial(prepare_kernel, pieces),
+        prepare_kernel,
         "prepare",
         [],
         [
-            ((rows, 2 * channels), jnp.bfloat16),
-            (in_proj.shape, in_proj.dtype),
-            (attn_gain.shape, attn_gain.dtype),
-            ((pieces, *query_pieces[0].shape), jnp.bfloat16),
-            (buffer, jnp.bfloat16),
+            (in_proj.shape, jnp.bfloat16),
+            ((layers, 2 * channels, 2 * channels), jnp.bfloat16),
+            ((layers, 3 * columns, 2 * channels), jnp.bfloat16),
         ],
-        far=[in_proj, attn_gain, *key_pieces, *value_pieces, *query_pieces],
-        scratch=[pltpu.VMEM(buffer, jnp.bfloat16), pltpu.SemaphoreType.DMA((5 * pieces + 2,))],
-    )
-
-
-def second_maps_kernel(after_ref, in_ref, gain_ref, weights_ref, out_ref):
-    make_maps(1, in_ref, gain_ref, weights_ref, out_ref)
-
-
-def queries_kernel(layer, planes, rows_ref, in_ref, gain_ref, query_ref, hidden_ref, out_ref):
+        far=[in_proj, attn_gain, key_proj, value_proj, query_proj],
+        after=after,
+        scratch=[
+            pltpu.VMEM(attn_gain.shape, jnp.float32),
+            pltpu.VMEM((layers, 3, features, columns), jnp.bfloat16),
+            pltpu.SemaphoreType.DMA((2 + 3 * layers,)),
+        ],
+    )
+
+
+def join_kernel(pieces, tail_ref, *refs):
+    sources, outs = refs[:pieces], refs[pieces:]
+    layers = tail_ref.shape[0]
+    columns = sources[0].shape[1] // 3
+    for layer in range(layers):
+        maps_ref, query_ref = outs[2 * layer : 2 * layer + 2]
+        total = pieces * columns
+        for j, source in enumerate(sources):
+            for at in range(2):
+                row = at * total + j * columns
+                maps_ref[row : row + columns, :] = source[layer, at * columns : (at + 1) * columns]
+            query_ref[j * columns : (j + 1) * columns, :] = source[layer, 2 * columns :]
+        maps_ref[2 * total :, :] = tail_ref[layer]
+
+
+def join(tail, pieces):
+    layers, rows, width = pieces[0].shape
+    total = len(pieces) * rows // 3
+    results = [((2 * total + tail.shape[1], width), jnp.bfloat16), ((total, width), jnp.bfloat16)]
+    return on_chip(
+        functools.partial(join_kernel, len(pieces)), "join", [tail, *pieces], results * layers
+    )
+
+
+def queries_kernel(layer, planes, rows_ref, in_ref, maps_ref, hidden_ref, out_ref):
     if planes == rows_ref.shape[0]:
         rows = rows_ref[...]
     else:
@@ -178,14 +187,14 @@
     hidden = dot(rows, in_ref[layer])
     hidden_ref[...] = hidden
     spread = lax.rsqrt(jnp.mean(hidden * hidden, axis=1, keepdims=True) + epsilon)
-    normed = (hidden * spread * gain_ref[layer : layer + 1, :]).astype(jnp.bfloat16)
-    for first in range(0, query_ref.shape[0], 2):
-        query = dot(normed, cat([query_ref[at, layer] for at in range(first, first + 2)], 1))
-        width = query.shape[1]
-        heads = width // HS
-        head = lax.broadcasted_iota(jnp.int32, (1, width), 1) // HS
-        same = head == lax.broadcasted_iota(jnp.int32, (width, 1), 0) // HS
-        same = jnp.where(same, 1.0, 0.0).astype(jnp.bfloat16)
+    twice = jnp.concatenate([rows, rows], axis=1)
+    groups, _, width = out_ref.shape
+    heads = width // HS
+    head = lax.broadcasted_iota(jnp.int32, (1, width), 1) // HS
+    same = head == lax.broadcasted_iota(jnp.int32, (width, 1), 0) // HS
+    same = jnp.where(same, 1.0, 0.0).astype(jnp.bfloat16)
+    for g in range(groups):
+        query = dot_nt(twice, maps_ref[g * width : (g + 1) * width, :]) * spread
         square = query * query
         high = square.astype(jnp.bfloat16)
         low = (square - high.astype(jnp.float32)).astype(jnp.bfloat16)
@@ -195,19 +204,17 @@
             band = jnp.where(head == h, query, 0.0).astype(jnp.bfloat16)
             for p in range(planes):
                 row = (p * heads + h) * count
-                out_ref[first // 2, row : row + count, :] = band[p * count : (p + 1) * count]
-
-
-def make_queries(layer, planes, count, rows, weights):
-    in_all, _, query_all = weights
-    width = 2 * query_all.shape[3]
+                out_ref[g, row : row + count, :] = band[p * count : (p + 1) * count]
+
+
+def make_queries(layer, planes, count, rows, in_all, maps, width):
     return on_chip(
         functools.partial(queries_kernel, layer, planes),
         "queries",
-        [rows, *weights],
+        [rows, in_all, maps],
         [
             ((planes * count, in_all.shape[2]), jnp.float32),
-            ((query_all.shape[0] // 2, planes * width // HS * count, width), jnp.bfloat16),
+            ((maps.shape[0] // width, planes * width // HS * count, width), jnp.bfloat16),
         ],
     )
 
@@ -561,24 +568,24 @@
         lax.ppermute(rounded, "seq", [(i, i ^ (b * per_plane)) for i in range(members)])
         for b in range(1, planes)
     ]
-    key_pieces, value_pieces = pieces_of(key_proj), pieces_of(value_proj)
-    query_pieces, mix_pieces = pieces_of(query_proj), pieces_of(mix_proj)
-    param_pieces = pieces_of(param_proj)
-    maps, *weights, later = prepare(in_proj, attn_gain, key_pieces, value_pieces, query_pieces)
+    mix_pieces, param_pieces = pieces_of(mix_proj), pieces_of(param_proj)
+    in_all, tail, own_maps = prepare(
+        in_proj, attn_gain, key_proj, value_proj, query_proj, []
+    )
     shape = (planes, count, channels)
-    mine, sibling = on_chip(
+    mine, sibling, own_maps = on_chip(
         functools.partial(arrange_kernel, planes),
         "arrange",
-        [*parts, maps],
-        [(shape, jnp.bfloat16), (shape, jnp.bfloat16)],
-    )
-    made = make_queries(0, planes, count, mine, weights)
-    held, held_log, mine = run(0, mine, sibling, maps, made, latents)
-    (maps,) = on_chip(
-        second_maps_kernel, "second_maps", [mine, *weights[:2], later], [(maps.shape, maps.dtype)]
-    )
-    made = make_queries(1, 1, count, mine, weights)
-    (packed,) = run(1, mine, None, maps, made, latents, (held, held_log))
+        [*parts, own_maps],
+        [(shape, jnp.bfloat16), (shape, jnp.bfloat16), (own_maps.shape, jnp.bfloat16)],
+        after=mix_pieces[1:] + param_pieces[1:],
+    )
+    first_maps, first_query, second_maps, second_query = join(tail, pieces_of(own_maps))
+    width = 2 * key_proj.shape[2]
+    made = make_queries(0, planes, count, mine, in_all, first_query, width)
+    held, held_log, mine = run(0, mine, sibling, first_maps, made, latents)
+    made = make_queries(1, 1, count, mine, in_all, second_query, width)
+    (packed,) = run(1, mine, None, second_maps, made, latents, (held, held_log))
     final_latent, token_loglik = on_chip(
         finish_kernel,
         "finish",

time: 45.9 us -> 45.5 us (level)
  waiting for transfers between devices: 5.07 us -> 8.05 us
  starting transfers between devices: 18.2 us -> 16 us
  Pallas kernels: 21.5 us -> 20.3 us
    ppermute x6, waiting for transfers between devices: 2.08 us -> 4.16 us  [in_plane(): arrived.append(lax.ppermute(mine, ('seq', 'head'), pairs))]
    ppermute x3, starting transfers between devices: 7.21 us -> 5.66 us  [body(): lax.ppermute(rounded, 'seq', [(i, i ^ b * per_plane) for i in range(membe...]
    pallas_call x19, Pallas kernels: 21.5 us -> 20.3 us  [on_chip(): pl.pallas_call(kernel, in_specs=[pl.BlockSpec(memory_space=pltpu.VMEM)] *...]
    ppermute x3, waiting for transfers between devices: 1.53 us -> 2.7 us  [body(): lax.ppermute(rounded, 'seq', [(i, i ^ b * per_plane) for i in range(membe...]
    ppermute x5 -> x3, starting transfers between devices: 1.54 us -> 0.67 us  [pieces_of(): lax.ppermute(array, 'head', [((i + j) % ways, i) for i in range(ways)])]
  transfers between devices with their start and end apart: 22 -> 20, of which waited for: 5 -> 6; matrix products, arithmetic and copies ran while one was open for 0% -> 0% of each run, Pallas kernels for 33% -> 31%
where the time goes in v9:
time: 45.5 us; the launch traced here: 45.4 us
  Pallas kernels  20.3 us (45%)
  starting transfers between devices  16 us (35%)
  waiting for transfers between devices  8.05 us (18%)
  between operations  0.88 us (2%)
    pallas_call x19, Pallas kernels, on_chip(): pl.pallas_call(kernel, in_specs=[pl.BlockSpec(memory_space=pltpu.VMEM)] *...  20.3 us
    ppermute x6, starting transfers between devices, in_plane(): arrived.append(lax.ppermute(mine, ('seq', 'head'), pairs))  7.55 us
    ppermute x3, starting transfers between devices, body(): lax.ppermute(rounded, 'seq', [(i, i ^ b * per_plane) for i in range(membe...  5.66 us
    ppermute x6, waiting for transfers between devices, in_plane(): arrived.append(lax.ppermute(mine, ('seq', 'head'), pairs))  4.16 us
    ppermute x3, waiting for transfers between devices, body(): lax.ppermute(rounded, 'seq', [(i, i ^ b * per_plane) for i in range(membe...  2.7 us
    ppermute x8, starting transfers between devices, swap(): return lax.ppermute(array, 'head', [(i, i ^ 1) for i in range(ways)])  2.17 us
    ppermute x8, waiting for transfers between devices, swap(): return lax.ppermute(array, 'head', [(i, i ^ 1) for i in range(ways)])  1.18 us
  transfers between devices with their start and end apart: 20, of which 6 were waited for; matrix products, arithmetic and copies ran while one was open for 0% of the time, Pallas kernels for 31%

profile of v9, /device:TPU:0, one launch (start us, length us, event | category | flops | bytes accessed | tf_op | source)
XLA Modules:
  0.0 45.4 jit_solution(16236090825346454470)
XLA Ops:
  1.2 0.9 %round.1.refs_0_ = bf16[192,128]{1,0:T(8,128)(2,1)S(1)} custom-call(f32[192,128]{1,0:T(8,128)} %latent_ref.3), custom_call_target="tpu_custom_call" | custom-call | tf_op jit(solution)/shard_map/round/pallas_call | solution.py:42
  2.1 3.1 %collective-permute-start = (bf16[192,128]{1,0:T(8,128)(2,1)S(1)}, bf16[192,128]{1,0:T(8,128)(2,1)S(1)}, u32[]{:S(2)}, u32[]{:S(2)}) collective-permute-start(bf16[192,128]{1,0:T(8,128)(2,1)S(1)} %round.1.refs_0_), channel_id=1, source_target_pairs={{0,8},{2,10},{4,12},{6,14},{8,0},{10,2},{12,4},{14,6},{16,24},{18,... | collective-permute-start | bytes 147464 | tf_op jit(solution)/shard_map/ppermute | solution.py:568
  5.2 2.6 %collective-permute-start.1 = (bf16[192,128]{1,0:T(8,128)(2,1)S(1)}, bf16[192,128]{1,0:T(8,128)(2,1)S(1)}, u32[]{:S(2)}, u32[]{:S(2)}) collective-permute-start(bf16[192,128]{1,0:T(8,128)(2,1)S(1)} %round.1.refs_0_), channel_id=1, source_target_pairs={{0,16},{2,18},{4,20},{6,22},{8,24},{10,26},{12,28},{14,30},{16,0},... | collective-permute-start | bytes 147464 | tf_op jit(solution)/shard_map/ppermute | solution.py:568
  7.8 3.2 %prepare.1 = (bf16[2,128,1536]{2,1,0:T(8,128)(2,1)S(1)}, bf16[2,256,256]{2,1,0:T(8,128)(2,1)S(1)}, bf16[2,384,256]{2,1,0:T(8,128)(2,1)S(1)}) custom-call(bf16[2,128,1536]{2,1,0:T(8,128)(2,1)} %in_src.1, f32[2,1536]{1,0:T(2,128)} %gain_src.1, bf16[2,1536,128]{2,1,0:T(8,128)(2,1)} %key_src.1, bf16[2,1536,128]{2,1,0:T(8,128)(2,1)} %value_src.1, ...), custom_call_target="tpu_custom_call" | custom-call | tf_op jit(solution)/shard_map/prepare/pallas_call | solution.py:42
  11.1 2.6 %collective-permute-done.2.refs_3_ = bf16[192,128]{1,0:T(8,128)(2,1)S(1)} collective-permute-done((bf16[192,128]{1,0:T(8,128)(2,1)S(1)}, bf16[192,128]{1,0:T(8,128)(2,1)S(1)}, u32[]{:S(2)}, u32[]{:S(2)}) %collective-permute-start.2) | collective-permute-done | bytes 49184 | tf_op jit(solution)/shard_map/ppermute | solution.py:568
  13.8 1.6 %collective-permute-start.7 = (bf16[4,96,128]{2,1,0:T(8,128)(2,1)S(1)}, bf16[4,96,128]{2,1,0:T(8,128)(2,1)S(1)}, u32[]{:S(2)}, u32[]{:S(2)}) collective-permute-start(bf16[4,96,128]{2,1,0:T(8,128)(2,1)S(1)} %get-tuple-element.48.rows_ref.refs_0_.refs_3_), channel_id=1, source_target_pairs={{0,2},{1,5},{2,0},{3,7},{4,6},{5,1},{6,4},{7,3},{8,10},{9,13},{10,... | collective-permute-start | bytes 294920 | tf_op jit(solution)/shard_map/ppermute | solution.py:514
  15.4 1.5 %collective-permute-start.8 = (bf16[4,96,128]{2,1,0:T(8,128)(2,1)S(1)}, bf16[4,96,128]{2,1,0:T(8,128)(2,1)S(1)}, u32[]{:S(2)}, u32[]{:S(2)}) collective-permute-start(bf16[4,96,128]{2,1,0:T(8,128)(2,1)S(1)} %get-tuple-element.48.rows_ref.refs_0_.refs_3_), channel_id=1, source_target_pairs={{0,4},{1,3},{2,6},{3,1},{4,0},{5,7},{6,2},{7,5},{8,12},{9,11},{10,... | collective-permute-start | bytes 294920 | tf_op jit(solution)/shard_map/ppermute | solution.py:514
  17.5 0.9 %queries.2 = (f32[384,1536]{1,0:T(8,128)S(1)}, bf16[1,1536,256]{2,1,0:T(8,128)(2,1)S(1)}) custom-call(bf16[4,96,128]{2,1,0:T(8,128)(2,1)S(1)} %get-tuple-element.48.rows_ref.refs_0_.refs_3_, bf16[2,128,1536]{2,1,0:T(8,128)(2,1)S(1)} %get-tuple-element.49.in_ref, bf16[256,256]{1,0:T(8,128)(2,1)S(1)} %get-tuple-element.50.maps_ref), custom_call_target="tpu_custom_call" | custom-call | tf_op jit(solution)/shard_map/queries/pallas_call | solution.py:42
  18.3 1.8 %attend.6 = (f32[1,1536,256]{2,1,0:T(8,128)S(1)}, f32[1,1536,128]{2,1,0:T(8,128)S(1)}, f32[1,1536,64]{2,1,0:T(8,128)S(1)}) custom-call(bf16[768,256]{1,0:T(8,128)(2,1)S(1)} %get-tuple-element.47.maps_ref, bf16[1,1536,256]{2,1,0:T(8,128)(2,1)S(1)} %get-tuple-element.51.query_ref, bf16[4,96,128]{2,1,0:T(8,128)(2,1)S(1)} %get-tuple-element.48.rows_ref.refs_0_.refs_3_, ...), custom_call_target="tpu_custom_call" | custom-call | tf_op jit(solution)/shard_map/attend/pallas_call | solution.py:42
  20.1 1.1 %collective-permute-done.8.refs_1_ = bf16[4,96,128]{2,1,0:T(8,128)(2,1)S(1)} collective-permute-done((bf16[4,96,128]{2,1,0:T(8,128)(2,1)S(1)}, bf16[4,96,128]{2,1,0:T(8,128)(2,1)S(1)}, u32[]{:S(2)}, u32[]{:S(2)}) %collective-permute-start.8) | collective-permute-done | bytes 98336 | tf_op jit(solution)/shard_map/ppermute | solution.py:514
  21.3 1.8 %attend.7 = (f32[1,1536,256]{2,1,0:T(8,128)S(1)}, f32[1,1536,128]{2,1,0:T(8,128)S(1)}, f32[1,1536,64]{2,1,0:T(8,128)S(1)}) custom-call(bf16[768,256]{1,0:T(8,128)(2,1)S(1)} %get-tuple-element.47.maps_ref, bf16[1,1536,256]{2,1,0:T(8,128)(2,1)S(1)} %get-tuple-element.51.query_ref, bf16[4,96,128]{2,1,0:T(8,128)(2,1)S(1)} %get-tuple-element.57.refs_0_.refs_4_, ...), custom_call_target="tpu_custom_call" | custom-call | tf_op jit(solution)/shard_map/attend/pallas_call | solution.py:42
  23.8 1.8 %attend.8 = (f32[1,1536,256]{2,1,0:T(8,128)S(1)}, f32[1,1536,128]{2,1,0:T(8,128)S(1)}, f32[1,1536,64]{2,1,0:T(8,128)S(1)}) custom-call(bf16[768,256]{1,0:T(8,128)(2,1)S(1)} %get-tuple-element.47.maps_ref, bf16[1,1536,256]{2,1,0:T(8,128)(2,1)S(1)} %get-tuple-element.51.query_ref, bf16[4,96,128]{2,1,0:T(8,128)(2,1)S(1)} %gate.5.refs_0_.refs_6_, ...), custom_call_target="tpu_custom_call" | custom-call | tf_op jit(solution)/shard_map/attend/pallas_call | solution.py:42
  25.7 3.7 %second_half.2 = (f32[96,128]{1,0:T(8,128)S(1)}, f32[96,128]{1,0:T(8,128)S(1)}, bf16[4,112,128]{2,1,0:T(8,128)(2,1)S(1)}) custom-call(bf16[768,256]{1,0:T(8,128)(2,1)S(1)} %get-tuple-element.47.maps_ref, bf16[1,1536,256]{2,1,0:T(8,128)(2,1)S(1)} %get-tuple-element.51.query_ref, f32[384,1536]{1,0:T(8,128)S(1)} %get-tuple-element.52.hidden_ref, ...), custom_call_target="tpu_custom_call" | custom-call | tf_op jit(solution)/shard_map/second_half/pallas_call | solution.py:42
  29.9 2.1 %collective-permute-start.14 = (bf16[4,112,128]{2,1,0:T(8,128)(2,1)S(1)}, bf16[4,112,128]{2,1,0:T(8,128)(2,1)S(1)}, u32[]{:S(2)}, u32[]{:S(2)}) collective-permute-start(bf16[4,112,128]{2,1,0:T(8,128)(2,1)S(1)} %get-tuple-element.65.rows_ref.refs_0_.refs_2_), channel_id=1, source_target_pairs={{0,4},{1,3},{2,6},{3,1},{4,0},{5,7},{6,2},{7,5},{8,12},{9,11},{10,... | collective-permute-start | bytes 344072 | tf_op jit(solution)/shard_map/ppermute | solution.py:514
  32.0 1.4 %collective-permute-start.12 = (bf16[4,112,128]{2,1,0:T(8,128)(2,1)S(1)}, bf16[4,112,128]{2,1,0:T(8,128)(2,1)S(1)}, u32[]{:S(2)}, u32[]{:S(2)}) collective-permute-start(bf16[4,112,128]{2,1,0:T(8,128)(2,1)S(1)} %get-tuple-element.65.rows_ref.refs_0_.refs_2_), channel_id=1, source_target_pairs={{0,6},{1,7},{2,4},{3,5},{4,2},{5,3},{6,0},{7,1},{8,14},{9,15},{10,... | collective-permute-start | bytes 344072 | tf_op jit(solution)/shard_map/ppermute | solution.py:514
  33.9 0.7 %attend.9 = (f32[1,384,256]{2,1,0:T(8,128)S(1)}, f32[1,384,128]{2,1,0:T(8,128)S(1)}) custom-call(bf16[768,256]{1,0:T(8,128)(2,1)S(1)} %get-tuple-element.46.maps_ref, bf16[1,384,256]{2,1,0:T(8,128)(2,1)S(1)} %get-tuple-element.67.query_ref, bf16[4,112,128]{2,1,0:T(8,128)(2,1)S(1)} %get-tuple-element.65.rows_ref.refs_0_.refs_2_), custom_call_target="tpu_custom_call" | custom-call | tf_op jit(solution)/shard_map/attend/pallas_call | solution.py:42
  34.6 1.1 %collective-permute-done.14.refs_1_ = bf16[4,112,128]{2,1,0:T(8,128)(2,1)S(1)} collective-permute-done((bf16[4,112,128]{2,1,0:T(8,128)(2,1)S(1)}, bf16[4,112,128]{2,1,0:T(8,128)(2,1)S(1)}, u32[]{:S(2)}, u32[]{:S(2)}) %collective-permute-start.14) | collective-permute-done | bytes 114720 | tf_op jit(solution)/shard_map/ppermute | solution.py:514
  35.8 0.7 %collective-permute-start.16 = (bf16[4,112,128]{2,1,0:T(8,128)(2,1)S(1)}, bf16[4,112,128]{2,1,0:T(8,128)(2,1)S(1)}, u32[]{:S(2)}, u32[]{:S(2)}) collective-permute-start(bf16[4,112,128]{2,1,0:T(8,128)(2,1)S(1)} %get-tuple-element.72.refs_0_.refs_3_), channel_id=1, source_target_pairs={{0,1},{1,0},{2,3},{3,2},{4,5},{5,4},{6,7},{7,6},{8,9},{9,8},{10,11... | collective-permute-start | bytes 344072 | tf_op jit(solution)/shard_map/ppermute | solution.py:496
  36.4 1.0 %attend.10 = (f32[1,384,256]{2,1,0:T(8,128)S(1)}, f32[1,384,128]{2,1,0:T(8,128)S(1)}) custom-call(bf16[768,256]{1,0:T(8,128)(2,1)S(1)} %get-tuple-element.46.maps_ref, bf16[1,384,256]{2,1,0:T(8,128)(2,1)S(1)} %get-tuple-element.67.query_ref, bf16[4,112,128]{2,1,0:T(8,128)(2,1)S(1)} %get-tuple-element.72.refs_0_.refs_3_, ...), custom_call_target="tpu_custom_call" | custom-call | tf_op jit(solution)/shard_map/attend/pallas_call | solution.py:42
  37.5 2.0 %collective-permute-done.12.refs_0_ = bf16[4,112,128]{2,1,0:T(8,128)(2,1)S(1)} collective-permute-done((bf16[4,112,128]{2,1,0:T(8,128)(2,1)S(1)}, bf16[4,112,128]{2,1,0:T(8,128)(2,1)S(1)}, u32[]{:S(2)}, u32[]{:S(2)}) %collective-permute-start.12) | collective-permute-done | bytes 114720 | tf_op jit(solution)/shard_map/ppermute | solution.py:514
  40.1 1.4 %attend.11 = (f32[1,384,256]{2,1,0:T(8,128)S(1)}, f32[1,384,128]{2,1,0:T(8,128)S(1)}) custom-call(bf16[768,256]{1,0:T(8,128)(2,1)S(1)} %get-tuple-element.46.maps_ref, bf16[1,384,256]{2,1,0:T(8,128)(2,1)S(1)} %get-tuple-element.67.query_ref, bf16[4,112,128]{2,1,0:T(8,128)(2,1)S(1)} %get-tuple-element.75.refs_0_.refs_5_, ...), custom_call_target="tpu_custom_call" | custom-call | tf_op jit(solution)/shard_map/attend/pallas_call | solution.py:42
  41.5 1.9 %second_half.3.own_ref = f32[104,128]{1,0:T(8,128)S(1)} custom-call(bf16[768,256]{1,0:T(8,128)(2,1)S(1)} %get-tuple-element.46.maps_ref, bf16[1,384,256]{2,1,0:T(8,128)(2,1)S(1)} %get-tuple-element.67.query_ref, f32[96,1536]{1,0:T(8,128)S(1)} %get-tuple-element.68.hidden_ref, f32[2,1536]{1,0:T(2,128)S(1)} %copy-done.3, f32[192,128]{1,0:T(8,128)S(1)} %copy-done.2, ...), custom_call_target="tpu_custom_call" | custom-call | tf_op jit(solution)/shard_map/second_half/pallas_call | solution.py:42
  43.5 1.2 %collective-permute-done.19.other_ref = f32[104,128]{1,0:T(8,128)S(1)} collective-permute-done((f32[104,128]{1,0:T(8,128)S(1)}, f32[104,128]{1,0:T(8,128)S(1)}, u32[]{:S(2)}, u32[]{:S(2)}) %collective-permute-start.19) | collective-permute-done | bytes 53280 | tf_op jit(solution)/shard_map/ppermute | solution.py:496
  44.7 0.7 %finish.1 = (f32[192,128]{1,0:T(8,128)}, f32[1,192]{1,0:T(1,128)}) custom-call(f32[104,128]{1,0:T(8,128)S(1)} %second_half.3.own_ref, f32[104,128]{1,0:T(8,128)S(1)} %collective-permute-done.19.other_ref), custom_call_target="tpu_custom_call" | custom-call | tf_op jit(solution)/shard_map/finish/pallas_call | solution.py:42
  (43 shorter events, 4.1 us)
Async XLA Ops:
  0.6 13.1 %collective-permute-start.3 = (bf16[2,128,1536]{2,1,0:T(8,128)(2,1)}, bf16[2,128,1536]{2,1,0:T(8,128)(2,1)S(1)}, u32[]{:S(2)}, u32[]{:S(2)}) collective-permute-start(bf16[2,128,1536]{2,1,0:T(8,128)(2,1)} %refs_10_.1), channel_id=1, source_target_pairs={{1,0},{0,1},{3,2},{2,3},{5,4},{4,5},{7,6},{6,7},{9,8},{8,9},{11,10... | collective-permute-start | bytes 2359304 | tf_op jit(solution)/shard_map/ppermute | solution.py:502
  1.1 12.5 %collective-permute-start.4 = (bf16[2,768,256]{2,1,0:T(8,128)(2,1)}, bf16[2,768,256]{2,1,0:T(8,128)(2,1)S(1)}, u32[]{:S(2)}, u32[]{:S(2)}) collective-permute-start(bf16[2,768,256]{2,1,0:T(8,128)(2,1)} %refs_12_.1), channel_id=1, source_target_pairs={{1,0},{0,1},{3,2},{2,3},{5,4},{4,5},{7,6},{6,7},{9,8},{8,9},{11,10... | collective-permute-start | bytes 2359304 | tf_op jit(solution)/shard_map/ppermute | solution.py:502
  2.1 8.8 %collective-permute-start = (bf16[192,128]{1,0:T(8,128)(2,1)S(1)}, bf16[192,128]{1,0:T(8,128)(2,1)S(1)}, u32[]{:S(2)}, u32[]{:S(2)}) collective-permute-start(bf16[192,128]{1,0:T(8,128)(2,1)S(1)} %round.1.refs_0_), channel_id=1, source_target_pairs={{0,8},{2,10},{4,12},{6,14},{8,0},{10,2},{12,4},{14,6},{16,24},{18,... | collective-permute-start | bytes 147464 | tf_op jit(solution)/shard_map/ppermute | solution.py:568
  5.2 5.9 %collective-permute-start.1 = (bf16[192,128]{1,0:T(8,128)(2,1)S(1)}, bf16[192,128]{1,0:T(8,128)(2,1)S(1)}, u32[]{:S(2)}, u32[]{:S(2)}) collective-permute-start(bf16[192,128]{1,0:T(8,128)(2,1)S(1)} %round.1.refs_0_), channel_id=1, source_target_pairs={{0,16},{2,18},{4,20},{6,22},{8,24},{10,26},{12,28},{14,30},{16,0},... | collective-permute-start | bytes 147464 | tf_op jit(solution)/shard_map/ppermute | solution.py:568
  7.8 5.9 %collective-permute-start.2 = (bf16[192,128]{1,0:T(8,128)(2,1)S(1)}, bf16[192,128]{1,0:T(8,128)(2,1)S(1)}, u32[]{:S(2)}, u32[]{:S(2)}) collective-permute-start(bf16[192,128]{1,0:T(8,128)(2,1)S(1)} %round.1.refs_0_), channel_id=1, source_target_pairs={{0,24},{2,26},{4,28},{6,30},{8,16},{10,18},{12,20},{14,22},{16,8},... | collective-permute-start | bytes 147464 | tf_op jit(solution)/shard_map/ppermute | solution.py:568
  13.8 3.6 %collective-permute-start.5 = (bf16[2,384,256]{2,1,0:T(8,128)(2,1)S(1)}, bf16[2,384,256]{2,1,0:T(8,128)(2,1)S(1)}, u32[]{:S(2)}, u32[]{:S(2)}) collective-permute-start(bf16[2,384,256]{2,1,0:T(8,128)(2,1)S(1)} %get-tuple-element.45.refs_0_), channel_id=1, source_target_pairs={{1,0},{0,1},{3,2},{2,3},{5,4},{4,5},{7,6},{6,7},{9,8},{8,9},{11,10... | collective-permute-start | bytes 1179656 | tf_op jit(solution)/shard_map/ppermute | solution.py:502
  13.8 6.3 %collective-permute-start.7 = (bf16[4,96,128]{2,1,0:T(8,128)(2,1)S(1)}, bf16[4,96,128]{2,1,0:T(8,128)(2,1)S(1)}, u32[]{:S(2)}, u32[]{:S(2)}) collective-permute-start(bf16[4,96,128]{2,1,0:T(8,128)(2,1)S(1)} %get-tuple-element.48.rows_ref.refs_0_.refs_3_), channel_id=1, source_target_pairs={{0,2},{1,5},{2,0},{3,7},{4,6},{5,1},{6,4},{7,3},{8,10},{9,13},{10,... | collective-permute-start | bytes 294920 | tf_op jit(solution)/shard_map/ppermute | solution.py:514
  15.4 5.8 %collective-permute-start.8 = (bf16[4,96,128]{2,1,0:T(8,128)(2,1)S(1)}, bf16[4,96,128]{2,1,0:T(8,128)(2,1)S(1)}, u32[]{:S(2)}, u32[]{:S(2)}) collective-permute-start(bf16[4,96,128]{2,1,0:T(8,128)(2,1)S(1)} %get-tuple-element.48.rows_ref.refs_0_.refs_3_), channel_id=1, source_target_pairs={{0,4},{1,3},{2,6},{3,1},{4,0},{5,7},{6,2},{7,5},{8,12},{9,11},{10,... | collective-permute-start | bytes 294920 | tf_op jit(solution)/shard_map/ppermute | solution.py:514
  16.9 6.7 %collective-permute-start.6 = (bf16[4,96,128]{2,1,0:T(8,128)(2,1)S(1)}, bf16[4,96,128]{2,1,0:T(8,128)(2,1)S(1)}, u32[]{:S(2)}, u32[]{:S(2)}) collective-permute-start(bf16[4,96,128]{2,1,0:T(8,128)(2,1)S(1)} %get-tuple-element.48.rows_ref.refs_0_.refs_3_), channel_id=1, source_target_pairs={{0,6},{1,7},{2,4},{3,5},{4,2},{5,3},{6,0},{7,1},{8,14},{9,15},{10,... | collective-permute-start | bytes 294920 | tf_op jit(solution)/shard_map/ppermute | solution.py:514
  21.2 2.6 %collective-permute-start.9 = (bf16[4,96,128]{2,1,0:T(8,128)(2,1)S(1)}, bf16[4,96,128]{2,1,0:T(8,128)(2,1)S(1)}, u32[]{:S(2)}, u32[]{:S(2)}) collective-permute-start(bf16[4,96,128]{2,1,0:T(8,128)(2,1)S(1)} %get-tuple-element.57.refs_0_.refs_4_), channel_id=1, source_target_pairs={{0,1},{1,0},{2,3},{3,2},{4,5},{5,4},{6,7},{7,6},{8,9},{9,8},{10,11... | collective-permute-start | bytes 294920 | tf_op jit(solution)/shard_map/ppermute | solution.py:496
  23.1 2.5 %collective-permute-start.10 = (bf16[4,96,128]{2,1,0:T(8,128)(2,1)S(1)}, bf16[4,96,128]{2,1,0:T(8,128)(2,1)S(1)}, u32[]{:S(2)}, u32[]{:S(2)}) collective-permute-start(bf16[4,96,128]{2,1,0:T(8,128)(2,1)S(1)} %get-tuple-element.58.refs_1_.refs_5_), channel_id=1, source_target_pairs={{0,1},{1,0},{2,3},{3,2},{4,5},{5,4},{6,7},{7,6},{8,9},{9,8},{10,11... | collective-permute-start | bytes 294920 | tf_op jit(solution)/shard_map/ppermute | solution.py:496
  23.7 2.0 %copy-start = (bf16[2,128,1536]{2,1,0:T(8,128)(2,1)S(1)}, bf16[2,128,1536]{2,1,0:T(8,128)(2,1)}, u32[]{:S(2)}) copy-start(bf16[2,128,1536]{2,1,0:T(8,128)(2,1)} %refs_10_.1) | copy-start | bytes 2359300
  23.7 2.0 %copy-start.1 = (bf16[2,768,256]{2,1,0:T(8,128)(2,1)S(1)}, bf16[2,768,256]{2,1,0:T(8,128)(2,1)}, u32[]{:S(2)}) copy-start(bf16[2,768,256]{2,1,0:T(8,128)(2,1)} %refs_12_.1) | copy-start | bytes 2359300
  23.7 2.0 %copy-start.2 = (f32[192,128]{1,0:T(8,128)S(1)}, f32[192,128]{1,0:T(8,128)}, u32[]{:S(2)}) copy-start(f32[192,128]{1,0:T(8,128)} %latent_ref.3) | copy-start | bytes 294916
  23.7 2.0 %copy-start.3 = (f32[2,1536]{1,0:T(2,128)S(1)}, f32[2,1536]{1,0:T(2,128)}, u32[]{:S(2)}) copy-start(f32[2,1536]{1,0:T(2,128)} %gain_ref.3) | copy-start | bytes 36868
  23.7 1.9 %collective-permute-start.11 = (bf16[4,96,128]{2,1,0:T(8,128)(2,1)S(1)}, bf16[4,96,128]{2,1,0:T(8,128)(2,1)S(1)}, u32[]{:S(2)}, u32[]{:S(2)}) collective-permute-start(bf16[4,96,128]{2,1,0:T(8,128)(2,1)S(1)} %gate.5.refs_0_.refs_6_), channel_id=1, source_target_pairs={{0,1},{1,0},{2,3},{3,2},{4,5},{5,4},{6,7},{7,6},{8,9},{9,8},{10,11... | collective-permute-start | bytes 294920 | tf_op jit(solution)/shard_map/ppermute | solution.py:496
  29.4 5.2 %collective-permute-start.13 = (bf16[4,112,128]{2,1,0:T(8,128)(2,1)S(1)}, bf16[4,112,128]{2,1,0:T(8,128)(2,1)S(1)}, u32[]{:S(2)}, u32[]{:S(2)}) collective-permute-start(bf16[4,112,128]{2,1,0:T(8,128)(2,1)S(1)} %get-tuple-element.65.rows_ref.refs_0_.refs_2_), channel_id=1, source_target_pairs={{0,2},{1,5},{2,0},{3,7},{4,6},{5,1},{6,4},{7,3},{8,10},{9,13},{10,... | collective-permute-start | bytes 344072 | tf_op jit(solution)/shard_map/ppermute | solution.py:514
  29.9 5.8 %collective-permute-start.14 = (bf16[4,112,128]{2,1,0:T(8,128)(2,1)S(1)}, bf16[4,112,128]{2,1,0:T(8,128)(2,1)S(1)}, u32[]{:S(2)}, u32[]{:S(2)}) collective-permute-start(bf16[4,112,128]{2,1,0:T(8,128)(2,1)S(1)} %get-tuple-element.65.rows_ref.refs_0_.refs_2_), channel_id=1, source_target_pairs={{0,4},{1,3},{2,6},{3,1},{4,0},{5,7},{6,2},{7,5},{8,12},{9,11},{10,... | collective-permute-start | bytes 344072 | tf_op jit(solution)/shard_map/ppermute | solution.py:514
  32.0 7.4 %collective-permute-start.12 = (bf16[4,112,128]{2,1,0:T(8,128)(2,1)S(1)}, bf16[4,112,128]{2,1,0:T(8,128)(2,1)S(1)}, u32[]{:S(2)}, u32[]{:S(2)}) collective-permute-start(bf16[4,112,128]{2,1,0:T(8,128)(2,1)S(1)} %get-tuple-element.65.rows_ref.refs_0_.refs_2_), channel_id=1, source_target_pairs={{0,6},{1,7},{2,4},{3,5},{4,2},{5,3},{6,0},{7,1},{8,14},{9,15},{10,... | collective-permute-start | bytes 344072 | tf_op jit(solution)/shard_map/ppermute | solution.py:514
  35.8 4.3 %collective-permute-start.16 = (bf16[4,112,128]{2,1,0:T(8,128)(2,1)S(1)}, bf16[4,112,128]{2,1,0:T(8,128)(2,1)S(1)}, u32[]{:S(2)}, u32[]{:S(2)}) collective-permute-start(bf16[4,112,128]{2,1,0:T(8,128)(2,1)S(1)} %get-tuple-element.72.refs_0_.refs_3_), channel_id=1, source_target_pairs={{0,1},{1,0},{2,3},{3,2},{4,5},{5,4},{6,7},{7,6},{8,9},{9,8},{10,11... | collective-permute-start | bytes 344072 | tf_op jit(solution)/shard_map/ppermute | solution.py:496
  37.4 2.7 %collective-permute-start.15 = (bf16[4,112,128]{2,1,0:T(8,128)(2,1)S(1)}, bf16[4,112,128]{2,1,0:T(8,128)(2,1)S(1)}, u32[]{:S(2)}, u32[]{:S(2)}) collective-permute-start(bf16[4,112,128]{2,1,0:T(8,128)(2,1)S(1)} %get-tuple-element.76), channel_id=1, source_target_pairs={{0,1},{1,0},{2,3},{3,2},{4,5},{5,4},{6,7},{7,6},{8,9},{9,8},{10,11... | collective-permute-start | bytes 344072 | tf_op jit(solution)/shard_map/ppermute | solution.py:496
  39.5 2.0 %collective-permute-start.17 = (bf16[4,112,128]{2,1,0:T(8,128)(2,1)S(1)}, bf16[4,112,128]{2,1,0:T(8,128)(2,1)S(1)}, u32[]{:S(2)}, u32[]{:S(2)}) collective-permute-start(bf16[4,112,128]{2,1,0:T(8,128)(2,1)S(1)} %get-tuple-element.79), channel_id=1, source_target_pairs={{0,1},{1,0},{2,3},{3,2},{4,5},{5,4},{6,7},{7,6},{8,9},{9,8},{10,11... | collective-permute-start | bytes 344072 | tf_op jit(solution)/shard_map/ppermute | solution.py:496
  39.6 1.9 %collective-permute-start.18 = (bf16[4,112,128]{2,1,0:T(8,128)(2,1)S(1)}, bf16[4,112,128]{2,1,0:T(8,128)(2,1)S(1)}, u32[]{:S(2)}, u32[]{:S(2)}) collective-permute-start(bf16[4,112,128]{2,1,0:T(8,128)(2,1)S(1)} %get-tuple-element.75.refs_0_.refs_5_), channel_id=1, source_target_pairs={{0,1},{1,0},{2,3},{3,2},{4,5},{5,4},{6,7},{7,6},{8,9},{9,8},{10,11... | collective-permute-start | bytes 344072 | tf_op jit(solution)/shard_map/ppermute | solution.py:496
  43.4 1.3 %collective-permute-start.19 = (f32[104,128]{1,0:T(8,128)S(1)}, f32[104,128]{1,0:T(8,128)S(1)}, u32[]{:S(2)}, u32[]{:S(2)}) collective-permute-start(f32[104,128]{1,0:T(8,128)S(1)} %second_half.3.own_ref), channel_id=1, source_target_pairs={{0,1},{1,0},{2,3},{3,2},{4,5},{5,4},{6,7},{7,6},{8,9},{9,8},{10,11... | collective-permute-start | bytes 159752 | tf_op jit(solution)/shard_map/ppermute | solution.py:496

commit v10 on v9

--- a/solution.py
+++ b/solution.py
@@ -69,11 +69,12 @@
     place = lax.axis_index("seq") // (lax.axis_size("seq") // planes)
     mine_ref, other_ref, maps_ref = refs[-3:]
     maps_ref[...] = refs[planes][...]
-    count = mine_ref.shape[1]
+    count = mine_ref.shape[0] // planes
     for step in range(planes):
         first, second = refs[step][:count, :], refs[step][count:, :]
-        mine_ref[place ^ step] = jnp.where(side_of() == 0, first, second)
-        other_ref[place ^ step] = jnp.where(side_of() == 0, second, first)
+        at = pl.ds(pl.multiple_of((place ^ step) * count, 16), count)
+        mine_ref[at, :] = jnp.where(side_of() == 0, first, second)
+        other_ref[at, :] = jnp.where(side_of() == 0, second, first)
 
 
 def gates_kernel(many, *refs):
@@ -176,14 +177,13 @@
 
 
 def queries_kernel(layer, planes, rows_ref, in_ref, maps_ref, hidden_ref, out_ref):
-    if planes == rows_ref.shape[0]:
+    total = hidden_ref.shape[0]
+    count = total // planes
+    if layer == 0:
         rows = rows_ref[...]
     else:
-        count = hidden_ref.shape[0]
-        place = lax.axis_index("seq") // (lax.axis_size("seq") // rows_ref.shape[0])
-        rows = rows_ref[place, :count, :]
-    rows = rows.reshape(hidden_ref.shape[0], rows_ref.shape[2])
-    count = rows.shape[0] // planes
+        place = lax.axis_index("seq") // (lax.axis_size("seq") // (rows_ref.shape[0] // count))
+        rows = rows_ref[pl.ds(pl.multiple_of(place * count, 16), count), :]
     hidden = dot(rows, in_ref[layer])
     hidden_ref[...] = hidden
     spread = lax.rsqrt(jnp.mean(hidden * hidden, axis=1, keepdims=True) + epsilon)
@@ -241,7 +241,10 @@
         for at in range(1, len(some)):
             key_place = jnp.where(lane >= at * count, lane - at * count + offsets[at], key_place)
         allowed = key_place <= query_place
-        parts = [cat([rows[p, :count, :] for rows, _, _ in some], 0) for p in range(planes)]
+        parts = [
+            cat([rows[p * count : (p + 1) * count] for rows, _, _ in some], 0)
+            for p in range(planes)
+        ]
         low_rows = [p * band for p in range(planes)]
     else:
         size = len(some) * planes * count
@@ -250,8 +253,7 @@
         base_place = lane + plane * (stride - count)
         key_place = jnp.concatenate([base_place + offset for offset in offsets], axis=1)
         allowed = key_place >= query_place + member // per_plane * stride
-        rows = [rows[:, :count, :].reshape(planes * count, rows.shape[2]) for rows, _, _ in some]
-        parts, low_rows = [cat(rows, 0)], [0]
+        parts, low_rows = [cat([rows[: planes * count] for rows, _, _ in some], 0)], [0]
 
     def keys_and_values(source, g):
         low = g * group_cols
@@ -329,11 +331,10 @@
     )
 
 
-def chosen_rows(others, per_plane, place, rows):
-    plane, chip = place // per_plane, place % per_plane
+def chosen_rows(others, per_plane, chip, start):
     result = None
     for step, ref in enumerate(others):
-        value = ref[plane, rows, :].astype(jnp.float32)
+        value = ref[pl.ds(start, 16), :].astype(jnp.float32)
         here = chip_of(step, per_plane, True) == chip
         result = value if result is None else jnp.where(here, value, result)
     return result
@@ -401,7 +402,8 @@
     if last:
         held_ref, held_log_ref, out_ref = refs[:3]
         before = member - 1 + side
-        edge = chosen_rows(others, per_plane, jnp.maximum(before, 0), slice(count, count + 16))
+        chip = (before + per_plane) % per_plane
+        edge = chosen_rows(others, per_plane, chip, planes * count)
         edge = jnp.where(before >= 0, edge[0:2] + edge[2:4] + edge[4:6], 0.0)
         edge_log = edge[1:2]
         start = pl.multiple_of(side * count, 8)
@@ -417,14 +419,17 @@
         out_ref[count:, :count] = jnp.broadcast_to(loglik, (8, count))
         return
     held_ref, held_log_ref, narrow_ref = refs[:3]
+    narrow_ref[planes * count :, :] = jnp.zeros((16, channels), jnp.bfloat16)
     own = latent_ref[pl.ds(pl.multiple_of(side * count, 8), count), :]
     for p in range(planes):
         shift_mu = shift_all[p * count : (p + 1) * count]
         log_scale = log_all[p * count : (p + 1) * count]
         following = p * per_plane + member % per_plane + side
-        after = chosen_rows(others, per_plane, jnp.minimum(following, members - 1), slice(0, 16))
+        following_row = pl.multiple_of(jnp.minimum(following, members - 1) // per_plane * count, 16)
+        after = chosen_rows(others, per_plane, following % per_plane, following_row)
         here = member // per_plane == p
-        values = jnp.where(here, own, rows_of[False][0][p, :count, :].astype(jnp.float32))
+        rows = rows_of[False][0][p * count : (p + 1) * count, :]
+        values = jnp.where(here, own, rows.astype(jnp.float32))
         values = pltpu.roll(values, count - 1, 0)
         values = jnp.where(token == count - 1, after[:1], values)
         result = (values - shift_mu) * jnp.exp(-log_scale)
@@ -436,14 +441,18 @@
             held_ref[...] = result
             held_log_ref[...] = log_scale
 
-        edge = jnp.concatenate([shift_mu[count - 1 :], log_scale[count - 1 :]], axis=0)
-        terms = []
-        for _ in range(3):
-            terms.append(edge.astype(jnp.bfloat16).astype(jnp.float32))
-            edge = edge - terms[-1]
-        rest = jnp.zeros((16 - 6, channels), jnp.float32)
-        narrow_ref[p, :count, :] = result.astype(jnp.bfloat16)
-        narrow_ref[p, count:, :] = jnp.concatenate(terms + [rest], axis=0).astype(jnp.bfloat16)
+        narrow_ref[p * count : (p + 1) * count, :] = result.astype(jnp.bfloat16)
+
+        @pl.when(member // per_plane - (member % per_plane + side) // per_plane == p)
+        def send(shift_mu=shift_mu, log_scale=log_scale):
+            edge = jnp.concatenate([shift_mu[count - 1 :], log_scale[count - 1 :]], axis=0)
+            terms = []
+            for _ in range(3):
+                terms.append(edge.astype(jnp.bfloat16).astype(jnp.float32))
+                edge = edge - terms[-1]
+            rest = jnp.zeros((16 - 6, channels), jnp.float32)
+            rows = jnp.concatenate(terms + [rest], axis=0)
+            narrow_ref[planes * count :, :] = rows.astype(jnp.bfloat16)
 
 
 def second_half(cfg, kinds, maps, queries, sums, hidden, param_gain, latents, mine, others, mix_pieces, param_pieces, held=()):
@@ -456,7 +465,7 @@
         results = [
             ((count, channels), jnp.float32),
             ((count, channels), jnp.float32),
-            ((planes, count + 16, channels), jnp.bfloat16),
+            ((planes * count + 16, channels), jnp.bfloat16),
         ]
     scratch = [pltpu.VMEM((cfg["features"], param_pieces[0].shape[2]), jnp.bfloat16)]
     scratch += [pltpu.VMEM(one.shape, jnp.float32) for one in sums]
@@ -527,21 +536,24 @@
         hidden, queries = made
         arrived = in_plane(mine)
         if per_plane == 4:
-            early = [(mine, 0, False)] + ([(sibling, 0, True)] if layer == 0 else [])
+            one, two, three = (1, 2, 3)
+            if layer == 1:
+                sibling = swap(mine)
+            others = {0: sibling}
+            early = [(mine, 0, False)] + [(sibling, 0, True)]
             sums = attend(cfg, maps, queries, early)
-            first, second, *own = gate_all(arrived[:2] + ([] if layer == 0 else [mine]), sums)
-            others = [sibling if layer == 0 else swap(own[0]), swap(first)]
-            if layer == 0:
-                others.append(swap(second))
-            sums = attend(cfg, maps, queries, [(first, 1, False), (second, 2, False)], sums)
-            third, *again = gate_all(arrived[2:] + ([] if layer == 0 else [second]), sums)
-            if layer == 1:
-                others.append(swap(again[0]))
-            others.append(swap(third))
-            more = [(third, 3, False)] + ([] if layer == 0 else [(others[0], 0, True)])
-            sums = attend(cfg, maps, queries, more + [(others[1], 1, True)], sums)
-            mines = [mine, first, second, third]
-            kinds = [(2, True), (3, True)]
+            mines = {0: mine}
+            mines[one], mines[two] = gate_all([arrived[one - 1], arrived[two - 1]], sums)
+            others[one] = swap(mines[one])
+            others[two] = swap(mines[two])
+            batch = [(mines[one], one, False), (mines[two], two, False)]
+            sums = attend(cfg, maps, queries, batch, sums)
+            (mines[three],) = gate_all([arrived[three - 1]], sums)
+            others[three] = swap(mines[three])
+            batch = [(mines[three], three, False), (others[one], one, True)]
+            sums = attend(cfg, maps, queries, batch, sums)
+            kinds = [(two, True), (three, True)]
+            mines, others = [[each[step] for step in range(4)] for each in (mines, others)]
         else:
             others = [swap(mine) if layer == 1 else sibling]
             sums = attend(cfg, maps, queries, [(mine, 0, False), (others[0], 0, True)])
@@ -572,7 +584,7 @@
     in_all, tail, own_maps = prepare(
         in_proj, attn_gain, key_proj, value_proj, query_proj, []
     )
-    shape = (planes, count, channels)
+    shape = (planes * count, channels)
     mine, sibling, own_maps = on_chip(
         functools.partial(arrange_kernel, planes),
         "arrange",

time: 45.5 us -> 44.2 us (0.971)
  waiting for transfers between devices: 8.05 us -> 7.2 us
    ppermute x6, waiting for transfers between devices: 4.16 us -> 3.11 us  [in_plane(): arrived.append(lax.ppermute(mine, ('seq', 'head'), pairs))]
    pallas_call x19, Pallas kernels: 20.3 us -> 19.9 us  [on_chip(): pl.pallas_call(kernel, in_specs=[pl.BlockSpec(memory_space=pltpu.VMEM)] *...]
  transfers between devices with their start and end apart: 20 -> 20, of which waited for: 6 -> 7; matrix products, arithmetic and copies ran while one was open for 0% -> 0% of each run, Pallas kernels for 31% -> 31%
where the time goes in v10:
time: 44.2 us; the launch traced here: 44 us
  Pallas kernels  19.9 us (45%)
  starting transfers between devices  16 us (36%)
  waiting for transfers between devices  7.2 us (16%)
  between operations  0.9 us (2%)
    pallas_call x19, Pallas kernels, on_chip(): pl.pallas_call(kernel, in_specs=[pl.BlockSpec(memory_space=pltpu.VMEM)] *...  19.9 us
    ppermute x6, starting transfers between devices, in_plane(): arrived.append(lax.ppermute(mine, ('seq', 'head'), pairs))  7.46 us
    ppermute x3, starting transfers between devices, body(): lax.ppermute(rounded, 'seq', [(i, i ^ b * per_plane) for i in range(membe...  5.66 us
    ppermute x6, waiting for transfers between devices, in_plane(): arrived.append(lax.ppermute(mine, ('seq', 'head'), pairs))  3.11 us
    ppermute x3, waiting for transfers between devices, body(): lax.ppermute(rounded, 'seq', [(i, i ^ b * per_plane) for i in range(membe...  2.7 us
    ppermute x8, starting transfers between devices, swap(): return lax.ppermute(array, 'head', [(i, i ^ 1) for i in range(ways)])  2.26 us
    ppermute x8, waiting for transfers between devices, swap(): return lax.ppermute(array, 'head', [(i, i ^ 1) for i in range(ways)])  1.38 us
  transfers between devices with their start and end apart: 20, of which 7 were waited for; matrix products, arithmetic and copies ran while one was open for 0% of the time, Pallas kernels for 31%

profile of v10, /device:TPU:0, one launch (start us, length us, event | category | flops | bytes accessed | tf_op | source)
XLA Modules:
  0.0 44.0 jit_solution(9374768289844082658)
XLA Ops:
  1.2 0.9 %round.1.refs_0_ = bf16[192,128]{1,0:T(8,128)(2,1)S(1)} custom-call(f32[192,128]{1,0:T(8,128)} %latent_ref.3), custom_call_target="tpu_custom_call" | custom-call | tf_op jit(solution)/shard_map/round/pallas_call | solution.py:42
  2.1 3.1 %collective-permute-start = (bf16[192,128]{1,0:T(8,128)(2,1)S(1)}, bf16[192,128]{1,0:T(8,128)(2,1)S(1)}, u32[]{:S(2)}, u32[]{:S(2)}) collective-permute-start(bf16[192,128]{1,0:T(8,128)(2,1)S(1)} %round.1.refs_0_), channel_id=1, source_target_pairs={{0,8},{2,10},{4,12},{6,14},{8,0},{10,2},{12,4},{14,6},{16,24},{18,... | collective-permute-start | bytes 147464 | tf_op jit(solution)/shard_map/ppermute | solution.py:580
  5.2 2.6 %collective-permute-start.1 = (bf16[192,128]{1,0:T(8,128)(2,1)S(1)}, bf16[192,128]{1,0:T(8,128)(2,1)S(1)}, u32[]{:S(2)}, u32[]{:S(2)}) collective-permute-start(bf16[192,128]{1,0:T(8,128)(2,1)S(1)} %round.1.refs_0_), channel_id=1, source_target_pairs={{0,16},{2,18},{4,20},{6,22},{8,24},{10,26},{12,28},{14,30},{16,0},... | collective-permute-start | bytes 147464 | tf_op jit(solution)/shard_map/ppermute | solution.py:580
  7.8 3.2 %prepare.1 = (bf16[2,128,1536]{2,1,0:T(8,128)(2,1)S(1)}, bf16[2,256,256]{2,1,0:T(8,128)(2,1)S(1)}, bf16[2,384,256]{2,1,0:T(8,128)(2,1)S(1)}) custom-call(bf16[2,128,1536]{2,1,0:T(8,128)(2,1)} %in_src.1, f32[2,1536]{1,0:T(2,128)} %gain_src.1, bf16[2,1536,128]{2,1,0:T(8,128)(2,1)} %key_src.1, bf16[2,1536,128]{2,1,0:T(8,128)(2,1)} %value_src.1, ...), custom_call_target="tpu_custom_call" | custom-call | tf_op jit(solution)/shard_map/prepare/pallas_call | solution.py:42
  11.1 2.6 %collective-permute-done.2.refs_3_ = bf16[192,128]{1,0:T(8,128)(2,1)S(1)} collective-permute-done((bf16[192,128]{1,0:T(8,128)(2,1)S(1)}, bf16[192,128]{1,0:T(8,128)(2,1)S(1)}, u32[]{:S(2)}, u32[]{:S(2)}) %collective-permute-start.2) | collective-permute-done | bytes 49184 | tf_op jit(solution)/shard_map/ppermute | solution.py:580
  13.8 1.6 %collective-permute-start.7 = (bf16[384,128]{1,0:T(8,128)(2,1)S(1)}, bf16[384,128]{1,0:T(8,128)(2,1)S(1)}, u32[]{:S(2)}, u32[]{:S(2)}) collective-permute-start(bf16[384,128]{1,0:T(8,128)(2,1)S(1)} %get-tuple-element.45.rows_ref.refs_0_.refs_3_), channel_id=1, source_target_pairs={{0,2},{1,5},{2,0},{3,7},{4,6},{5,1},{6,4},{7,3},{8,10},{9,13},{10,... | collective-permute-start | bytes 294920 | tf_op jit(solution)/shard_map/ppermute | solution.py:523
  15.4 1.5 %collective-permute-start.8 = (bf16[384,128]{1,0:T(8,128)(2,1)S(1)}, bf16[384,128]{1,0:T(8,128)(2,1)S(1)}, u32[]{:S(2)}, u32[]{:S(2)}) collective-permute-start(bf16[384,128]{1,0:T(8,128)(2,1)S(1)} %get-tuple-element.45.rows_ref.refs_0_.refs_3_), channel_id=1, source_target_pairs={{0,4},{1,3},{2,6},{3,1},{4,0},{5,7},{6,2},{7,5},{8,12},{9,11},{10,... | collective-permute-start | bytes 294920 | tf_op jit(solution)/shard_map/ppermute | solution.py:523
  17.5 0.9 %queries.2 = (f32[384,1536]{1,0:T(8,128)S(1)}, bf16[1,1536,256]{2,1,0:T(8,128)(2,1)S(1)}) custom-call(bf16[384,128]{1,0:T(8,128)(2,1)S(1)} %get-tuple-element.45.rows_ref.refs_0_.refs_3_, bf16[2,128,1536]{2,1,0:T(8,128)(2,1)S(1)} %get-tuple-element.46.in_ref, bf16[256,256]{1,0:T(8,128)(2,1)S(1)} %get-tuple-element.47.maps_ref), custom_call_target="tpu_custom_call" | custom-call | tf_op jit(solution)/shard_map/queries/pallas_call | solution.py:42
  18.3 1.8 %attend.6 = (f32[1,1536,256]{2,1,0:T(8,128)S(1)}, f32[1,1536,128]{2,1,0:T(8,128)S(1)}, f32[1,1536,64]{2,1,0:T(8,128)S(1)}) custom-call(bf16[768,256]{1,0:T(8,128)(2,1)S(1)} %get-tuple-element.44.maps_ref, bf16[1,1536,256]{2,1,0:T(8,128)(2,1)S(1)} %get-tuple-element.48.query_ref, bf16[384,128]{1,0:T(8,128)(2,1)S(1)} %get-tuple-element.45.rows_ref.refs_0_.refs_3_, ...), custom_call_target="tpu_custom_call" | custom-call | tf_op jit(solution)/shard_map/attend/pallas_call | solution.py:42
  20.1 1.1 %collective-permute-done.8.refs_1_ = bf16[384,128]{1,0:T(8,128)(2,1)S(1)} collective-permute-done((bf16[384,128]{1,0:T(8,128)(2,1)S(1)}, bf16[384,128]{1,0:T(8,128)(2,1)S(1)}, u32[]{:S(2)}, u32[]{:S(2)}) %collective-permute-start.8) | collective-permute-done | bytes 98336 | tf_op jit(solution)/shard_map/ppermute | solution.py:523
  21.3 1.8 %attend.7 = (f32[1,1536,256]{2,1,0:T(8,128)S(1)}, f32[1,1536,128]{2,1,0:T(8,128)S(1)}, f32[1,1536,64]{2,1,0:T(8,128)S(1)}) custom-call(bf16[768,256]{1,0:T(8,128)(2,1)S(1)} %get-tuple-element.44.maps_ref, bf16[1,1536,256]{2,1,0:T(8,128)(2,1)S(1)} %get-tuple-element.48.query_ref, bf16[384,128]{1,0:T(8,128)(2,1)S(1)} %get-tuple-element.54.refs_0_.refs_4_, ...), custom_call_target="tpu_custom_call" | custom-call | tf_op jit(solution)/shard_map/attend/pallas_call | solution.py:42
  23.1 0.6 %collective-permute-start.10 = (bf16[384,128]{1,0:T(8,128)(2,1)S(1)}, bf16[384,128]{1,0:T(8,128)(2,1)S(1)}, u32[]{:S(2)}, u32[]{:S(2)}) collective-permute-start(bf16[384,128]{1,0:T(8,128)(2,1)S(1)} %get-tuple-element.55.refs_1_.refs_5_), channel_id=1, source_target_pairs={{0,1},{1,0},{2,3},{3,2},{4,5},{5,4},{6,7},{7,6},{8,9},{9,8},{10,11... | collective-permute-start | bytes 294920 | tf_op jit(solution)/shard_map/ppermute | solution.py:505
  23.8 1.7 %attend.8 = (f32[1,1536,256]{2,1,0:T(8,128)S(1)}, f32[1,1536,128]{2,1,0:T(8,128)S(1)}, f32[1,1536,64]{2,1,0:T(8,128)S(1)}) custom-call(bf16[768,256]{1,0:T(8,128)(2,1)S(1)} %get-tuple-element.44.maps_ref, bf16[1,1536,256]{2,1,0:T(8,128)(2,1)S(1)} %get-tuple-element.48.query_ref, bf16[384,128]{1,0:T(8,128)(2,1)S(1)} %gate.5.refs_0_.refs_6_, ...), custom_call_target="tpu_custom_call" | custom-call | tf_op jit(solution)/shard_map/attend/pallas_call | solution.py:42
  25.6 3.6 %second_half.2 = (f32[96,128]{1,0:T(8,128)S(1)}, f32[96,128]{1,0:T(8,128)S(1)}, bf16[400,128]{1,0:T(8,128)(2,1)S(1)}) custom-call(bf16[768,256]{1,0:T(8,128)(2,1)S(1)} %get-tuple-element.44.maps_ref, bf16[1,1536,256]{2,1,0:T(8,128)(2,1)S(1)} %get-tuple-element.48.query_ref, f32[384,1536]{1,0:T(8,128)S(1)} %get-tuple-element.49.hidden_ref, ...), custom_call_target="tpu_custom_call" | custom-call | tf_op jit(solution)/shard_map/second_half/pallas_call | solution.py:42
  29.2 0.6 %collective-permute-start.15 = (bf16[400,128]{1,0:T(8,128)(2,1)S(1)}, bf16[400,128]{1,0:T(8,128)(2,1)S(1)}, u32[]{:S(2)}, u32[]{:S(2)}) collective-permute-start(bf16[400,128]{1,0:T(8,128)(2,1)S(1)} %get-tuple-element.62.rows_ref.refs_0_.refs_2_), channel_id=1, source_target_pairs={{0,1},{1,0},{2,3},{3,2},{4,5},{5,4},{6,7},{7,6},{8,9},{9,8},{10,11... | collective-permute-start | bytes 307208 | tf_op jit(solution)/shard_map/ppermute | solution.py:505
  30.2 2.0 %collective-permute-start.14 = (bf16[400,128]{1,0:T(8,128)(2,1)S(1)}, bf16[400,128]{1,0:T(8,128)(2,1)S(1)}, u32[]{:S(2)}, u32[]{:S(2)}) collective-permute-start(bf16[400,128]{1,0:T(8,128)(2,1)S(1)} %get-tuple-element.62.rows_ref.refs_0_.refs_2_), channel_id=1, source_target_pairs={{0,4},{1,3},{2,6},{3,1},{4,0},{5,7},{6,2},{7,5},{8,12},{9,11},{10,... | collective-permute-start | bytes 307208 | tf_op jit(solution)/shard_map/ppermute | solution.py:523
  32.2 1.5 %collective-permute-start.12 = (bf16[400,128]{1,0:T(8,128)(2,1)S(1)}, bf16[400,128]{1,0:T(8,128)(2,1)S(1)}, u32[]{:S(2)}, u32[]{:S(2)}) collective-permute-start(bf16[400,128]{1,0:T(8,128)(2,1)S(1)} %get-tuple-element.62.rows_ref.refs_0_.refs_2_), channel_id=1, source_target_pairs={{0,6},{1,7},{2,4},{3,5},{4,2},{5,3},{6,0},{7,1},{8,14},{9,15},{10,... | collective-permute-start | bytes 307208 | tf_op jit(solution)/shard_map/ppermute | solution.py:523
  34.2 0.9 %attend.9 = (f32[1,384,256]{2,1,0:T(8,128)S(1)}, f32[1,384,128]{2,1,0:T(8,128)S(1)}) custom-call(bf16[768,256]{1,0:T(8,128)(2,1)S(1)} %get-tuple-element.43.maps_ref, bf16[1,384,256]{2,1,0:T(8,128)(2,1)S(1)} %get-tuple-element.64.query_ref, bf16[400,128]{1,0:T(8,128)(2,1)S(1)} %get-tuple-element.62.rows_ref.refs_0_.refs_2_, ...), custom_call_target="tpu_custom_call" | custom-call | tf_op jit(solution)/shard_map/attend/pallas_call | solution.py:42
  35.6 0.9 %attend.10 = (f32[1,384,256]{2,1,0:T(8,128)S(1)}, f32[1,384,128]{2,1,0:T(8,128)S(1)}) custom-call(bf16[768,256]{1,0:T(8,128)(2,1)S(1)} %get-tuple-element.43.maps_ref, bf16[1,384,256]{2,1,0:T(8,128)(2,1)S(1)} %get-tuple-element.64.query_ref, bf16[400,128]{1,0:T(8,128)(2,1)S(1)} %get-tuple-element.68.refs_0_.refs_3_, ...), custom_call_target="tpu_custom_call" | custom-call | tf_op jit(solution)/shard_map/attend/pallas_call | solution.py:42
  37.0 1.8 %collective-permute-done.12.refs_0_ = bf16[400,128]{1,0:T(8,128)(2,1)S(1)} collective-permute-done((bf16[400,128]{1,0:T(8,128)(2,1)S(1)}, bf16[400,128]{1,0:T(8,128)(2,1)S(1)}, u32[]{:S(2)}, u32[]{:S(2)}) %collective-permute-start.12) | collective-permute-done | bytes 102432 | tf_op jit(solution)/shard_map/ppermute | solution.py:523
  38.9 0.9 %attend.11 = (f32[1,384,256]{2,1,0:T(8,128)S(1)}, f32[1,384,128]{2,1,0:T(8,128)S(1)}) custom-call(bf16[768,256]{1,0:T(8,128)(2,1)S(1)} %get-tuple-element.43.maps_ref, bf16[1,384,256]{2,1,0:T(8,128)(2,1)S(1)} %get-tuple-element.64.query_ref, bf16[400,128]{1,0:T(8,128)(2,1)S(1)} %gate.7.refs_0_.refs_5_, ...), custom_call_target="tpu_custom_call" | custom-call | tf_op jit(solution)/shard_map/attend/pallas_call | solution.py:42
  40.2 1.9 %second_half.3.own_ref = f32[104,128]{1,0:T(8,128)S(1)} custom-call(bf16[768,256]{1,0:T(8,128)(2,1)S(1)} %get-tuple-element.43.maps_ref, bf16[1,384,256]{2,1,0:T(8,128)(2,1)S(1)} %get-tuple-element.64.query_ref, f32[96,1536]{1,0:T(8,128)S(1)} %get-tuple-element.65.hidden_ref, f32[2,1536]{1,0:T(2,128)S(1)} %copy-done.3, f32[192,128]{1,0:T(8,128)S(1)} %copy-done.2, ...), custom_call_target="tpu_custom_call" | custom-call | tf_op jit(solution)/shard_map/second_half/pallas_call | solution.py:42
  42.3 1.0 %collective-permute-done.19.other_ref = f32[104,128]{1,0:T(8,128)S(1)} collective-permute-done((f32[104,128]{1,0:T(8,128)S(1)}, f32[104,128]{1,0:T(8,128)S(1)}, u32[]{:S(2)}, u32[]{:S(2)}) %collective-permute-start.19) | collective-permute-done | bytes 53280 | tf_op jit(solution)/shard_map/ppermute | solution.py:505
  43.4 0.7 %finish.1 = (f32[192,128]{1,0:T(8,128)}, f32[1,192]{1,0:T(1,128)}) custom-call(f32[104,128]{1,0:T(8,128)S(1)} %second_half.3.own_ref, f32[104,128]{1,0:T(8,128)S(1)} %collective-permute-done.19.other_ref), custom_call_target="tpu_custom_call" | custom-call | tf_op jit(solution)/shard_map/finish/pallas_call | solution.py:42
  (43 shorter events, 4.1 us)
Async XLA Ops:
  0.6 13.1 %collective-permute-start.3 = (bf16[2,128,1536]{2,1,0:T(8,128)(2,1)}, bf16[2,128,1536]{2,1,0:T(8,128)(2,1)S(1)}, u32[]{:S(2)}, u32[]{:S(2)}) collective-permute-start(bf16[2,128,1536]{2,1,0:T(8,128)(2,1)} %refs_10_.1), channel_id=1, source_target_pairs={{1,0},{0,1},{3,2},{2,3},{5,4},{4,5},{7,6},{6,7},{9,8},{8,9},{11,10... | collective-permute-start | bytes 2359304 | tf_op jit(solution)/shard_map/ppermute | solution.py:511
  1.1 12.5 %collective-permute-start.4 = (bf16[2,768,256]{2,1,0:T(8,128)(2,1)}, bf16[2,768,256]{2,1,0:T(8,128)(2,1)S(1)}, u32[]{:S(2)}, u32[]{:S(2)}) collective-permute-start(bf16[2,768,256]{2,1,0:T(8,128)(2,1)} %refs_12_.1), channel_id=1, source_target_pairs={{1,0},{0,1},{3,2},{2,3},{5,4},{4,5},{7,6},{6,7},{9,8},{8,9},{11,10... | collective-permute-start | bytes 2359304 | tf_op jit(solution)/shard_map/ppermute | solution.py:511
  2.1 8.8 %collective-permute-start = (bf16[192,128]{1,0:T(8,128)(2,1)S(1)}, bf16[192,128]{1,0:T(8,128)(2,1)S(1)}, u32[]{:S(2)}, u32[]{:S(2)}) collective-permute-start(bf16[192,128]{1,0:T(8,128)(2,1)S(1)} %round.1.refs_0_), channel_id=1, source_target_pairs={{0,8},{2,10},{4,12},{6,14},{8,0},{10,2},{12,4},{14,6},{16,24},{18,... | collective-permute-start | bytes 147464 | tf_op jit(solution)/shard_map/ppermute | solution.py:580
  5.2 5.9 %collective-permute-start.1 = (bf16[192,128]{1,0:T(8,128)(2,1)S(1)}, bf16[192,128]{1,0:T(8,128)(2,1)S(1)}, u32[]{:S(2)}, u32[]{:S(2)}) collective-permute-start(bf16[192,128]{1,0:T(8,128)(2,1)S(1)} %round.1.refs_0_), channel_id=1, source_target_pairs={{0,16},{2,18},{4,20},{6,22},{8,24},{10,26},{12,28},{14,30},{16,0},... | collective-permute-start | bytes 147464 | tf_op jit(solution)/shard_map/ppermute | solution.py:580
  7.8 5.9 %collective-permute-start.2 = (bf16[192,128]{1,0:T(8,128)(2,1)S(1)}, bf16[192,128]{1,0:T(8,128)(2,1)S(1)}, u32[]{:S(2)}, u32[]{:S(2)}) collective-permute-start(bf16[192,128]{1,0:T(8,128)(2,1)S(1)} %round.1.refs_0_), channel_id=1, source_target_pairs={{0,24},{2,26},{4,28},{6,30},{8,16},{10,18},{12,20},{14,22},{16,8},... | collective-permute-start | bytes 147464 | tf_op jit(solution)/shard_map/ppermute | solution.py:580
  13.8 3.6 %collective-permute-start.5 = (bf16[2,384,256]{2,1,0:T(8,128)(2,1)S(1)}, bf16[2,384,256]{2,1,0:T(8,128)(2,1)S(1)}, u32[]{:S(2)}, u32[]{:S(2)}) collective-permute-start(bf16[2,384,256]{2,1,0:T(8,128)(2,1)S(1)} %get-tuple-element.42.refs_0_), channel_id=1, source_target_pairs={{1,0},{0,1},{3,2},{2,3},{5,4},{4,5},{7,6},{6,7},{9,8},{8,9},{11,10... | collective-permute-start | bytes 1179656 | tf_op jit(solution)/shard_map/ppermute | solution.py:511
  13.8 6.3 %collective-permute-start.7 = (bf16[384,128]{1,0:T(8,128)(2,1)S(1)}, bf16[384,128]{1,0:T(8,128)(2,1)S(1)}, u32[]{:S(2)}, u32[]{:S(2)}) collective-permute-start(bf16[384,128]{1,0:T(8,128)(2,1)S(1)} %get-tuple-element.45.rows_ref.refs_0_.refs_3_), channel_id=1, source_target_pairs={{0,2},{1,5},{2,0},{3,7},{4,6},{5,1},{6,4},{7,3},{8,10},{9,13},{10,... | collective-permute-start | bytes 294920 | tf_op jit(solution)/shard_map/ppermute | solution.py:523
  15.4 5.8 %collective-permute-start.8 = (bf16[384,128]{1,0:T(8,128)(2,1)S(1)}, bf16[384,128]{1,0:T(8,128)(2,1)S(1)}, u32[]{:S(2)}, u32[]{:S(2)}) collective-permute-start(bf16[384,128]{1,0:T(8,128)(2,1)S(1)} %get-tuple-element.45.rows_ref.refs_0_.refs_3_), channel_id=1, source_target_pairs={{0,4},{1,3},{2,6},{3,1},{4,0},{5,7},{6,2},{7,5},{8,12},{9,11},{10,... | collective-permute-start | bytes 294920 | tf_op jit(solution)/shard_map/ppermute | solution.py:523
  16.9 6.7 %collective-permute-start.6 = (bf16[384,128]{1,0:T(8,128)(2,1)S(1)}, bf16[384,128]{1,0:T(8,128)(2,1)S(1)}, u32[]{:S(2)}, u32[]{:S(2)}) collective-permute-start(bf16[384,128]{1,0:T(8,128)(2,1)S(1)} %get-tuple-element.45.rows_ref.refs_0_.refs_3_), channel_id=1, source_target_pairs={{0,6},{1,7},{2,4},{3,5},{4,2},{5,3},{6,0},{7,1},{8,14},{9,15},{10,... | collective-permute-start | bytes 294920 | tf_op jit(solution)/shard_map/ppermute | solution.py:523
  21.2 2.6 %collective-permute-start.9 = (bf16[384,128]{1,0:T(8,128)(2,1)S(1)}, bf16[384,128]{1,0:T(8,128)(2,1)S(1)}, u32[]{:S(2)}, u32[]{:S(2)}) collective-permute-start(bf16[384,128]{1,0:T(8,128)(2,1)S(1)} %get-tuple-element.54.refs_0_.refs_4_), channel_id=1, source_target_pairs={{0,1},{1,0},{2,3},{3,2},{4,5},{5,4},{6,7},{7,6},{8,9},{9,8},{10,11... | collective-permute-start | bytes 294920 | tf_op jit(solution)/shard_map/ppermute | solution.py:505
  23.1 2.5 %collective-permute-start.10 = (bf16[384,128]{1,0:T(8,128)(2,1)S(1)}, bf16[384,128]{1,0:T(8,128)(2,1)S(1)}, u32[]{:S(2)}, u32[]{:S(2)}) collective-permute-start(bf16[384,128]{1,0:T(8,128)(2,1)S(1)} %get-tuple-element.55.refs_1_.refs_5_), channel_id=1, source_target_pairs={{0,1},{1,0},{2,3},{3,2},{4,5},{5,4},{6,7},{7,6},{8,9},{9,8},{10,11... | collective-permute-start | bytes 294920 | tf_op jit(solution)/shard_map/ppermute | solution.py:505
  23.6 1.9 %copy-start = (bf16[2,128,1536]{2,1,0:T(8,128)(2,1)S(1)}, bf16[2,128,1536]{2,1,0:T(8,128)(2,1)}, u32[]{:S(2)}) copy-start(bf16[2,128,1536]{2,1,0:T(8,128)(2,1)} %refs_10_.1) | copy-start | bytes 2359300
  23.6 1.9 %copy-start.1 = (bf16[2,768,256]{2,1,0:T(8,128)(2,1)S(1)}, bf16[2,768,256]{2,1,0:T(8,128)(2,1)}, u32[]{:S(2)}) copy-start(bf16[2,768,256]{2,1,0:T(8,128)(2,1)} %refs_12_.1) | copy-start | bytes 2359300
  23.6 1.9 %copy-start.2 = (f32[192,128]{1,0:T(8,128)S(1)}, f32[192,128]{1,0:T(8,128)}, u32[]{:S(2)}) copy-start(f32[192,128]{1,0:T(8,128)} %latent_ref.3) | copy-start | bytes 294916
  23.7 1.9 %copy-start.3 = (f32[2,1536]{1,0:T(2,128)S(1)}, f32[2,1536]{1,0:T(2,128)}, u32[]{:S(2)}) copy-start(f32[2,1536]{1,0:T(2,128)} %gain_ref.3) | copy-start | bytes 36868
  23.7 1.9 %collective-permute-start.11 = (bf16[384,128]{1,0:T(8,128)(2,1)S(1)}, bf16[384,128]{1,0:T(8,128)(2,1)S(1)}, u32[]{:S(2)}, u32[]{:S(2)}) collective-permute-start(bf16[384,128]{1,0:T(8,128)(2,1)S(1)} %gate.5.refs_0_.refs_6_), channel_id=1, source_target_pairs={{0,1},{1,0},{2,3},{3,2},{4,5},{5,4},{6,7},{7,6},{8,9},{9,8},{10,11... | collective-permute-start | bytes 294920 | tf_op jit(solution)/shard_map/ppermute | solution.py:505
  29.2 5.0 %collective-permute-start.15 = (bf16[400,128]{1,0:T(8,128)(2,1)S(1)}, bf16[400,128]{1,0:T(8,128)(2,1)S(1)}, u32[]{:S(2)}, u32[]{:S(2)}) collective-permute-start(bf16[400,128]{1,0:T(8,128)(2,1)S(1)} %get-tuple-element.62.rows_ref.refs_0_.refs_2_), channel_id=1, source_target_pairs={{0,1},{1,0},{2,3},{3,2},{4,5},{5,4},{6,7},{7,6},{8,9},{9,8},{10,11... | collective-permute-start | bytes 307208 | tf_op jit(solution)/shard_map/ppermute | solution.py:505
  29.8 5.4 %collective-permute-start.13 = (bf16[400,128]{1,0:T(8,128)(2,1)S(1)}, bf16[400,128]{1,0:T(8,128)(2,1)S(1)}, u32[]{:S(2)}, u32[]{:S(2)}) collective-permute-start(bf16[400,128]{1,0:T(8,128)(2,1)S(1)} %get-tuple-element.62.rows_ref.refs_0_.refs_2_), channel_id=1, source_target_pairs={{0,2},{1,5},{2,0},{3,7},{4,6},{5,1},{6,4},{7,3},{8,10},{9,13},{10,... | collective-permute-start | bytes 307208 | tf_op jit(solution)/shard_map/ppermute | solution.py:523
  30.2 5.2 %collective-permute-start.14 = (bf16[400,128]{1,0:T(8,128)(2,1)S(1)}, bf16[400,128]{1,0:T(8,128)(2,1)S(1)}, u32[]{:S(2)}, u32[]{:S(2)}) collective-permute-start(bf16[400,128]{1,0:T(8,128)(2,1)S(1)} %get-tuple-element.62.rows_ref.refs_0_.refs_2_), channel_id=1, source_target_pairs={{0,4},{1,3},{2,6},{3,1},{4,0},{5,7},{6,2},{7,5},{8,12},{9,11},{10,... | collective-permute-start | bytes 307208 | tf_op jit(solution)/shard_map/ppermute | solution.py:523
  32.2 6.6 %collective-permute-start.12 = (bf16[400,128]{1,0:T(8,128)(2,1)S(1)}, bf16[400,128]{1,0:T(8,128)(2,1)S(1)}, u32[]{:S(2)}, u32[]{:S(2)}) collective-permute-start(bf16[400,128]{1,0:T(8,128)(2,1)S(1)} %get-tuple-element.62.rows_ref.refs_0_.refs_2_), channel_id=1, source_target_pairs={{0,6},{1,7},{2,4},{3,5},{4,2},{5,3},{6,0},{7,1},{8,14},{9,15},{10,... | collective-permute-start | bytes 307208 | tf_op jit(solution)/shard_map/ppermute | solution.py:523
  35.4 3.5 %collective-permute-start.16 = (bf16[400,128]{1,0:T(8,128)(2,1)S(1)}, bf16[400,128]{1,0:T(8,128)(2,1)S(1)}, u32[]{:S(2)}, u32[]{:S(2)}) collective-permute-start(bf16[400,128]{1,0:T(8,128)(2,1)S(1)} %get-tuple-element.68.refs_0_.refs_3_), channel_id=1, source_target_pairs={{0,1},{1,0},{2,3},{3,2},{4,5},{5,4},{6,7},{7,6},{8,9},{9,8},{10,11... | collective-permute-start | bytes 307208 | tf_op jit(solution)/shard_map/ppermute | solution.py:505
  36.6 3.3 %collective-permute-start.17 = (bf16[400,128]{1,0:T(8,128)(2,1)S(1)}, bf16[400,128]{1,0:T(8,128)(2,1)S(1)}, u32[]{:S(2)}, u32[]{:S(2)}) collective-permute-start(bf16[400,128]{1,0:T(8,128)(2,1)S(1)} %get-tuple-element.69.refs_1_.refs_4_), channel_id=1, source_target_pairs={{0,1},{1,0},{2,3},{3,2},{4,5},{5,4},{6,7},{7,6},{8,9},{9,8},{10,11... | collective-permute-start | bytes 307208 | tf_op jit(solution)/shard_map/ppermute | solution.py:505
  38.8 1.4 %collective-permute-start.18 = (bf16[400,128]{1,0:T(8,128)(2,1)S(1)}, bf16[400,128]{1,0:T(8,128)(2,1)S(1)}, u32[]{:S(2)}, u32[]{:S(2)}) collective-permute-start(bf16[400,128]{1,0:T(8,128)(2,1)S(1)} %gate.7.refs_0_.refs_5_), channel_id=1, source_target_pairs={{0,1},{1,0},{2,3},{3,2},{4,5},{5,4},{6,7},{7,6},{8,9},{9,8},{10,11... | collective-permute-start | bytes 307208 | tf_op jit(solution)/shard_map/ppermute | solution.py:505
  42.1 1.3 %collective-permute-start.19 = (f32[104,128]{1,0:T(8,128)S(1)}, f32[104,128]{1,0:T(8,128)S(1)}, u32[]{:S(2)}, u32[]{:S(2)}) collective-permute-start(f32[104,128]{1,0:T(8,128)S(1)} %second_half.3.own_ref), channel_id=1, source_target_pairs={{0,1},{1,0},{2,3},{3,2},{4,5},{5,4},{6,7},{7,6},{8,9},{9,8},{10,11... | collective-permute-start | bytes 159752 | tf_op jit(solution)/shard_map/ppermute | solution.py:505

commit v11 on v10

--- a/solution.py
+++ b/solution.py
@@ -80,6 +80,31 @@
 def gates_kernel(many, *refs):
     for source, target in zip(refs[:many], refs[-many:]):
         target[...] = source[...]
+
+
+def stack_kernel(one_ref, two_ref, *refs):
+    rows = one_ref.shape[0]
+    for source, target, at in ((one_ref, refs[-3], 0), (two_ref, refs[-2], rows)):
+        target[...] = source[...]
+        refs[-1][at : at + rows, :] = source[...]
+
+
+def stack(one, two, made):
+    rows, channels = one.shape
+    shapes = [(rows, channels), (rows, channels), (2 * rows, channels)]
+    results = [(shape, one.dtype) for shape in shapes]
+    return on_chip(stack_kernel, "stack", [one, two, *made], results)
+
+
+def unstack_kernel(both_ref, one_ref, two_ref):
+    rows = one_ref.shape[0]
+    one_ref[...] = both_ref[:rows, :]
+    two_ref[...] = both_ref[rows:, :]
+
+
+def unstack(both):
+    shape = (both.shape[0] // 2, both.shape[1])
+    return on_chip(unstack_kernel, "unstack", [both], [(shape, both.dtype)] * 2)
 
 
 def gate_all(rows, made):
@@ -373,6 +398,10 @@
 
         lax.fori_loop(1, per_plane, one_step, 0)
 
+    share = features // pieces
+    for j, ref in enumerate(param_refs):
+        at = pl.multiple_of(lax.rem(way + j, pieces) * share, 16)
+        param_all[pl.ds(at, share), :] = ref[layer]
     mixture = hidden_ref[...]
     bands = mixture.shape[0] // count
     head = lax.broadcasted_iota(jnp.int32, (1, group_cols), 1) // HS
@@ -390,12 +419,8 @@
         rows = cat([ref[layer] for ref in mix_refs[2 * g : 2 * g + 2]], 0)
         mixture = mixture + dot(cat(attended, 0).astype(jnp.bfloat16), rows)
     spread = lax.rsqrt(jnp.mean(mixture * mixture, axis=1, keepdims=True) + epsilon)
-    scaled = (mixture * spread * gain_ref[layer : layer + 1, :]).astype(jnp.bfloat16)
-    share = features // pieces
-    for j, ref in enumerate(param_refs):
-        at = pl.multiple_of(lax.rem(way + j, pieces) * share, 16)
-        param_all[pl.ds(at, share), :] = ref[layer]
-    predicted = dot(scaled, param_all[...])
+    scaled = (mixture * gain_ref[layer : layer + 1, :]).astype(jnp.bfloat16)
+    predicted = dot(scaled, param_all[...]) * spread
     shift_all = predicted[:, :channels]
     log_all = 2.0 * jnp.tanh(0.5 * predicted[:, channels:])
     token = lax.broadcasted_iota(jnp.int32, (count, 1), 0)
@@ -543,9 +568,8 @@
             early = [(mine, 0, False)] + [(sibling, 0, True)]
             sums = attend(cfg, maps, queries, early)
             mines = {0: mine}
-            mines[one], mines[two] = gate_all([arrived[one - 1], arrived[two - 1]], sums)
-            others[one] = swap(mines[one])
-            others[two] = swap(mines[two])
+            mines[one], mines[two], both = stack(arrived[one - 1], arrived[two - 1], sums)
+            others[one], others[two] = unstack(swap(both))
             batch = [(mines[one], one, False), (mines[two], two, False)]
             sums = attend(cfg, maps, queries, batch, sums)
             (mines[three],) = gate_all([arrived[three - 1]], sums)

time: 44.2 us -> 43.8 us (level)
  starting transfers between devices: 16 us -> 15.5 us
    ppermute x8 -> x6, starting transfers between devices: 2.26 us -> 1.61 us  [swap(): return lax.ppermute(array, 'head', [(i, i ^ 1) for i in range(ways)])]
    pallas_call x19 -> x21, Pallas kernels: 19.9 us -> 19.7 us  [on_chip(): pl.pallas_call(kernel, in_specs=[pl.BlockSpec(memory_space=pltpu.VMEM)] *...]
    ppermute x8 -> x6, waiting for transfers between devices: 1.38 us -> 1.35 us  [swap(): return lax.ppermute(array, 'head', [(i, i ^ 1) for i in range(ways)])]
  transfers between devices with their start and end apart: 20 -> 18, of which waited for: 7 -> 7; matrix products, arithmetic and copies ran while one was open for 0% -> 0% of each run, Pallas kernels for 31% -> 32%
where the time goes in v11:
time: 43.8 us; the launch traced here: 43.6 us
  Pallas kernels  19.7 us (45%)
  starting transfers between devices  15.5 us (35%)
  waiting for transfers between devices  7.5 us (17%)
  between operations  0.91 us (2%)
    pallas_call x21, Pallas kernels, on_chip(): pl.pallas_call(kernel, in_specs=[pl.BlockSpec(memory_space=pltpu.VMEM)] *...  19.7 us
    ppermute x6, starting transfers between devices, in_plane(): arrived.append(lax.ppermute(mine, ('seq', 'head'), pairs))  7.51 us
    ppermute x3, starting transfers between devices, body(): lax.ppermute(rounded, 'seq', [(i, i ^ b * per_plane) for i in range(membe...  5.66 us
    ppermute x6, waiting for transfers between devices, in_plane(): arrived.append(lax.ppermute(mine, ('seq', 'head'), pairs))  3.43 us
    ppermute x3, waiting for transfers between devices, body(): lax.ppermute(rounded, 'seq', [(i, i ^ b * per_plane) for i in range(membe...  2.7 us
    ppermute x6, starting transfers between devices, swap(): return lax.ppermute(array, 'head', [(i, i ^ 1) for i in range(ways)])  1.61 us
    ppermute x6, waiting for transfers between devices, swap(): return lax.ppermute(array, 'head', [(i, i ^ 1) for i in range(ways)])  1.35 us
  transfers between devices with their start and end apart: 18, of which 7 were waited for; matrix products, arithmetic and copies ran while one was open for 0% of the time, Pallas kernels for 32%

profile of v11, /device:TPU:0, one launch (start us, length us, event | category | flops | bytes accessed | tf_op | source)
XLA Modules:
  0.0 43.6 jit_solution(15610761585163344828)
XLA Ops:
  1.2 0.9 %round.1.refs_0_ = bf16[192,128]{1,0:T(8,128)(2,1)S(1)} custom-call(f32[192,128]{1,0:T(8,128)} %latent_ref.3), custom_call_target="tpu_custom_call" | custom-call | tf_op jit(solution)/shard_map/round/pallas_call | solution.py:42
  2.1 3.1 %collective-permute-start = (bf16[192,128]{1,0:T(8,128)(2,1)S(1)}, bf16[192,128]{1,0:T(8,128)(2,1)S(1)}, u32[]{:S(2)}, u32[]{:S(2)}) collective-permute-start(bf16[192,128]{1,0:T(8,128)(2,1)S(1)} %round.1.refs_0_), channel_id=1, source_target_pairs={{0,8},{2,10},{4,12},{6,14},{8,0},{10,2},{12,4},{14,6},{16,24},{18,... | collective-permute-start | bytes 147464 | tf_op jit(solution)/shard_map/ppermute | solution.py:604
  5.2 2.6 %collective-permute-start.1 = (bf16[192,128]{1,0:T(8,128)(2,1)S(1)}, bf16[192,128]{1,0:T(8,128)(2,1)S(1)}, u32[]{:S(2)}, u32[]{:S(2)}) collective-permute-start(bf16[192,128]{1,0:T(8,128)(2,1)S(1)} %round.1.refs_0_), channel_id=1, source_target_pairs={{0,16},{2,18},{4,20},{6,22},{8,24},{10,26},{12,28},{14,30},{16,0},... | collective-permute-start | bytes 147464 | tf_op jit(solution)/shard_map/ppermute | solution.py:604
  7.8 3.2 %prepare.1 = (bf16[2,128,1536]{2,1,0:T(8,128)(2,1)S(1)}, bf16[2,256,256]{2,1,0:T(8,128)(2,1)S(1)}, bf16[2,384,256]{2,1,0:T(8,128)(2,1)S(1)}) custom-call(bf16[2,128,1536]{2,1,0:T(8,128)(2,1)} %in_src.1, f32[2,1536]{1,0:T(2,128)} %gain_src.1, bf16[2,1536,128]{2,1,0:T(8,128)(2,1)} %key_src.1, bf16[2,1536,128]{2,1,0:T(8,128)(2,1)} %value_src.1, ...), custom_call_target="tpu_custom_call" | custom-call | tf_op jit(solution)/shard_map/prepare/pallas_call | solution.py:42
  11.1 2.6 %collective-permute-done.2.refs_3_ = bf16[192,128]{1,0:T(8,128)(2,1)S(1)} collective-permute-done((bf16[192,128]{1,0:T(8,128)(2,1)S(1)}, bf16[192,128]{1,0:T(8,128)(2,1)S(1)}, u32[]{:S(2)}, u32[]{:S(2)}) %collective-permute-start.2) | collective-permute-done | bytes 49184 | tf_op jit(solution)/shard_map/ppermute | solution.py:604
  13.8 1.6 %collective-permute-start.7 = (bf16[384,128]{1,0:T(8,128)(2,1)S(1)}, bf16[384,128]{1,0:T(8,128)(2,1)S(1)}, u32[]{:S(2)}, u32[]{:S(2)}) collective-permute-start(bf16[384,128]{1,0:T(8,128)(2,1)S(1)} %get-tuple-element.51.rows_ref.refs_0_.refs_3_), channel_id=1, source_target_pairs={{0,2},{1,5},{2,0},{3,7},{4,6},{5,1},{6,4},{7,3},{8,10},{9,13},{10,... | collective-permute-start | bytes 294920 | tf_op jit(solution)/shard_map/ppermute | solution.py:548
  15.4 1.5 %collective-permute-start.8 = (bf16[384,128]{1,0:T(8,128)(2,1)S(1)}, bf16[384,128]{1,0:T(8,128)(2,1)S(1)}, u32[]{:S(2)}, u32[]{:S(2)}) collective-permute-start(bf16[384,128]{1,0:T(8,128)(2,1)S(1)} %get-tuple-element.51.rows_ref.refs_0_.refs_3_), channel_id=1, source_target_pairs={{0,4},{1,3},{2,6},{3,1},{4,0},{5,7},{6,2},{7,5},{8,12},{9,11},{10,... | collective-permute-start | bytes 294920 | tf_op jit(solution)/shard_map/ppermute | solution.py:548
  17.5 0.9 %queries.2 = (f32[384,1536]{1,0:T(8,128)S(1)}, bf16[1,1536,256]{2,1,0:T(8,128)(2,1)S(1)}) custom-call(bf16[384,128]{1,0:T(8,128)(2,1)S(1)} %get-tuple-element.51.rows_ref.refs_0_.refs_3_, bf16[2,128,1536]{2,1,0:T(8,128)(2,1)S(1)} %get-tuple-element.52.in_ref, bf16[256,256]{1,0:T(8,128)(2,1)S(1)} %get-tuple-element.53.maps_ref), custom_call_target="tpu_custom_call" | custom-call | tf_op jit(solution)/shard_map/queries/pallas_call | solution.py:42
  18.3 1.8 %attend.6 = (f32[1,1536,256]{2,1,0:T(8,128)S(1)}, f32[1,1536,128]{2,1,0:T(8,128)S(1)}, f32[1,1536,64]{2,1,0:T(8,128)S(1)}) custom-call(bf16[768,256]{1,0:T(8,128)(2,1)S(1)} %get-tuple-element.50.maps_ref, bf16[1,1536,256]{2,1,0:T(8,128)(2,1)S(1)} %get-tuple-element.54.query_ref, bf16[384,128]{1,0:T(8,128)(2,1)S(1)} %get-tuple-element.51.rows_ref.refs_0_.refs_3_, ...), custom_call_target="tpu_custom_call" | custom-call | tf_op jit(solution)/shard_map/attend/pallas_call | solution.py:42
  20.1 1.1 %collective-permute-done.8.two_ref = bf16[384,128]{1,0:T(8,128)(2,1)S(1)} collective-permute-done((bf16[384,128]{1,0:T(8,128)(2,1)S(1)}, bf16[384,128]{1,0:T(8,128)(2,1)S(1)}, u32[]{:S(2)}, u32[]{:S(2)}) %collective-permute-start.8) | collective-permute-done | bytes 98336 | tf_op jit(solution)/shard_map/ppermute | solution.py:548
  21.3 1.8 %attend.7 = (f32[1,1536,256]{2,1,0:T(8,128)S(1)}, f32[1,1536,128]{2,1,0:T(8,128)S(1)}, f32[1,1536,64]{2,1,0:T(8,128)S(1)}) custom-call(bf16[768,256]{1,0:T(8,128)(2,1)S(1)} %get-tuple-element.50.maps_ref, bf16[1,1536,256]{2,1,0:T(8,128)(2,1)S(1)} %get-tuple-element.54.query_ref, bf16[384,128]{1,0:T(8,128)(2,1)S(1)} %get-tuple-element.60.refs_0_.refs_4_, ...), custom_call_target="tpu_custom_call" | custom-call | tf_op jit(solution)/shard_map/attend/pallas_call | solution.py:42
  23.1 0.6 %collective-permute-start.10 = (bf16[384,128]{1,0:T(8,128)(2,1)S(1)}, bf16[384,128]{1,0:T(8,128)(2,1)S(1)}, u32[]{:S(2)}, u32[]{:S(2)}) collective-permute-start(bf16[384,128]{1,0:T(8,128)(2,1)S(1)} %gate.2.refs_0_.refs_6_), channel_id=1, source_target_pairs={{0,1},{1,0},{2,3},{3,2},{4,5},{5,4},{6,7},{7,6},{8,9},{9,8},{10,11... | collective-permute-start | bytes 294920 | tf_op jit(solution)/shard_map/ppermute | solution.py:530
  23.7 1.8 %attend.8 = (f32[1,1536,256]{2,1,0:T(8,128)S(1)}, f32[1,1536,128]{2,1,0:T(8,128)S(1)}, f32[1,1536,64]{2,1,0:T(8,128)S(1)}) custom-call(bf16[768,256]{1,0:T(8,128)(2,1)S(1)} %get-tuple-element.50.maps_ref, bf16[1,1536,256]{2,1,0:T(8,128)(2,1)S(1)} %get-tuple-element.54.query_ref, bf16[384,128]{1,0:T(8,128)(2,1)S(1)} %gate.2.refs_0_.refs_6_, ...), custom_call_target="tpu_custom_call" | custom-call | tf_op jit(solution)/shard_map/attend/pallas_call | solution.py:42
  25.6 3.5 %second_half.2 = (f32[96,128]{1,0:T(8,128)S(1)}, f32[96,128]{1,0:T(8,128)S(1)}, bf16[400,128]{1,0:T(8,128)(2,1)S(1)}) custom-call(bf16[768,256]{1,0:T(8,128)(2,1)S(1)} %get-tuple-element.50.maps_ref, bf16[1,1536,256]{2,1,0:T(8,128)(2,1)S(1)} %get-tuple-element.54.query_ref, f32[384,1536]{1,0:T(8,128)S(1)} %get-tuple-element.55.hidden_ref, ...), custom_call_target="tpu_custom_call" | custom-call | tf_op jit(solution)/shard_map/second_half/pallas_call | solution.py:42
  29.1 0.7 %collective-permute-start.12 = (bf16[400,128]{1,0:T(8,128)(2,1)S(1)}, bf16[400,128]{1,0:T(8,128)(2,1)S(1)}, u32[]{:S(2)}, u32[]{:S(2)}) collective-permute-start(bf16[400,128]{1,0:T(8,128)(2,1)S(1)} %get-tuple-element.71.rows_ref.refs_0_.refs_2_), channel_id=1, source_target_pairs={{0,2},{1,5},{2,0},{3,7},{4,6},{5,1},{6,4},{7,3},{8,10},{9,13},{10,... | collective-permute-start | bytes 307208 | tf_op jit(solution)/shard_map/ppermute | solution.py:548
  29.9 1.9 %collective-permute-start.13 = (bf16[400,128]{1,0:T(8,128)(2,1)S(1)}, bf16[400,128]{1,0:T(8,128)(2,1)S(1)}, u32[]{:S(2)}, u32[]{:S(2)}) collective-permute-start(bf16[400,128]{1,0:T(8,128)(2,1)S(1)} %get-tuple-element.71.rows_ref.refs_0_.refs_2_), channel_id=1, source_target_pairs={{0,4},{1,3},{2,6},{3,1},{4,0},{5,7},{6,2},{7,5},{8,12},{9,11},{10,... | collective-permute-start | bytes 307208 | tf_op jit(solution)/shard_map/ppermute | solution.py:548
  31.7 1.4 %collective-permute-start.11 = (bf16[400,128]{1,0:T(8,128)(2,1)S(1)}, bf16[400,128]{1,0:T(8,128)(2,1)S(1)}, u32[]{:S(2)}, u32[]{:S(2)}) collective-permute-start(bf16[400,128]{1,0:T(8,128)(2,1)S(1)} %get-tuple-element.71.rows_ref.refs_0_.refs_2_), channel_id=1, source_target_pairs={{0,6},{1,7},{2,4},{3,5},{4,2},{5,3},{6,0},{7,1},{8,14},{9,15},{10,... | collective-permute-start | bytes 307208 | tf_op jit(solution)/shard_map/ppermute | solution.py:548
  33.6 0.9 %attend.9 = (f32[1,384,256]{2,1,0:T(8,128)S(1)}, f32[1,384,128]{2,1,0:T(8,128)S(1)}) custom-call(bf16[768,256]{1,0:T(8,128)(2,1)S(1)} %get-tuple-element.49.maps_ref, bf16[1,384,256]{2,1,0:T(8,128)(2,1)S(1)} %get-tuple-element.73.query_ref, bf16[400,128]{1,0:T(8,128)(2,1)S(1)} %get-tuple-element.71.rows_ref.refs_0_.refs_2_, ...), custom_call_target="tpu_custom_call" | custom-call | tf_op jit(solution)/shard_map/attend/pallas_call | solution.py:42
  35.7 0.9 %attend.10 = (f32[1,384,256]{2,1,0:T(8,128)S(1)}, f32[1,384,128]{2,1,0:T(8,128)S(1)}) custom-call(bf16[768,256]{1,0:T(8,128)(2,1)S(1)} %get-tuple-element.49.maps_ref, bf16[1,384,256]{2,1,0:T(8,128)(2,1)S(1)} %get-tuple-element.73.query_ref, bf16[400,128]{1,0:T(8,128)(2,1)S(1)} %get-tuple-element.77.refs_0_.refs_3_, ...), custom_call_target="tpu_custom_call" | custom-call | tf_op jit(solution)/shard_map/attend/pallas_call | solution.py:42
  36.7 1.8 %collective-permute-done.11.refs_0_ = bf16[400,128]{1,0:T(8,128)(2,1)S(1)} collective-permute-done((bf16[400,128]{1,0:T(8,128)(2,1)S(1)}, bf16[400,128]{1,0:T(8,128)(2,1)S(1)}, u32[]{:S(2)}, u32[]{:S(2)}) %collective-permute-start.11) | collective-permute-done | bytes 102432 | tf_op jit(solution)/shard_map/ppermute | solution.py:548
  38.6 0.9 %attend.11 = (f32[1,384,256]{2,1,0:T(8,128)S(1)}, f32[1,384,128]{2,1,0:T(8,128)S(1)}) custom-call(bf16[768,256]{1,0:T(8,128)(2,1)S(1)} %get-tuple-element.49.maps_ref, bf16[1,384,256]{2,1,0:T(8,128)(2,1)S(1)} %get-tuple-element.73.query_ref, bf16[400,128]{1,0:T(8,128)(2,1)S(1)} %gate.3.refs_0_.refs_5_, ...), custom_call_target="tpu_custom_call" | custom-call | tf_op jit(solution)/shard_map/attend/pallas_call | solution.py:42
  39.9 1.8 %second_half.3.own_ref = f32[104,128]{1,0:T(8,128)S(1)} custom-call(bf16[768,256]{1,0:T(8,128)(2,1)S(1)} %get-tuple-element.49.maps_ref, bf16[1,384,256]{2,1,0:T(8,128)(2,1)S(1)} %get-tuple-element.73.query_ref, f32[96,1536]{1,0:T(8,128)S(1)} %get-tuple-element.74.hidden_ref, f32[2,1536]{1,0:T(2,128)S(1)} %copy-done.3, f32[192,128]{1,0:T(8,128)S(1)} %copy-done.2, ...), custom_call_target="tpu_custom_call" | custom-call | tf_op jit(solution)/shard_map/second_half/pallas_call | solution.py:42
  41.9 1.0 %collective-permute-done.17.other_ref = f32[104,128]{1,0:T(8,128)S(1)} collective-permute-done((f32[104,128]{1,0:T(8,128)S(1)}, f32[104,128]{1,0:T(8,128)S(1)}, u32[]{:S(2)}, u32[]{:S(2)}) %collective-permute-start.17) | collective-permute-done | bytes 53280 | tf_op jit(solution)/shard_map/ppermute | solution.py:530
  43.0 0.7 %finish.1 = (f32[192,128]{1,0:T(8,128)}, f32[1,192]{1,0:T(1,128)}) custom-call(f32[104,128]{1,0:T(8,128)S(1)} %second_half.3.own_ref, f32[104,128]{1,0:T(8,128)S(1)} %collective-permute-done.17.other_ref), custom_call_target="tpu_custom_call" | custom-call | tf_op jit(solution)/shard_map/finish/pallas_call | solution.py:42
  (41 shorter events, 4.0 us)
Async XLA Ops:
  0.6 13.1 %collective-permute-start.3 = (bf16[2,128,1536]{2,1,0:T(8,128)(2,1)}, bf16[2,128,1536]{2,1,0:T(8,128)(2,1)S(1)}, u32[]{:S(2)}, u32[]{:S(2)}) collective-permute-start(bf16[2,128,1536]{2,1,0:T(8,128)(2,1)} %refs_10_.1), channel_id=1, source_target_pairs={{1,0},{0,1},{3,2},{2,3},{5,4},{4,5},{7,6},{6,7},{9,8},{8,9},{11,10... | collective-permute-start | bytes 2359304 | tf_op jit(solution)/shard_map/ppermute | solution.py:536
  1.1 12.5 %collective-permute-start.4 = (bf16[2,768,256]{2,1,0:T(8,128)(2,1)}, bf16[2,768,256]{2,1,0:T(8,128)(2,1)S(1)}, u32[]{:S(2)}, u32[]{:S(2)}) collective-permute-start(bf16[2,768,256]{2,1,0:T(8,128)(2,1)} %refs_12_.1), channel_id=1, source_target_pairs={{1,0},{0,1},{3,2},{2,3},{5,4},{4,5},{7,6},{6,7},{9,8},{8,9},{11,10... | collective-permute-start | bytes 2359304 | tf_op jit(solution)/shard_map/ppermute | solution.py:536
  2.1 8.8 %collective-permute-start = (bf16[192,128]{1,0:T(8,128)(2,1)S(1)}, bf16[192,128]{1,0:T(8,128)(2,1)S(1)}, u32[]{:S(2)}, u32[]{:S(2)}) collective-permute-start(bf16[192,128]{1,0:T(8,128)(2,1)S(1)} %round.1.refs_0_), channel_id=1, source_target_pairs={{0,8},{2,10},{4,12},{6,14},{8,0},{10,2},{12,4},{14,6},{16,24},{18,... | collective-permute-start | bytes 147464 | tf_op jit(solution)/shard_map/ppermute | solution.py:604
  5.2 5.9 %collective-permute-start.1 = (bf16[192,128]{1,0:T(8,128)(2,1)S(1)}, bf16[192,128]{1,0:T(8,128)(2,1)S(1)}, u32[]{:S(2)}, u32[]{:S(2)}) collective-permute-start(bf16[192,128]{1,0:T(8,128)(2,1)S(1)} %round.1.refs_0_), channel_id=1, source_target_pairs={{0,16},{2,18},{4,20},{6,22},{8,24},{10,26},{12,28},{14,30},{16,0},... | collective-permute-start | bytes 147464 | tf_op jit(solution)/shard_map/ppermute | solution.py:604
  7.8 5.9 %collective-permute-start.2 = (bf16[192,128]{1,0:T(8,128)(2,1)S(1)}, bf16[192,128]{1,0:T(8,128)(2,1)S(1)}, u32[]{:S(2)}, u32[]{:S(2)}) collective-permute-start(bf16[192,128]{1,0:T(8,128)(2,1)S(1)} %round.1.refs_0_), channel_id=1, source_target_pairs={{0,24},{2,26},{4,28},{6,30},{8,16},{10,18},{12,20},{14,22},{16,8},... | collective-permute-start | bytes 147464 | tf_op jit(solution)/shard_map/ppermute | solution.py:604
  13.8 3.6 %collective-permute-start.5 = (bf16[2,384,256]{2,1,0:T(8,128)(2,1)S(1)}, bf16[2,384,256]{2,1,0:T(8,128)(2,1)S(1)}, u32[]{:S(2)}, u32[]{:S(2)}) collective-permute-start(bf16[2,384,256]{2,1,0:T(8,128)(2,1)S(1)} %get-tuple-element.48.refs_0_), channel_id=1, source_target_pairs={{1,0},{0,1},{3,2},{2,3},{5,4},{4,5},{7,6},{6,7},{9,8},{8,9},{11,10... | collective-permute-start | bytes 1179656 | tf_op jit(solution)/shard_map/ppermute | solution.py:536
  13.8 6.3 %collective-permute-start.7 = (bf16[384,128]{1,0:T(8,128)(2,1)S(1)}, bf16[384,128]{1,0:T(8,128)(2,1)S(1)}, u32[]{:S(2)}, u32[]{:S(2)}) collective-permute-start(bf16[384,128]{1,0:T(8,128)(2,1)S(1)} %get-tuple-element.51.rows_ref.refs_0_.refs_3_), channel_id=1, source_target_pairs={{0,2},{1,5},{2,0},{3,7},{4,6},{5,1},{6,4},{7,3},{8,10},{9,13},{10,... | collective-permute-start | bytes 294920 | tf_op jit(solution)/shard_map/ppermute | solution.py:548
  15.4 5.8 %collective-permute-start.8 = (bf16[384,128]{1,0:T(8,128)(2,1)S(1)}, bf16[384,128]{1,0:T(8,128)(2,1)S(1)}, u32[]{:S(2)}, u32[]{:S(2)}) collective-permute-start(bf16[384,128]{1,0:T(8,128)(2,1)S(1)} %get-tuple-element.51.rows_ref.refs_0_.refs_3_), channel_id=1, source_target_pairs={{0,4},{1,3},{2,6},{3,1},{4,0},{5,7},{6,2},{7,5},{8,12},{9,11},{10,... | collective-permute-start | bytes 294920 | tf_op jit(solution)/shard_map/ppermute | solution.py:548
  16.9 6.2 %collective-permute-start.6 = (bf16[384,128]{1,0:T(8,128)(2,1)S(1)}, bf16[384,128]{1,0:T(8,128)(2,1)S(1)}, u32[]{:S(2)}, u32[]{:S(2)}) collective-permute-start(bf16[384,128]{1,0:T(8,128)(2,1)S(1)} %get-tuple-element.51.rows_ref.refs_0_.refs_3_), channel_id=1, source_target_pairs={{0,6},{1,7},{2,4},{3,5},{4,2},{5,3},{6,0},{7,1},{8,14},{9,15},{10,... | collective-permute-start | bytes 294920 | tf_op jit(solution)/shard_map/ppermute | solution.py:548
  21.2 2.4 %collective-permute-start.9 = (bf16[768,128]{1,0:T(8,128)(2,1)S(1)}, bf16[768,128]{1,0:T(8,128)(2,1)S(1)}, u32[]{:S(2)}, u32[]{:S(2)}) collective-permute-start(bf16[768,128]{1,0:T(8,128)(2,1)S(1)} %get-tuple-element.65), channel_id=1, source_target_pairs={{0,1},{1,0},{2,3},{3,2},{4,5},{5,4},{6,7},{7,6},{8,9},{9,8},{10,11... | collective-permute-start | bytes 589832 | tf_op jit(solution)/shard_map/ppermute | solution.py:530
  23.1 2.4 %collective-permute-start.10 = (bf16[384,128]{1,0:T(8,128)(2,1)S(1)}, bf16[384,128]{1,0:T(8,128)(2,1)S(1)}, u32[]{:S(2)}, u32[]{:S(2)}) collective-permute-start(bf16[384,128]{1,0:T(8,128)(2,1)S(1)} %gate.2.refs_0_.refs_6_), channel_id=1, source_target_pairs={{0,1},{1,0},{2,3},{3,2},{4,5},{5,4},{6,7},{7,6},{8,9},{9,8},{10,11... | collective-permute-start | bytes 294920 | tf_op jit(solution)/shard_map/ppermute | solution.py:530
  23.7 1.8 %copy-start = (bf16[2,128,1536]{2,1,0:T(8,128)(2,1)S(1)}, bf16[2,128,1536]{2,1,0:T(8,128)(2,1)}, u32[]{:S(2)}) copy-start(bf16[2,128,1536]{2,1,0:T(8,128)(2,1)} %refs_10_.1) | copy-start | bytes 2359300
  23.7 1.8 %copy-start.1 = (bf16[2,768,256]{2,1,0:T(8,128)(2,1)S(1)}, bf16[2,768,256]{2,1,0:T(8,128)(2,1)}, u32[]{:S(2)}) copy-start(bf16[2,768,256]{2,1,0:T(8,128)(2,1)} %refs_12_.1) | copy-start | bytes 2359300
  23.7 1.8 %copy-start.2 = (f32[192,128]{1,0:T(8,128)S(1)}, f32[192,128]{1,0:T(8,128)}, u32[]{:S(2)}) copy-start(f32[192,128]{1,0:T(8,128)} %latent_ref.3) | copy-start | bytes 294916
  23.7 1.8 %copy-start.3 = (f32[2,1536]{1,0:T(2,128)S(1)}, f32[2,1536]{1,0:T(2,128)}, u32[]{:S(2)}) copy-start(f32[2,1536]{1,0:T(2,128)} %gain_ref.3) | copy-start | bytes 36868
  29.1 4.6 %collective-permute-start.14 = (bf16[400,128]{1,0:T(8,128)(2,1)S(1)}, bf16[400,128]{1,0:T(8,128)(2,1)S(1)}, u32[]{:S(2)}, u32[]{:S(2)}) collective-permute-start(bf16[400,128]{1,0:T(8,128)(2,1)S(1)} %get-tuple-element.71.rows_ref.refs_0_.refs_2_), channel_id=1, source_target_pairs={{0,1},{1,0},{2,3},{3,2},{4,5},{5,4},{6,7},{7,6},{8,9},{9,8},{10,11... | collective-permute-start | bytes 307208 | tf_op jit(solution)/shard_map/ppermute | solution.py:530
  29.1 5.4 %collective-permute-start.12 = (bf16[400,128]{1,0:T(8,128)(2,1)S(1)}, bf16[400,128]{1,0:T(8,128)(2,1)S(1)}, u32[]{:S(2)}, u32[]{:S(2)}) collective-permute-start(bf16[400,128]{1,0:T(8,128)(2,1)S(1)} %get-tuple-element.71.rows_ref.refs_0_.refs_2_), channel_id=1, source_target_pairs={{0,2},{1,5},{2,0},{3,7},{4,6},{5,1},{6,4},{7,3},{8,10},{9,13},{10,... | collective-permute-start | bytes 307208 | tf_op jit(solution)/shard_map/ppermute | solution.py:548
  29.9 5.3 %collective-permute-start.13 = (bf16[400,128]{1,0:T(8,128)(2,1)S(1)}, bf16[400,128]{1,0:T(8,128)(2,1)S(1)}, u32[]{:S(2)}, u32[]{:S(2)}) collective-permute-start(bf16[400,128]{1,0:T(8,128)(2,1)S(1)} %get-tuple-element.71.rows_ref.refs_0_.refs_2_), channel_id=1, source_target_pairs={{0,4},{1,3},{2,6},{3,1},{4,0},{5,7},{6,2},{7,5},{8,12},{9,11},{10,... | collective-permute-start | bytes 307208 | tf_op jit(solution)/shard_map/ppermute | solution.py:548
  31.7 6.8 %collective-permute-start.11 = (bf16[400,128]{1,0:T(8,128)(2,1)S(1)}, bf16[400,128]{1,0:T(8,128)(2,1)S(1)}, u32[]{:S(2)}, u32[]{:S(2)}) collective-permute-start(bf16[400,128]{1,0:T(8,128)(2,1)S(1)} %get-tuple-element.71.rows_ref.refs_0_.refs_2_), channel_id=1, source_target_pairs={{0,6},{1,7},{2,4},{3,5},{4,2},{5,3},{6,0},{7,1},{8,14},{9,15},{10,... | collective-permute-start | bytes 307208 | tf_op jit(solution)/shard_map/ppermute | solution.py:548
  35.2 3.4 %collective-permute-start.15 = (bf16[800,128]{1,0:T(8,128)(2,1)S(1)}, bf16[800,128]{1,0:T(8,128)(2,1)S(1)}, u32[]{:S(2)}, u32[]{:S(2)}) collective-permute-start(bf16[800,128]{1,0:T(8,128)(2,1)S(1)} %get-tuple-element.81), channel_id=1, source_target_pairs={{0,1},{1,0},{2,3},{3,2},{4,5},{5,4},{6,7},{7,6},{8,9},{9,8},{10,11... | collective-permute-start | bytes 614408 | tf_op jit(solution)/shard_map/ppermute | solution.py:530
  38.5 1.4 %collective-permute-start.16 = (bf16[400,128]{1,0:T(8,128)(2,1)S(1)}, bf16[400,128]{1,0:T(8,128)(2,1)S(1)}, u32[]{:S(2)}, u32[]{:S(2)}) collective-permute-start(bf16[400,128]{1,0:T(8,128)(2,1)S(1)} %gate.3.refs_0_.refs_5_), channel_id=1, source_target_pairs={{0,1},{1,0},{2,3},{3,2},{4,5},{5,4},{6,7},{7,6},{8,9},{9,8},{10,11... | collective-permute-start | bytes 307208 | tf_op jit(solution)/shard_map/ppermute | solution.py:530
  41.7 1.3 %collective-permute-start.17 = (f32[104,128]{1,0:T(8,128)S(1)}, f32[104,128]{1,0:T(8,128)S(1)}, u32[]{:S(2)}, u32[]{:S(2)}) collective-permute-start(f32[104,128]{1,0:T(8,128)S(1)} %second_half.3.own_ref), channel_id=1, source_target_pairs={{0,1},{1,0},{2,3},{3,2},{4,5},{5,4},{6,7},{7,6},{8,9},{9,8},{10,11... | collective-permute-start | bytes 159752 | tf_op jit(solution)/shard_map/ppermute | solution.py:530

commit v12 on v11

--- a/solution.py
+++ b/solution.py
@@ -419,8 +419,8 @@
         rows = cat([ref[layer] for ref in mix_refs[2 * g : 2 * g + 2]], 0)
         mixture = mixture + dot(cat(attended, 0).astype(jnp.bfloat16), rows)
     spread = lax.rsqrt(jnp.mean(mixture * mixture, axis=1, keepdims=True) + epsilon)
-    scaled = (mixture * gain_ref[layer : layer + 1, :]).astype(jnp.bfloat16)
-    predicted = dot(scaled, param_all[...]) * spread
+    scaled = (mixture * spread * gain_ref[layer : layer + 1, :]).astype(jnp.bfloat16)
+    predicted = dot(scaled, param_all[...])
     shift_all = predicted[:, :channels]
     log_all = 2.0 * jnp.tanh(0.5 * predicted[:, channels:])
     token = lax.broadcasted_iota(jnp.int32, (count, 1), 0)

time: 43.8 us -> 44 us (level)
  transfers between devices with their start and end apart: 18 -> 18, of which waited for: 7 -> 7; matrix products, arithmetic and copies ran while one was open for 0% -> 0% of each run, Pallas kernels for 32% -> 31%
where the time goes in v12:
time: 44 us; the launch traced here: 43.9 us
  Pallas kernels  20 us (45%)
  starting transfers between devices  15.5 us (35%)
  waiting for transfers between devices  7.5 us (17%)
  between operations  0.91 us (2%)
    pallas_call x21, Pallas kernels, on_chip(): pl.pallas_call(kernel, in_specs=[pl.BlockSpec(memory_space=pltpu.VMEM)] *...  20 us
    ppermute x6, starting transfers between devices, in_plane(): arrived.append(lax.ppermute(mine, ('seq', 'head'), pairs))  7.5 us
    ppermute x3, starting transfers between devices, body(): lax.ppermute(rounded, 'seq', [(i, i ^ b * per_plane) for i in range(membe...  5.66 us
    ppermute x6, waiting for transfers between devices, in_plane(): arrived.append(lax.ppermute(mine, ('seq', 'head'), pairs))  3.44 us
    ppermute x3, waiting for transfers between devices, body(): lax.ppermute(rounded, 'seq', [(i, i ^ b * per_plane) for i in range(membe...  2.7 us
    ppermute x6, starting transfers between devices, swap(): return lax.ppermute(array, 'head', [(i, i ^ 1) for i in range(ways)])  1.63 us
    ppermute x6, waiting for transfers between devices, swap(): return lax.ppermute(array, 'head', [(i, i ^ 1) for i in range(ways)])  1.35 us
  transfers between devices with their start and end apart: 18, of which 7 were waited for; matrix products, arithmetic and copies ran while one was open for 0% of the time, Pallas kernels for 31%

profile of v12, /device:TPU:0, one launch (start us, length us, event | category | flops | bytes accessed | tf_op | source)
XLA Modules:
  0.0 43.9 jit_solution(6402723521215080351)
XLA Ops:
  1.2 0.9 %round.1.refs_0_ = bf16[192,128]{1,0:T(8,128)(2,1)S(1)} custom-call(f32[192,128]{1,0:T(8,128)} %latent_ref.3), custom_call_target="tpu_custom_call" | custom-call | tf_op jit(solution)/shard_map/round/pallas_call | solution.py:42
  2.1 3.1 %collective-permute-start = (bf16[192,128]{1,0:T(8,128)(2,1)S(1)}, bf16[192,128]{1,0:T(8,128)(2,1)S(1)}, u32[]{:S(2)}, u32[]{:S(2)}) collective-permute-start(bf16[192,128]{1,0:T(8,128)(2,1)S(1)} %round.1.refs_0_), channel_id=1, source_target_pairs={{0,8},{2,10},{4,12},{6,14},{8,0},{10,2},{12,4},{14,6},{16,24},{18,... | collective-permute-start | bytes 147464 | tf_op jit(solution)/shard_map/ppermute | solution.py:604
  5.2 2.6 %collective-permute-start.1 = (bf16[192,128]{1,0:T(8,128)(2,1)S(1)}, bf16[192,128]{1,0:T(8,128)(2,1)S(1)}, u32[]{:S(2)}, u32[]{:S(2)}) collective-permute-start(bf16[192,128]{1,0:T(8,128)(2,1)S(1)} %round.1.refs_0_), channel_id=1, source_target_pairs={{0,16},{2,18},{4,20},{6,22},{8,24},{10,26},{12,28},{14,30},{16,0},... | collective-permute-start | bytes 147464 | tf_op jit(solution)/shard_map/ppermute | solution.py:604
  7.8 3.2 %prepare.1 = (bf16[2,128,1536]{2,1,0:T(8,128)(2,1)S(1)}, bf16[2,256,256]{2,1,0:T(8,128)(2,1)S(1)}, bf16[2,384,256]{2,1,0:T(8,128)(2,1)S(1)}) custom-call(bf16[2,128,1536]{2,1,0:T(8,128)(2,1)} %in_src.1, f32[2,1536]{1,0:T(2,128)} %gain_src.1, bf16[2,1536,128]{2,1,0:T(8,128)(2,1)} %key_src.1, bf16[2,1536,128]{2,1,0:T(8,128)(2,1)} %value_src.1, ...), custom_call_target="tpu_custom_call" | custom-call | tf_op jit(solution)/shard_map/prepare/pallas_call | solution.py:42
  11.1 2.6 %collective-permute-done.2.refs_3_ = bf16[192,128]{1,0:T(8,128)(2,1)S(1)} collective-permute-done((bf16[192,128]{1,0:T(8,128)(2,1)S(1)}, bf16[192,128]{1,0:T(8,128)(2,1)S(1)}, u32[]{:S(2)}, u32[]{:S(2)}) %collective-permute-start.2) | collective-permute-done | bytes 49184 | tf_op jit(solution)/shard_map/ppermute | solution.py:604
  13.8 1.6 %collective-permute-start.7 = (bf16[384,128]{1,0:T(8,128)(2,1)S(1)}, bf16[384,128]{1,0:T(8,128)(2,1)S(1)}, u32[]{:S(2)}, u32[]{:S(2)}) collective-permute-start(bf16[384,128]{1,0:T(8,128)(2,1)S(1)} %get-tuple-element.51.rows_ref.refs_0_.refs_3_), channel_id=1, source_target_pairs={{0,2},{1,5},{2,0},{3,7},{4,6},{5,1},{6,4},{7,3},{8,10},{9,13},{10,... | collective-permute-start | bytes 294920 | tf_op jit(solution)/shard_map/ppermute | solution.py:548
  15.4 1.5 %collective-permute-start.8 = (bf16[384,128]{1,0:T(8,128)(2,1)S(1)}, bf16[384,128]{1,0:T(8,128)(2,1)S(1)}, u32[]{:S(2)}, u32[]{:S(2)}) collective-permute-start(bf16[384,128]{1,0:T(8,128)(2,1)S(1)} %get-tuple-element.51.rows_ref.refs_0_.refs_3_), channel_id=1, source_target_pairs={{0,4},{1,3},{2,6},{3,1},{4,0},{5,7},{6,2},{7,5},{8,12},{9,11},{10,... | collective-permute-start | bytes 294920 | tf_op jit(solution)/shard_map/ppermute | solution.py:548
  17.5 0.9 %queries.2 = (f32[384,1536]{1,0:T(8,128)S(1)}, bf16[1,1536,256]{2,1,0:T(8,128)(2,1)S(1)}) custom-call(bf16[384,128]{1,0:T(8,128)(2,1)S(1)} %get-tuple-element.51.rows_ref.refs_0_.refs_3_, bf16[2,128,1536]{2,1,0:T(8,128)(2,1)S(1)} %get-tuple-element.52.in_ref, bf16[256,256]{1,0:T(8,128)(2,1)S(1)} %get-tuple-element.53.maps_ref), custom_call_target="tpu_custom_call" | custom-call | tf_op jit(solution)/shard_map/queries/pallas_call | solution.py:42
  18.3 1.8 %attend.6 = (f32[1,1536,256]{2,1,0:T(8,128)S(1)}, f32[1,1536,128]{2,1,0:T(8,128)S(1)}, f32[1,1536,64]{2,1,0:T(8,128)S(1)}) custom-call(bf16[768,256]{1,0:T(8,128)(2,1)S(1)} %get-tuple-element.50.maps_ref, bf16[1,1536,256]{2,1,0:T(8,128)(2,1)S(1)} %get-tuple-element.54.query_ref, bf16[384,128]{1,0:T(8,128)(2,1)S(1)} %get-tuple-element.51.rows_ref.refs_0_.refs_3_, ...), custom_call_target="tpu_custom_call" | custom-call | tf_op jit(solution)/shard_map/attend/pallas_call | solution.py:42
  20.1 1.1 %collective-permute-done.8.two_ref = bf16[384,128]{1,0:T(8,128)(2,1)S(1)} collective-permute-done((bf16[384,128]{1,0:T(8,128)(2,1)S(1)}, bf16[384,128]{1,0:T(8,128)(2,1)S(1)}, u32[]{:S(2)}, u32[]{:S(2)}) %collective-permute-start.8) | collective-permute-done | bytes 98336 | tf_op jit(solution)/shard_map/ppermute | solution.py:548
  21.3 1.8 %attend.7 = (f32[1,1536,256]{2,1,0:T(8,128)S(1)}, f32[1,1536,128]{2,1,0:T(8,128)S(1)}, f32[1,1536,64]{2,1,0:T(8,128)S(1)}) custom-call(bf16[768,256]{1,0:T(8,128)(2,1)S(1)} %get-tuple-element.50.maps_ref, bf16[1,1536,256]{2,1,0:T(8,128)(2,1)S(1)} %get-tuple-element.54.query_ref, bf16[384,128]{1,0:T(8,128)(2,1)S(1)} %get-tuple-element.60.refs_0_.refs_4_, ...), custom_call_target="tpu_custom_call" | custom-call | tf_op jit(solution)/shard_map/attend/pallas_call | solution.py:42
  23.1 0.6 %collective-permute-start.10 = (bf16[384,128]{1,0:T(8,128)(2,1)S(1)}, bf16[384,128]{1,0:T(8,128)(2,1)S(1)}, u32[]{:S(2)}, u32[]{:S(2)}) collective-permute-start(bf16[384,128]{1,0:T(8,128)(2,1)S(1)} %gate.2.refs_0_.refs_6_), channel_id=1, source_target_pairs={{0,1},{1,0},{2,3},{3,2},{4,5},{5,4},{6,7},{7,6},{8,9},{9,8},{10,11... | collective-permute-start | bytes 294920 | tf_op jit(solution)/shard_map/ppermute | solution.py:530
  23.7 1.8 %attend.8 = (f32[1,1536,256]{2,1,0:T(8,128)S(1)}, f32[1,1536,128]{2,1,0:T(8,128)S(1)}, f32[1,1536,64]{2,1,0:T(8,128)S(1)}) custom-call(bf16[768,256]{1,0:T(8,128)(2,1)S(1)} %get-tuple-element.50.maps_ref, bf16[1,1536,256]{2,1,0:T(8,128)(2,1)S(1)} %get-tuple-element.54.query_ref, bf16[384,128]{1,0:T(8,128)(2,1)S(1)} %gate.2.refs_0_.refs_6_, ...), custom_call_target="tpu_custom_call" | custom-call | tf_op jit(solution)/shard_map/attend/pallas_call | solution.py:42
  25.6 3.6 %second_half.2 = (f32[96,128]{1,0:T(8,128)S(1)}, f32[96,128]{1,0:T(8,128)S(1)}, bf16[400,128]{1,0:T(8,128)(2,1)S(1)}) custom-call(bf16[768,256]{1,0:T(8,128)(2,1)S(1)} %get-tuple-element.50.maps_ref, bf16[1,1536,256]{2,1,0:T(8,128)(2,1)S(1)} %get-tuple-element.54.query_ref, f32[384,1536]{1,0:T(8,128)S(1)} %get-tuple-element.55.hidden_ref, ...), custom_call_target="tpu_custom_call" | custom-call | tf_op jit(solution)/shard_map/second_half/pallas_call | solution.py:42
  29.3 0.7 %collective-permute-start.12 = (bf16[400,128]{1,0:T(8,128)(2,1)S(1)}, bf16[400,128]{1,0:T(8,128)(2,1)S(1)}, u32[]{:S(2)}, u32[]{:S(2)}) collective-permute-start(bf16[400,128]{1,0:T(8,128)(2,1)S(1)} %get-tuple-element.71.rows_ref.refs_0_.refs_2_), channel_id=1, source_target_pairs={{0,2},{1,5},{2,0},{3,7},{4,6},{5,1},{6,4},{7,3},{8,10},{9,13},{10,... | collective-permute-start | bytes 307208 | tf_op jit(solution)/shard_map/ppermute | solution.py:548
  30.0 1.9 %collective-permute-start.13 = (bf16[400,128]{1,0:T(8,128)(2,1)S(1)}, bf16[400,128]{1,0:T(8,128)(2,1)S(1)}, u32[]{:S(2)}, u32[]{:S(2)}) collective-permute-start(bf16[400,128]{1,0:T(8,128)(2,1)S(1)} %get-tuple-element.71.rows_ref.refs_0_.refs_2_), channel_id=1, source_target_pairs={{0,4},{1,3},{2,6},{3,1},{4,0},{5,7},{6,2},{7,5},{8,12},{9,11},{10,... | collective-permute-start | bytes 307208 | tf_op jit(solution)/shard_map/ppermute | solution.py:548
  31.9 1.4 %collective-permute-start.11 = (bf16[400,128]{1,0:T(8,128)(2,1)S(1)}, bf16[400,128]{1,0:T(8,128)(2,1)S(1)}, u32[]{:S(2)}, u32[]{:S(2)}) collective-permute-start(bf16[400,128]{1,0:T(8,128)(2,1)S(1)} %get-tuple-element.71.rows_ref.refs_0_.refs_2_), channel_id=1, source_target_pairs={{0,6},{1,7},{2,4},{3,5},{4,2},{5,3},{6,0},{7,1},{8,14},{9,15},{10,... | collective-permute-start | bytes 307208 | tf_op jit(solution)/shard_map/ppermute | solution.py:548
  33.8 0.9 %attend.9 = (f32[1,384,256]{2,1,0:T(8,128)S(1)}, f32[1,384,128]{2,1,0:T(8,128)S(1)}) custom-call(bf16[768,256]{1,0:T(8,128)(2,1)S(1)} %get-tuple-element.49.maps_ref, bf16[1,384,256]{2,1,0:T(8,128)(2,1)S(1)} %get-tuple-element.73.query_ref, bf16[400,128]{1,0:T(8,128)(2,1)S(1)} %get-tuple-element.71.rows_ref.refs_0_.refs_2_, ...), custom_call_target="tpu_custom_call" | custom-call | tf_op jit(solution)/shard_map/attend/pallas_call | solution.py:42
  35.9 0.9 %attend.10 = (f32[1,384,256]{2,1,0:T(8,128)S(1)}, f32[1,384,128]{2,1,0:T(8,128)S(1)}) custom-call(bf16[768,256]{1,0:T(8,128)(2,1)S(1)} %get-tuple-element.49.maps_ref, bf16[1,384,256]{2,1,0:T(8,128)(2,1)S(1)} %get-tuple-element.73.query_ref, bf16[400,128]{1,0:T(8,128)(2,1)S(1)} %get-tuple-element.77.refs_0_.refs_3_, ...), custom_call_target="tpu_custom_call" | custom-call | tf_op jit(solution)/shard_map/attend/pallas_call | solution.py:42
  36.8 1.8 %collective-permute-done.11.refs_0_ = bf16[400,128]{1,0:T(8,128)(2,1)S(1)} collective-permute-done((bf16[400,128]{1,0:T(8,128)(2,1)S(1)}, bf16[400,128]{1,0:T(8,128)(2,1)S(1)}, u32[]{:S(2)}, u32[]{:S(2)}) %collective-permute-start.11) | collective-permute-done | bytes 102432 | tf_op jit(solution)/shard_map/ppermute | solution.py:548
  38.8 0.9 %attend.11 = (f32[1,384,256]{2,1,0:T(8,128)S(1)}, f32[1,384,128]{2,1,0:T(8,128)S(1)}) custom-call(bf16[768,256]{1,0:T(8,128)(2,1)S(1)} %get-tuple-element.49.maps_ref, bf16[1,384,256]{2,1,0:T(8,128)(2,1)S(1)} %get-tuple-element.73.query_ref, bf16[400,128]{1,0:T(8,128)(2,1)S(1)} %gate.3.refs_0_.refs_5_, ...), custom_call_target="tpu_custom_call" | custom-call | tf_op jit(solution)/shard_map/attend/pallas_call | solution.py:42
  40.0 1.9 %second_half.3.own_ref = f32[104,128]{1,0:T(8,128)S(1)} custom-call(bf16[768,256]{1,0:T(8,128)(2,1)S(1)} %get-tuple-element.49.maps_ref, bf16[1,384,256]{2,1,0:T(8,128)(2,1)S(1)} %get-tuple-element.73.query_ref, f32[96,1536]{1,0:T(8,128)S(1)} %get-tuple-element.74.hidden_ref, f32[2,1536]{1,0:T(2,128)S(1)} %copy-done.3, f32[192,128]{1,0:T(8,128)S(1)} %copy-done.2, ...), custom_call_target="tpu_custom_call" | custom-call | tf_op jit(solution)/shard_map/second_half/pallas_call | solution.py:42
  42.2 1.0 %collective-permute-done.17.other_ref = f32[104,128]{1,0:T(8,128)S(1)} collective-permute-done((f32[104,128]{1,0:T(8,128)S(1)}, f32[104,128]{1,0:T(8,128)S(1)}, u32[]{:S(2)}, u32[]{:S(2)}) %collective-permute-start.17) | collective-permute-done | bytes 53280 | tf_op jit(solution)/shard_map/ppermute | solution.py:530
  43.2 0.7 %finish.1 = (f32[192,128]{1,0:T(8,128)}, f32[1,192]{1,0:T(1,128)}) custom-call(f32[104,128]{1,0:T(8,128)S(1)} %second_half.3.own_ref, f32[104,128]{1,0:T(8,128)S(1)} %collective-permute-done.17.other_ref), custom_call_target="tpu_custom_call" | custom-call | tf_op jit(solution)/shard_map/finish/pallas_call | solution.py:42
  (41 shorter events, 4.0 us)
Async XLA Ops:
  0.6 13.1 %collective-permute-start.3 = (bf16[2,128,1536]{2,1,0:T(8,128)(2,1)}, bf16[2,128,1536]{2,1,0:T(8,128)(2,1)S(1)}, u32[]{:S(2)}, u32[]{:S(2)}) collective-permute-start(bf16[2,128,1536]{2,1,0:T(8,128)(2,1)} %refs_10_.1), channel_id=1, source_target_pairs={{1,0},{0,1},{3,2},{2,3},{5,4},{4,5},{7,6},{6,7},{9,8},{8,9},{11,10... | collective-permute-start | bytes 2359304 | tf_op jit(solution)/shard_map/ppermute | solution.py:536
  1.1 12.5 %collective-permute-start.4 = (bf16[2,768,256]{2,1,0:T(8,128)(2,1)}, bf16[2,768,256]{2,1,0:T(8,128)(2,1)S(1)}, u32[]{:S(2)}, u32[]{:S(2)}) collective-permute-start(bf16[2,768,256]{2,1,0:T(8,128)(2,1)} %refs_12_.1), channel_id=1, source_target_pairs={{1,0},{0,1},{3,2},{2,3},{5,4},{4,5},{7,6},{6,7},{9,8},{8,9},{11,10... | collective-permute-start | bytes 2359304 | tf_op jit(solution)/shard_map/ppermute | solution.py:536
  2.1 8.8 %collective-permute-start = (bf16[192,128]{1,0:T(8,128)(2,1)S(1)}, bf16[192,128]{1,0:T(8,128)(2,1)S(1)}, u32[]{:S(2)}, u32[]{:S(2)}) collective-permute-start(bf16[192,128]{1,0:T(8,128)(2,1)S(1)} %round.1.refs_0_), channel_id=1, source_target_pairs={{0,8},{2,10},{4,12},{6,14},{8,0},{10,2},{12,4},{14,6},{16,24},{18,... | collective-permute-start | bytes 147464 | tf_op jit(solution)/shard_map/ppermute | solution.py:604
  5.2 5.9 %collective-permute-start.1 = (bf16[192,128]{1,0:T(8,128)(2,1)S(1)}, bf16[192,128]{1,0:T(8,128)(2,1)S(1)}, u32[]{:S(2)}, u32[]{:S(2)}) collective-permute-start(bf16[192,128]{1,0:T(8,128)(2,1)S(1)} %round.1.refs_0_), channel_id=1, source_target_pairs={{0,16},{2,18},{4,20},{6,22},{8,24},{10,26},{12,28},{14,30},{16,0},... | collective-permute-start | bytes 147464 | tf_op jit(solution)/shard_map/ppermute | solution.py:604
  7.8 5.9 %collective-permute-start.2 = (bf16[192,128]{1,0:T(8,128)(2,1)S(1)}, bf16[192,128]{1,0:T(8,128)(2,1)S(1)}, u32[]{:S(2)}, u32[]{:S(2)}) collective-permute-start(bf16[192,128]{1,0:T(8,128)(2,1)S(1)} %round.1.refs_0_), channel_id=1, source_target_pairs={{0,24},{2,26},{4,28},{6,30},{8,16},{10,18},{12,20},{14,22},{16,8},... | collective-permute-start | bytes 147464 | tf_op jit(solution)/shard_map/ppermute | solution.py:604
  13.8 3.6 %collective-permute-start.5 = (bf16[2,384,256]{2,1,0:T(8,128)(2,1)S(1)}, bf16[2,384,256]{2,1,0:T(8,128)(2,1)S(1)}, u32[]{:S(2)}, u32[]{:S(2)}) collective-permute-start(bf16[2,384,256]{2,1,0:T(8,128)(2,1)S(1)} %get-tuple-element.48.refs_0_), channel_id=1, source_target_pairs={{1,0},{0,1},{3,2},{2,3},{5,4},{4,5},{7,6},{6,7},{9,8},{8,9},{11,10... | collective-permute-start | bytes 1179656 | tf_op jit(solution)/shard_map/ppermute | solution.py:536
  13.8 6.3 %collective-permute-start.7 = (bf16[384,128]{1,0:T(8,128)(2,1)S(1)}, bf16[384,128]{1,0:T(8,128)(2,1)S(1)}, u32[]{:S(2)}, u32[]{:S(2)}) collective-permute-start(bf16[384,128]{1,0:T(8,128)(2,1)S(1)} %get-tuple-element.51.rows_ref.refs_0_.refs_3_), channel_id=1, source_target_pairs={{0,2},{1,5},{2,0},{3,7},{4,6},{5,1},{6,4},{7,3},{8,10},{9,13},{10,... | collective-permute-start | bytes 294920 | tf_op jit(solution)/shard_map/ppermute | solution.py:548
  15.4 5.8 %collective-permute-start.8 = (bf16[384,128]{1,0:T(8,128)(2,1)S(1)}, bf16[384,128]{1,0:T(8,128)(2,1)S(1)}, u32[]{:S(2)}, u32[]{:S(2)}) collective-permute-start(bf16[384,128]{1,0:T(8,128)(2,1)S(1)} %get-tuple-element.51.rows_ref.refs_0_.refs_3_), channel_id=1, source_target_pairs={{0,4},{1,3},{2,6},{3,1},{4,0},{5,7},{6,2},{7,5},{8,12},{9,11},{10,... | collective-permute-start | bytes 294920 | tf_op jit(solution)/shard_map/ppermute | solution.py:548
  16.9 6.2 %collective-permute-start.6 = (bf16[384,128]{1,0:T(8,128)(2,1)S(1)}, bf16[384,128]{1,0:T(8,128)(2,1)S(1)}, u32[]{:S(2)}, u32[]{:S(2)}) collective-permute-start(bf16[384,128]{1,0:T(8,128)(2,1)S(1)} %get-tuple-element.51.rows_ref.refs_0_.refs_3_), channel_id=1, source_target_pairs={{0,6},{1,7},{2,4},{3,5},{4,2},{5,3},{6,0},{7,1},{8,14},{9,15},{10,... | collective-permute-start | bytes 294920 | tf_op jit(solution)/shard_map/ppermute | solution.py:548
  21.2 2.4 %collective-permute-start.9 = (bf16[768,128]{1,0:T(8,128)(2,1)S(1)}, bf16[768,128]{1,0:T(8,128)(2,1)S(1)}, u32[]{:S(2)}, u32[]{:S(2)}) collective-permute-start(bf16[768,128]{1,0:T(8,128)(2,1)S(1)} %get-tuple-element.65), channel_id=1, source_target_pairs={{0,1},{1,0},{2,3},{3,2},{4,5},{5,4},{6,7},{7,6},{8,9},{9,8},{10,11... | collective-permute-start | bytes 589832 | tf_op jit(solution)/shard_map/ppermute | solution.py:530
  23.1 2.4 %collective-permute-start.10 = (bf16[384,128]{1,0:T(8,128)(2,1)S(1)}, bf16[384,128]{1,0:T(8,128)(2,1)S(1)}, u32[]{:S(2)}, u32[]{:S(2)}) collective-permute-start(bf16[384,128]{1,0:T(8,128)(2,1)S(1)} %gate.2.refs_0_.refs_6_), channel_id=1, source_target_pairs={{0,1},{1,0},{2,3},{3,2},{4,5},{5,4},{6,7},{7,6},{8,9},{9,8},{10,11... | collective-permute-start | bytes 294920 | tf_op jit(solution)/shard_map/ppermute | solution.py:530
  23.7 1.8 %copy-start = (bf16[2,128,1536]{2,1,0:T(8,128)(2,1)S(1)}, bf16[2,128,1536]{2,1,0:T(8,128)(2,1)}, u32[]{:S(2)}) copy-start(bf16[2,128,1536]{2,1,0:T(8,128)(2,1)} %refs_10_.1) | copy-start | bytes 2359300
  23.7 1.8 %copy-start.1 = (bf16[2,768,256]{2,1,0:T(8,128)(2,1)S(1)}, bf16[2,768,256]{2,1,0:T(8,128)(2,1)}, u32[]{:S(2)}) copy-start(bf16[2,768,256]{2,1,0:T(8,128)(2,1)} %refs_12_.1) | copy-start | bytes 2359300
  23.7 1.8 %copy-start.2 = (f32[192,128]{1,0:T(8,128)S(1)}, f32[192,128]{1,0:T(8,128)}, u32[]{:S(2)}) copy-start(f32[192,128]{1,0:T(8,128)} %latent_ref.3) | copy-start | bytes 294916
  23.7 1.8 %copy-start.3 = (f32[2,1536]{1,0:T(2,128)S(1)}, f32[2,1536]{1,0:T(2,128)}, u32[]{:S(2)}) copy-start(f32[2,1536]{1,0:T(2,128)} %gain_ref.3) | copy-start | bytes 36868
  29.2 4.6 %collective-permute-start.14 = (bf16[400,128]{1,0:T(8,128)(2,1)S(1)}, bf16[400,128]{1,0:T(8,128)(2,1)S(1)}, u32[]{:S(2)}, u32[]{:S(2)}) collective-permute-start(bf16[400,128]{1,0:T(8,128)(2,1)S(1)} %get-tuple-element.71.rows_ref.refs_0_.refs_2_), channel_id=1, source_target_pairs={{0,1},{1,0},{2,3},{3,2},{4,5},{5,4},{6,7},{7,6},{8,9},{9,8},{10,11... | collective-permute-start | bytes 307208 | tf_op jit(solution)/shard_map/ppermute | solution.py:530
  29.3 5.4 %collective-permute-start.12 = (bf16[400,128]{1,0:T(8,128)(2,1)S(1)}, bf16[400,128]{1,0:T(8,128)(2,1)S(1)}, u32[]{:S(2)}, u32[]{:S(2)}) collective-permute-start(bf16[400,128]{1,0:T(8,128)(2,1)S(1)} %get-tuple-element.71.rows_ref.refs_0_.refs_2_), channel_id=1, source_target_pairs={{0,2},{1,5},{2,0},{3,7},{4,6},{5,1},{6,4},{7,3},{8,10},{9,13},{10,... | collective-permute-start | bytes 307208 | tf_op jit(solution)/shard_map/ppermute | solution.py:548
  30.0 5.3 %collective-permute-start.13 = (bf16[400,128]{1,0:T(8,128)(2,1)S(1)}, bf16[400,128]{1,0:T(8,128)(2,1)S(1)}, u32[]{:S(2)}, u32[]{:S(2)}) collective-permute-start(bf16[400,128]{1,0:T(8,128)(2,1)S(1)} %get-tuple-element.71.rows_ref.refs_0_.refs_2_), channel_id=1, source_target_pairs={{0,4},{1,3},{2,6},{3,1},{4,0},{5,7},{6,2},{7,5},{8,12},{9,11},{10,... | collective-permute-start | bytes 307208 | tf_op jit(solution)/shard_map/ppermute | solution.py:548
  31.9 6.8 %collective-permute-start.11 = (bf16[400,128]{1,0:T(8,128)(2,1)S(1)}, bf16[400,128]{1,0:T(8,128)(2,1)S(1)}, u32[]{:S(2)}, u32[]{:S(2)}) collective-permute-start(bf16[400,128]{1,0:T(8,128)(2,1)S(1)} %get-tuple-element.71.rows_ref.refs_0_.refs_2_), channel_id=1, source_target_pairs={{0,6},{1,7},{2,4},{3,5},{4,2},{5,3},{6,0},{7,1},{8,14},{9,15},{10,... | collective-permute-start | bytes 307208 | tf_op jit(solution)/shard_map/ppermute | solution.py:548
  35.3 3.4 %collective-permute-start.15 = (bf16[800,128]{1,0:T(8,128)(2,1)S(1)}, bf16[800,128]{1,0:T(8,128)(2,1)S(1)}, u32[]{:S(2)}, u32[]{:S(2)}) collective-permute-start(bf16[800,128]{1,0:T(8,128)(2,1)S(1)} %get-tuple-element.81), channel_id=1, source_target_pairs={{0,1},{1,0},{2,3},{3,2},{4,5},{5,4},{6,7},{7,6},{8,9},{9,8},{10,11... | collective-permute-start | bytes 614408 | tf_op jit(solution)/shard_map/ppermute | solution.py:530
  38.6 1.4 %collective-permute-start.16 = (bf16[400,128]{1,0:T(8,128)(2,1)S(1)}, bf16[400,128]{1,0:T(8,128)(2,1)S(1)}, u32[]{:S(2)}, u32[]{:S(2)}) collective-permute-start(bf16[400,128]{1,0:T(8,128)(2,1)S(1)} %gate.3.refs_0_.refs_5_), channel_id=1, source_target_pairs={{0,1},{1,0},{2,3},{3,2},{4,5},{5,4},{6,7},{7,6},{8,9},{9,8},{10,11... | collective-permute-start | bytes 307208 | tf_op jit(solution)/shard_map/ppermute | solution.py:530
  41.9 1.3 %collective-permute-start.17 = (f32[104,128]{1,0:T(8,128)S(1)}, f32[104,128]{1,0:T(8,128)S(1)}, u32[]{:S(2)}, u32[]{:S(2)}) collective-permute-start(f32[104,128]{1,0:T(8,128)S(1)} %second_half.3.own_ref), channel_id=1, source_target_pairs={{0,1},{1,0},{2,3},{3,2},{4,5},{5,4},{6,7},{7,6},{8,9},{9,8},{10,11... | collective-permute-start | bytes 159752 | tf_op jit(solution)/shard_map/ppermute | solution.py:530
